TPU v7x, 512 devices: a whole 4x8x8 slice. The times are simulated.
512 devices in a mesh: dp: 32 (over y_hi, z, core), tensor: 16 (over x, y_lo).
Axes of the slice: x: 4, y: 8 (y_hi: 2, y_lo: 4; y = y_hi * 4 + y_lo), z: 8, core: 2. Of those that a mesh axis runs over, the one named last changes fastest.
Arguments:
- tokens: bfloat16 [32768, 8192], P('dp', 'tensor'), may hold values from -6 to 6
- value_weight: bfloat16 [8192, 512], P('tensor', 'dp'), may hold values from -0.0625 to 0.0625
- seq_lengths: int32 [32, 3], P('dp'), may hold values from 1 to 512, 1024 in all within a row
- task_ids: int32 [32, 2], replicated, may hold values from 0 to 31
- task_embed: bfloat16 [32, 1024], replicated, may hold values from -6 to 6
- hyper_in: bfloat16 [1024, 512], P(None, 'dp'), may hold values from -0.1875 to 0.1875
- head_a: bfloat16 [512, 65536], P('dp', 'tensor'), may hold values from -0.25 to 0.25
- head_b: bfloat16 [512, 4096], P('dp', 'tensor'), may hold values from -0.25 to 0.25
- cotangent: bfloat16 [32768, 512], P(('dp', 'tensor')), may hold values from -6 to 6
Outputs:
- values: bfloat16 [32768, 512], P(('dp', 'tensor'))
- grad_tokens: bfloat16 [32768, 8192], P('dp', 'tensor')
- grad_head_a: float32 [512, 65536], P('dp', 'tensor')
- grad_head_b: float32 [512, 4096], P('dp', 'tensor')
- grad_hyper_in: float32 [1024, 512], P(None, 'dp')
Inputs may be any that keep to these rules, and one draw needn't show every extreme that they name: `seq_lengths`: each row lists a group's 2 task batch lengths in order and then its count of padding rows; each row sums to 1024 and its largest entry is exactly 512.
All inputs are finite; a program needn't handle non-finite values.
Results may differ from a plain program's by a relative error of at most 0.0065.
Values may be sent and summed in bfloat16 or wider, within the bound.
No kernel may reach another device: no remote copies, remote signals or barrier semaphores. Data moves between devices by JAX's collectives and lax.ppermute only.
A program may use at most 64 MiB of HBM per device.

v0:
```python
import math

import jax
import jax.numpy as jnp
from jax import lax
from jax.sharding import PartitionSpec as P

D = 8192
KV = 512
R = 8
NTASK = 32
SEQS = 2


precise = lax.Precision.HIGHEST
inner_dims = (((1,), (1,)), ((), ()))
outer_dims = (((0,), (0,)), ((), ()))


def silu_slope(pre_act):
    sigma = jax.nn.sigmoid(pre_act)
    return sigma * (1.0 + pre_act * (1.0 - sigma))


def shards(
    tokens, value_weight, seq_lengths, task_ids, task_embed, hyper_in, head_a, head_b, cotangent
):
    group_index = lax.axis_index("dp")
    rows_total = tokens.shape[0]
    width_own = tokens.shape[1]
    outputs_own = KV // lax.axis_size("tensor")
    pre_act = jnp.dot(task_embed, hyper_in, preferred_element_type=jnp.float32)
    hidden = jax.nn.silu(pre_act).astype(jnp.bfloat16)
    down_sums, up_sums = lax.psum(
        (
            jnp.dot(hidden, head_a, preferred_element_type=jnp.float32),
            jnp.dot(hidden, head_b, preferred_element_type=jnp.float32),
        ),
        "dp",
    )
    adapt_down = (down_sums * (1.0 / math.sqrt(D))).astype(jnp.bfloat16)
    adapt_up = (up_sums * (1.0 / math.sqrt(R))).astype(jnp.bfloat16)
    chosen = lax.dynamic_index_in_dim(task_ids, group_index, 0, keepdims=False)
    lengths = seq_lengths[0]
    finish = jnp.cumsum(lengths)
    anchor = finish - lengths
    places = jnp.arange(rows_total, dtype=jnp.int32)[:, None]
    inside = (places >= anchor[None, :SEQS]) & (places < finish[None, :SEQS])
    col_mask = jnp.repeat(inside.astype(jnp.float32), R, axis=1)
    down_cat = (
        jnp.take(adapt_down, chosen, axis=0)
        .reshape(SEQS, width_own, R)
        .transpose(1, 0, 2)
        .reshape(width_own, SEQS * R)
    )
    up_pick = jnp.take(adapt_up, chosen, axis=0)
    up_whole = lax.all_gather(up_pick, "tensor", axis=1, tiled=True)
    up_cat = up_whole.reshape(SEQS, KV, R).transpose(1, 0, 2).reshape(KV, SEQS * R)
    weight_full = lax.all_gather(value_weight, "dp", axis=1, tiled=True)
    frozen = jnp.dot(tokens, weight_full, preferred_element_type=jnp.float32)
    low_part = jnp.dot(tokens, down_cat, preferred_element_type=jnp.float32) * col_mask
    frozen_rows, low_rows = (
        lax.psum_scatter(frozen, "tensor", scatter_dimension=0, tiled=True),
        lax.psum_scatter(low_part, "tensor", scatter_dimension=0, tiled=True),
    )
    adapter = lax.dot_general(low_rows, up_cat.astype(jnp.float32), inner_dims, precision=precise)
    values = (frozen_rows + adapter).astype(jnp.bfloat16)
    grad_full = lax.all_gather(cotangent, "tensor", axis=0, tiled=True)
    back_low = (jnp.dot(grad_full, up_cat, preferred_element_type=jnp.float32) * col_mask).astype(
        jnp.bfloat16
    )
    adapter_back = lax.dot_general(
        back_low, down_cat, inner_dims, preferred_element_type=jnp.float32
    )
    frozen_back = lax.dot_general(
        grad_full, weight_full, inner_dims, preferred_element_type=jnp.float32
    )
    grad_tokens = (frozen_back + adapter_back).astype(jnp.bfloat16)
    down_grad = lax.dot_general(tokens, back_low, outer_dims, preferred_element_type=jnp.float32)
    up_part = lax.dot_general(
        cotangent.astype(jnp.float32), low_rows, outer_dims, precision=precise
    )
    up_grad = lax.psum_scatter(up_part, "tensor", scatter_dimension=0, tiled=True)
    down_seq = down_grad.reshape(width_own, SEQS, R).transpose(1, 0, 2).reshape(SEQS, width_own * R)
    up_seq = up_grad.reshape(outputs_own, SEQS, R).transpose(1, 0, 2).reshape(SEQS, outputs_own * R)
    task_range = jnp.arange(NTASK, dtype=jnp.int32)[None, :]
    one_hot = (chosen[:, None] == task_range).astype(jnp.float32)
    down_task, up_task = lax.psum(
        (
            jnp.dot(one_hot.T, down_seq, precision=precise),
            jnp.dot(one_hot.T, up_seq, precision=precise),
        ),
        "dp",
    )
    down_task = down_task * (1.0 / math.sqrt(D))
    up_task = up_task * (1.0 / math.sqrt(R))
    hidden_wide = hidden.astype(jnp.float32)
    grad_head_a = jnp.dot(hidden_wide.T, down_task, precision=precise)
    grad_head_b = jnp.dot(hidden_wide.T, up_task, precision=precise)
    down_hidden = lax.dot_general(
        down_task, head_a.astype(jnp.float32), inner_dims, precision=precise
    )
    up_hidden = lax.dot_general(up_task, head_b.astype(jnp.float32), inner_dims, precision=precise)
    grad_hidden = lax.psum(down_hidden + up_hidden, "tensor")
    grad_pre = grad_hidden * silu_slope(pre_act)
    grad_hyper_in = lax.dot_general(
        task_embed.astype(jnp.float32), grad_pre, outer_dims, precision=precise
    )
    return (values, grad_tokens, grad_head_a, grad_head_b, grad_hyper_in)


def solution(mesh):
    placed = (
        P("dp", "tensor"),
        P("tensor", "dp"),
        P("dp", None),
        P(),
        P(),
        P(None, "dp"),
        P("dp", "tensor"),
        P("dp", "tensor"),
        P(("dp", "tensor"), None),
    )
    return jax.shard_map(
        shards,
        mesh=mesh,
        in_specs=placed,
        out_specs=(
            P(("dp", "tensor"), None),
            P("dp", "tensor"),
            P("dp", "tensor"),
            P("dp", "tensor"),
            P(None, "dp"),
        ),
        check_vma=False,
    )
```

profile of v0, /device:TPU:56, one launch (start us, length us, event | category | flops | bytes accessed | tf_op | source)
XLA Modules:
  0.0 1365.0 jit_solution(2596191972782572090)
XLA Ops:
  7.2 1.1 multiply_convert_fusion.2
  8.3 2.0 fusion.36
  10.3 0.9 dynamic-slice_reduce_fusion
  12.8 342.5 %all-reduce.5.cloned.1.call-done = f32[32,4096]{1,0:T(8,128)} async-done(((f32[32,4096]{1,0:T(8,128)}), f32[32,4096]{1,0:T(8,128)}) %all-reduce.5.cloned.1.call-update) | async-done | bytes 524304 | tf_op jit(solution)/shard_map/psum | solution.py:34
  355.3 1.1 multiply_convert_fusion
  357.9 1.0 copy.22
  359.0 80.0 %reduce-scatter.10.cloned.1.call-done = f32[64,16]{1,0:T(8,128)} async-done(((f32[1024,16]{1,0:T(8,128)}), f32[64,16]{1,0:T(8,128)}) %reduce-scatter.10.cloned.1.call-update) | async-done | bytes 4112
  439.1 1.0 convolution_bitcast_fusion.3
  441.7 83.5 %reduce-scatter.12.cloned.1.call-done = f32[32,16]{1,0:T(8,128)} async-done(((f32[512,16]{1,0:T(8,128)}), f32[32,16]{1,0:T(8,128)}) %reduce-scatter.12.cloned.1.call-update) | async-done | bytes 2064
  526.2 0.9 fusion.25
  527.7 310.9 %all-reduce.9.cloned.1.call-done = (f32[32,256]{1,0:T(8,128)}, f32[32,256]{1,0:T(8,128)}) async-done(((f32[32,256]{1,0:T(8,128)}, f32[32,256]{1,0:T(8,128)}), (f32[32,256]{1,0:T(8,128)}, f32[32,256]{1,0:T(8,128)})) %all-reduce.9.cloned.1.call-update) | async-done | bytes 65552 | tf_op jit(solution)/shard_map/psum | solution.py:34
  840.1 35.2 %all_gather.10 = bf16[2,4096]{1,0:T(2,128)(2,1)S(1)} all-gather(bf16[2,256]{1,0:T(2,128)(2,1)S(1)} %broadcast_select_fusion), channel_id=1, replica_groups=mesh['dp'=32,'tensor'=16] {'tensor'}, dimensions={1}, use_global_device_ids=true | all-gather | bytes 17408 | tf_op jit(solution)/shard_map/all_gather | solution.py:57
  875.7 42.6 %all-gather.2.cloned.1.call-done = bf16[1024,512]{1,0:T(8,128)(2,1)} async-done(((bf16[64,512]{1,0:T(8,128)(2,1)}), bf16[1024,512]{1,0:T(8,128)(2,1)}) %all-gather.2.cloned.1.call-update) | async-done | bytes 1048592 | tf_op jit(solution)/shard_map/all_gather | solution.py:68
  918.2 1.6 fusion.3
  920.6 1.3 fusion.26
  922.0 53.9 %all_gather.9 = bf16[512,512]{0,1:T(8,128)(2,1)S(1)} all-gather(bf16[512,16]{0,1:T(8,128)(2,1)S(1)} %copy-done.8), channel_id=1, replica_groups=mesh['dp'=32,'tensor'=16] {'dp'}, dimensions={1}, use_global_device_ids=true | all-gather | bytes 540672 | tf_op jit(solution)/shard_map/all_gather | solution.py:59
  975.9 2.1 fusion.35
  979.5 1.4 add_convert_fusion
  981.0 285.4 %all-reduce.7.cloned.1.call-done = f32[32,4096]{1,0:T(8,128)} async-done(((f32[32,4096]{1,0:T(8,128)}), f32[32,4096]{1,0:T(8,128)}) %all-reduce.7.cloned.1.call-update) | async-done | bytes 524304 | tf_op jit(solution)/shard_map/psum | solution.py:88
  1266.4 1.4 fusion.4
  1267.9 37.3 %psum.39 = f32[32,16]{0,1:T(8,128)S(1)} all-reduce(f32[32,16]{0,1:T(8,128)S(1)} %convolution_add_fusion.1), channel_id=1, replica_groups=mesh['dp'=32,'tensor'=16] {'tensor'}, use_global_device_ids=true, to_apply=%region_8.9 | all-reduce | flops 512 | bytes 4096 | tf_op jit(solution)/shard_map/psum | solution.py:104
  1306.0 2.1 fusion.6
  1308.1 48.3 %reduce-scatter.8.cloned.1.call-done = f32[64,512]{1,0:T(8,128)} async-done(((f32[1024,512]{1,0:T(8,128)}), f32[64,512]{1,0:T(8,128)}) %reduce-scatter.8.cloned.1.call-update) | async-done | bytes 131088 | tf_op jit(solution)/shard_map/reduce_scatter | solution.py:63
  1356.4 1.7 fusion
  (61 shorter events, 11.6 us)
Async XLA Ops:
  7.2 350.4 %copy-start = (bf16[1024,512]{1,0:T(8,128)(2,1)S(1)}, bf16[1024,512]{1,0:T(8,128)(2,1)}, u32[]{:S(2)}) copy-start(bf16[1024,512]{1,0:T(8,128)(2,1)} %param.9) | copy-start | bytes 3145732
  7.2 348.1 %all-reduce.5.cloned.1.call-start = ((), (), s32[]{:S(2)}) async-start(), calls=%async_computation.4 | async-start | bytes 1048576 | tf_op jit(solution)/shard_map/psum | solution.py:34
  10.3 428.8 %reduce-scatter.10.cloned.1.call-start = ((), (), s32[]{:S(2)}) async-start(), calls=%async_computation.7 | async-start | bytes 557056
  12.8 426.3 %copy-start.3 = (bf16[64,512]{1,0:T(8,128)(2,1)S(1)}, bf16[64,512]{1,0:T(8,128)(2,1)}, u32[]{:S(2)}) copy-start(bf16[64,512]{1,0:T(8,128)(2,1)} %param.17) | copy-start | bytes 196612
  356.4 84.5 %copy-start.7 = (bf16[16,256]{1,0:T(8,128)(2,1)S(1)}, bf16[16,256]{1,0:T(8,128)(2,1)}, u32[]{:S(2)}) copy-start(bf16[16,256]{1,0:T(8,128)(2,1)} %param.16) | copy-start | bytes 24580
  359.0 166.2 %reduce-scatter.12.cloned.1.call-start = ((), (), s32[]{:S(2)}) async-start(), calls=%async_computation.8 | async-start | bytes 278528
  440.9 397.8 %all-reduce.9.cloned.1.call-start = ((), (), s32[]{:S(2)}) async-start(), calls=%async_computation.9 | async-start | bytes 131072 | tf_op jit(solution)/shard_map/psum | solution.py:34
  527.1 391.2 %all-gather.2.cloned.1.call-start = ((), (), s32[]{:S(2)}) async-start(), calls=%async_computation.5 | async-start | bytes 1114112 | tf_op jit(solution)/shard_map/all_gather | solution.py:68
  527.7 738.7 %all-reduce.7.cloned.1.call-start = ((), (), s32[]{:S(2)}) async-start(), calls=%async_computation.6 | async-start | bytes 1048576 | tf_op jit(solution)/shard_map/psum | solution.py:88
  875.7 46.3 %copy-start.8 = (bf16[512,16]{0,1:T(8,128)(2,1)S(1)}, bf16[512,16]{0,1:T(8,128)(2,1)}, u32[]{:S(2)}) copy-start(bf16[512,16]{0,1:T(8,128)(2,1)} %param.10) | copy-start | bytes 49156
  921.9 434.5 %reduce-scatter.8.cloned.1.call-start = ((), (), s32[]{:S(2)}) async-start(), calls=%async_computation.3 | async-start | bytes 2228224 | tf_op jit(solution)/shard_map/reduce_scatter | solution.py:63
  975.9 2.1 copy-start.5
  975.9 2.9 copy-start.1
  979.5 286.9 %copy-start.2 = (bf16[16,4096]{1,0:T(8,128)(2,1)S(1)}, bf16[16,4096]{1,0:T(8,128)(2,1)}, u32[]{:S(2)}) copy-start(bf16[16,4096]{1,0:T(8,128)(2,1)} %param.15) | copy-start | bytes 393220
  979.5 325.7 %copy-start.6 = (bf16[32,1024]{1,0:T(8,128)(2,1)S(1)}, bf16[32,1024]{1,0:T(8,128)(2,1)}, u32[]{:S(2)}) copy-start(bf16[32,1024]{1,0:T(8,128)(2,1)} %param.13) | copy-start | bytes 196612
  979.5 376.9 %copy-start.4 = (f32[64,16]{1,0:T(8,128)S(1)}, f32[64,16]{1,0:T(8,128)}, u32[]{:S(2)}) copy-start(f32[64,16]{1,0:T(8,128)} %reduce-scatter.10.cloned.1.call-done) | copy-start | bytes 12292
Sparse Core Ops, SparseCore 0:
  11.5 343.7 all-reduce.4
  359.1 79.9 reduce-scatter.9
  442.4 82.7 reduce-scatter.11
  528.9 309.7 all-reduce.8
  840.6 77.6 all-gather.1
  922.1 344.2 all-reduce.6
  1269.4 86.9 reduce-scatter.7
where the time goes:
time: 1370 us; the launch traced here: 1360 us
  waiting for transfers between devices  1190 us (87%)
  blocking collectives  126 us (9%)
  matrix products  20.3 us (1%)
  between operations  14.3 us (1%)
    psum x2, waiting for transfers between devices, shards(): lax.psum((jnp.dot(hidden, head_a, preferred_element_type=jnp.float32), jn...  653 us
    psum x1, waiting for transfers between devices, shards(): lax.psum((jnp.dot(one_hot.T, down_seq, precision=precise), jnp.dot(one_ho...  285 us
    unnamed x9, waiting for transfers between devices  164 us
    all_gather x1, blocking collectives, shards(): weight_full = lax.all_gather(value_weight, 'dp', axis=1, tiled=True)  53.9 us
    reduce_scatter x1, waiting for transfers between devices, shards(): lax.psum_scatter(frozen, 'tensor', scatter_dimension=0, tiled=True)  48.3 us
    all_gather x1, waiting for transfers between devices, shards(): grad_full = lax.all_gather(cotangent, 'tensor', axis=0, tiled=True)  42.6 us
    psum x1, blocking collectives, shards(): grad_hidden = lax.psum(down_hidden + up_hidden, 'tensor')  37.3 us
    all_gather x1, blocking collectives, shards(): up_whole = lax.all_gather(up_pick, 'tensor', axis=1, tiled=True)  35.2 us
  transfers between devices with their start and end apart: 7, of which 7 were waited for; matrix products, arithmetic and copies ran while one was open for 1% of the time, Pallas kernels for 0%

commit v1 on v0

v1 whole, which is shorter than its diff:
```python
import math

import jax
import jax.numpy as jnp
from jax import lax
from jax.sharding import PartitionSpec as P

D = 8192
KV = 512
R = 8
NTASK = 32
SEQS = 2
ADA = SEQS * R

precise = lax.Precision.HIGHEST
inner_dims = (((1,), (1,)), ((), ()))
outer_dims = (((0,), (0,)), ((), ()))
bf16 = jnp.bfloat16
f32 = jnp.float32

Y_RUN = 4


def silu_slope(pre_act):
    sigma = jax.nn.sigmoid(pre_act)
    return sigma * (1.0 + pre_act * (1.0 - sigma))


def spread(block, axes, count, **kw):
    copies = jnp.broadcast_to(block[None], (count,) + block.shape)
    return lax.all_to_all(copies, axes, 0, 0, **kw)


def shards(
    tokens, value_weight, seq_lengths, task_ids, task_embed, hyper_in, head_a, head_b, cotangent
):
    n_dp = lax.axis_size("dp")
    n_tensor = lax.axis_size("tensor")
    n_x = n_tensor // Y_RUN
    rows_total, width_own = tokens.shape
    rows_own = rows_total // n_tensor
    outputs_own = KV // n_tensor
    along_y = [[x * Y_RUN + y for y in range(Y_RUN)] for x in range(n_x)]
    along_x = [[x * Y_RUN + y for x in range(n_x)] for y in range(Y_RUN)]

    weight_t = spread(value_weight.T, "dp", n_dp).reshape(KV, width_own)

    cot_run = spread(cotangent, "tensor", Y_RUN, axis_index_groups=along_y)
    cot_full = spread(
        cot_run.reshape(Y_RUN * rows_own, KV), "tensor", n_x, axis_index_groups=along_x
    ).reshape(rows_total, KV)

    pre_act = jnp.dot(task_embed, hyper_in, preferred_element_type=f32)
    hidden = jax.nn.silu(pre_act).astype(bf16)
    every_id = task_ids.reshape(n_dp * SEQS)
    one_hot = (every_id[:, None] == jnp.arange(NTASK, dtype=jnp.int32)[None, :]).astype(bf16)
    hidden_pick = jnp.dot(one_hot, hidden, preferred_element_type=f32).astype(bf16)
    terms = jnp.concatenate(
        (
            jnp.dot(hidden_pick, head_a, preferred_element_type=f32),
            jnp.dot(hidden_pick, head_b, preferred_element_type=f32),
        ),
        axis=1,
    ).astype(bf16)
    down_width = width_own * R
    up_width = outputs_own * R
    sums = jnp.sum(
        lax.all_to_all(terms.reshape(n_dp, SEQS, -1), "dp", 0, 0).astype(f32), axis=0
    )
    down_pick = (sums[:, :down_width] * (1.0 / math.sqrt(D))).astype(bf16)
    up_pick = (sums[:, down_width:] * (1.0 / math.sqrt(R))).astype(bf16)
    down_cat = down_pick.reshape(SEQS, width_own, R).transpose(1, 0, 2).reshape(width_own, ADA)

    lengths = seq_lengths[0]
    finish = jnp.cumsum(lengths)
    anchor = finish - lengths
    places = jnp.arange(rows_total, dtype=jnp.int32)[:, None]
    inside = (places >= anchor[None, :SEQS]) & (places < finish[None, :SEQS])
    col_mask = jnp.repeat(inside.astype(f32), R, axis=1)

    frozen = lax.dot_general(tokens, weight_t, inner_dims, preferred_element_type=f32).astype(bf16)
    low_part = (jnp.dot(tokens, down_cat, preferred_element_type=f32) * col_mask).astype(bf16)
    up_part = lax.dot_general(cot_full, low_part, outer_dims, preferred_element_type=f32).astype(
        bf16
    )
    low_lines = rows_own * ADA // KV
    up_lines = outputs_own * ADA // KV
    pick_lines = SEQS * up_width // KV
    block = jnp.concatenate(
        (
            frozen.reshape(n_tensor, rows_own, KV),
            low_part.reshape(n_tensor, low_lines, KV),
            up_part.reshape(n_tensor, up_lines, KV),
            jnp.broadcast_to(up_pick.reshape(1, pick_lines, KV), (n_tensor, pick_lines, KV)),
        ),
        axis=1,
    ).reshape(n_x, Y_RUN, -1, KV)
    summed = rows_own + low_lines + up_lines
    from_x = lax.all_to_all(block, "tensor", 0, 0, axis_index_groups=along_x)
    x_sums = jnp.sum(from_x[:, :, :summed].astype(f32), axis=0).astype(bf16)
    x_picks = from_x[:, :, summed:].transpose(1, 0, 2, 3).reshape(Y_RUN, n_x * pick_lines, KV)
    from_y = lax.all_to_all(
        jnp.concatenate((x_sums, x_picks), axis=1), "tensor", 0, 0, axis_index_groups=along_y
    )
    whole = jnp.sum(from_y[:, :summed].astype(f32), axis=0)
    frozen_rows = whole[:rows_own]
    low_rows = whole[rows_own : rows_own + low_lines].reshape(rows_own, ADA)
    up_grad = whole[rows_own + low_lines :].reshape(outputs_own, ADA)
    up_cat = (
        from_y[:, summed:]
        .reshape(Y_RUN, n_x, SEQS, outputs_own, R)
        .transpose(1, 0, 3, 2, 4)
        .reshape(KV, ADA)
    )

    back_low = (jnp.dot(cot_full, up_cat, preferred_element_type=f32) * col_mask).astype(bf16)
    down_grad = lax.dot_general(tokens, back_low, outer_dims, preferred_element_type=f32)
    down_seq = down_grad.reshape(width_own, SEQS, R).transpose(1, 0, 2).reshape(SEQS, down_width)
    up_seq = up_grad.reshape(outputs_own, SEQS, R).transpose(1, 0, 2).reshape(SEQS, up_width)
    grads = spread(
        jnp.concatenate((down_seq, up_seq), axis=1).astype(bf16), "dp", n_dp
    ).reshape(n_dp * SEQS, -1)
    down_all = grads[:, :down_width]
    up_all = grads[:, down_width:]

    down_scale = 1.0 / math.sqrt(D)
    up_scale = 1.0 / math.sqrt(R)
    hidden_part = lax.dot_general(down_all, head_a, inner_dims, preferred_element_type=f32)
    hidden_part = hidden_part * down_scale + up_scale * lax.dot_general(
        up_all, head_b, inner_dims, preferred_element_type=f32
    )
    by_task = lax.dot_general(
        one_hot.astype(f32), hidden_part, outer_dims, precision=precise
    )
    grad_hidden = jnp.sum(spread(by_task, "tensor", n_tensor), axis=0)
    grad_head_a = down_scale * lax.dot_general(
        hidden_pick, down_all, outer_dims, preferred_element_type=f32
    )
    grad_head_b = up_scale * lax.dot_general(
        hidden_pick, up_all, outer_dims, preferred_element_type=f32
    )
    grad_pre = grad_hidden * silu_slope(pre_act)
    grad_hyper_in = lax.dot_general(
        task_embed.astype(f32), grad_pre, outer_dims, precision=precise
    )

    adapter = lax.dot_general(
        low_rows.astype(f32), up_cat.astype(f32), inner_dims, precision=precise
    )
    values = (frozen_rows + adapter).astype(bf16)
    adapter_back = lax.dot_general(back_low, down_cat, inner_dims, preferred_element_type=f32)
    frozen_back = jnp.dot(cot_full, weight_t, preferred_element_type=f32)
    grad_tokens = (frozen_back + adapter_back).astype(bf16)
    return (values, grad_tokens, grad_head_a, grad_head_b, grad_hyper_in)


def solution(mesh):
    placed = (
        P("dp", "tensor"),
        P("tensor", "dp"),
        P("dp", None),
        P(),
        P(),
        P(None, "dp"),
        P("dp", "tensor"),
        P("dp", "tensor"),
        P(("dp", "tensor"), None),
    )
    return jax.shard_map(
        shards,
        mesh=mesh,
        in_specs=placed,
        out_specs=(
            P(("dp", "tensor"), None),
            P("dp", "tensor"),
            P("dp", "tensor"),
            P("dp", "tensor"),
            P(None, "dp"),
        ),
        check_vma=False,
    )
```

time: 1370 us -> 177 us (0.13)
  the two profiles are of different devices: /device:TPU:56 before, /device:TPU:2 now
where the time goes in v1:
time: 177 us; the launch traced here: 176 us
  waiting for transfers between devices  73.1 us (41%)
  starting transfers between devices  41.4 us (23%)
  blocking collectives  30.5 us (17%)
  matrix products  12.6 us (7%)
  local copies, waits for them, and re-layouts  11.8 us (7%)
  other arithmetic  5.54 us (3%)
    all_to_all x5, waiting for transfers between devices, spread(): return lax.all_to_all(copies, axes, 0, 0, **kw)  54.2 us
    all_to_all x5, starting transfers between devices, spread(): return lax.all_to_all(copies, axes, 0, 0, **kw)  36.6 us
    all_to_all x1, waiting for transfers between devices, shards(): lax.all_to_all(terms.reshape(n_dp, SEQS, -1), 'dp', 0, 0).astype(f32)  18.9 us
    all_to_all x1, blocking collectives, shards(): from_x = lax.all_to_all(block, 'tensor', 0, 0, axis_index_groups=along_x)  16.4 us
    all_to_all x1, blocking collectives, shards(): lax.all_to_all(jnp.concatenate((x_sums, x_picks), axis=1), 'tensor', 0, 0...  14.1 us
    broadcast_in_dim x4, local copies, waits for them, and re-layouts, spread(): copies = jnp.broadcast_to(block[None], (count,) + block.shape)  5.42 us
    all_to_all x1, starting transfers between devices, shards(): lax.all_to_all(terms.reshape(n_dp, SEQS, -1), 'dp', 0, 0).astype(f32)  4.8 us
  transfers between devices with their start and end apart: 6, of which 6 were waited for; matrix products, arithmetic and copies ran while one was open for 9% of the time, Pallas kernels for 0%

profile of v1, /device:TPU:2, one launch (start us, length us, event | category | flops | bytes accessed | tf_op | source)
XLA Modules:
  0.0 175.9 jit_solution(1326492650932667900)
XLA Ops:
  0.6 1.6 broadcast_in_dim.20
  2.3 5.0 %all-to-all-start.2 = ((bf16[4,64,512]{2,1,0:T(8,128)(2,1)}), bf16[4,64,512]{2,1,0:T(8,128)(2,1)S(1)}, u32[]{:S(2)}, u32[]{:S(2)}) async-start(bf16[4,64,512]{2,1,0:T(8,128)(2,1)} %broadcast_in_dim.20), calls=%async_computation.2 | async-start | bytes 524288 | tf_op jit(solution)/shard_map/all_to_all | solution.py:31
  8.2 1.0 fusion.29
  9.3 6.9 %all-to-all-done.2 = bf16[4,64,512]{2,1,0:T(8,128)(2,1)S(1)} async-done(((bf16[4,64,512]{2,1,0:T(8,128)(2,1)}), bf16[4,64,512]{2,1,0:T(8,128)(2,1)S(1)}, u32[]{:S(2)}, u32[]{:S(2)}) %all-to-all-start.2) | async-done | bytes 262176 | tf_op jit(solution)/shard_map/all_to_all | solution.py:31
  16.2 1.6 broadcast_in_dim.18
  17.8 14.8 %all-to-all-start = ((bf16[32,16,512]{2,1,0:T(8,128)(2,1)}), bf16[32,16,512]{2,1,0:T(8,128)(2,1)S(1)}, u32[]{:S(2)}, u32[]{:S(2)}) async-start(bf16[32,16,512]{2,1,0:T(8,128)(2,1)} %broadcast_in_dim.18), calls=%async_computation | async-start | bytes 1048576 | tf_op jit(solution)/shard_map/all_to_all | solution.py:31
  33.5 1.3 pad_maximum_fusion.1
  34.8 18.1 %all-to-all-done = bf16[32,16,512]{2,1,0:T(8,128)(2,1)S(1)} async-done(((bf16[32,16,512]{2,1,0:T(8,128)(2,1)}), bf16[32,16,512]{2,1,0:T(8,128)(2,1)S(1)}, u32[]{:S(2)}, u32[]{:S(2)}) %all-to-all-start) | async-done | bytes 524320 | tf_op jit(solution)/shard_map/all_to_all | solution.py:31
  52.8 4.8 %all-to-all-start.1 = ((bf16[32,2,4352]{2,1,0:T(2,128)(2,1)}), bf16[32,2,4352]{2,1,0:T(2,128)(2,1)S(1)}, u32[]{:S(2)}, u32[]{:S(2)}) async-start(bf16[32,2,4352]{2,1,0:T(2,128)(2,1)} %pad_maximum_fusion.1), calls=%async_computation.1 | async-start | bytes 1114112 | tf_op jit(solution)/shard_map/all_to_all | solution.py:68
  59.5 18.9 %all-to-all-done.1 = bf16[32,2,4352]{2,1,0:T(2,128)(2,1)S(1)} async-done(((bf16[32,2,4352]{2,1,0:T(2,128)(2,1)}), bf16[32,2,4352]{2,1,0:T(2,128)(2,1)S(1)}, u32[]{:S(2)}, u32[]{:S(2)}) %all-to-all-start.1) | async-done | bytes 557088 | tf_op jit(solution)/shard_map/all_to_all | solution.py:68
  78.4 1.1 broadcast_in_dim.22
  79.5 4.8 %all-to-all-start.3 = ((bf16[4,256,512]{2,1,0:T(8,128)(2,1)}), bf16[4,256,512]{2,1,0:T(8,128)(2,1)S(1)}, u32[]{:S(2)}, u32[]{:S(2)}) async-start(bf16[4,256,512]{2,1,0:T(8,128)(2,1)} %broadcast_in_dim.22), calls=%async_computation.3 | async-start | bytes 2097152 | tf_op jit(solution)/shard_map/all_to_all | solution.py:31
  84.3 1.5 convert_reduce_fusion
  87.2 9.8 %all-to-all-done.3 = bf16[4,256,512]{2,1,0:T(8,128)(2,1)S(1)} async-done(((bf16[4,256,512]{2,1,0:T(8,128)(2,1)}), bf16[4,256,512]{2,1,0:T(8,128)(2,1)S(1)}, u32[]{:S(2)}, u32[]{:S(2)}) %all-to-all-start.3) | async-done | bytes 1048608 | tf_op jit(solution)/shard_map/all_to_all | solution.py:31
  98.5 16.4 %all_to_all.40 = bf16[4,4,68,512]{3,1,2,0:T(4,128)(2,1)S(1)} all-to-all(bf16[4,4,68,512]{3,1,2,0:T(4,128)(2,1)S(1)} %pad_maximum_fusion), channel_id=1, replica_groups={{0,4,8,12},{1,5,9,13},{2,6,10,14},{3,7,11,15},{16,20,24,28},{17,21,25,2..., dimensions={0} | all-to-all | bytes 2228224 | tf_op jit(solution)/shard_map/all_to_all | solution.py:99
  115.8 14.1 %all_to_all.41 = bf16[4,71,512]{2,1,0:T(8,128)(2,1)S(1)} all-to-all(bf16[4,71,512]{2,1,0:T(8,128)(2,1)S(1)} %copy.50), channel_id=1, replica_groups={{0,1,2,3},{4,5,6,7},{8,9,10,11},{12,13,14,15},{16,17,18,19},{20,21,22,2..., dimensions={0} | all-to-all | bytes 581632 | tf_op jit(solution)/shard_map/all_to_all | solution.py:102
  131.9 1.1 broadcast_in_dim.25
  133.0 3.9 %all-to-all-start.6 = ((bf16[32,2,4352]{2,1,0:T(2,128)(2,1)}), bf16[32,2,4352]{2,1,0:T(2,128)(2,1)S(1)}, u32[]{:S(2)}, u32[]{:S(2)}) async-start(bf16[32,2,4352]{2,1,0:T(2,128)(2,1)} %broadcast_in_dim.25), calls=%async_computation.6 | async-start | bytes 1114112 | tf_op jit(solution)/shard_map/all_to_all | solution.py:31
  136.9 2.1 %fusion.30 = f32[1024,512]{1,0:T(8,128)} fusion(bf16[1024,512]{1,0:T(8,128)(2,1)S(1)} %bitcast.87, bf16[512,512]{1,0:T(8,128)(2,1)S(1)} %bitcast.89), kind=kOutput, calls=%fused_computation.64 | convolution fusion | flops 536870912 | bytes 3670016 | tf_op jit(solution)/shard_map/dot_general | solution.py:152
  139.9 3.0 %add_convert_fusion = bf16[1024,512]{1,0:T(8,128)(2,1)} fusion(f32[1024,512]{1,0:T(8,128)} %fusion.30, bf16[1024,16]{0,1:T(8,128)(2,1)S(1)} %fusion.4, bf16[512,2,8]{0,2,1:T(8,128)(2,1)S(1)} %copy.41), kind=kOutput, calls=%fused_computation.2 | convolution fusion | flops 17825792 | bytes 3194880 | tf_op jit(solution)/shard_map/dot_general | solution.py:151
  142.9 13.5 %all-to-all-done.6 = bf16[32,2,4352]{2,1,0:T(2,128)(2,1)S(1)} async-done(((bf16[32,2,4352]{2,1,0:T(2,128)(2,1)}), bf16[32,2,4352]{2,1,0:T(2,128)(2,1)S(1)}, u32[]{:S(2)}, u32[]{:S(2)}) %all-to-all-start.6) | async-done | bytes 557088 | tf_op jit(solution)/shard_map/all_to_all | solution.py:31
  156.9 0.9 convolution_multiply_fusion
  158.9 8.1 %all-to-all-start.7 = ((f32[16,1,512]{2,1,0:T(1,128)}), f32[16,1,512]{2,1,0:T(1,128)S(1)}, u32[]{:S(2)}, u32[]{:S(2)}) async-start(f32[16,1,512]{2,1,0:T(1,128)} %reshape.115), calls=%async_computation.7 | async-start | bytes 65536 | tf_op jit(solution)/shard_map/all_to_all | solution.py:31
  167.8 5.9 %all-to-all-done.7 = f32[16,1,512]{2,1,0:T(1,128)S(1)} async-done(((f32[16,1,512]{2,1,0:T(1,128)}), f32[16,1,512]{2,1,0:T(1,128)S(1)}, u32[]{:S(2)}, u32[]{:S(2)}) %all-to-all-start.7) | async-done | bytes 32800 | tf_op jit(solution)/shard_map/all_to_all | solution.py:31
  (78 shorter events, 14.7 us)
Async XLA Ops:
  0.6 57.3 %copy-start = (bf16[1024,512]{1,0:T(8,128)(2,1)S(1)}, bf16[1024,512]{1,0:T(8,128)(2,1)}, u32[]{:S(2)}) copy-start(bf16[1024,512]{1,0:T(8,128)(2,1)} %param.9) | copy-start | bytes 3145732
  2.3 30.3 %copy-start.7 = (bf16[16,256]{1,0:T(8,128)(2,1)S(1)}, bf16[16,256]{1,0:T(8,128)(2,1)}, u32[]{:S(2)}) copy-start(bf16[16,256]{1,0:T(8,128)(2,1)} %param.16) | copy-start | bytes 24580
  2.3 30.5 %copy-start.5 = (bf16[16,4096]{1,0:T(8,128)(2,1)S(1)}, bf16[16,4096]{1,0:T(8,128)(2,1)}, u32[]{:S(2)}) copy-start(bf16[16,4096]{1,0:T(8,128)(2,1)} %param.15) | copy-start | bytes 393220
  2.3 13.9 %all-to-all-start.2 = ((bf16[4,64,512]{2,1,0:T(8,128)(2,1)}), bf16[4,64,512]{2,1,0:T(8,128)(2,1)S(1)}, u32[]{:S(2)}, u32[]{:S(2)}) async-start(bf16[4,64,512]{2,1,0:T(8,128)(2,1)} %broadcast_in_dim.20), calls=%async_computation.2 | async-start | bytes 524288 | tf_op jit(solution)/shard_map/all_to_all | solution.py:31
  17.8 35.1 %all-to-all-start = ((bf16[32,16,512]{2,1,0:T(8,128)(2,1)}), bf16[32,16,512]{2,1,0:T(8,128)(2,1)S(1)}, u32[]{:S(2)}, u32[]{:S(2)}) async-start(bf16[32,16,512]{2,1,0:T(8,128)(2,1)} %broadcast_in_dim.18), calls=%async_computation | async-start | bytes 1048576 | tf_op jit(solution)/shard_map/all_to_all | solution.py:31
  33.4 24.2 %copy-start.8 = (s32[1,3]{1,0:T(1,128)S(1)}, s32[1,3]{1,0:T(1,128)}, u32[]{:S(2)}) copy-start(s32[1,3]{1,0:T(1,128)} %param.11) | copy-start | bytes 40
  52.8 5.8 %copy-start.2 = (bf16[32,16,512]{2,1,0:T(8,128)(2,1)}, bf16[32,16,512]{2,1,0:T(8,128)(2,1)S(1)}, u32[]{:S(2)}) copy-start(bf16[32,16,512]{2,1,0:T(8,128)(2,1)S(1)} %all-to-all-done) | copy-start | bytes 1572868
  52.8 25.5 %all-to-all-start.1 = ((bf16[32,2,4352]{2,1,0:T(2,128)(2,1)}), bf16[32,2,4352]{2,1,0:T(2,128)(2,1)S(1)}, u32[]{:S(2)}, u32[]{:S(2)}) async-start(bf16[32,2,4352]{2,1,0:T(2,128)(2,1)} %pad_maximum_fusion.1), calls=%async_computation.1 | async-start | bytes 1114112 | tf_op jit(solution)/shard_map/all_to_all | solution.py:68
  78.4 1.1 copy-start.1
  79.5 17.6 %all-to-all-start.3 = ((bf16[4,256,512]{2,1,0:T(8,128)(2,1)}), bf16[4,256,512]{2,1,0:T(8,128)(2,1)S(1)}, u32[]{:S(2)}, u32[]{:S(2)}) async-start(bf16[4,256,512]{2,1,0:T(8,128)(2,1)} %broadcast_in_dim.22), calls=%async_computation.3 | async-start | bytes 2097152 | tf_op jit(solution)/shard_map/all_to_all | solution.py:31
  131.4 5.5 %copy-start.3 = (bf16[32,16,512]{2,1,0:T(8,128)(2,1)S(1)}, bf16[32,16,512]{2,1,0:T(8,128)(2,1)}, u32[]{:S(2)}) copy-start(bf16[32,16,512]{2,1,0:T(8,128)(2,1)} %copy-done.2) | copy-start | bytes 1572868
  133.0 23.4 %all-to-all-start.6 = ((bf16[32,2,4352]{2,1,0:T(2,128)(2,1)}), bf16[32,2,4352]{2,1,0:T(2,128)(2,1)S(1)}, u32[]{:S(2)}, u32[]{:S(2)}) async-start(bf16[32,2,4352]{2,1,0:T(2,128)(2,1)} %broadcast_in_dim.25), calls=%async_computation.6 | async-start | bytes 1114112 | tf_op jit(solution)/shard_map/all_to_all | solution.py:31
  142.9 13.8 %copy-start.6 = (bf16[16,4096]{1,0:T(8,128)(2,1)S(1)}, bf16[16,4096]{1,0:T(8,128)(2,1)}, u32[]{:S(2)}) copy-start(bf16[16,4096]{1,0:T(8,128)(2,1)} %param.15) | copy-start | bytes 393220
  156.6 18.4 %copy-start.4 = (bf16[32,1024]{1,0:T(8,128)(2,1)S(1)}, bf16[32,1024]{1,0:T(8,128)(2,1)}, u32[]{:S(2)}) copy-start(bf16[32,1024]{1,0:T(8,128)(2,1)} %param.13) | copy-start | bytes 196612
  158.9 14.8 %all-to-all-start.7 = ((f32[16,1,512]{2,1,0:T(1,128)}), f32[16,1,512]{2,1,0:T(1,128)S(1)}, u32[]{:S(2)}, u32[]{:S(2)}) async-start(f32[16,1,512]{2,1,0:T(1,128)} %reshape.115), calls=%async_computation.7 | async-start | bytes 65536 | tf_op jit(solution)/shard_map/all_to_all | solution.py:31

commit v2 on v1

--- a/solution.py
+++ b/solution.py
@@ -29,6 +29,16 @@
 def spread(block, axes, count, **kw):
     copies = jnp.broadcast_to(block[None], (count,) + block.shape)
     return lax.all_to_all(copies, axes, 0, 0, **kw)
+
+
+def gathered(block, part, count, stride, total):
+    every = jnp.zeros((count,) + block.shape, block.dtype)
+    every = lax.dynamic_update_index_in_dim(every, block, part, 0)
+    for step in range(1, count):
+        pairs = [(i, i ^ (step * stride)) for i in range(total)]
+        other = lax.ppermute(block, "tensor", pairs)
+        every = lax.dynamic_update_index_in_dim(every, other, part ^ step, 0)
+    return every.reshape((count * block.shape[0],) + block.shape[1:])
 
 
 def shards(
@@ -43,12 +53,9 @@
     along_y = [[x * Y_RUN + y for y in range(Y_RUN)] for x in range(n_x)]
     along_x = [[x * Y_RUN + y for x in range(n_x)] for y in range(Y_RUN)]
 
-    weight_t = spread(value_weight.T, "dp", n_dp).reshape(KV, width_own)
-
-    cot_run = spread(cotangent, "tensor", Y_RUN, axis_index_groups=along_y)
-    cot_full = spread(
-        cot_run.reshape(Y_RUN * rows_own, KV), "tensor", n_x, axis_index_groups=along_x
-    ).reshape(rows_total, KV)
+    place = lax.axis_index("tensor")
+    cot_run = gathered(cotangent, place % Y_RUN, Y_RUN, 1, n_tensor)
+    cot_full = gathered(cot_run, place // Y_RUN, n_x, Y_RUN, n_tensor)
 
     pre_act = jnp.dot(task_embed, hyper_in, preferred_element_type=f32)
     hidden = jax.nn.silu(pre_act).astype(bf16)
@@ -64,9 +71,18 @@
     ).astype(bf16)
     down_width = width_own * R
     up_width = outputs_own * R
-    sums = jnp.sum(
-        lax.all_to_all(terms.reshape(n_dp, SEQS, -1), "dp", 0, 0).astype(f32), axis=0
-    )
+    weight_own = value_weight.T
+    term_lines = SEQS * (down_width + up_width) // width_own
+    sent = jnp.concatenate(
+        (
+            terms.reshape(n_dp, term_lines, width_own),
+            jnp.broadcast_to(weight_own[None], (n_dp,) + weight_own.shape),
+        ),
+        axis=1,
+    )
+    came = lax.all_to_all(sent, "dp", 0, 0)
+    weight_t = came[:, term_lines:].reshape(KV, width_own)
+    sums = jnp.sum(came[:, :term_lines].astype(f32), axis=0).reshape(SEQS, -1)
     down_pick = (sums[:, :down_width] * (1.0 / math.sqrt(D))).astype(bf16)
     up_pick = (sums[:, down_width:] * (1.0 / math.sqrt(R))).astype(bf16)
     down_cat = down_pick.reshape(SEQS, width_own, R).transpose(1, 0, 2).reshape(width_own, ADA)
@@ -78,7 +94,19 @@
     inside = (places >= anchor[None, :SEQS]) & (places < finish[None, :SEQS])
     col_mask = jnp.repeat(inside.astype(f32), R, axis=1)
 
-    frozen = lax.dot_general(tokens, weight_t, inner_dims, preferred_element_type=f32).astype(bf16)
+    frozen = lax.dot_general(tokens, weight_t, inner_dims, preferred_element_type=f32)
+    frozen_rows = lax.psum_scatter(
+        frozen.reshape(n_x, Y_RUN * rows_own, KV),
+        "tensor",
+        scatter_dimension=0,
+        axis_index_groups=along_x,
+    )
+    frozen_rows = lax.psum_scatter(
+        frozen_rows.reshape(Y_RUN, rows_own, KV),
+        "tensor",
+        scatter_dimension=0,
+        axis_index_groups=along_y,
+    )
     low_part = (jnp.dot(tokens, down_cat, preferred_element_type=f32) * col_mask).astype(bf16)
     up_part = lax.dot_general(cot_full, low_part, outer_dims, preferred_element_type=f32).astype(
         bf16
@@ -88,28 +116,21 @@
     pick_lines = SEQS * up_width // KV
     block = jnp.concatenate(
         (
-            frozen.reshape(n_tensor, rows_own, KV),
             low_part.reshape(n_tensor, low_lines, KV),
             up_part.reshape(n_tensor, up_lines, KV),
             jnp.broadcast_to(up_pick.reshape(1, pick_lines, KV), (n_tensor, pick_lines, KV)),
         ),
         axis=1,
-    ).reshape(n_x, Y_RUN, -1, KV)
-    summed = rows_own + low_lines + up_lines
-    from_x = lax.all_to_all(block, "tensor", 0, 0, axis_index_groups=along_x)
-    x_sums = jnp.sum(from_x[:, :, :summed].astype(f32), axis=0).astype(bf16)
-    x_picks = from_x[:, :, summed:].transpose(1, 0, 2, 3).reshape(Y_RUN, n_x * pick_lines, KV)
-    from_y = lax.all_to_all(
-        jnp.concatenate((x_sums, x_picks), axis=1), "tensor", 0, 0, axis_index_groups=along_y
-    )
-    whole = jnp.sum(from_y[:, :summed].astype(f32), axis=0)
-    frozen_rows = whole[:rows_own]
-    low_rows = whole[rows_own : rows_own + low_lines].reshape(rows_own, ADA)
-    up_grad = whole[rows_own + low_lines :].reshape(outputs_own, ADA)
+    )
+    summed = low_lines + up_lines
+    came = lax.all_to_all(block, "tensor", 0, 0)
+    whole = jnp.sum(came[:, :summed].astype(f32), axis=0)
+    low_rows = whole[:low_lines].reshape(rows_own, ADA)
+    up_grad = whole[low_lines:].reshape(outputs_own, ADA)
     up_cat = (
-        from_y[:, summed:]
-        .reshape(Y_RUN, n_x, SEQS, outputs_own, R)
-        .transpose(1, 0, 3, 2, 4)
+        came[:, summed:]
+        .reshape(n_tensor, SEQS, outputs_own, R)
+        .transpose(0, 2, 1, 3)
         .reshape(KV, ADA)
     )
 

time: 177 us -> 160 us (0.904)
  the two profiles are of different devices: /device:TPU:2 before, /device:TPU:56 now
where the time goes in v2:
time: 160 us; the launch traced here: 158 us
  starting transfers between devices  52.2 us (33%)
  waiting for transfers between devices  44.2 us (28%)
  blocking collectives  16.1 us (10%)
  local copies, waits for them, and re-layouts  14.8 us (9%)
  between operations  14.5 us (9%)
  matrix products  13.4 us (8%)
  other arithmetic  2.75 us (2%)
    ppermute x6, starting transfers between devices, gathered(): other = lax.ppermute(block, 'tensor', pairs)  19.4 us
    all_to_all x2, waiting for transfers between devices, spread(): return lax.all_to_all(copies, axes, 0, 0, **kw)  17.4 us
    all_to_all x2, starting transfers between devices, spread(): return lax.all_to_all(copies, axes, 0, 0, **kw)  16.7 us
    all_to_all x1, blocking collectives, shards(): came = lax.all_to_all(block, 'tensor', 0, 0)  16.1 us
    all_to_all x1, starting transfers between devices, shards(): came = lax.all_to_all(sent, 'dp', 0, 0)  16 us
    reduce_scatter x1, waiting for transfers between devices, shards(): lax.psum_scatter(frozen_rows.reshape(Y_RUN, rows_own, KV), 'tensor', scat...  9.92 us
    ppermute x6, waiting for transfers between devices, gathered(): other = lax.ppermute(block, 'tensor', pairs)  9.33 us
    all_to_all x1, waiting for transfers between devices, shards(): came = lax.all_to_all(sent, 'dp', 0, 0)  7.54 us
  transfers between devices with their start and end apart: 11, of which 6 were waited for; matrix products, arithmetic and copies ran while one was open for 15% of the time, Pallas kernels for 0%

profile of v2, /device:TPU:56, one launch (start us, length us, event | category | flops | bytes accessed | tf_op | source)
XLA Modules:
  0.0 157.9 jit_solution(715007340849547685)
XLA Ops:
  7.2 3.4 %collective-permute-start = (bf16[64,512]{1,0:T(8,128)(2,1)}, bf16[64,512]{1,0:T(8,128)(2,1)S(1)}, u32[]{:S(2)}, u32[]{:S(2)}) collective-permute-start(bf16[64,512]{1,0:T(8,128)(2,1)} %param.17), channel_id=1, source_target_pairs={{0,1},{1,0},{2,3},{3,2},{4,5},{5,4},{6,7},{7,6},{8,9},{9,8},{10,11... | collective-permute-start | bytes 196616 | tf_op jit(solution)/shard_map/ppermute | solution.py:39
  10.6 4.2 %collective-permute-start.2 = (bf16[64,512]{1,0:T(8,128)(2,1)}, bf16[64,512]{1,0:T(8,128)(2,1)S(1)}, u32[]{:S(2)}, u32[]{:S(2)}) collective-permute-start(bf16[64,512]{1,0:T(8,128)(2,1)} %param.17), channel_id=1, source_target_pairs={{0,3},{1,2},{2,1},{3,0},{4,7},{5,6},{6,5},{7,4},{8,11},{9,10},{10,... | collective-permute-start | bytes 196616 | tf_op jit(solution)/shard_map/ppermute | solution.py:39
  14.8 1.9 %collective-permute-start.1 = (bf16[64,512]{1,0:T(8,128)(2,1)}, bf16[64,512]{1,0:T(8,128)(2,1)S(1)}, u32[]{:S(2)}, u32[]{:S(2)}) collective-permute-start(bf16[64,512]{1,0:T(8,128)(2,1)} %param.17), channel_id=1, source_target_pairs={{0,2},{1,3},{2,0},{3,1},{4,6},{5,7},{6,4},{7,5},{8,10},{9,11},{10,... | collective-permute-start | bytes 196616 | tf_op jit(solution)/shard_map/ppermute | solution.py:39
  19.6 1.2 convolution_convert_fusion
  21.4 1.4 pad_maximum_fusion
  22.8 16.0 %all-to-all-start = ((bf16[32,33,512]{2,1,0:T(8,128)(2,1)}), bf16[32,33,512]{2,1,0:T(8,128)(2,1)S(1)}, u32[]{:S(2)}, u32[]{:S(2)}) async-start(bf16[32,33,512]{2,1,0:T(8,128)(2,1)} %pad_maximum_fusion), calls=%async_computation | async-start | bytes 2621440 | tf_op jit(solution)/shard_map/all_to_all | solution.py:83
  42.4 3.4 %collective-permute-start.3 = (bf16[256,512]{1,0:T(8,128)(2,1)}, bf16[256,512]{1,0:T(8,128)(2,1)S(1)}, u32[]{:S(2)}, u32[]{:S(2)}) collective-permute-start(bf16[256,512]{1,0:T(8,128)(2,1)} %bitcast.19), channel_id=1, source_target_pairs={{0,4},{1,5},{2,6},{3,7},{4,0},{5,1},{6,2},{7,3},{8,12},{9,13},{10,... | collective-permute-start | bytes 786440 | tf_op jit(solution)/shard_map/ppermute | solution.py:39
  45.8 4.0 %collective-permute-start.5 = (bf16[256,512]{1,0:T(8,128)(2,1)}, bf16[256,512]{1,0:T(8,128)(2,1)S(1)}, u32[]{:S(2)}, u32[]{:S(2)}) collective-permute-start(bf16[256,512]{1,0:T(8,128)(2,1)} %bitcast.19), channel_id=1, source_target_pairs={{0,12},{1,13},{2,14},{3,15},{4,8},{5,9},{6,10},{7,11},{8,4},{9,5},... | collective-permute-start | bytes 786440 | tf_op jit(solution)/shard_map/ppermute | solution.py:39
  49.8 2.5 %collective-permute-start.4 = (bf16[256,512]{1,0:T(8,128)(2,1)}, bf16[256,512]{1,0:T(8,128)(2,1)S(1)}, u32[]{:S(2)}, u32[]{:S(2)}) collective-permute-start(bf16[256,512]{1,0:T(8,128)(2,1)} %bitcast.19), channel_id=1, source_target_pairs={{0,8},{1,9},{2,10},{3,11},{4,12},{5,13},{6,14},{7,15},{8,0},{9,1},... | collective-permute-start | bytes 786440 | tf_op jit(solution)/shard_map/ppermute | solution.py:39
  52.5 1.0 bitcast_dynamic-update-slice_fusion.3
  53.5 7.9 %collective-permute-done.4 = bf16[256,512]{1,0:T(8,128)(2,1)S(1)} collective-permute-done((bf16[256,512]{1,0:T(8,128)(2,1)}, bf16[256,512]{1,0:T(8,128)(2,1)S(1)}, u32[]{:S(2)}, u32[]{:S(2)}) %collective-permute-start.4) | collective-permute-done | bytes 262176 | tf_op jit(solution)/shard_map/ppermute | solution.py:39
  61.4 1.5 collective-permute-done.5
  62.9 7.5 %all-to-all-done = bf16[32,33,512]{2,1,0:T(8,128)(2,1)S(1)} async-done(((bf16[32,33,512]{2,1,0:T(8,128)(2,1)}), bf16[32,33,512]{2,1,0:T(8,128)(2,1)S(1)}, u32[]{:S(2)}, u32[]{:S(2)}) %all-to-all-start) | async-done | bytes 1081376 | tf_op jit(solution)/shard_map/all_to_all | solution.py:83
  71.6 2.1 %convolution_bitcast_fusion = f32[1024,512]{0,1:T(8,128)} fusion(bf16[512,512]{1,0:T(8,128)(2,1)S(1)} %bitcast.102, bf16[1024,512]{1,0:T(8,128)(2,1)S(1)} %copy-done), kind=kOutput, calls=%fused_computation.3 | convolution fusion | flops 536870912 | bytes 3670016 | tf_op jit(solution)/shard_map/dot_general | solution.py:97
  73.6 2.9 %copy.36 = f32[1024,512]{1,0:T(8,128)} copy(f32[1024,512]{0,1:T(8,128)} %convolution_bitcast_fusion) | data formatting | bytes 4194304 | tf_op jit(solution)/shard_map/reshape | solution.py:99
  78.6 16.1 %all_to_all.20 = bf16[16,4,512]{2,1,0:T(4,128)(2,1)S(1)} all-to-all(bf16[16,4,512]{2,1,0:T(4,128)(2,1)S(1)} %pad_maximum_fusion.2), channel_id=1, replica_groups=mesh['dp'=32,'tensor'=16] {'tensor'}, dimensions={0} | all-to-all | bytes 131072 | tf_op jit(solution)/shard_map/all_to_all | solution.py:126
  96.5 1.1 broadcast_in_dim.78
  97.6 9.1 %all-to-all-start.2 = ((bf16[32,2,4352]{2,1,0:T(2,128)(2,1)}), bf16[32,2,4352]{2,1,0:T(2,128)(2,1)S(1)}, u32[]{:S(2)}, u32[]{:S(2)}) async-start(bf16[32,2,4352]{2,1,0:T(2,128)(2,1)} %broadcast_in_dim.78), calls=%async_computation.4 | async-start | bytes 1114112 | tf_op jit(solution)/shard_map/all_to_all | solution.py:31
  107.3 1.7 %add_convert_fusion = bf16[1024,512]{1,0:T(8,128)(2,1)} fusion(f32[1024,512]{1,0:T(8,128)S(1)} %fusion.12, bf16[1024,512]{1,0:T(8,128)(2,1)S(1)} %bitcast.100, bf16[512,512]{1,0:T(8,128)(2,1)S(1)} %bitcast.103), kind=kOutput, calls=%fused_computation.2 | convolution fusion | flops 537919488 | bytes 4718592 | tf_op jit(solution)/shard_map/dot_general | solution.py:173
  109.0 14.1 %all-to-all-done.2 = bf16[32,2,4352]{2,1,0:T(2,128)(2,1)S(1)} async-done(((bf16[32,2,4352]{2,1,0:T(2,128)(2,1)}), bf16[32,2,4352]{2,1,0:T(2,128)(2,1)S(1)}, u32[]{:S(2)}, u32[]{:S(2)}) %all-to-all-start.2) | async-done | bytes 557088 | tf_op jit(solution)/shard_map/all_to_all | solution.py:31
  124.6 7.7 %all-to-all-start.3 = ((f32[16,1,512]{2,1,0:T(1,128)}), f32[16,1,512]{2,1,0:T(1,128)S(1)}, u32[]{:S(2)}, u32[]{:S(2)}) async-start(f32[16,1,512]{2,1,0:T(1,128)} %reshape.118), calls=%async_computation.5 | async-start | bytes 65536 | tf_op jit(solution)/shard_map/all_to_all | solution.py:31
  133.9 3.3 %all-to-all-done.3 = f32[16,1,512]{2,1,0:T(1,128)S(1)} async-done(((f32[16,1,512]{2,1,0:T(1,128)}), f32[16,1,512]{2,1,0:T(1,128)S(1)}, u32[]{:S(2)}, u32[]{:S(2)}) %all-to-all-start.3) | async-done | bytes 32800 | tf_op jit(solution)/shard_map/all_to_all | solution.py:31
  139.4 9.9 %reduce-scatter.5.cloned.1.call-done = f32[1,64,512]{2,1,0:T(8,128)} async-done(((f32[4,64,512]{2,1,0:T(8,128)}), f32[1,64,512]{2,1,0:T(8,128)}) %reduce-scatter.5.cloned.1.call-update) | async-done | bytes 131088 | tf_op jit(solution)/shard_map/reduce_scatter | solution.py:104
  149.3 1.7 %fusion = bf16[64,512]{1,0:T(8,128)(2,1)} fusion(f32[64,16]{1,0:T(8,128)S(1)} %reshape.111, bf16[512,16]{0,1:T(8,128)(2,1)S(1)} %reshape.113, f32[1,64,512]{2,1,0:T(8,128)} %reduce-scatter.5.cloned.1.call-done), kind=kOutput, calls=%fused_computation.7 | convolution fusion | flops 6356992 | bytes 217088 | tf_op jit(solution)/shard_map/dot_general | solution.py:168
  (94 shorter events, 18.1 us)
Async XLA Ops:
  7.2 64.4 %copy-start = (bf16[1024,512]{1,0:T(8,128)(2,1)S(1)}, bf16[1024,512]{1,0:T(8,128)(2,1)}, u32[]{:S(2)}) copy-start(bf16[1024,512]{1,0:T(8,128)(2,1)} %param.9) | copy-start | bytes 3145732
  7.2 14.2 %copy-start.7 = (bf16[512,16]{0,1:T(8,128)(2,1)S(1)}, bf16[512,16]{0,1:T(8,128)(2,1)}, u32[]{:S(2)}) copy-start(bf16[512,16]{0,1:T(8,128)(2,1)} %param.10) | copy-start | bytes 49156
  7.2 33.2 %collective-permute-start = (bf16[64,512]{1,0:T(8,128)(2,1)}, bf16[64,512]{1,0:T(8,128)(2,1)S(1)}, u32[]{:S(2)}, u32[]{:S(2)}) collective-permute-start(bf16[64,512]{1,0:T(8,128)(2,1)} %param.17), channel_id=1, source_target_pairs={{0,1},{1,0},{2,3},{3,2},{4,5},{5,4},{6,7},{7,6},{8,9},{9,8},{10,11... | collective-permute-start | bytes 196616 | tf_op jit(solution)/shard_map/ppermute | solution.py:39
  10.6 31.1 %collective-permute-start.2 = (bf16[64,512]{1,0:T(8,128)(2,1)}, bf16[64,512]{1,0:T(8,128)(2,1)S(1)}, u32[]{:S(2)}, u32[]{:S(2)}) collective-permute-start(bf16[64,512]{1,0:T(8,128)(2,1)} %param.17), channel_id=1, source_target_pairs={{0,3},{1,2},{2,1},{3,0},{4,7},{5,6},{6,5},{7,4},{8,11},{9,10},{10,... | collective-permute-start | bytes 196616 | tf_op jit(solution)/shard_map/ppermute | solution.py:39
  14.8 26.3 %collective-permute-start.1 = (bf16[64,512]{1,0:T(8,128)(2,1)}, bf16[64,512]{1,0:T(8,128)(2,1)S(1)}, u32[]{:S(2)}, u32[]{:S(2)}) collective-permute-start(bf16[64,512]{1,0:T(8,128)(2,1)} %param.17), channel_id=1, source_target_pairs={{0,2},{1,3},{2,0},{3,1},{4,6},{5,7},{6,4},{7,5},{8,10},{9,11},{10,... | collective-permute-start | bytes 196616 | tf_op jit(solution)/shard_map/ppermute | solution.py:39
  21.4 17.5 %copy-start.8 = (s32[1,3]{1,0:T(1,128)S(1)}, s32[1,3]{1,0:T(1,128)}, u32[]{:S(2)}) copy-start(s32[1,3]{1,0:T(1,128)} %param.11) | copy-start | bytes 40
  22.8 17.0 %copy-start.5 = (bf16[64,512]{1,0:T(8,128)(2,1)S(1)}, bf16[64,512]{1,0:T(8,128)(2,1)}, u32[]{:S(2)}) copy-start(bf16[64,512]{1,0:T(8,128)(2,1)} %param.17) | copy-start | bytes 196612
  22.8 47.6 %all-to-all-start = ((bf16[32,33,512]{2,1,0:T(8,128)(2,1)}), bf16[32,33,512]{2,1,0:T(8,128)(2,1)S(1)}, u32[]{:S(2)}, u32[]{:S(2)}) async-start(bf16[32,33,512]{2,1,0:T(8,128)(2,1)} %pad_maximum_fusion), calls=%async_computation | async-start | bytes 2621440 | tf_op jit(solution)/shard_map/all_to_all | solution.py:83
  38.8 84.8 %reduce-scatter.3.cloned.1.call-start = ((), (), s32[]{:S(2)}) async-start(), calls=%async_computation.6 | async-start | bytes 2621440 | tf_op jit(solution)/shard_map/reduce_scatter | solution.py:98
  42.4 11.1 %collective-permute-start.3 = (bf16[256,512]{1,0:T(8,128)(2,1)}, bf16[256,512]{1,0:T(8,128)(2,1)S(1)}, u32[]{:S(2)}, u32[]{:S(2)}) collective-permute-start(bf16[256,512]{1,0:T(8,128)(2,1)} %bitcast.19), channel_id=1, source_target_pairs={{0,4},{1,5},{2,6},{3,7},{4,0},{5,1},{6,2},{7,3},{8,12},{9,13},{10,... | collective-permute-start | bytes 786440 | tf_op jit(solution)/shard_map/ppermute | solution.py:39
  45.8 17.0 %collective-permute-start.5 = (bf16[256,512]{1,0:T(8,128)(2,1)}, bf16[256,512]{1,0:T(8,128)(2,1)S(1)}, u32[]{:S(2)}, u32[]{:S(2)}) collective-permute-start(bf16[256,512]{1,0:T(8,128)(2,1)} %bitcast.19), channel_id=1, source_target_pairs={{0,12},{1,13},{2,14},{3,15},{4,8},{5,9},{6,10},{7,11},{8,4},{9,5},... | collective-permute-start | bytes 786440 | tf_op jit(solution)/shard_map/ppermute | solution.py:39
  49.8 11.5 %collective-permute-start.4 = (bf16[256,512]{1,0:T(8,128)(2,1)}, bf16[256,512]{1,0:T(8,128)(2,1)S(1)}, u32[]{:S(2)}, u32[]{:S(2)}) collective-permute-start(bf16[256,512]{1,0:T(8,128)(2,1)} %bitcast.19), channel_id=1, source_target_pairs={{0,8},{1,9},{2,10},{3,11},{4,12},{5,13},{6,14},{7,15},{8,0},{9,1},... | collective-permute-start | bytes 786440 | tf_op jit(solution)/shard_map/ppermute | solution.py:39
  70.8 0.8 copy-start.1
  96.2 11.1 %copy-start.2 = (bf16[32,16,512]{2,1,0:T(8,128)(2,1)S(1)}, bf16[32,16,512]{2,1,0:T(8,128)(2,1)}, u32[]{:S(2)}) copy-start(bf16[32,16,512]{2,1,0:T(8,128)(2,1)} %copy-done.1) | copy-start | bytes 1572868
  97.6 25.4 %all-to-all-start.2 = ((bf16[32,2,4352]{2,1,0:T(2,128)(2,1)}), bf16[32,2,4352]{2,1,0:T(2,128)(2,1)S(1)}, u32[]{:S(2)}, u32[]{:S(2)}) async-start(bf16[32,2,4352]{2,1,0:T(2,128)(2,1)} %broadcast_in_dim.78), calls=%async_computation.4 | async-start | bytes 1114112 | tf_op jit(solution)/shard_map/all_to_all | solution.py:31
  106.7 42.7 %reduce-scatter.5.cloned.1.call-start = ((), (), s32[]{:S(2)}) async-start(), calls=%async_computation.7 | async-start | bytes 655360 | tf_op jit(solution)/shard_map/reduce_scatter | solution.py:104
  107.3 16.0 %copy-start.4 = (bf16[16,4096]{1,0:T(8,128)(2,1)S(1)}, bf16[16,4096]{1,0:T(8,128)(2,1)}, u32[]{:S(2)}) copy-start(bf16[16,4096]{1,0:T(8,128)(2,1)} %param.15) | copy-start | bytes 393220
  107.3 16.2 %copy-start.6 = (bf16[16,256]{1,0:T(8,128)(2,1)S(1)}, bf16[16,256]{1,0:T(8,128)(2,1)}, u32[]{:S(2)}) copy-start(bf16[16,256]{1,0:T(8,128)(2,1)} %param.16) | copy-start | bytes 24580
  109.0 29.6 %copy-start.3 = (bf16[32,1024]{1,0:T(8,128)(2,1)S(1)}, bf16[32,1024]{1,0:T(8,128)(2,1)}, u32[]{:S(2)}) copy-start(bf16[32,1024]{1,0:T(8,128)(2,1)} %param.13) | copy-start | bytes 196612
  124.6 12.6 %all-to-all-start.3 = ((f32[16,1,512]{2,1,0:T(1,128)}), f32[16,1,512]{2,1,0:T(1,128)S(1)}, u32[]{:S(2)}, u32[]{:S(2)}) async-start(f32[16,1,512]{2,1,0:T(1,128)} %reshape.118), calls=%async_computation.5 | async-start | bytes 65536 | tf_op jit(solution)/shard_map/all_to_all | solution.py:31
Sparse Core Ops, SparseCore 0:
  76.7 35.4 reduce-scatter.2
  123.8 25.4 reduce-scatter.4

commit v3 on v2

v3 whole, which is shorter than its diff:
```python
import math

import jax
import jax.numpy as jnp
from jax import lax
from jax.sharding import PartitionSpec as P

D = 8192
KV = 512
R = 8
NTASK = 32
SEQS = 2
ADA = SEQS * R

precise = lax.Precision.HIGHEST
inner_dims = (((1,), (1,)), ((), ()))
outer_dims = (((0,), (0,)), ((), ()))
bf16 = jnp.bfloat16
f32 = jnp.float32

CORES = 2
Y_RUN = 4


def silu_slope(pre_act):
    sigma = jax.nn.sigmoid(pre_act)
    return sigma * (1.0 + pre_act * (1.0 - sigma))


def spread(block, axes, count, **kw):
    copies = jnp.broadcast_to(block[None], (count,) + block.shape)
    return lax.all_to_all(copies, axes, 0, 0, **kw)


def swapped(block, axis, distance):
    pairs = [(i, i ^ distance) for i in range(lax.axis_size(axis))]
    return lax.ppermute(block, axis, pairs)


def gathered(block, part, count, stride):
    every = jnp.zeros((count,) + block.shape, block.dtype)
    every = lax.dynamic_update_index_in_dim(every, block, part, 0)
    for step in range(1, count):
        other = swapped(block, "tensor", step * stride)
        every = lax.dynamic_update_index_in_dim(every, other, part ^ step, 0)
    return every.reshape((count * block.shape[0],) + block.shape[1:])


def summed_rows(rows, place, total):
    distance = total // 2
    while distance:
        halves = rows.reshape((2, rows.shape[0] // 2) + rows.shape[1:])
        bit = (place // distance) % 2
        kept = lax.dynamic_index_in_dim(halves, bit, 0, keepdims=False)
        given = lax.dynamic_index_in_dim(halves, 1 - bit, 0, keepdims=False)
        other = swapped(given, "tensor", distance)
        rows = kept.astype(f32) + other.astype(f32)
        distance //= 2
        if distance:
            rows = rows.astype(bf16)
    return rows


def shards(
    tokens, value_weight, seq_lengths, task_ids, task_embed, hyper_in, head_a, head_b, cotangent
):
    n_dp = lax.axis_size("dp")
    n_chips = n_dp // CORES
    n_tensor = lax.axis_size("tensor")
    n_x = n_tensor // Y_RUN
    rows_total, width_own = tokens.shape
    rows_own = rows_total // n_tensor
    outputs_own = KV // n_tensor
    down_width = width_own * R
    up_width = outputs_own * R
    same_core = [[chip * CORES + core for chip in range(n_chips)] for core in range(CORES)]
    core = lax.axis_index("dp") % CORES
    place = lax.axis_index("tensor")

    pre_act = jnp.dot(task_embed, hyper_in, preferred_element_type=f32)
    hidden = jax.nn.silu(pre_act).astype(bf16)

    def chosen_by(which):
        ids = lax.dynamic_index_in_dim(
            task_ids.reshape(n_chips, CORES, SEQS), which, 1, keepdims=False
        ).reshape(n_chips * SEQS)
        hot = (ids[:, None] == jnp.arange(NTASK, dtype=jnp.int32)[None, :]).astype(bf16)
        return hot, jnp.dot(hot, hidden, preferred_element_type=f32).astype(bf16)

    def terms_of(pick):
        return jnp.concatenate(
            (
                jnp.dot(pick, head_a, preferred_element_type=f32),
                jnp.dot(pick, head_b, preferred_element_type=f32),
            ),
            axis=1,
        )

    hot_mate, pick_mate = chosen_by(1 - core)
    hot_mine, pick_mine = chosen_by(core)
    from_mate = swapped(terms_of(pick_mate).astype(bf16), "dp", 1)
    terms = (terms_of(pick_mine) + from_mate.astype(f32)).astype(bf16)
    weight_own = value_weight.T
    term_lines = SEQS * (down_width + up_width) // width_own
    sent = jnp.concatenate(
        (
            terms.reshape(n_chips, term_lines, width_own),
            jnp.broadcast_to(weight_own[None], (n_chips,) + weight_own.shape),
        ),
        axis=1,
    )
    came = lax.all_to_all(sent, "dp", 0, 0, axis_index_groups=same_core)
    sums = jnp.sum(came[:, :term_lines].astype(f32), axis=0).reshape(SEQS, -1)
    down_pick = (sums[:, :down_width] * (1.0 / math.sqrt(D))).astype(bf16)
    up_pick = (sums[:, down_width:] * (1.0 / math.sqrt(R))).astype(bf16)
    down_cat = down_pick.reshape(SEQS, width_own, R).transpose(1, 0, 2).reshape(width_own, ADA)

    cot_run = gathered(cotangent, place % Y_RUN, Y_RUN, 1)
    cot_full = gathered(cot_run, place // Y_RUN, n_x, Y_RUN)

    lengths = seq_lengths[0]
    finish = jnp.cumsum(lengths)
    anchor = finish - lengths
    places = jnp.arange(rows_total, dtype=jnp.int32)[:, None]
    inside = (places >= anchor[None, :SEQS]) & (places < finish[None, :SEQS])
    col_mask = jnp.repeat(inside.astype(f32), R, axis=1)

    low_part = (jnp.dot(tokens, down_cat, preferred_element_type=f32) * col_mask).astype(bf16)
    up_part = lax.dot_general(cot_full, low_part, outer_dims, preferred_element_type=f32).astype(
        bf16
    )
    low_lines = rows_own * ADA // KV
    up_lines = outputs_own * ADA // KV
    pick_lines = SEQS * up_width // KV
    block = jnp.concatenate(
        (
            low_part.reshape(n_tensor, low_lines, KV),
            up_part.reshape(n_tensor, up_lines, KV),
            jnp.broadcast_to(up_pick.reshape(1, pick_lines, KV), (n_tensor, pick_lines, KV)),
        ),
        axis=1,
    )
    summed = low_lines + up_lines
    low_came = lax.all_to_all(block, "tensor", 0, 0)
    whole = jnp.sum(low_came[:, :summed].astype(f32), axis=0)
    low_rows = whole[:low_lines].reshape(rows_own, ADA)
    up_grad = whole[low_lines:].reshape(outputs_own, ADA)
    up_cat = (
        low_came[:, summed:]
        .reshape(n_tensor, SEQS, outputs_own, R)
        .transpose(0, 2, 1, 3)
        .reshape(KV, ADA)
    )

    weight_mine = came[:, term_lines:]
    weight_mate = swapped(weight_mine, "dp", 1)
    weight_t = jnp.stack(
        (
            jnp.where(core == 0, weight_mine, weight_mate),
            jnp.where(core == 0, weight_mate, weight_mine),
        ),
        axis=1,
    ).reshape(KV, width_own)
    frozen = lax.dot_general(tokens, weight_t, inner_dims, preferred_element_type=f32).astype(bf16)
    frozen_rows = summed_rows(frozen, place, n_tensor)

    back_low = (jnp.dot(cot_full, up_cat, preferred_element_type=f32) * col_mask).astype(bf16)
    down_grad = lax.dot_general(tokens, back_low, outer_dims, preferred_element_type=f32)
    down_seq = down_grad.reshape(width_own, SEQS, R).transpose(1, 0, 2).reshape(SEQS, down_width)
    up_seq = up_grad.reshape(outputs_own, SEQS, R).transpose(1, 0, 2).reshape(SEQS, up_width)
    grads_mine = spread(
        jnp.concatenate((down_seq, up_seq), axis=1).astype(bf16),
        "dp",
        n_chips,
        axis_index_groups=same_core,
    )
    grads_mate = swapped(grads_mine, "dp", 1)

    down_scale = 1.0 / math.sqrt(D)
    up_scale = 1.0 / math.sqrt(R)

    def head_terms(grads, pick, hot):
        rows = grads.reshape(n_chips * SEQS, -1)
        down_rows = rows[:, :down_width]
        up_rows = rows[:, down_width:]
        part = down_scale * lax.dot_general(
            down_rows, head_a, inner_dims, preferred_element_type=f32
        ) + up_scale * lax.dot_general(up_rows, head_b, inner_dims, preferred_element_type=f32)
        return (
            lax.dot_general(hot.astype(f32), part, outer_dims, precision=precise),
            lax.dot_general(pick, down_rows, outer_dims, preferred_element_type=f32),
            lax.dot_general(pick, up_rows, outer_dims, preferred_element_type=f32),
        )

    of_mine = head_terms(grads_mine, pick_mine, hot_mine)
    of_mate = head_terms(grads_mate, pick_mate, hot_mate)
    by_task = of_mine[0] + of_mate[0]
    grad_head_a = down_scale * (of_mine[1] + of_mate[1])
    grad_head_b = up_scale * (of_mine[2] + of_mate[2])
    grad_hidden = jnp.sum(spread(by_task, "tensor", n_tensor), axis=0)
    grad_pre = grad_hidden * silu_slope(pre_act)
    grad_hyper_in = lax.dot_general(
        task_embed.astype(f32), grad_pre, outer_dims, precision=precise
    )

    adapter = lax.dot_general(
        low_rows.astype(f32), up_cat.astype(f32), inner_dims, precision=precise
    )
    values = (frozen_rows + adapter).astype(bf16)
    adapter_back = lax.dot_general(back_low, down_cat, inner_dims, preferred_element_type=f32)
    frozen_back = jnp.dot(cot_full, weight_t, preferred_element_type=f32)
    grad_tokens = (frozen_back + adapter_back).astype(bf16)
    return (values, grad_tokens, grad_head_a, grad_head_b, grad_hyper_in)


def solution(mesh):
    placed = (
        P("dp", "tensor"),
        P("tensor", "dp"),
        P("dp", None),
        P(),
        P(),
        P(None, "dp"),
        P("dp", "tensor"),
        P("dp", "tensor"),
        P(("dp", "tensor"), None),
    )
    return jax.shard_map(
        shards,
        mesh=mesh,
        in_specs=placed,
        out_specs=(
            P(("dp", "tensor"), None),
            P("dp", "tensor"),
            P("dp", "tensor"),
            P("dp", "tensor"),
            P(None, "dp"),
        ),
        check_vma=False,
    )
```

time: 160 us -> 147 us (0.919)
  starting transfers between devices: 52.2 us -> 78 us
  waiting for transfers between devices: 44.2 us -> 22.9 us
  blocking collectives: 16.1 us -> 0 us
  between operations: 14.5 us -> 1.4 us
  matrix products: 13.4 us -> 25.5 us
  other arithmetic: 2.75 us -> 5.96 us
  local copies, waits for them, and re-layouts: 14.8 us -> 12.3 us
    ppermute x6 -> x13, starting transfers between devices: 19.4 us -> 37 us  [swapped(): return lax.ppermute(block, axis, pairs)]
    all_to_all x2, waiting for transfers between devices: 17.4 us -> 0.05 us  [spread(): return lax.all_to_all(copies, axes, 0, 0, **kw)]
    all_to_all x1 -> x0, blocking collectives: 16.1 us -> none  [shards(): came = lax.all_to_all(block, 'tensor', 0, 0)]
    reduce_scatter x2 -> x0, waiting for transfers between devices: 9.92 us -> none  [the longest x1 9.92 us: shards(): lax.psum_scatter(frozen_rows.reshape(Y_RUN, rows_own, KV), 'tensor', scat...]
    ppermute x6 -> x13, waiting for transfers between devices: 9.33 us -> 19.1 us  [swapped(): return lax.ppermute(block, axis, pairs)]
    dot_general x8 -> x16, matrix products: 4.49 us -> 14 us  [the longest x2 3.08 us: head_terms(): lax.dot_general(pick, down_rows, outer_dims, preferred_element_type=f32)]
    all_to_all x1 -> x2, starting transfers between devices: 16 us -> 22.9 us  [the longest x1 15.7 us: shards(): came = lax.all_to_all(sent, 'dp', 0, 0, axis_index_groups=same_core)]
    all_to_all x1 -> x2, waiting for transfers between devices: 7.54 us -> 3.69 us  [the longest x1 2.44 us: shards(): low_came = lax.all_to_all(block, 'tensor', 0, 0)]
  transfers between devices with their start and end apart: 11 -> 17, of which waited for: 6 -> 7; matrix products, arithmetic and copies ran while one was open for 15% -> 27% of each run, Pallas kernels for 0% -> 0%
where the time goes in v3:
time: 147 us; the launch traced here: 146 us
  starting transfers between devices  78 us (53%)
  matrix products  25.5 us (17%)
  waiting for transfers between devices  22.9 us (16%)
  local copies, waits for them, and re-layouts  12.3 us (8%)
  other arithmetic  5.96 us (4%)
    ppermute x13, starting transfers between devices, swapped(): return lax.ppermute(block, axis, pairs)  37 us
    ppermute x13, waiting for transfers between devices, swapped(): return lax.ppermute(block, axis, pairs)  19.1 us
    all_to_all x2, starting transfers between devices, spread(): return lax.all_to_all(copies, axes, 0, 0, **kw)  18 us
    all_to_all x1, starting transfers between devices, shards(): came = lax.all_to_all(sent, 'dp', 0, 0, axis_index_groups=same_core)  15.7 us
    all_to_all x1, starting transfers between devices, shards(): low_came = lax.all_to_all(block, 'tensor', 0, 0)  7.26 us
    dot_general x1, matrix products, shards(): frozen_back = jnp.dot(cot_full, weight_t, preferred_element_type=f32)  3.45 us
    dot_general x2, matrix products, head_terms(): lax.dot_general(pick, down_rows, outer_dims, preferred_element_type=f32)  3.08 us
  transfers between devices with their start and end apart: 17, of which 7 were waited for; matrix products, arithmetic and copies ran while one was open for 27% of the time, Pallas kernels for 0%

profile of v3, /device:TPU:56, one launch (start us, length us, event | category | flops | bytes accessed | tf_op | source)
XLA Modules:
  0.0 146.0 jit_solution(15891825058574202619)
XLA Ops:
  0.7 3.4 %collective-permute-start.6 = (bf16[64,512]{1,0:T(8,128)(2,1)}, bf16[64,512]{1,0:T(8,128)(2,1)S(1)}, u32[]{:S(2)}, u32[]{:S(2)}) collective-permute-start(bf16[64,512]{1,0:T(8,128)(2,1)} %param.17), channel_id=1, source_target_pairs={{0,1},{1,0},{2,3},{3,2},{4,5},{5,4},{6,7},{7,6},{8,9},{9,8},{10,11... | collective-permute-start | bytes 196616 | tf_op jit(solution)/shard_map/ppermute | solution.py:37
  4.1 4.0 %collective-permute-start.7 = (bf16[64,512]{1,0:T(8,128)(2,1)}, bf16[64,512]{1,0:T(8,128)(2,1)S(1)}, u32[]{:S(2)}, u32[]{:S(2)}) collective-permute-start(bf16[64,512]{1,0:T(8,128)(2,1)} %param.17), channel_id=1, source_target_pairs={{0,2},{1,3},{2,0},{3,1},{4,6},{5,7},{6,4},{7,5},{8,10},{9,11},{10,... | collective-permute-start | bytes 196616 | tf_op jit(solution)/shard_map/ppermute | solution.py:37
  8.1 2.8 %collective-permute-start.8 = (bf16[64,512]{1,0:T(8,128)(2,1)}, bf16[64,512]{1,0:T(8,128)(2,1)S(1)}, u32[]{:S(2)}, u32[]{:S(2)}) collective-permute-start(bf16[64,512]{1,0:T(8,128)(2,1)} %param.17), channel_id=1, source_target_pairs={{0,3},{1,2},{2,1},{3,0},{4,7},{5,6},{6,5},{7,4},{8,11},{9,10},{10,... | collective-permute-start | bytes 196616 | tf_op jit(solution)/shard_map/ppermute | solution.py:37
  16.0 1.9 %collective-permute-start = (bf16[32,4352]{1,0:T(8,128)(2,1)S(1)}, bf16[32,4352]{1,0:T(8,128)(2,1)S(1)}, u32[]{:S(2)}, u32[]{:S(2)}) collective-permute-start(bf16[32,4352]{1,0:T(8,128)(2,1)S(1)} %pad_maximum_fusion.2), channel_id=1, source_target_pairs={{0,16},{16,0},{32,48},{48,32},{64,80},{80,64},{96,112},{112,96},{1... | collective-permute-start | bytes 835592 | tf_op jit(solution)/shard_map/ppermute | solution.py:37
  21.3 3.4 %collective-permute-start.9 = (bf16[256,512]{1,0:T(8,128)(2,1)S(1)}, bf16[256,512]{1,0:T(8,128)(2,1)S(1)}, u32[]{:S(2)}, u32[]{:S(2)}) collective-permute-start(bf16[256,512]{1,0:T(8,128)(2,1)S(1)} %bitcast.148), channel_id=1, source_target_pairs={{0,4},{1,5},{2,6},{3,7},{4,0},{5,1},{6,2},{7,3},{8,12},{9,13},{10,... | collective-permute-start | bytes 786440 | tf_op jit(solution)/shard_map/ppermute | solution.py:37
  26.1 15.7 %all-to-all-start = ((bf16[16,33,512]{2,1,0:T(8,128)(2,1)}), bf16[16,33,512]{2,1,0:T(8,128)(2,1)S(1)}, u32[]{:S(2)}, u32[]{:S(2)}) async-start(bf16[16,33,512]{2,1,0:T(8,128)(2,1)} %pad_maximum_fusion), calls=%async_computation | async-start | bytes 1310720 | tf_op jit(solution)/shard_map/all_to_all | solution.py:112
  41.8 4.6 %collective-permute-start.10 = (bf16[256,512]{1,0:T(8,128)(2,1)S(1)}, bf16[256,512]{1,0:T(8,128)(2,1)S(1)}, u32[]{:S(2)}, u32[]{:S(2)}) collective-permute-start(bf16[256,512]{1,0:T(8,128)(2,1)S(1)} %bitcast.149), channel_id=1, source_target_pairs={{0,8},{1,9},{2,10},{3,11},{4,12},{5,13},{6,14},{7,15},{8,0},{9,1},... | collective-permute-start | bytes 786440 | tf_op jit(solution)/shard_map/ppermute | solution.py:37
  46.5 2.4 %collective-permute-start.11 = (bf16[256,512]{1,0:T(8,128)(2,1)S(1)}, bf16[256,512]{1,0:T(8,128)(2,1)S(1)}, u32[]{:S(2)}, u32[]{:S(2)}) collective-permute-start(bf16[256,512]{1,0:T(8,128)(2,1)S(1)} %bitcast.150), channel_id=1, source_target_pairs={{0,12},{1,13},{2,14},{3,15},{4,8},{5,9},{6,10},{7,11},{8,4},{9,5},... | collective-permute-start | bytes 786440 | tf_op jit(solution)/shard_map/ppermute | solution.py:37
  49.0 4.2 %collective-permute-done.10 = bf16[256,512]{1,0:T(8,128)(2,1)S(1)} collective-permute-done((bf16[256,512]{1,0:T(8,128)(2,1)S(1)}, bf16[256,512]{1,0:T(8,128)(2,1)S(1)}, u32[]{:S(2)}, u32[]{:S(2)}) %collective-permute-start.10) | collective-permute-done | bytes 262176 | tf_op jit(solution)/shard_map/ppermute | solution.py:37
  53.2 5.5 %collective-permute-done.11 = bf16[256,512]{1,0:T(8,128)(2,1)S(1)} collective-permute-done((bf16[256,512]{1,0:T(8,128)(2,1)S(1)}, bf16[256,512]{1,0:T(8,128)(2,1)S(1)}, u32[]{:S(2)}, u32[]{:S(2)}) %collective-permute-start.11) | collective-permute-done | bytes 262176 | tf_op jit(solution)/shard_map/ppermute | solution.py:37
  62.8 7.3 %all-to-all-start.1 = ((bf16[16,4,512]{2,1,0:T(4,128)(2,1)}), bf16[16,4,512]{2,1,0:T(4,128)(2,1)S(1)}, u32[]{:S(2)}, u32[]{:S(2)}) async-start(bf16[16,4,512]{2,1,0:T(4,128)(2,1)} %pad_maximum_fusion.3), calls=%async_computation.1 | async-start | bytes 131072 | tf_op jit(solution)/shard_map/all_to_all | solution.py:144
  70.8 1.9 %collective-permute-start.1 = (bf16[16,16,512]{2,1,0:T(8,128)(2,1)}, bf16[16,16,512]{2,1,0:T(8,128)(2,1)}, u32[]{:S(2)}, u32[]{:S(2)}) collective-permute-start(bf16[16,16,512]{2,1,0:T(8,128)(2,1)} %slice.58), channel_id=1, source_target_pairs={{0,16},{16,0},{32,48},{48,32},{64,80},{80,64},{96,112},{112,96},{1... | collective-permute-start | bytes 786440 | tf_op jit(solution)/shard_map/ppermute | solution.py:37
  72.7 2.4 %all-to-all-done.1 = bf16[16,4,512]{2,1,0:T(4,128)(2,1)S(1)} async-done(((bf16[16,4,512]{2,1,0:T(4,128)(2,1)}), bf16[16,4,512]{2,1,0:T(4,128)(2,1)S(1)}, u32[]{:S(2)}, u32[]{:S(2)}) %all-to-all-start.1) | async-done | bytes 65568 | tf_op jit(solution)/shard_map/all_to_all | solution.py:144
  78.8 10.8 %all-to-all-start.2 = ((bf16[16,2,4352]{2,1,0:T(2,128)(2,1)}), bf16[16,2,4352]{2,1,0:T(2,128)(2,1)S(1)}, u32[]{:S(2)}, u32[]{:S(2)}) async-start(bf16[16,2,4352]{2,1,0:T(2,128)(2,1)} %broadcast_in_dim.79), calls=%async_computation.2 | async-start | bytes 557056 | tf_op jit(solution)/shard_map/all_to_all | solution.py:32
  89.6 1.8 %fusion.21 = f32[1024,512]{1,0:T(8,128)} fusion(bf16[1024,16]{0,1:T(8,128)(2,1)S(1)} %fusion.4, bf16[512,2,8]{0,2,1:T(8,128)(2,1)S(1)} %copy.35), kind=kOutput, calls=%fused_computation.66 | convolution fusion | flops 16777216 | bytes 2146304 | tf_op jit(solution)/shard_map/dot_general | solution.py:210
  97.4 3.2 %collective-permute-start.2 = (bf16[512,512]{1,0:T(8,128)(2,1)}, bf16[512,512]{1,0:T(8,128)(2,1)}, u32[]{:S(2)}, u32[]{:S(2)}) collective-permute-start(bf16[512,512]{1,0:T(8,128)(2,1)} %dynamic-slice_bitcast_fusion), channel_id=1, source_target_pairs={{0,8},{1,9},{2,10},{3,11},{4,12},{5,13},{6,14},{7,15},{8,0},{9,1},... | collective-permute-start | bytes 1572872 | tf_op jit(solution)/shard_map/ppermute | solution.py:37
  100.6 3.5 %add_convert_fusion = bf16[1024,512]{1,0:T(8,128)(2,1)} fusion(f32[1024,512]{1,0:T(8,128)} %fusion.21, bf16[1024,512]{1,0:T(8,128)(2,1)S(1)} %bitcast.141, bf16[512,512]{1,0:T(8,128)(2,1)} %bitcast.145), kind=kOutput, calls=%fused_computation.3 | convolution fusion | flops 537919488 | bytes 4718592 | tf_op jit(solution)/shard_map/dot_general | solution.py:211
  106.7 1.9 %collective-permute-start.12 = (bf16[16,2,4352]{2,1,0:T(2,128)(2,1)S(1)}, bf16[16,2,4352]{2,1,0:T(2,128)(2,1)}, u32[]{:S(2)}, u32[]{:S(2)}) collective-permute-start(bf16[16,2,4352]{2,1,0:T(2,128)(2,1)S(1)} %all-to-all-done.2), channel_id=1, source_target_pairs={{0,16},{16,0},{32,48},{48,32},{64,80},{80,64},{96,112},{112,96},{1... | collective-permute-start | bytes 835592 | tf_op jit(solution)/shard_map/ppermute | solution.py:37
  114.4 3.0 %collective-permute-start.3 = (bf16[256,512]{1,0:T(8,128)(2,1)S(1)}, bf16[256,512]{1,0:T(8,128)(2,1)S(1)}, u32[]{:S(2)}, u32[]{:S(2)}) collective-permute-start(bf16[256,512]{1,0:T(8,128)(2,1)S(1)} %dynamic-slice_bitcast_fusion.1), channel_id=1, source_target_pairs={{0,4},{1,5},{2,6},{3,7},{4,0},{5,1},{6,2},{7,3},{8,12},{9,13},{10,... | collective-permute-start | bytes 786440 | tf_op jit(solution)/shard_map/ppermute | solution.py:37
  121.1 7.2 %all-to-all-start.3 = ((f32[16,1,512]{2,1,0:T(1,128)}), f32[16,1,512]{2,1,0:T(1,128)S(1)}, u32[]{:S(2)}, u32[]{:S(2)}) async-start(f32[16,1,512]{2,1,0:T(1,128)} %reshape.155), calls=%async_computation.3 | async-start | bytes 65536 | tf_op jit(solution)/shard_map/all_to_all | solution.py:32
  130.0 2.5 %collective-permute-start.4 = (bf16[128,512]{1,0:T(8,128)(2,1)S(1)}, bf16[128,512]{1,0:T(8,128)(2,1)S(1)}, u32[]{:S(2)}, u32[]{:S(2)}) collective-permute-start(bf16[128,512]{1,0:T(8,128)(2,1)S(1)} %dynamic-slice_bitcast_fusion.2), channel_id=1, source_target_pairs={{0,2},{1,3},{2,0},{3,1},{4,6},{5,7},{6,4},{7,5},{8,10},{9,11},{10,... | collective-permute-start | bytes 393224 | tf_op jit(solution)/shard_map/ppermute | solution.py:37
  134.6 4.5 %collective-permute-done.4 = bf16[128,512]{1,0:T(8,128)(2,1)S(1)} collective-permute-done((bf16[128,512]{1,0:T(8,128)(2,1)S(1)}, bf16[128,512]{1,0:T(8,128)(2,1)S(1)}, u32[]{:S(2)}, u32[]{:S(2)}) %collective-permute-start.4) | collective-permute-done | bytes 131104 | tf_op jit(solution)/shard_map/ppermute | solution.py:37
  139.2 1.9 %collective-permute-start.5 = (bf16[64,512]{1,0:T(8,128)(2,1)S(1)}, bf16[64,512]{1,0:T(8,128)(2,1)S(1)}, u32[]{:S(2)}, u32[]{:S(2)}) collective-permute-start(bf16[64,512]{1,0:T(8,128)(2,1)S(1)} %dynamic-slice_bitcast_fusion.3), channel_id=1, source_target_pairs={{0,1},{1,0},{2,3},{3,2},{4,5},{5,4},{6,7},{7,6},{8,9},{9,8},{10,11... | collective-permute-start | bytes 196616 | tf_op jit(solution)/shard_map/ppermute | solution.py:37
  142.0 3.4 %collective-permute-done.5 = bf16[64,512]{1,0:T(8,128)(2,1)S(1)} collective-permute-done((bf16[64,512]{1,0:T(8,128)(2,1)S(1)}, bf16[64,512]{1,0:T(8,128)(2,1)S(1)}, u32[]{:S(2)}, u32[]{:S(2)}) %collective-permute-start.5) | collective-permute-done | bytes 65568 | tf_op jit(solution)/shard_map/ppermute | solution.py:37
  (142 shorter events, 41.3 us)
Async XLA Ops:
  0.6 60.0 %copy-start = (bf16[1024,512]{1,0:T(8,128)(2,1)S(1)}, bf16[1024,512]{1,0:T(8,128)(2,1)}, u32[]{:S(2)}) copy-start(bf16[1024,512]{1,0:T(8,128)(2,1)} %param.9) | copy-start | bytes 3145732
  0.6 20.5 %copy-start.8 = (bf16[64,512]{1,0:T(8,128)(2,1)S(1)}, bf16[64,512]{1,0:T(8,128)(2,1)}, u32[]{:S(2)}) copy-start(bf16[64,512]{1,0:T(8,128)(2,1)} %param.17) | copy-start | bytes 196612
  0.7 20.3 %copy-start.15 = (s32[1,3]{1,0:T(1,128)S(1)}, s32[1,3]{1,0:T(1,128)}, u32[]{:S(2)}) copy-start(s32[1,3]{1,0:T(1,128)} %param.11) | copy-start | bytes 40
  0.7 20.6 %collective-permute-start.6 = (bf16[64,512]{1,0:T(8,128)(2,1)}, bf16[64,512]{1,0:T(8,128)(2,1)S(1)}, u32[]{:S(2)}, u32[]{:S(2)}) collective-permute-start(bf16[64,512]{1,0:T(8,128)(2,1)} %param.17), channel_id=1, source_target_pairs={{0,1},{1,0},{2,3},{3,2},{4,5},{5,4},{6,7},{7,6},{8,9},{9,8},{10,11... | collective-permute-start | bytes 196616 | tf_op jit(solution)/shard_map/ppermute | solution.py:37
  4.1 17.2 %collective-permute-start.7 = (bf16[64,512]{1,0:T(8,128)(2,1)}, bf16[64,512]{1,0:T(8,128)(2,1)S(1)}, u32[]{:S(2)}, u32[]{:S(2)}) collective-permute-start(bf16[64,512]{1,0:T(8,128)(2,1)} %param.17), channel_id=1, source_target_pairs={{0,2},{1,3},{2,0},{3,1},{4,6},{5,7},{6,4},{7,5},{8,10},{9,11},{10,... | collective-permute-start | bytes 196616 | tf_op jit(solution)/shard_map/ppermute | solution.py:37
  8.1 13.2 %collective-permute-start.8 = (bf16[64,512]{1,0:T(8,128)(2,1)}, bf16[64,512]{1,0:T(8,128)(2,1)S(1)}, u32[]{:S(2)}, u32[]{:S(2)}) collective-permute-start(bf16[64,512]{1,0:T(8,128)(2,1)} %param.17), channel_id=1, source_target_pairs={{0,3},{1,2},{2,1},{3,0},{4,7},{5,6},{6,5},{7,4},{8,11},{9,10},{10,... | collective-permute-start | bytes 196616 | tf_op jit(solution)/shard_map/ppermute | solution.py:37
  16.0 8.8 %collective-permute-start = (bf16[32,4352]{1,0:T(8,128)(2,1)S(1)}, bf16[32,4352]{1,0:T(8,128)(2,1)S(1)}, u32[]{:S(2)}, u32[]{:S(2)}) collective-permute-start(bf16[32,4352]{1,0:T(8,128)(2,1)S(1)} %pad_maximum_fusion.2), channel_id=1, source_target_pairs={{0,16},{16,0},{32,48},{48,32},{64,80},{80,64},{96,112},{112,96},{1... | collective-permute-start | bytes 835592 | tf_op jit(solution)/shard_map/ppermute | solution.py:37
  21.3 27.7 %collective-permute-start.9 = (bf16[256,512]{1,0:T(8,128)(2,1)S(1)}, bf16[256,512]{1,0:T(8,128)(2,1)S(1)}, u32[]{:S(2)}, u32[]{:S(2)}) collective-permute-start(bf16[256,512]{1,0:T(8,128)(2,1)S(1)} %bitcast.148), channel_id=1, source_target_pairs={{0,4},{1,5},{2,6},{3,7},{4,0},{5,1},{6,2},{7,3},{8,12},{9,13},{10,... | collective-permute-start | bytes 786440 | tf_op jit(solution)/shard_map/ppermute | solution.py:37
  26.1 33.9 %all-to-all-start = ((bf16[16,33,512]{2,1,0:T(8,128)(2,1)}), bf16[16,33,512]{2,1,0:T(8,128)(2,1)S(1)}, u32[]{:S(2)}, u32[]{:S(2)}) async-start(bf16[16,33,512]{2,1,0:T(8,128)(2,1)} %pad_maximum_fusion), calls=%async_computation | async-start | bytes 1310720 | tf_op jit(solution)/shard_map/all_to_all | solution.py:112
  41.8 11.4 %collective-permute-start.10 = (bf16[256,512]{1,0:T(8,128)(2,1)S(1)}, bf16[256,512]{1,0:T(8,128)(2,1)S(1)}, u32[]{:S(2)}, u32[]{:S(2)}) collective-permute-start(bf16[256,512]{1,0:T(8,128)(2,1)S(1)} %bitcast.149), channel_id=1, source_target_pairs={{0,8},{1,9},{2,10},{3,11},{4,12},{5,13},{6,14},{7,15},{8,0},{9,1},... | collective-permute-start | bytes 786440 | tf_op jit(solution)/shard_map/ppermute | solution.py:37
  46.5 12.2 %collective-permute-start.11 = (bf16[256,512]{1,0:T(8,128)(2,1)S(1)}, bf16[256,512]{1,0:T(8,128)(2,1)S(1)}, u32[]{:S(2)}, u32[]{:S(2)}) collective-permute-start(bf16[256,512]{1,0:T(8,128)(2,1)S(1)} %bitcast.150), channel_id=1, source_target_pairs={{0,12},{1,13},{2,14},{3,15},{4,8},{5,9},{6,10},{7,11},{8,4},{9,5},... | collective-permute-start | bytes 786440 | tf_op jit(solution)/shard_map/ppermute | solution.py:37
  62.8 12.4 %all-to-all-start.1 = ((bf16[16,4,512]{2,1,0:T(4,128)(2,1)}), bf16[16,4,512]{2,1,0:T(4,128)(2,1)S(1)}, u32[]{:S(2)}, u32[]{:S(2)}) async-start(bf16[16,4,512]{2,1,0:T(4,128)(2,1)} %pad_maximum_fusion.3), calls=%async_computation.1 | async-start | bytes 131072 | tf_op jit(solution)/shard_map/all_to_all | solution.py:144
  70.8 20.6 %collective-permute-start.1 = (bf16[16,16,512]{2,1,0:T(8,128)(2,1)}, bf16[16,16,512]{2,1,0:T(8,128)(2,1)}, u32[]{:S(2)}, u32[]{:S(2)}) collective-permute-start(bf16[16,16,512]{2,1,0:T(8,128)(2,1)} %slice.58), channel_id=1, source_target_pairs={{0,16},{16,0},{32,48},{48,32},{64,80},{80,64},{96,112},{112,96},{1... | collective-permute-start | bytes 786440 | tf_op jit(solution)/shard_map/ppermute | solution.py:37
  78.8 25.3 %all-to-all-start.2 = ((bf16[16,2,4352]{2,1,0:T(2,128)(2,1)}), bf16[16,2,4352]{2,1,0:T(2,128)(2,1)S(1)}, u32[]{:S(2)}, u32[]{:S(2)}) async-start(bf16[16,2,4352]{2,1,0:T(2,128)(2,1)} %broadcast_in_dim.79), calls=%async_computation.2 | async-start | bytes 557056 | tf_op jit(solution)/shard_map/all_to_all | solution.py:32
  97.4 15.7 %collective-permute-start.2 = (bf16[512,512]{1,0:T(8,128)(2,1)}, bf16[512,512]{1,0:T(8,128)(2,1)}, u32[]{:S(2)}, u32[]{:S(2)}) collective-permute-start(bf16[512,512]{1,0:T(8,128)(2,1)} %dynamic-slice_bitcast_fusion), channel_id=1, source_target_pairs={{0,8},{1,9},{2,10},{3,11},{4,12},{5,13},{6,14},{7,15},{8,0},{9,1},... | collective-permute-start | bytes 1572872 | tf_op jit(solution)/shard_map/ppermute | solution.py:37
  106.7 10.7 %collective-permute-start.12 = (bf16[16,2,4352]{2,1,0:T(2,128)(2,1)S(1)}, bf16[16,2,4352]{2,1,0:T(2,128)(2,1)}, u32[]{:S(2)}, u32[]{:S(2)}) collective-permute-start(bf16[16,2,4352]{2,1,0:T(2,128)(2,1)S(1)} %all-to-all-done.2), channel_id=1, source_target_pairs={{0,16},{16,0},{32,48},{48,32},{64,80},{80,64},{96,112},{112,96},{1... | collective-permute-start | bytes 835592 | tf_op jit(solution)/shard_map/ppermute | solution.py:37
  114.3 18.2 %copy-start.6 = (bf16[32,16]{0,1:T(8,128)(2,1)S(1)}, bf16[32,16]{0,1:T(8,128)(2,1)}, u32[]{:S(2)}) copy-start(bf16[32,16]{0,1:T(8,128)(2,1)} %copy-done.5) | copy-start | bytes 3076
  114.3 26.8 %copy-start.9 = (bf16[32,1024]{1,0:T(8,128)(2,1)S(1)}, bf16[32,1024]{1,0:T(8,128)(2,1)}, u32[]{:S(2)}) copy-start(bf16[32,1024]{1,0:T(8,128)(2,1)} %param.13) | copy-start | bytes 196612
  114.3 26.8 %copy-start.12 = (f32[32,16]{0,1:T(8,128)S(1)}, f32[32,16]{0,1:T(8,128)}, u32[]{:S(2)}) copy-start(f32[32,16]{0,1:T(8,128)} %get-tuple-element.10) | copy-start | bytes 6148
  114.3 31.0 %copy-start.4 = (f32[64,512]{1,0:T(8,128)S(1)}, f32[64,512]{1,0:T(8,128)}, u32[]{:S(2)}) copy-start(f32[64,512]{1,0:T(8,128)} %fusion.46) | copy-start | bytes 393220
  114.4 15.5 %collective-permute-start.3 = (bf16[256,512]{1,0:T(8,128)(2,1)S(1)}, bf16[256,512]{1,0:T(8,128)(2,1)S(1)}, u32[]{:S(2)}, u32[]{:S(2)}) collective-permute-start(bf16[256,512]{1,0:T(8,128)(2,1)S(1)} %dynamic-slice_bitcast_fusion.1), channel_id=1, source_target_pairs={{0,4},{1,5},{2,6},{3,7},{4,0},{5,1},{6,2},{7,3},{8,12},{9,13},{10,... | collective-permute-start | bytes 786440 | tf_op jit(solution)/shard_map/ppermute | solution.py:37
  121.1 12.2 %all-to-all-start.3 = ((f32[16,1,512]{2,1,0:T(1,128)}), f32[16,1,512]{2,1,0:T(1,128)S(1)}, u32[]{:S(2)}, u32[]{:S(2)}) async-start(f32[16,1,512]{2,1,0:T(1,128)} %reshape.155), calls=%async_computation.3 | async-start | bytes 65536 | tf_op jit(solution)/shard_map/all_to_all | solution.py:32
  130.0 9.2 %collective-permute-start.4 = (bf16[128,512]{1,0:T(8,128)(2,1)S(1)}, bf16[128,512]{1,0:T(8,128)(2,1)S(1)}, u32[]{:S(2)}, u32[]{:S(2)}) collective-permute-start(bf16[128,512]{1,0:T(8,128)(2,1)S(1)} %dynamic-slice_bitcast_fusion.2), channel_id=1, source_target_pairs={{0,2},{1,3},{2,0},{3,1},{4,6},{5,7},{6,4},{7,5},{8,10},{9,11},{10,... | collective-permute-start | bytes 393224 | tf_op jit(solution)/shard_map/ppermute | solution.py:37
  139.2 6.2 %collective-permute-start.5 = (bf16[64,512]{1,0:T(8,128)(2,1)S(1)}, bf16[64,512]{1,0:T(8,128)(2,1)S(1)}, u32[]{:S(2)}, u32[]{:S(2)}) collective-permute-start(bf16[64,512]{1,0:T(8,128)(2,1)S(1)} %dynamic-slice_bitcast_fusion.3), channel_id=1, source_target_pairs={{0,1},{1,0},{2,3},{3,2},{4,5},{5,4},{6,7},{7,6},{8,9},{9,8},{10,11... | collective-permute-start | bytes 196616 | tf_op jit(solution)/shard_map/ppermute | solution.py:37
  (9 other events, 57.1 us)

commit v4 on v3

v4 whole, which is shorter than its diff:
```python
import math

import jax
import jax.numpy as jnp
from jax import lax
from jax.sharding import PartitionSpec as P

D = 8192
KV = 512
R = 8
NTASK = 32
SEQS = 2
ADA = SEQS * R

precise = lax.Precision.HIGHEST
inner_dims = (((1,), (1,)), ((), ()))
outer_dims = (((0,), (0,)), ((), ()))
bf16 = jnp.bfloat16
f32 = jnp.float32

CORES = 2
Y_RUN = 4


def silu_slope(pre_act):
    sigma = jax.nn.sigmoid(pre_act)
    return sigma * (1.0 + pre_act * (1.0 - sigma))


def spread(block, axes, count, **kw):
    copies = jnp.broadcast_to(block[None], (count,) + block.shape)
    return lax.all_to_all(copies, axes, 0, 0, **kw)


def swapped(block, axis, distance):
    pairs = [(i, i ^ distance) for i in range(lax.axis_size(axis))]
    return lax.ppermute(block, axis, pairs)


def zero_after(value):
    first = value.reshape(-1)[0].astype(f32)
    return (jnp.floor(first) > first).astype(jnp.int32)


def parts_of(value):
    parts = []
    for _ in range(3):
        part = lax.reduce_precision(value, 8, 7)
        parts.append(part.astype(bf16))
        value = value - part
    return parts


def shards(
    tokens, value_weight, seq_lengths, task_ids, task_embed, hyper_in, head_a, head_b, cotangent
):
    n_dp = lax.axis_size("dp")
    n_chips = n_dp // CORES
    n_tensor = lax.axis_size("tensor")
    n_x = n_tensor // Y_RUN
    rows_total, width_own = tokens.shape
    rows_own = rows_total // n_tensor
    outputs_own = KV // n_tensor
    down_width = width_own * R
    up_width = outputs_own * R
    along_y = [[x * Y_RUN + y for y in range(Y_RUN)] for x in range(n_x)]
    along_x = [[x * Y_RUN + y for x in range(n_x)] for y in range(Y_RUN)]
    same_core = [[chip * CORES + core for chip in range(n_chips)] for core in range(CORES)]
    core = lax.axis_index("dp") % CORES
    place = lax.axis_index("tensor")

    pre_act = jnp.dot(task_embed, hyper_in, preferred_element_type=f32)
    hidden = jax.nn.silu(pre_act).astype(bf16)

    def chosen_by(which):
        ids = lax.dynamic_index_in_dim(
            task_ids.reshape(n_chips, CORES, SEQS), which, 1, keepdims=False
        ).reshape(n_chips * SEQS)
        hot = (ids[:, None] == jnp.arange(NTASK, dtype=jnp.int32)[None, :]).astype(bf16)
        return hot, jnp.dot(hot, hidden, preferred_element_type=f32).astype(bf16)

    def terms_of(pick):
        return jnp.concatenate(
            (
                jnp.dot(pick, head_a, preferred_element_type=f32),
                jnp.dot(pick, head_b, preferred_element_type=f32),
            ),
            axis=1,
        )

    hot_mate, pick_mate = chosen_by(1 - core)
    hot_mine, pick_mine = chosen_by(core)
    from_mate = swapped(terms_of(pick_mate).astype(bf16), "dp", 1)
    terms = (terms_of(pick_mine) + from_mate.astype(f32)).astype(bf16)
    term_width = down_width + up_width
    weight_own = value_weight.T.reshape(1, SEQS, -1)
    sent = jnp.concatenate(
        (
            terms.reshape(n_chips, SEQS, term_width),
            jnp.broadcast_to(weight_own, (n_chips,) + weight_own.shape[1:]),
        ),
        axis=2,
    )
    came = lax.all_to_all(sent, "dp", 0, 0, axis_index_groups=same_core)
    sums = jnp.sum(came[:, :, :term_width].astype(f32), axis=0)
    down_pick = (sums[:, :down_width] * (1.0 / math.sqrt(D))).astype(bf16)
    up_pick = (sums[:, down_width:] * (1.0 / math.sqrt(R))).astype(bf16)
    down_cat_t = (
        down_pick.reshape(SEQS, width_own, R).transpose(0, 2, 1).reshape(ADA, width_own)
    )
    up_pick_t = (
        up_pick.reshape(SEQS, outputs_own, R).transpose(0, 2, 1).reshape(ADA, outputs_own)
    )

    lengths = seq_lengths[0]
    finish = jnp.cumsum(lengths)
    anchor = finish - lengths
    places = jnp.arange(rows_total, dtype=jnp.int32)[None, :]
    inside = (places >= anchor[:SEQS, None]) & (places < finish[:SEQS, None])
    row_mask = jnp.repeat(inside.astype(f32), R, axis=0)

    low_part = (
        lax.dot_general(down_cat_t, tokens, inner_dims, preferred_element_type=f32) * row_mask
    ).astype(bf16)
    low_lines = ADA * rows_total // KV

    def as_lines(rows):
        return jnp.concatenate(
            [rows[:, i * KV : (i + 1) * KV] for i in range(rows_total // KV)], axis=0
        )

    def as_rows(lines):
        return jnp.concatenate(
            [lines[i * ADA : (i + 1) * ADA] for i in range(rows_total // KV)], axis=1
        )

    up_line = up_pick_t.reshape(-1, KV)
    block = jnp.concatenate((cotangent, as_lines(low_part), up_line), axis=0)
    from_y = spread(block, "tensor", Y_RUN, axis_index_groups=along_y)
    low_y = jnp.sum(from_y[:, rows_own : rows_own + low_lines].astype(f32), axis=0).astype(bf16)
    run_rows = Y_RUN * rows_own
    run = jnp.concatenate(
        (
            from_y[:, :rows_own].reshape(run_rows, KV),
            low_y,
            from_y[:, rows_own + low_lines :].reshape(-1, KV),
        ),
        axis=0,
    )
    from_x = spread(run, "tensor", n_x, axis_index_groups=along_x)
    cot_full = from_x[:, :run_rows].reshape(rows_total, KV)
    low_rank = as_rows(
        jnp.sum(from_x[:, run_rows : run_rows + low_lines].astype(f32), axis=0)
    )
    up_cat_t = (
        from_x[:, run_rows + low_lines :]
        .reshape(n_tensor, ADA, outputs_own)
        .transpose(1, 0, 2)
        .reshape(ADA, KV)
    )

    weight_mine = came[:, :, term_width:]
    weight_mate = swapped(weight_mine, "dp", 1)
    weight_mine = weight_mine.reshape(n_chips, KV // n_dp, width_own)
    weight_mate = weight_mate.reshape(n_chips, KV // n_dp, width_own)
    weight_t = jnp.stack(
        (
            jnp.where(core == 0, weight_mine, weight_mate),
            jnp.where(core == 0, weight_mate, weight_mine),
        ),
        axis=1,
    ).reshape(KV, width_own)
    weight_full = lax.optimization_barrier(weight_t.T)
    frozen = jnp.dot(tokens, weight_full, preferred_element_type=f32).astype(bf16)

    back_low = (
        lax.dot_general(up_cat_t, cot_full, inner_dims, preferred_element_type=f32) * row_mask
    ).astype(bf16)
    down_grad = jnp.dot(back_low, tokens, preferred_element_type=f32)
    down_seq = down_grad.reshape(SEQS, R, width_own).transpose(0, 2, 1).reshape(SEQS, down_width)
    low_parts = jnp.concatenate(parts_of(low_rank), axis=0)
    up_grad = jnp.sum(
        jnp.dot(low_parts, cot_full, preferred_element_type=f32).reshape(3, ADA, KV), axis=0
    )
    up_grad = lax.dynamic_slice_in_dim(up_grad, place * outputs_own, outputs_own, 1)
    up_seq = up_grad.reshape(SEQS, R, outputs_own).transpose(0, 2, 1).reshape(SEQS, up_width)
    own_grads = jnp.concatenate((down_seq, up_seq), axis=1).astype(bf16)
    grads_mine = spread(own_grads, "dp", n_chips, axis_index_groups=same_core)
    adapter_back = lax.dot_general(back_low, down_cat_t, outer_dims, preferred_element_type=f32)
    frozen_back = jnp.dot(cot_full, weight_t, preferred_element_type=f32)
    grad_tokens = (frozen_back + adapter_back).astype(bf16)
    frozen_x = frozen.reshape(n_x, Y_RUN * rows_own, KV)
    place_x = place // Y_RUN
    frozen_kept = lax.dynamic_index_in_dim(frozen_x, place_x, 0, keepdims=False)
    later = zero_after(grad_tokens[:1, :1])
    frozen_came = [
        swapped(
            lax.dynamic_index_in_dim(frozen_x, (place_x ^ step) + later, 0, keepdims=False),
            "tensor",
            step * Y_RUN,
        )
        for step in range(1, n_x)
    ]
    grads_mate = swapped(grads_mine, "dp", 1)

    down_scale = 1.0 / math.sqrt(D)
    up_scale = 1.0 / math.sqrt(R)

    def hidden_terms(grads, hot):
        rows = grads.reshape(n_chips * SEQS, -1)
        part = down_scale * lax.dot_general(
            rows[:, :down_width], head_a, inner_dims, preferred_element_type=f32
        ) + up_scale * lax.dot_general(
            rows[:, down_width:], head_b, inner_dims, preferred_element_type=f32
        )
        return lax.dot_general(hot.astype(f32), part, outer_dims, precision=precise)

    by_task = hidden_terms(grads_mine, hot_mine) + hidden_terms(grads_mate, hot_mate)
    hidden_x = jnp.sum(
        spread(by_task.reshape(1, -1), "tensor", n_x, axis_index_groups=along_x), axis=0
    )

    rows_x = frozen_kept.astype(f32)
    for other in frozen_came:
        rows_x = rows_x + other.astype(f32)
    last = jnp.concatenate(
        (
            rows_x.astype(bf16).reshape(Y_RUN, rows_own, KV),
            jnp.broadcast_to(
                jnp.concatenate(parts_of(hidden_x), axis=0).reshape(1, -1, KV),
                (Y_RUN, 3 * hidden_x.size // KV, KV),
            ),
        ),
        axis=1,
    )
    last = jnp.sum(
        lax.all_to_all(last, "tensor", 0, 0, axis_index_groups=along_y).astype(f32), axis=0
    )
    frozen_rows = last[:rows_own]
    grad_hidden = jnp.sum(last[rows_own:].reshape((3,) + by_task.shape), axis=0)

    last_zero = zero_after(hidden_x).astype(bf16)

    def head_grads(grads, pick):
        rows = grads.reshape(n_chips * SEQS, -1)
        pick = pick + last_zero
        return (
            lax.dot_general(pick, rows[:, :down_width], outer_dims, preferred_element_type=f32),
            lax.dot_general(pick, rows[:, down_width:], outer_dims, preferred_element_type=f32),
        )

    of_mine = head_grads(grads_mine, pick_mine)
    of_mate = head_grads(grads_mate, pick_mate)
    grad_head_a = down_scale * (of_mine[0] + of_mate[0])
    grad_head_b = up_scale * (of_mine[1] + of_mate[1])
    grad_pre = grad_hidden * silu_slope(pre_act)
    grad_hyper_in = lax.dot_general(
        task_embed.astype(f32), grad_pre, outer_dims, precision=precise
    )

    low_own = lax.dynamic_slice_in_dim(low_rank, place * rows_own, rows_own, 1)
    adapter = lax.dot_general(low_own, up_cat_t.astype(f32), outer_dims, precision=precise)
    values = (frozen_rows + adapter).astype(bf16)
    return (values, grad_tokens, grad_head_a, grad_head_b, grad_hyper_in)


def solution(mesh):
    placed = (
        P("dp", "tensor"),
        P("tensor", "dp"),
        P("dp", None),
        P(),
        P(),
        P(None, "dp"),
        P("dp", "tensor"),
        P("dp", "tensor"),
        P(("dp", "tensor"), None),
    )
    return jax.shard_map(
        shards,
        mesh=mesh,
        in_specs=placed,
        out_specs=(
            P(("dp", "tensor"), None),
            P("dp", "tensor"),
            P("dp", "tensor"),
            P("dp", "tensor"),
            P(None, "dp"),
        ),
        check_vma=False,
    )
```

time: 147 us -> 148 us (level)
  waiting for transfers between devices: 22.9 us -> 41.9 us
  starting transfers between devices: 78 us -> 61.4 us
  matrix products: 25.5 us -> 15.9 us
  local copies, waits for them, and re-layouts: 12.3 us -> 18 us
  between operations: 1.4 us -> 3.83 us
    ppermute x13 -> x6, starting transfers between devices: 37 us -> 16.3 us  [swapped(): return lax.ppermute(block, axis, pairs)]
    all_to_all x2 -> x4, waiting for transfers between devices: 0.05 us -> 19.5 us  [spread(): return lax.all_to_all(copies, axes, 0, 0, **kw)]
    ppermute x13 -> x6, waiting for transfers between devices: 19.1 us -> 1.48 us  [swapped(): return lax.ppermute(block, axis, pairs)]
    all_to_all x1, waiting for transfers between devices: 1.25 us -> 15.9 us  [shards(): came = lax.all_to_all(sent, 'dp', 0, 0, axis_index_groups=same_core)]
    dot_general x17, matrix products: 15.2 us -> 7.28 us  [the longest x1 1.71 us: shards(): jnp.dot(tokens, weight_full, preferred_element_type=f32).astype(bf16)]
    all_to_all x2 -> x4, starting transfers between devices: 18 us -> 23.6 us  [spread(): return lax.all_to_all(copies, axes, 0, 0, **kw)]
    broadcast_in_dim x1 -> x5, local copies, waits for them, and re-layouts: 0.84 us -> 3.47 us  [spread(): copies = jnp.broadcast_to(block[None], (count,) + block.shape)]
    all_to_all x1, waiting for transfers between devices: 2.44 us -> 5.04 us  [shards(): lax.all_to_all(last, 'tensor', 0, 0, axis_index_groups=along_y).astype(f32)]
  transfers between devices with their start and end apart: 17 -> 12, of which waited for: 7 -> 7; matrix products, arithmetic and copies ran while one was open for 27% -> 15% of each run, Pallas kernels for 0% -> 0%
where the time goes in v4:
time: 148 us; the launch traced here: 147 us
  starting transfers between devices  61.4 us (41%)
  waiting for transfers between devices  41.9 us (28%)
  local copies, waits for them, and re-layouts  18 us (12%)
  matrix products  15.9 us (11%)
  other arithmetic  6.18 us (4%)
  between operations  3.83 us (3%)
    all_to_all x4, starting transfers between devices, spread(): return lax.all_to_all(copies, axes, 0, 0, **kw)  23.6 us
    all_to_all x4, waiting for transfers between devices, spread(): return lax.all_to_all(copies, axes, 0, 0, **kw)  19.5 us
    ppermute x6, starting transfers between devices, swapped(): return lax.ppermute(block, axis, pairs)  16.3 us
    all_to_all x1, waiting for transfers between devices, shards(): came = lax.all_to_all(sent, 'dp', 0, 0, axis_index_groups=same_core)  15.9 us
    all_to_all x1, starting transfers between devices, shards(): came = lax.all_to_all(sent, 'dp', 0, 0, axis_index_groups=same_core)  15.7 us
    all_to_all x1, starting transfers between devices, shards(): lax.all_to_all(last, 'tensor', 0, 0, axis_index_groups=along_y).astype(f32)  5.87 us
    all_to_all x1, waiting for transfers between devices, shards(): lax.all_to_all(last, 'tensor', 0, 0, axis_index_groups=along_y).astype(f32)  5.04 us
    broadcast_in_dim x5, local copies, waits for them, and re-layouts, spread(): copies = jnp.broadcast_to(block[None], (count,) + block.shape)  3.47 us
  transfers between devices with their start and end apart: 12, of which 7 were waited for; matrix products, arithmetic and copies ran while one was open for 15% of the time, Pallas kernels for 0%

profile of v4, /device:TPU:56, one launch (start us, length us, event | category | flops | bytes accessed | tf_op | source)
XLA Modules:
  0.0 147.3 jit_solution(7439004882001133800)
XLA Ops:
  1.9 1.6 %multiply_convert_fusion = (bf16[32,16]{0,1:T(8,128)(2,1)S(1)}, f32[32,16]{0,1:T(8,128)}) fusion(bf16[32,1024]{1,0:T(8,128)(2,1)} %param.13, bf16[1024,16]{0,1:T(8,128)(2,1)} %param.14), kind=kOutput, calls=%fused_computation.88 | convolution fusion | flops 1051136 | bytes 101376 | tf_op jit(solution)/shard_map/dot_general | solution.py:72
  5.8 1.9 %collective-permute-start = (bf16[32,4352]{1,0:T(8,128)(2,1)S(1)}, bf16[32,4352]{1,0:T(8,128)(2,1)S(1)}, u32[]{:S(2)}, u32[]{:S(2)}) collective-permute-start(bf16[32,4352]{1,0:T(8,128)(2,1)S(1)} %pad_maximum_fusion.3), channel_id=1, source_target_pairs={{0,16},{16,0},{32,48},{48,32},{64,80},{80,64},{96,112},{112,96},{1... | collective-permute-start | bytes 835592 | tf_op jit(solution)/shard_map/ppermute | solution.py:37
  11.9 1.3 pad_maximum_fusion
  13.1 15.7 %all-to-all-start = ((bf16[16,2,8448]{2,1,0:T(2,128)(2,1)}), bf16[16,2,8448]{2,1,0:T(2,128)(2,1)S(1)}, u32[]{:S(2)}, u32[]{:S(2)}) async-start(bf16[16,2,8448]{2,1,0:T(2,128)(2,1)} %pad_maximum_fusion), calls=%async_computation | async-start | bytes 1081344 | tf_op jit(solution)/shard_map/all_to_all | solution.py:104
  29.1 15.9 %all-to-all-done = bf16[16,2,8448]{2,1,0:T(2,128)(2,1)S(1)} async-done(((bf16[16,2,8448]{2,1,0:T(2,128)(2,1)}), bf16[16,2,8448]{2,1,0:T(2,128)(2,1)S(1)}, u32[]{:S(2)}, u32[]{:S(2)}) %all-to-all-start) | async-done | bytes 540704 | tf_op jit(solution)/shard_map/all_to_all | solution.py:104
  47.2 6.0 %all-to-all-start.1 = ((bf16[4,97,512]{2,1,0:T(8,128)(2,1)}), bf16[4,97,512]{2,1,0:T(8,128)(2,1)S(1)}, u32[]{:S(2)}, u32[]{:S(2)}) async-start(bf16[4,97,512]{2,1,0:T(8,128)(2,1)} %broadcast_in_dim.21), calls=%async_computation.1 | async-start | bytes 851968 | tf_op jit(solution)/shard_map/all_to_all | solution.py:32
  54.2 1.9 %collective-permute-start.1 = (bf16[16,2,4096]{2,1,0:T(2,128)(2,1)}, bf16[16,2,4096]{2,1,0:T(2,128)(2,1)}, u32[]{:S(2)}, u32[]{:S(2)}) collective-permute-start(bf16[16,2,4096]{2,1,0:T(2,128)(2,1)} %slice.102), channel_id=1, source_target_pairs={{0,16},{16,0},{32,48},{48,32},{64,80},{80,64},{96,112},{112,96},{1... | collective-permute-start | bytes 786440 | tf_op jit(solution)/shard_map/ppermute | solution.py:37
  56.2 6.6 %all-to-all-done.1 = bf16[4,97,512]{2,1,0:T(8,128)(2,1)S(1)} async-done(((bf16[4,97,512]{2,1,0:T(8,128)(2,1)}), bf16[4,97,512]{2,1,0:T(8,128)(2,1)S(1)}, u32[]{:S(2)}, u32[]{:S(2)}) %all-to-all-start.1) | async-done | bytes 397344 | tf_op jit(solution)/shard_map/all_to_all | solution.py:32
  64.0 4.3 %all-to-all-start.2 = ((bf16[4,292,512]{2,1,0:T(8,128)(2,1)}), bf16[4,292,512]{2,1,0:T(8,128)(2,1)S(1)}, u32[]{:S(2)}, u32[]{:S(2)}) async-start(bf16[4,292,512]{2,1,0:T(8,128)(2,1)} %broadcast_in_dim.22), calls=%async_computation.2 | async-start | bytes 2424832 | tf_op jit(solution)/shard_map/all_to_all | solution.py:32
  68.3 2.1 %broadcast_select_fusion = (bf16[16,2,4096]{2,1,0:T(2,128)(2,1)}, bf16[16,2,4096]{2,1,0:T(2,128)(2,1)S(1)}) fusion(bf16[16,2,4096]{2,1,0:T(2,128)(2,1)} %collective-permute-done.1, pred[]{:T(512)S(6)} %eq.36, bf16[16,2,8448]{2,1,0:T(2,128)(2,1)S(1)} %all-to-all-done), kind=kLoop, calls=%fused_computation.37 | loop fusion | flops 262144 | bytes 1048577 | tf_op jit(solution)/shard_map/jit(_where)/select_n | solution.py:169
  71.7 1.7 %fusion.1 = bf16[1024,512]{0,1:T(8,128)(2,1)} fusion(bf16[512,512]{0,1:T(8,128)(2,1)S(1)} %bitcast.100, bf16[1024,512]{1,0:T(8,128)(2,1)S(1)} %copy-done), kind=kOutput, calls=%fused_computation.5 | convolution fusion | flops 537395200 | bytes 2621440 | tf_op jit(solution)/shard_map/dot_general | solution.py:174
  73.4 2.3 %copy.85 = bf16[1024,512]{1,0:T(8,128)(2,1)} copy(bf16[1024,512]{0,1:T(8,128)(2,1)} %fusion.1) | data formatting | bytes 2097152 | tf_op jit(solution)/shard_map/reshape | solution.py:192
  75.7 9.2 %all-to-all-done.2 = bf16[4,292,512]{2,1,0:T(8,128)(2,1)S(1)} async-done(((bf16[4,292,512]{2,1,0:T(8,128)(2,1)}), bf16[4,292,512]{2,1,0:T(8,128)(2,1)S(1)}, u32[]{:S(2)}, u32[]{:S(2)}) %all-to-all-start.2) | async-done | bytes 1196064 | tf_op jit(solution)/shard_map/all_to_all | solution.py:32
  89.5 10.0 %all-to-all-start.3 = ((bf16[16,2,4352]{2,1,0:T(2,128)(2,1)}), bf16[16,2,4352]{2,1,0:T(2,128)(2,1)S(1)}, u32[]{:S(2)}, u32[]{:S(2)}) async-start(bf16[16,2,4352]{2,1,0:T(2,128)(2,1)} %broadcast_in_dim.23), calls=%async_computation.3 | async-start | bytes 557056 | tf_op jit(solution)/shard_map/all_to_all | solution.py:32
  100.0 1.8 %add_convert_fusion = bf16[1024,512]{1,0:T(8,128)(2,1)S(1)} fusion(f32[1024,512]{1,0:T(8,128)S(1)} %fusion.21, bf16[1024,512]{1,0:T(8,128)(2,1)S(1)} %bitcast.97, bf16[512,512]{1,0:T(8,128)(2,1)} %bitcast.101), kind=kOutput, calls=%fused_computation.3 | convolution fusion | flops 537919488 | bytes 4718592 | tf_op jit(solution)/shard_map/dot_general | solution.py:190
  105.5 2.6 %collective-permute-start.2 = (bf16[256,512]{1,0:T(8,128)(2,1)}, bf16[256,512]{1,0:T(8,128)(2,1)}, u32[]{:S(2)}, u32[]{:S(2)}) collective-permute-start(bf16[256,512]{1,0:T(8,128)(2,1)} %get-tuple-element.5), channel_id=1, source_target_pairs={{0,4},{1,5},{2,6},{3,7},{4,0},{5,1},{6,2},{7,3},{8,12},{9,13},{10,... | collective-permute-start | bytes 786440 | tf_op jit(solution)/shard_map/ppermute | solution.py:37
  108.1 4.0 %collective-permute-start.3 = (bf16[256,512]{1,0:T(8,128)(2,1)}, bf16[256,512]{1,0:T(8,128)(2,1)}, u32[]{:S(2)}, u32[]{:S(2)}) collective-permute-start(bf16[256,512]{1,0:T(8,128)(2,1)} %get-tuple-element.7), channel_id=1, source_target_pairs={{0,8},{1,9},{2,10},{3,11},{4,12},{5,13},{6,14},{7,15},{8,0},{9,1},... | collective-permute-start | bytes 786440 | tf_op jit(solution)/shard_map/ppermute | solution.py:37
  112.1 4.0 %collective-permute-start.4 = (bf16[256,512]{1,0:T(8,128)(2,1)}, bf16[256,512]{1,0:T(8,128)(2,1)}, u32[]{:S(2)}, u32[]{:S(2)}) collective-permute-start(bf16[256,512]{1,0:T(8,128)(2,1)} %get-tuple-element.6), channel_id=1, source_target_pairs={{0,12},{1,13},{2,14},{3,15},{4,8},{5,9},{6,10},{7,11},{8,4},{9,5},... | collective-permute-start | bytes 786440 | tf_op jit(solution)/shard_map/ppermute | solution.py:37
  116.4 1.9 %collective-permute-start.5 = (bf16[16,2,4352]{2,1,0:T(2,128)(2,1)S(1)}, bf16[16,2,4352]{2,1,0:T(2,128)(2,1)S(1)}, u32[]{:S(2)}, u32[]{:S(2)}) collective-permute-start(bf16[16,2,4352]{2,1,0:T(2,128)(2,1)S(1)} %all-to-all-done.3), channel_id=1, source_target_pairs={{0,16},{16,0},{32,48},{48,32},{64,80},{80,64},{96,112},{112,96},{1... | collective-permute-start | bytes 835592 | tf_op jit(solution)/shard_map/ppermute | solution.py:37
  121.3 3.2 %all-to-all-start.4 = ((f32[4,1,512]{2,1,0:T(1,128)}), f32[4,1,512]{2,1,0:T(1,128)S(1)}, u32[]{:S(2)}, u32[]{:S(2)}) async-start(f32[4,1,512]{2,1,0:T(1,128)} %broadcast_in_dim.25), calls=%async_computation.4 | async-start | bytes 16384 | tf_op jit(solution)/shard_map/all_to_all | solution.py:32
  124.9 1.2 fusion.12
  126.1 3.7 %all-to-all-done.4 = f32[4,1,512]{2,1,0:T(1,128)S(1)} async-done(((f32[4,1,512]{2,1,0:T(1,128)}), f32[4,1,512]{2,1,0:T(1,128)S(1)}, u32[]{:S(2)}, u32[]{:S(2)}) %all-to-all-start.4) | async-done | bytes 8224 | tf_op jit(solution)/shard_map/all_to_all | solution.py:32
  132.8 5.9 %all-to-all-start.5 = ((bf16[4,67,512]{2,1,0:T(8,128)(2,1)}), bf16[4,67,512]{2,1,0:T(8,128)(2,1)S(1)}, u32[]{:S(2)}, u32[]{:S(2)}) async-start(bf16[4,67,512]{2,1,0:T(8,128)(2,1)} %pad_maximum_fusion.2), calls=%async_computation.5 | async-start | bytes 589824 | tf_op jit(solution)/shard_map/all_to_all | solution.py:237
  140.2 5.0 %all-to-all-done.5 = bf16[4,67,512]{2,1,0:T(8,128)(2,1)S(1)} async-done(((bf16[4,67,512]{2,1,0:T(8,128)(2,1)}), bf16[4,67,512]{2,1,0:T(8,128)(2,1)S(1)}, u32[]{:S(2)}, u32[]{:S(2)}) %all-to-all-start.5) | async-done | bytes 274464 | tf_op jit(solution)/shard_map/all_to_all | solution.py:237
  (136 shorter events, 29.5 us)
Async XLA Ops:
  0.6 45.1 %copy-start = (bf16[1024,512]{1,0:T(8,128)(2,1)S(1)}, bf16[1024,512]{1,0:T(8,128)(2,1)}, u32[]{:S(2)}) copy-start(bf16[1024,512]{1,0:T(8,128)(2,1)} %param.9) | copy-start | bytes 3145732
  5.8 5.7 %collective-permute-start = (bf16[32,4352]{1,0:T(8,128)(2,1)S(1)}, bf16[32,4352]{1,0:T(8,128)(2,1)S(1)}, u32[]{:S(2)}, u32[]{:S(2)}) collective-permute-start(bf16[32,4352]{1,0:T(8,128)(2,1)S(1)} %pad_maximum_fusion.3), channel_id=1, source_target_pairs={{0,16},{16,0},{32,48},{48,32},{64,80},{80,64},{96,112},{112,96},{1... | collective-permute-start | bytes 835592 | tf_op jit(solution)/shard_map/ppermute | solution.py:37
  11.4 17.4 %copy-start.17 = (s32[1,3]{1,0:T(1,128)S(1)}, s32[1,3]{1,0:T(1,128)}, u32[]{:S(2)}) copy-start(s32[1,3]{1,0:T(1,128)} %param.11) | copy-start | bytes 40
  11.8 34.6 %copy-start.10 = (bf16[64,512]{1,0:T(8,128)(2,1)S(1)}, bf16[64,512]{1,0:T(8,128)(2,1)}, u32[]{:S(2)}) copy-start(bf16[64,512]{1,0:T(8,128)(2,1)} %param.17) | copy-start | bytes 196612
  13.1 31.9 %all-to-all-start = ((bf16[16,2,8448]{2,1,0:T(2,128)(2,1)}), bf16[16,2,8448]{2,1,0:T(2,128)(2,1)S(1)}, u32[]{:S(2)}, u32[]{:S(2)}) async-start(bf16[16,2,8448]{2,1,0:T(2,128)(2,1)} %pad_maximum_fusion), calls=%async_computation | async-start | bytes 1081344 | tf_op jit(solution)/shard_map/all_to_all | solution.py:104
  47.2 15.5 %all-to-all-start.1 = ((bf16[4,97,512]{2,1,0:T(8,128)(2,1)}), bf16[4,97,512]{2,1,0:T(8,128)(2,1)S(1)}, u32[]{:S(2)}, u32[]{:S(2)}) async-start(bf16[4,97,512]{2,1,0:T(8,128)(2,1)} %broadcast_in_dim.21), calls=%async_computation.1 | async-start | bytes 851968 | tf_op jit(solution)/shard_map/all_to_all | solution.py:32
  54.2 14.1 %collective-permute-start.1 = (bf16[16,2,4096]{2,1,0:T(2,128)(2,1)}, bf16[16,2,4096]{2,1,0:T(2,128)(2,1)}, u32[]{:S(2)}, u32[]{:S(2)}) collective-permute-start(bf16[16,2,4096]{2,1,0:T(2,128)(2,1)} %slice.102), channel_id=1, source_target_pairs={{0,16},{16,0},{32,48},{48,32},{64,80},{80,64},{96,112},{112,96},{1... | collective-permute-start | bytes 786440 | tf_op jit(solution)/shard_map/ppermute | solution.py:37
  64.0 20.9 %all-to-all-start.2 = ((bf16[4,292,512]{2,1,0:T(8,128)(2,1)}), bf16[4,292,512]{2,1,0:T(8,128)(2,1)S(1)}, u32[]{:S(2)}, u32[]{:S(2)}) async-start(bf16[4,292,512]{2,1,0:T(8,128)(2,1)} %broadcast_in_dim.22), calls=%async_computation.2 | async-start | bytes 2424832 | tf_op jit(solution)/shard_map/all_to_all | solution.py:32
  71.7 13.3 %copy-start.2 = (bf16[16,2,16,512]{3,2,1,0:T(8,128)(2,1)}, bf16[16,2,16,512]{3,2,1,0:T(8,128)(2,1)S(1)}, u32[]{:S(2)}) copy-start(bf16[16,2,16,512]{3,2,1,0:T(8,128)(2,1)S(1)} %constant_dynamic-update-slice_fusion) | copy-start | bytes 1572868
  89.5 26.6 %all-to-all-start.3 = ((bf16[16,2,4352]{2,1,0:T(2,128)(2,1)}), bf16[16,2,4352]{2,1,0:T(2,128)(2,1)S(1)}, u32[]{:S(2)}, u32[]{:S(2)}) async-start(bf16[16,2,4352]{2,1,0:T(2,128)(2,1)} %broadcast_in_dim.23), calls=%async_computation.3 | async-start | bytes 557056 | tf_op jit(solution)/shard_map/all_to_all | solution.py:32
  102.8 13.5 %copy-start.4 = (bf16[16,4096]{1,0:T(8,128)(2,1)S(1)}, bf16[16,4096]{1,0:T(8,128)(2,1)}, u32[]{:S(2)}) copy-start(bf16[16,4096]{1,0:T(8,128)(2,1)} %param.15) | copy-start | bytes 393220
  102.8 15.6 %copy-start.5 = (bf16[16,256]{1,0:T(8,128)(2,1)S(1)}, bf16[16,256]{1,0:T(8,128)(2,1)}, u32[]{:S(2)}) copy-start(bf16[16,256]{1,0:T(8,128)(2,1)} %param.16) | copy-start | bytes 24580
  102.8 15.7 %copy-start.16 = (s32[32]{0:T(128)S(1)}, s32[32]{0:T(128)}, u32[]{:S(2)}) copy-start(s32[32]{0:T(128)} %copy-done.15) | copy-start | bytes 388
  102.8 17.5 %copy-start.14 = (s32[32]{0:T(128)S(1)}, s32[32]{0:T(128)}, u32[]{:S(2)}) copy-start(s32[32]{0:T(128)} %copy-done.13) | copy-start | bytes 388
  105.5 26.1 %copy-start.9 = (bf16[32,16]{0,1:T(8,128)(2,1)S(1)}, bf16[32,16]{0,1:T(8,128)(2,1)}, u32[]{:S(2)}) copy-start(bf16[32,16]{0,1:T(8,128)(2,1)} %copy-done.8) | copy-start | bytes 3076
  105.5 19.0 %collective-permute-start.2 = (bf16[256,512]{1,0:T(8,128)(2,1)}, bf16[256,512]{1,0:T(8,128)(2,1)}, u32[]{:S(2)}, u32[]{:S(2)}) collective-permute-start(bf16[256,512]{1,0:T(8,128)(2,1)} %get-tuple-element.5), channel_id=1, source_target_pairs={{0,4},{1,5},{2,6},{3,7},{4,0},{5,1},{6,2},{7,3},{8,12},{9,13},{10,... | collective-permute-start | bytes 786440 | tf_op jit(solution)/shard_map/ppermute | solution.py:37
  108.1 16.4 %collective-permute-start.3 = (bf16[256,512]{1,0:T(8,128)(2,1)}, bf16[256,512]{1,0:T(8,128)(2,1)}, u32[]{:S(2)}, u32[]{:S(2)}) collective-permute-start(bf16[256,512]{1,0:T(8,128)(2,1)} %get-tuple-element.7), channel_id=1, source_target_pairs={{0,8},{1,9},{2,10},{3,11},{4,12},{5,13},{6,14},{7,15},{8,0},{9,1},... | collective-permute-start | bytes 786440 | tf_op jit(solution)/shard_map/ppermute | solution.py:37
  112.1 12.7 %collective-permute-start.4 = (bf16[256,512]{1,0:T(8,128)(2,1)}, bf16[256,512]{1,0:T(8,128)(2,1)}, u32[]{:S(2)}, u32[]{:S(2)}) collective-permute-start(bf16[256,512]{1,0:T(8,128)(2,1)} %get-tuple-element.6), channel_id=1, source_target_pairs={{0,12},{1,13},{2,14},{3,15},{4,8},{5,9},{6,10},{7,11},{8,4},{9,5},... | collective-permute-start | bytes 786440 | tf_op jit(solution)/shard_map/ppermute | solution.py:37
  116.4 3.5 %collective-permute-start.5 = (bf16[16,2,4352]{2,1,0:T(2,128)(2,1)S(1)}, bf16[16,2,4352]{2,1,0:T(2,128)(2,1)S(1)}, u32[]{:S(2)}, u32[]{:S(2)}) collective-permute-start(bf16[16,2,4352]{2,1,0:T(2,128)(2,1)S(1)} %all-to-all-done.3), channel_id=1, source_target_pairs={{0,16},{16,0},{32,48},{48,32},{64,80},{80,64},{96,112},{112,96},{1... | collective-permute-start | bytes 835592 | tf_op jit(solution)/shard_map/ppermute | solution.py:37
  118.7 19.9 %copy-start.7 = (bf16[32,16]{0,1:T(8,128)(2,1)S(1)}, bf16[32,16]{0,1:T(8,128)(2,1)}, u32[]{:S(2)}) copy-start(bf16[32,16]{0,1:T(8,128)(2,1)} %copy-done.6) | copy-start | bytes 3076
  121.3 8.5 %all-to-all-start.4 = ((f32[4,1,512]{2,1,0:T(1,128)}), f32[4,1,512]{2,1,0:T(1,128)S(1)}, u32[]{:S(2)}, u32[]{:S(2)}) async-start(f32[4,1,512]{2,1,0:T(1,128)} %broadcast_in_dim.25), calls=%async_computation.4 | async-start | bytes 16384 | tf_op jit(solution)/shard_map/all_to_all | solution.py:32
  124.5 21.9 %copy-start.11 = (bf16[32,1024]{1,0:T(8,128)(2,1)S(1)}, bf16[32,1024]{1,0:T(8,128)(2,1)}, u32[]{:S(2)}) copy-start(bf16[32,1024]{1,0:T(8,128)(2,1)} %param.13) | copy-start | bytes 196612
  124.6 21.9 %copy-start.12 = (f32[32,16]{0,1:T(8,128)S(1)}, f32[32,16]{0,1:T(8,128)}, u32[]{:S(2)}) copy-start(f32[32,16]{0,1:T(8,128)} %get-tuple-element.23) | copy-start | bytes 6148
  132.8 12.5 %all-to-all-start.5 = ((bf16[4,67,512]{2,1,0:T(8,128)(2,1)}), bf16[4,67,512]{2,1,0:T(8,128)(2,1)S(1)}, u32[]{:S(2)}, u32[]{:S(2)}) async-start(bf16[4,67,512]{2,1,0:T(8,128)(2,1)} %pad_maximum_fusion.2), calls=%async_computation.5 | async-start | bytes 589824 | tf_op jit(solution)/shard_map/all_to_all | solution.py:237
  (6 other events, 14.8 us)

commit v5 on v4

--- a/solution.py
+++ b/solution.py
@@ -49,6 +49,15 @@
         parts.append(part.astype(bf16))
         value = value - part
     return parts
+
+
+def gathered(block, part, count, stride, later=0):
+    every = jnp.zeros((count,) + block.shape, block.dtype)
+    every = lax.dynamic_update_index_in_dim(every, block, part + later, 0)
+    for step in range(1, count):
+        other = swapped(block, "tensor", step * stride)
+        every = lax.dynamic_update_index_in_dim(every, other, (part ^ step) + later, 0)
+    return every.reshape((count * block.shape[0],) + block.shape[1:])
 
 
 def shards(
@@ -112,6 +121,8 @@
         up_pick.reshape(SEQS, outputs_own, R).transpose(0, 2, 1).reshape(ADA, outputs_own)
     )
 
+    cot_own = cotangent + zero_after(sent[:1, :1, :1]).astype(bf16)
+    cot_run = gathered(cot_own, place % Y_RUN, Y_RUN, 1)
     lengths = seq_lengths[0]
     finish = jnp.cumsum(lengths)
     anchor = finish - lengths
@@ -122,42 +133,12 @@
     low_part = (
         lax.dot_general(down_cat_t, tokens, inner_dims, preferred_element_type=f32) * row_mask
     ).astype(bf16)
-    low_lines = ADA * rows_total // KV
-
-    def as_lines(rows):
-        return jnp.concatenate(
-            [rows[:, i * KV : (i + 1) * KV] for i in range(rows_total // KV)], axis=0
-        )
-
-    def as_rows(lines):
-        return jnp.concatenate(
-            [lines[i * ADA : (i + 1) * ADA] for i in range(rows_total // KV)], axis=1
-        )
-
-    up_line = up_pick_t.reshape(-1, KV)
-    block = jnp.concatenate((cotangent, as_lines(low_part), up_line), axis=0)
-    from_y = spread(block, "tensor", Y_RUN, axis_index_groups=along_y)
-    low_y = jnp.sum(from_y[:, rows_own : rows_own + low_lines].astype(f32), axis=0).astype(bf16)
-    run_rows = Y_RUN * rows_own
-    run = jnp.concatenate(
-        (
-            from_y[:, :rows_own].reshape(run_rows, KV),
-            low_y,
-            from_y[:, rows_own + low_lines :].reshape(-1, KV),
-        ),
-        axis=0,
-    )
-    from_x = spread(run, "tensor", n_x, axis_index_groups=along_x)
-    cot_full = from_x[:, :run_rows].reshape(rows_total, KV)
-    low_rank = as_rows(
-        jnp.sum(from_x[:, run_rows : run_rows + low_lines].astype(f32), axis=0)
-    )
-    up_cat_t = (
-        from_x[:, run_rows + low_lines :]
-        .reshape(n_tensor, ADA, outputs_own)
-        .transpose(1, 0, 2)
-        .reshape(ADA, KV)
-    )
+    cot_full = gathered(
+        cot_run, place // Y_RUN, n_x, Y_RUN, zero_after(jnp.max(low_part, axis=0))
+    )
+    low_came = spread(jnp.concatenate((low_part, up_pick_t), axis=1), "tensor", n_tensor)
+    low_rank = jnp.sum(low_came[:, :, :rows_total].astype(f32), axis=0)
+    up_cat_t = low_came[:, :, rows_total:].transpose(1, 0, 2).reshape(ADA, KV)
 
     weight_mine = came[:, :, term_width:]
     weight_mate = swapped(weight_mine, "dp", 1)

time: 148 us -> 151 us (1.020)
  waiting for transfers between devices: 41.9 us -> 18.6 us
  starting transfers between devices: 61.4 us -> 83.8 us
  between operations: 3.83 us -> 6.53 us
  other arithmetic: 6.18 us -> 7.88 us
    ppermute x6 -> x12, starting transfers between devices: 16.3 us -> 36.8 us  [swapped(): return lax.ppermute(block, axis, pairs)]
    all_to_all x1, waiting for transfers between devices: 15.9 us -> 0.01 us  [shards(): came = lax.all_to_all(sent, 'dp', 0, 0, axis_index_groups=same_core)]
    all_to_all x4 -> x3, waiting for transfers between devices: 19.5 us -> 5.73 us  [spread(): return lax.all_to_all(copies, axes, 0, 0, **kw)]
    ppermute x6 -> x12, waiting for transfers between devices: 1.48 us -> 7.86 us  [swapped(): return lax.ppermute(block, axis, pairs)]
    dynamic_update_slice x0 -> x7, local copies, waits for them, and re-layouts: none -> 2.02 us  [the longest x6 1.99 us: gathered(): lax.dynamic_update_index_in_dim(every, other, (part ^ step) + later, 0)]
    broadcast_in_dim x5 -> x4, local copies, waits for them, and re-layouts: 3.47 us -> 2.47 us  [spread(): copies = jnp.broadcast_to(block[None], (count,) + block.shape)]
    all_to_all x4 -> x3, starting transfers between devices: 23.6 us -> 24.1 us  [spread(): return lax.all_to_all(copies, axes, 0, 0, **kw)]
  transfers between devices with their start and end apart: 12 -> 17, of which waited for: 7 -> 6; matrix products, arithmetic and copies ran while one was open for 15% -> 15% of each run, Pallas kernels for 0% -> 0%
where the time goes in v5:
time: 151 us; the launch traced here: 150 us
  starting transfers between devices  83.8 us (55%)
  waiting for transfers between devices  18.6 us (12%)
  local copies, waits for them, and re-layouts  18.1 us (12%)
  matrix products  14.9 us (10%)
  other arithmetic  7.88 us (5%)
  between operations  6.53 us (4%)
    ppermute x12, starting transfers between devices, swapped(): return lax.ppermute(block, axis, pairs)  36.8 us
    all_to_all x3, starting transfers between devices, spread(): return lax.all_to_all(copies, axes, 0, 0, **kw)  24.1 us
    all_to_all x1, starting transfers between devices, shards(): came = lax.all_to_all(sent, 'dp', 0, 0, axis_index_groups=same_core)  15.7 us
    ppermute x12, waiting for transfers between devices, swapped(): return lax.ppermute(block, axis, pairs)  7.86 us
    all_to_all x1, starting transfers between devices, shards(): lax.all_to_all(last, 'tensor', 0, 0, axis_index_groups=along_y).astype(f32)  7.16 us
    all_to_all x3, waiting for transfers between devices, spread(): return lax.all_to_all(copies, axes, 0, 0, **kw)  5.73 us
    all_to_all x1, waiting for transfers between devices, shards(): lax.all_to_all(last, 'tensor', 0, 0, axis_index_groups=along_y).astype(f32)  5.04 us
  transfers between devices with their start and end apart: 17, of which 6 were waited for; matrix products, arithmetic and copies ran while one was open for 15% of the time, Pallas kernels for 0%

profile of v5, /device:TPU:56, one launch (start us, length us, event | category | flops | bytes accessed | tf_op | source)
XLA Modules:
  0.0 149.9 jit_solution(13901702559860620476)
XLA Ops:
  1.9 1.6 %multiply_convert_fusion = (bf16[32,16]{0,1:T(8,128)(2,1)S(1)}, f32[32,16]{0,1:T(8,128)}) fusion(bf16[32,1024]{1,0:T(8,128)(2,1)} %param.13, bf16[1024,16]{0,1:T(8,128)(2,1)} %param.14), kind=kOutput, calls=%fused_computation.93 | convolution fusion | flops 1051136 | bytes 101376 | tf_op jit(solution)/shard_map/dot_general | solution.py:81
  5.8 1.9 %collective-permute-start = (bf16[32,4352]{1,0:T(8,128)(2,1)S(1)}, bf16[32,4352]{1,0:T(8,128)(2,1)S(1)}, u32[]{:S(2)}, u32[]{:S(2)}) collective-permute-start(bf16[32,4352]{1,0:T(8,128)(2,1)S(1)} %pad_maximum_fusion.2), channel_id=1, source_target_pairs={{0,16},{16,0},{32,48},{48,32},{64,80},{80,64},{96,112},{112,96},{1... | collective-permute-start | bytes 835592 | tf_op jit(solution)/shard_map/ppermute | solution.py:37
  14.7 15.7 %all-to-all-start = ((bf16[16,2,8448]{2,1,0:T(2,128)(2,1)}), bf16[16,2,8448]{2,1,0:T(2,128)(2,1)S(1)}, u32[]{:S(2)}, u32[]{:S(2)}) async-start(bf16[16,2,8448]{2,1,0:T(2,128)(2,1)} %pad_maximum_fusion), calls=%async_computation | async-start | bytes 1081344 | tf_op jit(solution)/shard_map/all_to_all | solution.py:113
  31.7 3.3 %collective-permute-start.2 = (bf16[64,512]{1,0:T(8,128)(2,1)S(1)}, bf16[64,512]{1,0:T(8,128)(2,1)S(1)}, u32[]{:S(2)}, u32[]{:S(2)}) collective-permute-start(bf16[64,512]{1,0:T(8,128)(2,1)S(1)} %get-tuple-element.6), channel_id=1, source_target_pairs={{0,1},{1,0},{2,3},{3,2},{4,5},{5,4},{6,7},{7,6},{8,9},{9,8},{10,11... | collective-permute-start | bytes 196616 | tf_op jit(solution)/shard_map/ppermute | solution.py:37
  35.1 4.0 %collective-permute-start.3 = (bf16[64,512]{1,0:T(8,128)(2,1)S(1)}, bf16[64,512]{1,0:T(8,128)(2,1)S(1)}, u32[]{:S(2)}, u32[]{:S(2)}) collective-permute-start(bf16[64,512]{1,0:T(8,128)(2,1)S(1)} %get-tuple-element.6), channel_id=1, source_target_pairs={{0,2},{1,3},{2,0},{3,1},{4,6},{5,7},{6,4},{7,5},{8,10},{9,11},{10,... | collective-permute-start | bytes 196616 | tf_op jit(solution)/shard_map/ppermute | solution.py:37
  39.1 2.8 %collective-permute-start.4 = (bf16[64,512]{1,0:T(8,128)(2,1)S(1)}, bf16[64,512]{1,0:T(8,128)(2,1)S(1)}, u32[]{:S(2)}, u32[]{:S(2)}) collective-permute-start(bf16[64,512]{1,0:T(8,128)(2,1)S(1)} %get-tuple-element.6), channel_id=1, source_target_pairs={{0,3},{1,2},{2,1},{3,0},{4,7},{5,6},{6,5},{7,4},{8,11},{9,10},{10,... | collective-permute-start | bytes 196616 | tf_op jit(solution)/shard_map/ppermute | solution.py:37
  41.9 5.8 %collective-permute-done.2 = bf16[64,512]{1,0:T(8,128)(2,1)S(1)} collective-permute-done((bf16[64,512]{1,0:T(8,128)(2,1)S(1)}, bf16[64,512]{1,0:T(8,128)(2,1)S(1)}, u32[]{:S(2)}, u32[]{:S(2)}) %collective-permute-start.2) | collective-permute-done | bytes 65568 | tf_op jit(solution)/shard_map/ppermute | solution.py:37
  48.6 3.4 %collective-permute-start.5 = (bf16[256,512]{1,0:T(8,128)(2,1)S(1)}, bf16[256,512]{1,0:T(8,128)(2,1)}, u32[]{:S(2)}, u32[]{:S(2)}) collective-permute-start(bf16[256,512]{1,0:T(8,128)(2,1)S(1)} %bitcast.125), channel_id=1, source_target_pairs={{0,4},{1,5},{2,6},{3,7},{4,0},{5,1},{6,2},{7,3},{8,12},{9,13},{10,... | collective-permute-start | bytes 786440 | tf_op jit(solution)/shard_map/ppermute | solution.py:37
  52.0 4.6 %collective-permute-start.6 = (bf16[256,512]{1,0:T(8,128)(2,1)S(1)}, bf16[256,512]{1,0:T(8,128)(2,1)}, u32[]{:S(2)}, u32[]{:S(2)}) collective-permute-start(bf16[256,512]{1,0:T(8,128)(2,1)S(1)} %bitcast.126), channel_id=1, source_target_pairs={{0,8},{1,9},{2,10},{3,11},{4,12},{5,13},{6,14},{7,15},{8,0},{9,1},... | collective-permute-start | bytes 786440 | tf_op jit(solution)/shard_map/ppermute | solution.py:37
  56.7 2.4 %collective-permute-start.7 = (bf16[256,512]{1,0:T(8,128)(2,1)S(1)}, bf16[256,512]{1,0:T(8,128)(2,1)S(1)}, u32[]{:S(2)}, u32[]{:S(2)}) collective-permute-start(bf16[256,512]{1,0:T(8,128)(2,1)S(1)} %bitcast.127), channel_id=1, source_target_pairs={{0,12},{1,13},{2,14},{3,15},{4,8},{5,9},{6,10},{7,11},{8,4},{9,5},... | collective-permute-start | bytes 786440 | tf_op jit(solution)/shard_map/ppermute | solution.py:37
  63.1 7.8 %all-to-all-start.1 = ((bf16[16,16,1056]{2,1,0:T(8,128)(2,1)}), bf16[16,16,1056]{2,1,0:T(8,128)(2,1)}, u32[]{:S(2)}, u32[]{:S(2)}) async-start(bf16[16,16,1056]{2,1,0:T(8,128)(2,1)} %broadcast_in_dim.84), calls=%async_computation.1 | async-start | bytes 1179648 | tf_op jit(solution)/shard_map/all_to_all | solution.py:32
  71.9 1.9 %collective-permute-start.1 = (bf16[16,2,4096]{2,1,0:T(2,128)(2,1)}, bf16[16,2,4096]{2,1,0:T(2,128)(2,1)}, u32[]{:S(2)}, u32[]{:S(2)}) collective-permute-start(bf16[16,2,4096]{2,1,0:T(2,128)(2,1)} %slice.78), channel_id=1, source_target_pairs={{0,16},{16,0},{32,48},{48,32},{64,80},{80,64},{96,112},{112,96},{1... | collective-permute-start | bytes 786440 | tf_op jit(solution)/shard_map/ppermute | solution.py:37
  78.6 1.7 %fusion.1 = bf16[1024,512]{0,1:T(8,128)(2,1)} fusion(bf16[512,512]{0,1:T(8,128)(2,1)S(1)} %bitcast.122, bf16[1024,512]{1,0:T(8,128)(2,1)S(1)} %copy-done), kind=kOutput, calls=%fused_computation.5 | convolution fusion | flops 537395200 | bytes 2621440 | tf_op jit(solution)/shard_map/dot_general | solution.py:155
  80.3 1.5 copy.68
  81.8 1.7 %all-to-all-done.1 = bf16[16,16,1056]{2,1,0:T(8,128)(2,1)} async-done(((bf16[16,16,1056]{2,1,0:T(8,128)(2,1)}), bf16[16,16,1056]{2,1,0:T(8,128)(2,1)}, u32[]{:S(2)}, u32[]{:S(2)}) %all-to-all-start.1) | async-done | bytes 540704 | tf_op jit(solution)/shard_map/all_to_all | solution.py:32
  88.2 12.1 %all-to-all-start.2 = ((bf16[16,2,4352]{2,1,0:T(2,128)(2,1)}), bf16[16,2,4352]{2,1,0:T(2,128)(2,1)S(1)}, u32[]{:S(2)}, u32[]{:S(2)}) async-start(bf16[16,2,4352]{2,1,0:T(2,128)(2,1)} %broadcast_in_dim.85), calls=%async_computation.2 | async-start | bytes 557056 | tf_op jit(solution)/shard_map/all_to_all | solution.py:32
  105.8 5.0 %collective-permute-start.10 = (bf16[256,512]{1,0:T(8,128)(2,1)}, bf16[256,512]{1,0:T(8,128)(2,1)}, u32[]{:S(2)}, u32[]{:S(2)}) collective-permute-start(bf16[256,512]{1,0:T(8,128)(2,1)} %get-tuple-element.8), channel_id=1, source_target_pairs={{0,12},{1,13},{2,14},{3,15},{4,8},{5,9},{6,10},{7,11},{8,4},{9,5},... | collective-permute-start | bytes 786440 | tf_op jit(solution)/shard_map/ppermute | solution.py:37
  110.8 2.2 %collective-permute-start.8 = (bf16[256,512]{1,0:T(8,128)(2,1)}, bf16[256,512]{1,0:T(8,128)(2,1)}, u32[]{:S(2)}, u32[]{:S(2)}) collective-permute-start(bf16[256,512]{1,0:T(8,128)(2,1)} %get-tuple-element.7), channel_id=1, source_target_pairs={{0,4},{1,5},{2,6},{3,7},{4,0},{5,1},{6,2},{7,3},{8,12},{9,13},{10,... | collective-permute-start | bytes 786440 | tf_op jit(solution)/shard_map/ppermute | solution.py:37
  113.0 3.4 %collective-permute-start.9 = (bf16[256,512]{1,0:T(8,128)(2,1)}, bf16[256,512]{1,0:T(8,128)(2,1)}, u32[]{:S(2)}, u32[]{:S(2)}) collective-permute-start(bf16[256,512]{1,0:T(8,128)(2,1)} %get-tuple-element.9), channel_id=1, source_target_pairs={{0,8},{1,9},{2,10},{3,11},{4,12},{5,13},{6,14},{7,15},{8,0},{9,1},... | collective-permute-start | bytes 786440 | tf_op jit(solution)/shard_map/ppermute | solution.py:37
  116.7 1.9 %collective-permute-start.11 = (bf16[16,2,4352]{2,1,0:T(2,128)(2,1)S(1)}, bf16[16,2,4352]{2,1,0:T(2,128)(2,1)S(1)}, u32[]{:S(2)}, u32[]{:S(2)}) collective-permute-start(bf16[16,2,4352]{2,1,0:T(2,128)(2,1)S(1)} %all-to-all-done.2), channel_id=1, source_target_pairs={{0,16},{16,0},{32,48},{48,32},{64,80},{80,64},{96,112},{112,96},{1... | collective-permute-start | bytes 835592 | tf_op jit(solution)/shard_map/ppermute | solution.py:37
  121.5 4.3 %all-to-all-start.3 = ((f32[4,1,512]{2,1,0:T(1,128)}), f32[4,1,512]{2,1,0:T(1,128)S(1)}, u32[]{:S(2)}, u32[]{:S(2)}) async-start(f32[4,1,512]{2,1,0:T(1,128)} %broadcast_in_dim.87), calls=%async_computation.3 | async-start | bytes 16384 | tf_op jit(solution)/shard_map/all_to_all | solution.py:32
  127.1 4.0 %all-to-all-done.3 = f32[4,1,512]{2,1,0:T(1,128)S(1)} async-done(((f32[4,1,512]{2,1,0:T(1,128)}), f32[4,1,512]{2,1,0:T(1,128)S(1)}, u32[]{:S(2)}, u32[]{:S(2)}) %all-to-all-start.3) | async-done | bytes 8224 | tf_op jit(solution)/shard_map/all_to_all | solution.py:32
  134.1 7.2 %all-to-all-start.4 = ((bf16[4,67,512]{2,1,0:T(8,128)(2,1)}), bf16[4,67,512]{2,1,0:T(8,128)(2,1)S(1)}, u32[]{:S(2)}, u32[]{:S(2)}) async-start(bf16[4,67,512]{2,1,0:T(8,128)(2,1)} %pad_maximum_fusion.1), calls=%async_computation.4 | async-start | bytes 589824 | tf_op jit(solution)/shard_map/all_to_all | solution.py:218
  142.8 5.0 %all-to-all-done.4 = bf16[4,67,512]{2,1,0:T(8,128)(2,1)S(1)} async-done(((bf16[4,67,512]{2,1,0:T(8,128)(2,1)}), bf16[4,67,512]{2,1,0:T(8,128)(2,1)S(1)}, u32[]{:S(2)}, u32[]{:S(2)}) %all-to-all-start.4) | async-done | bytes 274464 | tf_op jit(solution)/shard_map/all_to_all | solution.py:218
  (145 shorter events, 38.1 us)
Async XLA Ops:
  0.6 59.2 %copy-start = (bf16[1024,512]{1,0:T(8,128)(2,1)S(1)}, bf16[1024,512]{1,0:T(8,128)(2,1)}, u32[]{:S(2)}) copy-start(bf16[1024,512]{1,0:T(8,128)(2,1)} %param.9) | copy-start | bytes 3145732
  5.8 6.7 %collective-permute-start = (bf16[32,4352]{1,0:T(8,128)(2,1)S(1)}, bf16[32,4352]{1,0:T(8,128)(2,1)S(1)}, u32[]{:S(2)}, u32[]{:S(2)}) collective-permute-start(bf16[32,4352]{1,0:T(8,128)(2,1)S(1)} %pad_maximum_fusion.2), channel_id=1, source_target_pairs={{0,16},{16,0},{32,48},{48,32},{64,80},{80,64},{96,112},{112,96},{1... | collective-permute-start | bytes 835592 | tf_op jit(solution)/shard_map/ppermute | solution.py:37
  12.5 19.2 %copy-start.10 = (bf16[64,512]{1,0:T(8,128)(2,1)S(1)}, bf16[64,512]{1,0:T(8,128)(2,1)}, u32[]{:S(2)}) copy-start(bf16[64,512]{1,0:T(8,128)(2,1)} %param.17) | copy-start | bytes 196612
  14.7 44.4 %all-to-all-start = ((bf16[16,2,8448]{2,1,0:T(2,128)(2,1)}), bf16[16,2,8448]{2,1,0:T(2,128)(2,1)S(1)}, u32[]{:S(2)}, u32[]{:S(2)}) async-start(bf16[16,2,8448]{2,1,0:T(2,128)(2,1)} %pad_maximum_fusion), calls=%async_computation | async-start | bytes 1081344 | tf_op jit(solution)/shard_map/all_to_all | solution.py:113
  31.7 16.0 %collective-permute-start.2 = (bf16[64,512]{1,0:T(8,128)(2,1)S(1)}, bf16[64,512]{1,0:T(8,128)(2,1)S(1)}, u32[]{:S(2)}, u32[]{:S(2)}) collective-permute-start(bf16[64,512]{1,0:T(8,128)(2,1)S(1)} %get-tuple-element.6), channel_id=1, source_target_pairs={{0,1},{1,0},{2,3},{3,2},{4,5},{5,4},{6,7},{7,6},{8,9},{9,8},{10,11... | collective-permute-start | bytes 196616 | tf_op jit(solution)/shard_map/ppermute | solution.py:37
  35.1 13.5 %collective-permute-start.3 = (bf16[64,512]{1,0:T(8,128)(2,1)S(1)}, bf16[64,512]{1,0:T(8,128)(2,1)S(1)}, u32[]{:S(2)}, u32[]{:S(2)}) collective-permute-start(bf16[64,512]{1,0:T(8,128)(2,1)S(1)} %get-tuple-element.6), channel_id=1, source_target_pairs={{0,2},{1,3},{2,0},{3,1},{4,6},{5,7},{6,4},{7,5},{8,10},{9,11},{10,... | collective-permute-start | bytes 196616 | tf_op jit(solution)/shard_map/ppermute | solution.py:37
  39.1 9.5 %collective-permute-start.4 = (bf16[64,512]{1,0:T(8,128)(2,1)S(1)}, bf16[64,512]{1,0:T(8,128)(2,1)S(1)}, u32[]{:S(2)}, u32[]{:S(2)}) collective-permute-start(bf16[64,512]{1,0:T(8,128)(2,1)S(1)} %get-tuple-element.6), channel_id=1, source_target_pairs={{0,3},{1,2},{2,1},{3,0},{4,7},{5,6},{6,5},{7,4},{8,11},{9,10},{10,... | collective-permute-start | bytes 196616 | tf_op jit(solution)/shard_map/ppermute | solution.py:37
  48.6 25.3 %collective-permute-start.5 = (bf16[256,512]{1,0:T(8,128)(2,1)S(1)}, bf16[256,512]{1,0:T(8,128)(2,1)}, u32[]{:S(2)}, u32[]{:S(2)}) collective-permute-start(bf16[256,512]{1,0:T(8,128)(2,1)S(1)} %bitcast.125), channel_id=1, source_target_pairs={{0,4},{1,5},{2,6},{3,7},{4,0},{5,1},{6,2},{7,3},{8,12},{9,13},{10,... | collective-permute-start | bytes 786440 | tf_op jit(solution)/shard_map/ppermute | solution.py:37
  52.0 22.9 %collective-permute-start.6 = (bf16[256,512]{1,0:T(8,128)(2,1)S(1)}, bf16[256,512]{1,0:T(8,128)(2,1)}, u32[]{:S(2)}, u32[]{:S(2)}) collective-permute-start(bf16[256,512]{1,0:T(8,128)(2,1)S(1)} %bitcast.126), channel_id=1, source_target_pairs={{0,8},{1,9},{2,10},{3,11},{4,12},{5,13},{6,14},{7,15},{8,0},{9,1},... | collective-permute-start | bytes 786440 | tf_op jit(solution)/shard_map/ppermute | solution.py:37
  56.7 19.3 %collective-permute-start.7 = (bf16[256,512]{1,0:T(8,128)(2,1)S(1)}, bf16[256,512]{1,0:T(8,128)(2,1)S(1)}, u32[]{:S(2)}, u32[]{:S(2)}) collective-permute-start(bf16[256,512]{1,0:T(8,128)(2,1)S(1)} %bitcast.127), channel_id=1, source_target_pairs={{0,12},{1,13},{2,14},{3,15},{4,8},{5,9},{6,10},{7,11},{8,4},{9,5},... | collective-permute-start | bytes 786440 | tf_op jit(solution)/shard_map/ppermute | solution.py:37
  63.1 20.4 %all-to-all-start.1 = ((bf16[16,16,1056]{2,1,0:T(8,128)(2,1)}), bf16[16,16,1056]{2,1,0:T(8,128)(2,1)}, u32[]{:S(2)}, u32[]{:S(2)}) async-start(bf16[16,16,1056]{2,1,0:T(8,128)(2,1)} %broadcast_in_dim.84), calls=%async_computation.1 | async-start | bytes 1179648 | tf_op jit(solution)/shard_map/all_to_all | solution.py:32
  71.9 4.1 %collective-permute-start.1 = (bf16[16,2,4096]{2,1,0:T(2,128)(2,1)}, bf16[16,2,4096]{2,1,0:T(2,128)(2,1)}, u32[]{:S(2)}, u32[]{:S(2)}) collective-permute-start(bf16[16,2,4096]{2,1,0:T(2,128)(2,1)} %slice.78), channel_id=1, source_target_pairs={{0,16},{16,0},{32,48},{48,32},{64,80},{80,64},{96,112},{112,96},{1... | collective-permute-start | bytes 786440 | tf_op jit(solution)/shard_map/ppermute | solution.py:37
  88.2 28.1 %all-to-all-start.2 = ((bf16[16,2,4352]{2,1,0:T(2,128)(2,1)}), bf16[16,2,4352]{2,1,0:T(2,128)(2,1)S(1)}, u32[]{:S(2)}, u32[]{:S(2)}) async-start(bf16[16,2,4352]{2,1,0:T(2,128)(2,1)} %broadcast_in_dim.85), calls=%async_computation.2 | async-start | bytes 557056 | tf_op jit(solution)/shard_map/all_to_all | solution.py:32
  103.0 17.5 %copy-start.14 = (s32[32]{0:T(128)S(1)}, s32[32]{0:T(128)}, u32[]{:S(2)}) copy-start(s32[32]{0:T(128)} %copy-done.13) | copy-start | bytes 388
  105.8 27.2 %copy-start.9 = (bf16[32,16]{0,1:T(8,128)(2,1)S(1)}, bf16[32,16]{0,1:T(8,128)(2,1)}, u32[]{:S(2)}) copy-start(bf16[32,16]{0,1:T(8,128)(2,1)} %copy-done.8) | copy-start | bytes 3076
  105.8 20.0 %collective-permute-start.10 = (bf16[256,512]{1,0:T(8,128)(2,1)}, bf16[256,512]{1,0:T(8,128)(2,1)}, u32[]{:S(2)}, u32[]{:S(2)}) collective-permute-start(bf16[256,512]{1,0:T(8,128)(2,1)} %get-tuple-element.8), channel_id=1, source_target_pairs={{0,12},{1,13},{2,14},{3,15},{4,8},{5,9},{6,10},{7,11},{8,4},{9,5},... | collective-permute-start | bytes 786440 | tf_op jit(solution)/shard_map/ppermute | solution.py:37
  110.8 15.0 %collective-permute-start.8 = (bf16[256,512]{1,0:T(8,128)(2,1)}, bf16[256,512]{1,0:T(8,128)(2,1)}, u32[]{:S(2)}, u32[]{:S(2)}) collective-permute-start(bf16[256,512]{1,0:T(8,128)(2,1)} %get-tuple-element.7), channel_id=1, source_target_pairs={{0,4},{1,5},{2,6},{3,7},{4,0},{5,1},{6,2},{7,3},{8,12},{9,13},{10,... | collective-permute-start | bytes 786440 | tf_op jit(solution)/shard_map/ppermute | solution.py:37
  113.0 12.8 %collective-permute-start.9 = (bf16[256,512]{1,0:T(8,128)(2,1)}, bf16[256,512]{1,0:T(8,128)(2,1)}, u32[]{:S(2)}, u32[]{:S(2)}) collective-permute-start(bf16[256,512]{1,0:T(8,128)(2,1)} %get-tuple-element.9), channel_id=1, source_target_pairs={{0,8},{1,9},{2,10},{3,11},{4,12},{5,13},{6,14},{7,15},{8,0},{9,1},... | collective-permute-start | bytes 786440 | tf_op jit(solution)/shard_map/ppermute | solution.py:37
  116.7 3.5 %collective-permute-start.11 = (bf16[16,2,4352]{2,1,0:T(2,128)(2,1)S(1)}, bf16[16,2,4352]{2,1,0:T(2,128)(2,1)S(1)}, u32[]{:S(2)}, u32[]{:S(2)}) collective-permute-start(bf16[16,2,4352]{2,1,0:T(2,128)(2,1)S(1)} %all-to-all-done.2), channel_id=1, source_target_pairs={{0,16},{16,0},{32,48},{48,32},{64,80},{80,64},{96,112},{112,96},{1... | collective-permute-start | bytes 835592 | tf_op jit(solution)/shard_map/ppermute | solution.py:37
  118.9 22.3 %copy-start.7 = (bf16[32,16]{0,1:T(8,128)(2,1)S(1)}, bf16[32,16]{0,1:T(8,128)(2,1)}, u32[]{:S(2)}) copy-start(bf16[32,16]{0,1:T(8,128)(2,1)} %copy-done.6) | copy-start | bytes 3076
  121.5 9.6 %all-to-all-start.3 = ((f32[4,1,512]{2,1,0:T(1,128)}), f32[4,1,512]{2,1,0:T(1,128)S(1)}, u32[]{:S(2)}, u32[]{:S(2)}) async-start(f32[4,1,512]{2,1,0:T(1,128)} %broadcast_in_dim.87), calls=%async_computation.3 | async-start | bytes 16384 | tf_op jit(solution)/shard_map/all_to_all | solution.py:32
  125.8 23.3 %copy-start.11 = (bf16[32,1024]{1,0:T(8,128)(2,1)S(1)}, bf16[32,1024]{1,0:T(8,128)(2,1)}, u32[]{:S(2)}) copy-start(bf16[32,1024]{1,0:T(8,128)(2,1)} %param.13) | copy-start | bytes 196612
  125.8 23.3 %copy-start.12 = (f32[32,16]{0,1:T(8,128)S(1)}, f32[32,16]{0,1:T(8,128)}, u32[]{:S(2)}) copy-start(f32[32,16]{0,1:T(8,128)} %get-tuple-element.21) | copy-start | bytes 6148
  134.1 13.8 %all-to-all-start.4 = ((bf16[4,67,512]{2,1,0:T(8,128)(2,1)}), bf16[4,67,512]{2,1,0:T(8,128)(2,1)S(1)}, u32[]{:S(2)}, u32[]{:S(2)}) async-start(bf16[4,67,512]{2,1,0:T(8,128)(2,1)} %pad_maximum_fusion.1), calls=%async_computation.4 | async-start | bytes 589824 | tf_op jit(solution)/shard_map/all_to_all | solution.py:218
  (10 other events, 60.4 us)

commit v6 on v5

v6 whole, which is shorter than its diff:
```python
import math

import jax
import jax.numpy as jnp
from jax import lax
from jax.sharding import PartitionSpec as P

D = 8192
KV = 512
R = 8
NTASK = 32
SEQS = 2
ADA = SEQS * R

precise = lax.Precision.HIGHEST
inner_dims = (((1,), (1,)), ((), ()))
outer_dims = (((0,), (0,)), ((), ()))
bf16 = jnp.bfloat16
f32 = jnp.float32

CORES = 2
Y_RUN = 4


def silu_slope(pre_act):
    sigma = jax.nn.sigmoid(pre_act)
    return sigma * (1.0 + pre_act * (1.0 - sigma))


def spread(block, axes, count, **kw):
    copies = jnp.broadcast_to(block[None], (count,) + block.shape)
    return lax.all_to_all(copies, axes, 0, 0, **kw)


def swapped(block, axis, distance):
    pairs = [(i, i ^ distance) for i in range(lax.axis_size(axis))]
    return lax.ppermute(block, axis, pairs)


def zero_after(value):
    first = value.reshape(-1)[0].astype(f32)
    return (jnp.floor(first) > first).astype(jnp.int32)


def parts_of(value):
    parts = []
    for _ in range(3):
        part = lax.reduce_precision(value, 8, 7)
        parts.append(part.astype(bf16))
        value = value - part
    return parts


def gathered(block, part, count, stride):
    every = jnp.zeros((count,) + block.shape, block.dtype)
    every = lax.dynamic_update_index_in_dim(every, block, part, 0)
    for step in range(1, count):
        other = swapped(block, "tensor", step * stride)
        every = lax.dynamic_update_index_in_dim(every, other, part ^ step, 0)
    return every.reshape((count * block.shape[0],) + block.shape[1:])


def shards(
    tokens, value_weight, seq_lengths, task_ids, task_embed, hyper_in, head_a, head_b, cotangent
):
    n_dp = lax.axis_size("dp")
    n_chips = n_dp // CORES
    n_tensor = lax.axis_size("tensor")
    n_x = n_tensor // Y_RUN
    rows_total, width_own = tokens.shape
    rows_own = rows_total // n_tensor
    outputs_own = KV // n_tensor
    down_width = width_own * R
    up_width = outputs_own * R
    along_y = [[x * Y_RUN + y for y in range(Y_RUN)] for x in range(n_x)]
    along_x = [[x * Y_RUN + y for x in range(n_x)] for y in range(Y_RUN)]
    same_core = [[chip * CORES + core for chip in range(n_chips)] for core in range(CORES)]
    core = lax.axis_index("dp") % CORES
    place = lax.axis_index("tensor")

    cot_run = spread(cotangent, "tensor", Y_RUN, axis_index_groups=along_y).reshape(-1, KV)

    pre_act = jnp.dot(task_embed, hyper_in, preferred_element_type=f32)
    hidden = jax.nn.silu(pre_act).astype(bf16)

    def chosen_by(which):
        ids = lax.dynamic_index_in_dim(
            task_ids.reshape(n_chips, CORES, SEQS), which, 1, keepdims=False
        ).reshape(n_chips * SEQS)
        hot = (ids[:, None] == jnp.arange(NTASK, dtype=jnp.int32)[None, :]).astype(bf16)
        return hot, jnp.dot(hot, hidden, preferred_element_type=f32).astype(bf16)

    heads = jnp.concatenate((head_a, head_b), axis=1)

    def terms_of(pick):
        return jnp.dot(pick, heads, preferred_element_type=f32)

    hot_mate, pick_mate = chosen_by(1 - core)
    hot_mine, pick_mine = chosen_by(core)
    from_mate = swapped(terms_of(pick_mate).astype(bf16), "dp", 1)
    terms = (terms_of(pick_mine) + from_mate.astype(f32)).astype(bf16)
    term_width = down_width + up_width
    weight_own = value_weight.T.reshape(1, SEQS, -1)
    sent = jnp.concatenate(
        (
            terms.reshape(n_chips, SEQS, term_width),
            jnp.broadcast_to(weight_own, (n_chips,) + weight_own.shape[1:]),
        ),
        axis=2,
    )
    came = lax.all_to_all(sent, "dp", 0, 0, axis_index_groups=same_core)
    sums = jnp.sum(came[:, :, :term_width].astype(f32), axis=0)
    down_pick = (sums[:, :down_width] * (1.0 / math.sqrt(D))).astype(bf16)
    up_pick = (sums[:, down_width:] * (1.0 / math.sqrt(R))).astype(bf16)
    down_cat = down_pick.reshape(SEQS, width_own, R).transpose(1, 0, 2).reshape(width_own, ADA)

    place_x = place // Y_RUN
    cot_full = gathered(cot_run, place_x, n_x, Y_RUN)

    first, second = seq_lengths[0, 0], seq_lengths[0, 1]
    places = jnp.arange(rows_total, dtype=jnp.int32)[:, None]
    in_second = (places >= first) & (places < first + second)
    in_first = jnp.broadcast_to(places < first, (rows_total, R))
    col_mask = jnp.concatenate(
        (in_first, jnp.broadcast_to(in_second, (rows_total, R))), axis=1
    ).astype(f32)

    low_part = (jnp.dot(tokens, down_cat, preferred_element_type=f32) * col_mask).astype(bf16)
    up_part = lax.dot_general(cot_full, low_part, outer_dims, preferred_element_type=f32).astype(
        bf16
    )
    low_lines = rows_own * ADA // KV
    up_lines = outputs_own * ADA // KV
    pick_lines = SEQS * up_width // KV
    block = jnp.concatenate(
        (
            low_part.reshape(n_tensor, low_lines, KV),
            up_part.reshape(n_tensor, up_lines, KV),
            jnp.broadcast_to(up_pick.reshape(1, pick_lines, KV), (n_tensor, pick_lines, KV)),
        ),
        axis=1,
    )
    summed = low_lines + up_lines
    low_came = lax.all_to_all(block, "tensor", 0, 0)
    whole = jnp.sum(low_came[:, :summed].astype(f32), axis=0)
    low_rows = whole[:low_lines].reshape(rows_own, ADA)
    up_grad = whole[low_lines:].reshape(outputs_own, ADA)
    up_cat = (
        low_came[:, summed:]
        .reshape(n_tensor, SEQS, outputs_own, R)
        .transpose(0, 2, 1, 3)
        .reshape(KV, ADA)
    )

    weight_mine = came[:, :, term_width:]
    weight_mate = swapped(weight_mine, "dp", 1)
    weight_mine = weight_mine.reshape(n_chips, KV // n_dp, width_own)
    weight_mate = weight_mate.reshape(n_chips, KV // n_dp, width_own)
    weight_t = jnp.stack(
        (
            jnp.where(core == 0, weight_mine, weight_mate),
            jnp.where(core == 0, weight_mate, weight_mine),
        ),
        axis=1,
    ).reshape(KV, width_own)
    frozen_t = lax.dot_general(
        weight_t, tokens, inner_dims, preferred_element_type=f32
    ).astype(bf16)

    down_scale = 1.0 / math.sqrt(D)
    up_scale = 1.0 / math.sqrt(R)
    back_low = (jnp.dot(cot_full, up_cat, preferred_element_type=f32) * col_mask).astype(bf16)
    down_grad = down_scale * lax.dot_general(
        tokens, back_low, outer_dims, preferred_element_type=f32
    )
    up_grad = up_scale * up_grad
    down_seq = down_grad.reshape(width_own, SEQS, R).transpose(1, 0, 2).reshape(SEQS, down_width)
    up_seq = up_grad.reshape(outputs_own, SEQS, R).transpose(1, 0, 2).reshape(SEQS, up_width)
    own_grads = jnp.concatenate((down_seq, up_seq), axis=1).astype(bf16)
    grads_mine = spread(own_grads, "dp", n_chips, axis_index_groups=same_core)

    adapter_back = lax.dot_general(back_low, down_cat, inner_dims, preferred_element_type=f32)
    frozen_back = jnp.dot(cot_full, weight_t, preferred_element_type=f32)
    grad_tokens = (frozen_back + adapter_back).astype(bf16)
    run_rows = Y_RUN * rows_own

    def run_of(x):
        return lax.dynamic_slice_in_dim(frozen_t, x * run_rows, run_rows, 1)

    frozen_kept = run_of(place_x)
    frozen_came = [
        swapped(run_of(place_x ^ step), "tensor", step * Y_RUN)
        for step in range(1, n_x)
    ]
    grads_mate = swapped(grads_mine, "dp", 1)

    def hidden_terms(grads, hot):
        part = lax.dot_general(
            grads.reshape(n_chips * SEQS, -1), heads, inner_dims, preferred_element_type=f32
        )
        return lax.dot_general(hot.astype(f32), part, outer_dims, precision=precise)

    by_task = hidden_terms(grads_mine, hot_mine) + hidden_terms(grads_mate, hot_mate)
    hidden_x = jnp.sum(
        spread(by_task.reshape(1, -1), "tensor", n_x, axis_index_groups=along_x), axis=0
    )

    rows_x = frozen_kept.astype(f32)
    for other in frozen_came:
        rows_x = rows_x + other.astype(f32)
    last = jnp.concatenate(
        (
            rows_x.astype(bf16).T.reshape(Y_RUN, rows_own, KV),
            jnp.broadcast_to(
                jnp.concatenate(parts_of(hidden_x), axis=0).reshape(1, -1, KV),
                (Y_RUN, 3 * hidden_x.size // KV, KV),
            ),
        ),
        axis=1,
    )
    last = jnp.sum(
        lax.all_to_all(last, "tensor", 0, 0, axis_index_groups=along_y).astype(f32), axis=0
    )
    frozen_rows = last[:rows_own]
    grad_hidden = jnp.sum(last[rows_own:].reshape((3,) + by_task.shape), axis=0)

    last_zero = zero_after(hidden_x).astype(bf16)

    def head_grads(grads, pick):
        return lax.dot_general(
            pick + last_zero,
            grads.reshape(n_chips * SEQS, -1),
            outer_dims,
            preferred_element_type=f32,
        )

    grad_heads = head_grads(grads_mine, pick_mine) + head_grads(grads_mate, pick_mate)
    grad_head_a = grad_heads[:, :down_width]
    grad_head_b = grad_heads[:, down_width:]
    grad_pre = grad_hidden * silu_slope(pre_act)
    grad_hyper_in = lax.dot_general(
        task_embed.astype(f32), grad_pre, outer_dims, precision=precise
    )

    adapter = lax.dot_general(
        low_rows.astype(f32), up_cat.astype(f32), inner_dims, precision=precise
    )
    values = (frozen_rows + adapter).astype(bf16)
    return (values, grad_tokens, grad_head_a, grad_head_b, grad_hyper_in)


def solution(mesh):
    placed = (
        P("dp", "tensor"),
        P("tensor", "dp"),
        P("dp", None),
        P(),
        P(),
        P(None, "dp"),
        P("dp", "tensor"),
        P("dp", "tensor"),
        P(("dp", "tensor"), None),
    )
    return jax.shard_map(
        shards,
        mesh=mesh,
        in_specs=placed,
        out_specs=(
            P(("dp", "tensor"), None),
            P("dp", "tensor"),
            P("dp", "tensor"),
            P("dp", "tensor"),
            P(None, "dp"),
        ),
        check_vma=False,
    )
```

time: 151 us -> 142 us (0.940)
  waiting for transfers between devices: 18.6 us -> 26.6 us
  starting transfers between devices: 83.8 us -> 77.1 us
  matrix products: 14.9 us -> 10.1 us
  between operations: 6.53 us -> 3.74 us
  local copies, waits for them, and re-layouts: 18.1 us -> 15.5 us
    ppermute x12 -> x9, starting transfers between devices: 36.8 us -> 26.6 us  [swapped(): return lax.ppermute(block, axis, pairs)]
    all_to_all x0 -> x1, starting transfers between devices: none -> 6.65 us  [shards(): low_came = lax.all_to_all(block, 'tensor', 0, 0)]
    dot_general x19 -> x13, matrix products: 11 us -> 5.83 us  [the longest x1 1.79 us: shards(): lax.dot_general(back_low, down_cat, inner_dims, preferred_element_type=f32)]
    all_to_all x0 -> x1, waiting for transfers between devices: none -> 2.98 us  [shards(): low_came = lax.all_to_all(block, 'tensor', 0, 0)]
    ppermute x12 -> x9, waiting for transfers between devices: 7.86 us -> 10.5 us  [swapped(): return lax.ppermute(block, axis, pairs)]
    all_to_all x3, starting transfers between devices: 24.1 us -> 21.7 us  [spread(): return lax.all_to_all(copies, axes, 0, 0, **kw)]
    all_to_all x3, waiting for transfers between devices: 5.73 us -> 8.12 us  [spread(): return lax.all_to_all(copies, axes, 0, 0, **kw)]
    dynamic_update_slice x7 -> x4, local copies, waits for them, and re-layouts: 2.02 us -> 0.09 us  [the longest x3 0.07 us: gathered(): every = lax.dynamic_update_index_in_dim(every, other, part ^ step, 0)]
  transfers between devices with their start and end apart: 17 -> 15, of which waited for: 6 -> 7; matrix products, arithmetic and copies ran while one was open for 15% -> 16% of each run, Pallas kernels for 0% -> 0%
where the time goes in v6:
time: 142 us; the launch traced here: 140 us
  starting transfers between devices  77.1 us (54%)
  waiting for transfers between devices  26.6 us (19%)
  local copies, waits for them, and re-layouts  15.5 us (11%)
  matrix products  10.1 us (7%)
  other arithmetic  7.34 us (5%)
  between operations  3.74 us (3%)
    ppermute x9, starting transfers between devices, swapped(): return lax.ppermute(block, axis, pairs)  26.6 us
    all_to_all x3, starting transfers between devices, spread(): return lax.all_to_all(copies, axes, 0, 0, **kw)  21.7 us
    all_to_all x1, starting transfers between devices, shards(): came = lax.all_to_all(sent, 'dp', 0, 0, axis_index_groups=same_core)  15.7 us
    ppermute x9, waiting for transfers between devices, swapped(): return lax.ppermute(block, axis, pairs)  10.5 us
    all_to_all x3, waiting for transfers between devices, spread(): return lax.all_to_all(copies, axes, 0, 0, **kw)  8.12 us
    all_to_all x1, starting transfers between devices, shards(): low_came = lax.all_to_all(block, 'tensor', 0, 0)  6.65 us
    all_to_all x1, starting transfers between devices, shards(): lax.all_to_all(last, 'tensor', 0, 0, axis_index_groups=along_y).astype(f32)  6.5 us
    all_to_all x1, waiting for transfers between devices, shards(): lax.all_to_all(last, 'tensor', 0, 0, axis_index_groups=along_y).astype(f32)  4.97 us
  transfers between devices with their start and end apart: 15, of which 7 were waited for; matrix products, arithmetic and copies ran while one was open for 16% of the time, Pallas kernels for 0%

profile of v6, /device:TPU:56, one launch (start us, length us, event | category | flops | bytes accessed | tf_op | source)
XLA Modules:
  0.0 140.4 jit_solution(16925969103098042894)
XLA Ops:
  5.0 1.9 %collective-permute-start = (bf16[32,4352]{1,0:T(8,128)(2,1)S(1)}, bf16[32,4352]{1,0:T(8,128)(2,1)S(1)}, u32[]{:S(2)}, u32[]{:S(2)}) collective-permute-start(bf16[32,4352]{1,0:T(8,128)(2,1)S(1)} %convolution_convert_fusion), channel_id=1, source_target_pairs={{0,16},{16,0},{32,48},{48,32},{64,80},{80,64},{96,112},{112,96},{1... | collective-permute-start | bytes 835592 | tf_op jit(solution)/shard_map/ppermute | solution.py:37
  8.5 6.4 %all-to-all-start.1 = ((bf16[4,64,512]{2,1,0:T(8,128)(2,1)}), bf16[4,64,512]{2,1,0:T(8,128)(2,1)S(1)}, u32[]{:S(2)}, u32[]{:S(2)}) async-start(bf16[4,64,512]{2,1,0:T(8,128)(2,1)} %broadcast_in_dim.72), calls=%async_computation.1 | async-start | bytes 524288 | tf_op jit(solution)/shard_map/all_to_all | solution.py:32
  18.0 4.4 %all-to-all-done.1 = bf16[4,64,512]{2,1,0:T(8,128)(2,1)S(1)} async-done(((bf16[4,64,512]{2,1,0:T(8,128)(2,1)}), bf16[4,64,512]{2,1,0:T(8,128)(2,1)S(1)}, u32[]{:S(2)}, u32[]{:S(2)}) %all-to-all-start.1) | async-done | bytes 262176 | tf_op jit(solution)/shard_map/all_to_all | solution.py:32
  22.3 15.7 %all-to-all-start = ((bf16[16,2,8448]{2,1,0:T(2,128)(2,1)}), bf16[16,2,8448]{2,1,0:T(2,128)(2,1)S(1)}, u32[]{:S(2)}, u32[]{:S(2)}) async-start(bf16[16,2,8448]{2,1,0:T(2,128)(2,1)} %pad_maximum_fusion), calls=%async_computation | async-start | bytes 1081344 | tf_op jit(solution)/shard_map/all_to_all | solution.py:111
  38.0 3.4 %collective-permute-start.5 = (bf16[256,512]{1,0:T(8,128)(2,1)S(1)}, bf16[256,512]{1,0:T(8,128)(2,1)S(1)}, u32[]{:S(2)}, u32[]{:S(2)}) collective-permute-start(bf16[256,512]{1,0:T(8,128)(2,1)S(1)} %bitcast.92), channel_id=1, source_target_pairs={{0,4},{1,5},{2,6},{3,7},{4,0},{5,1},{6,2},{7,3},{8,12},{9,13},{10,... | collective-permute-start | bytes 786440 | tf_op jit(solution)/shard_map/ppermute | solution.py:37
  44.0 4.6 %collective-permute-start.6 = (bf16[256,512]{1,0:T(8,128)(2,1)S(1)}, bf16[256,512]{1,0:T(8,128)(2,1)S(1)}, u32[]{:S(2)}, u32[]{:S(2)}) collective-permute-start(bf16[256,512]{1,0:T(8,128)(2,1)S(1)} %bitcast.93), channel_id=1, source_target_pairs={{0,8},{1,9},{2,10},{3,11},{4,12},{5,13},{6,14},{7,15},{8,0},{9,1},... | collective-permute-start | bytes 786440 | tf_op jit(solution)/shard_map/ppermute | solution.py:37
  48.6 2.4 %collective-permute-start.7 = (bf16[256,512]{1,0:T(8,128)(2,1)S(1)}, bf16[256,512]{1,0:T(8,128)(2,1)S(1)}, u32[]{:S(2)}, u32[]{:S(2)}) collective-permute-start(bf16[256,512]{1,0:T(8,128)(2,1)S(1)} %bitcast.94), channel_id=1, source_target_pairs={{0,12},{1,13},{2,14},{3,15},{4,8},{5,9},{6,10},{7,11},{8,4},{9,5},... | collective-permute-start | bytes 786440 | tf_op jit(solution)/shard_map/ppermute | solution.py:37
  51.2 4.0 %collective-permute-done.6 = bf16[256,512]{1,0:T(8,128)(2,1)S(1)} collective-permute-done((bf16[256,512]{1,0:T(8,128)(2,1)S(1)}, bf16[256,512]{1,0:T(8,128)(2,1)S(1)}, u32[]{:S(2)}, u32[]{:S(2)}) %collective-permute-start.6) | collective-permute-done | bytes 262176 | tf_op jit(solution)/shard_map/ppermute | solution.py:37
  55.2 5.5 %collective-permute-done.7 = bf16[256,512]{1,0:T(8,128)(2,1)S(1)} collective-permute-done((bf16[256,512]{1,0:T(8,128)(2,1)S(1)}, bf16[256,512]{1,0:T(8,128)(2,1)S(1)}, u32[]{:S(2)}, u32[]{:S(2)}) %collective-permute-start.7) | collective-permute-done | bytes 262176 | tf_op jit(solution)/shard_map/ppermute | solution.py:37
  63.7 6.6 %all-to-all-start.2 = ((bf16[16,4,512]{2,1,0:T(4,128)(2,1)}), bf16[16,4,512]{2,1,0:T(4,128)(2,1)S(1)}, u32[]{:S(2)}, u32[]{:S(2)}) async-start(bf16[16,4,512]{2,1,0:T(4,128)(2,1)} %pad_maximum_fusion.3), calls=%async_computation.2 | async-start | bytes 131072 | tf_op jit(solution)/shard_map/all_to_all | solution.py:144
  70.6 1.9 %collective-permute-start.1 = (bf16[16,2,4096]{2,1,0:T(2,128)(2,1)S(1)}, bf16[16,2,4096]{2,1,0:T(2,128)(2,1)}, u32[]{:S(2)}, u32[]{:S(2)}) collective-permute-start(bf16[16,2,4096]{2,1,0:T(2,128)(2,1)S(1)} %slice.61), channel_id=1, source_target_pairs={{0,16},{16,0},{32,48},{48,32},{64,80},{80,64},{96,112},{112,96},{1... | collective-permute-start | bytes 786440 | tf_op jit(solution)/shard_map/ppermute | solution.py:37
  72.5 3.0 %all-to-all-done.2 = bf16[16,4,512]{2,1,0:T(4,128)(2,1)S(1)} async-done(((bf16[16,4,512]{2,1,0:T(4,128)(2,1)}), bf16[16,4,512]{2,1,0:T(4,128)(2,1)S(1)}, u32[]{:S(2)}, u32[]{:S(2)}) %all-to-all-start.2) | async-done | bytes 65568 | tf_op jit(solution)/shard_map/all_to_all | solution.py:144
  78.2 12.0 %all-to-all-start.3 = ((bf16[16,2,4352]{2,1,0:T(2,128)(2,1)}), bf16[16,2,4352]{2,1,0:T(2,128)(2,1)S(1)}, u32[]{:S(2)}, u32[]{:S(2)}) async-start(bf16[16,2,4352]{2,1,0:T(2,128)(2,1)} %broadcast_in_dim.79), calls=%async_computation.3 | async-start | bytes 557056 | tf_op jit(solution)/shard_map/all_to_all | solution.py:32
  90.3 1.8 %fusion.8 = f32[1024,512]{1,0:T(8,128)} fusion(bf16[1024,16]{0,1:T(8,128)(2,1)S(1)} %fusion.3, bf16[512,2,8]{0,2,1:T(8,128)(2,1)S(1)} %copy.45), kind=kOutput, calls=%fused_computation.39 | convolution fusion | flops 16777216 | bytes 2146304 | tf_op jit(solution)/shard_map/dot_general | solution.py:182
  92.1 2.1 %broadcast_select_fusion.1 = (bf16[16,2,4096]{2,1,0:T(2,128)(2,1)}, bf16[16,2,4096]{2,1,0:T(2,128)(2,1)S(1)}) fusion(bf16[16,2,4096]{2,1,0:T(2,128)(2,1)} %collective-permute-done.1, pred[]{:T(512)S(6)} %eq.36, bf16[16,2,8448]{2,1,0:T(2,128)(2,1)S(1)} %all-to-all-done), kind=kLoop, calls=%fused_computation.26 | loop fusion | flops 262144 | bytes 1048577 | tf_op jit(solution)/shard_map/jit(_where)/select_n | solution.py:161
  97.4 2.5 %collective-permute-start.2 = (bf16[512,256]{1,0:T(8,128)(2,1)}, bf16[512,256]{1,0:T(8,128)(2,1)}, u32[]{:S(2)}, u32[]{:S(2)}) collective-permute-start(bf16[512,256]{1,0:T(8,128)(2,1)} %get-tuple-element.5), channel_id=1, source_target_pairs={{0,4},{1,5},{2,6},{3,7},{4,0},{5,1},{6,2},{7,3},{8,12},{9,13},{10,... | collective-permute-start | bytes 786440 | tf_op jit(solution)/shard_map/ppermute | solution.py:37
  99.9 4.0 %collective-permute-start.3 = (bf16[512,256]{1,0:T(8,128)(2,1)}, bf16[512,256]{1,0:T(8,128)(2,1)}, u32[]{:S(2)}, u32[]{:S(2)}) collective-permute-start(bf16[512,256]{1,0:T(8,128)(2,1)} %get-tuple-element.7), channel_id=1, source_target_pairs={{0,8},{1,9},{2,10},{3,11},{4,12},{5,13},{6,14},{7,15},{8,0},{9,1},... | collective-permute-start | bytes 786440 | tf_op jit(solution)/shard_map/ppermute | solution.py:37
  103.9 4.0 %collective-permute-start.4 = (bf16[512,256]{1,0:T(8,128)(2,1)S(1)}, bf16[512,256]{1,0:T(8,128)(2,1)}, u32[]{:S(2)}, u32[]{:S(2)}) collective-permute-start(bf16[512,256]{1,0:T(8,128)(2,1)S(1)} %get-tuple-element.6), channel_id=1, source_target_pairs={{0,12},{1,13},{2,14},{3,15},{4,8},{5,9},{6,10},{7,11},{8,4},{9,5},... | collective-permute-start | bytes 786440 | tf_op jit(solution)/shard_map/ppermute | solution.py:37
  107.9 1.7 %add_convert_fusion = bf16[1024,512]{1,0:T(8,128)(2,1)} fusion(f32[1024,512]{1,0:T(8,128)S(1)} %copy-done.1, bf16[1024,512]{1,0:T(8,128)(2,1)S(1)} %bitcast.89, bf16[512,512]{1,0:T(8,128)(2,1)S(1)} %bitcast.91), kind=kOutput, calls=%fused_computation.2 | convolution fusion | flops 537919488 | bytes 4718592 | tf_op jit(solution)/shard_map/dot_general | solution.py:183
  109.5 1.9 %collective-permute-start.8 = (bf16[16,2,4352]{2,1,0:T(2,128)(2,1)S(1)}, bf16[16,2,4352]{2,1,0:T(2,128)(2,1)S(1)}, u32[]{:S(2)}, u32[]{:S(2)}) collective-permute-start(bf16[16,2,4352]{2,1,0:T(2,128)(2,1)S(1)} %all-to-all-done.3), channel_id=1, source_target_pairs={{0,16},{16,0},{32,48},{48,32},{64,80},{80,64},{96,112},{112,96},{1... | collective-permute-start | bytes 835592 | tf_op jit(solution)/shard_map/ppermute | solution.py:37
  114.3 3.2 %all-to-all-start.4 = ((f32[4,1,512]{2,1,0:T(1,128)}), f32[4,1,512]{2,1,0:T(1,128)S(1)}, u32[]{:S(2)}, u32[]{:S(2)}) async-start(f32[4,1,512]{2,1,0:T(1,128)} %broadcast_in_dim.81), calls=%async_computation.4 | async-start | bytes 16384 | tf_op jit(solution)/shard_map/all_to_all | solution.py:32
  119.1 3.8 %all-to-all-done.4 = f32[4,1,512]{2,1,0:T(1,128)S(1)} async-done(((f32[4,1,512]{2,1,0:T(1,128)}), f32[4,1,512]{2,1,0:T(1,128)S(1)}, u32[]{:S(2)}, u32[]{:S(2)}) %all-to-all-start.4) | async-done | bytes 8224 | tf_op jit(solution)/shard_map/all_to_all | solution.py:32
  125.4 6.5 %all-to-all-start.5 = ((bf16[4,67,512]{2,1,0:T(8,128)(2,1)}), bf16[4,67,512]{2,1,0:T(8,128)(2,1)S(1)}, u32[]{:S(2)}, u32[]{:S(2)}) async-start(bf16[4,67,512]{2,1,0:T(8,128)(2,1)} %pad_maximum_fusion.2), calls=%async_computation.5 | async-start | bytes 589824 | tf_op jit(solution)/shard_map/all_to_all | solution.py:222
  133.6 5.0 %all-to-all-done.5 = bf16[4,67,512]{2,1,0:T(8,128)(2,1)S(1)} async-done(((bf16[4,67,512]{2,1,0:T(8,128)(2,1)}), bf16[4,67,512]{2,1,0:T(8,128)(2,1)S(1)}, u32[]{:S(2)}, u32[]{:S(2)}) %all-to-all-start.5) | async-done | bytes 274464 | tf_op jit(solution)/shard_map/all_to_all | solution.py:222
  (110 shorter events, 28.4 us)
Async XLA Ops:
  0.6 60.9 %copy-start = (bf16[1024,512]{1,0:T(8,128)(2,1)S(1)}, bf16[1024,512]{1,0:T(8,128)(2,1)}, u32[]{:S(2)}) copy-start(bf16[1024,512]{1,0:T(8,128)(2,1)} %param.9) | copy-start | bytes 3145732
  5.0 11.1 %collective-permute-start = (bf16[32,4352]{1,0:T(8,128)(2,1)S(1)}, bf16[32,4352]{1,0:T(8,128)(2,1)S(1)}, u32[]{:S(2)}, u32[]{:S(2)}) collective-permute-start(bf16[32,4352]{1,0:T(8,128)(2,1)S(1)} %convolution_convert_fusion), channel_id=1, source_target_pairs={{0,16},{16,0},{32,48},{48,32},{64,80},{80,64},{96,112},{112,96},{1... | collective-permute-start | bytes 835592 | tf_op jit(solution)/shard_map/ppermute | solution.py:37
  8.5 33.0 %copy-start.4 = (s32[1,3]{1,0:T(1,128)S(1)}, s32[1,3]{1,0:T(1,128)}, u32[]{:S(2)}) copy-start(s32[1,3]{1,0:T(1,128)} %param.11) | copy-start | bytes 40
  8.5 13.9 %all-to-all-start.1 = ((bf16[4,64,512]{2,1,0:T(8,128)(2,1)}), bf16[4,64,512]{2,1,0:T(8,128)(2,1)S(1)}, u32[]{:S(2)}, u32[]{:S(2)}) async-start(bf16[4,64,512]{2,1,0:T(8,128)(2,1)} %broadcast_in_dim.72), calls=%async_computation.1 | async-start | bytes 524288 | tf_op jit(solution)/shard_map/all_to_all | solution.py:32
  22.3 38.4 %all-to-all-start = ((bf16[16,2,8448]{2,1,0:T(2,128)(2,1)}), bf16[16,2,8448]{2,1,0:T(2,128)(2,1)S(1)}, u32[]{:S(2)}, u32[]{:S(2)}) async-start(bf16[16,2,8448]{2,1,0:T(2,128)(2,1)} %pad_maximum_fusion), calls=%async_computation | async-start | bytes 1081344 | tf_op jit(solution)/shard_map/all_to_all | solution.py:111
  38.0 13.1 %collective-permute-start.5 = (bf16[256,512]{1,0:T(8,128)(2,1)S(1)}, bf16[256,512]{1,0:T(8,128)(2,1)S(1)}, u32[]{:S(2)}, u32[]{:S(2)}) collective-permute-start(bf16[256,512]{1,0:T(8,128)(2,1)S(1)} %bitcast.92), channel_id=1, source_target_pairs={{0,4},{1,5},{2,6},{3,7},{4,0},{5,1},{6,2},{7,3},{8,12},{9,13},{10,... | collective-permute-start | bytes 786440 | tf_op jit(solution)/shard_map/ppermute | solution.py:37
  44.0 11.2 %collective-permute-start.6 = (bf16[256,512]{1,0:T(8,128)(2,1)S(1)}, bf16[256,512]{1,0:T(8,128)(2,1)S(1)}, u32[]{:S(2)}, u32[]{:S(2)}) collective-permute-start(bf16[256,512]{1,0:T(8,128)(2,1)S(1)} %bitcast.93), channel_id=1, source_target_pairs={{0,8},{1,9},{2,10},{3,11},{4,12},{5,13},{6,14},{7,15},{8,0},{9,1},... | collective-permute-start | bytes 786440 | tf_op jit(solution)/shard_map/ppermute | solution.py:37
  48.6 12.1 %collective-permute-start.7 = (bf16[256,512]{1,0:T(8,128)(2,1)S(1)}, bf16[256,512]{1,0:T(8,128)(2,1)S(1)}, u32[]{:S(2)}, u32[]{:S(2)}) collective-permute-start(bf16[256,512]{1,0:T(8,128)(2,1)S(1)} %bitcast.94), channel_id=1, source_target_pairs={{0,12},{1,13},{2,14},{3,15},{4,8},{5,9},{6,10},{7,11},{8,4},{9,5},... | collective-permute-start | bytes 786440 | tf_op jit(solution)/shard_map/ppermute | solution.py:37
  63.7 11.8 %all-to-all-start.2 = ((bf16[16,4,512]{2,1,0:T(4,128)(2,1)}), bf16[16,4,512]{2,1,0:T(4,128)(2,1)S(1)}, u32[]{:S(2)}, u32[]{:S(2)}) async-start(bf16[16,4,512]{2,1,0:T(4,128)(2,1)} %pad_maximum_fusion.3), calls=%async_computation.2 | async-start | bytes 131072 | tf_op jit(solution)/shard_map/all_to_all | solution.py:144
  70.6 21.5 %collective-permute-start.1 = (bf16[16,2,4096]{2,1,0:T(2,128)(2,1)S(1)}, bf16[16,2,4096]{2,1,0:T(2,128)(2,1)}, u32[]{:S(2)}, u32[]{:S(2)}) collective-permute-start(bf16[16,2,4096]{2,1,0:T(2,128)(2,1)S(1)} %slice.61), channel_id=1, source_target_pairs={{0,16},{16,0},{32,48},{48,32},{64,80},{80,64},{96,112},{112,96},{1... | collective-permute-start | bytes 786440 | tf_op jit(solution)/shard_map/ppermute | solution.py:37
  78.2 31.3 %all-to-all-start.3 = ((bf16[16,2,4352]{2,1,0:T(2,128)(2,1)}), bf16[16,2,4352]{2,1,0:T(2,128)(2,1)S(1)}, u32[]{:S(2)}, u32[]{:S(2)}) async-start(bf16[16,2,4352]{2,1,0:T(2,128)(2,1)} %broadcast_in_dim.79), calls=%async_computation.3 | async-start | bytes 557056 | tf_op jit(solution)/shard_map/all_to_all | solution.py:32
  95.6 12.3 %copy-start.1 = (f32[1024,512]{1,0:T(8,128)S(1)}, f32[1024,512]{1,0:T(8,128)}, u32[]{:S(2)}) copy-start(f32[1024,512]{1,0:T(8,128)} %fusion.8) | copy-start | bytes 6291460
  96.3 11.5 %copy-start.2 = (bf16[512,1024]{1,0:T(8,128)(2,1)}, bf16[512,1024]{1,0:T(8,128)(2,1)S(1)}, u32[]{:S(2)}) copy-start(bf16[512,1024]{1,0:T(8,128)(2,1)S(1)} %convolution_convert_fusion.1) | copy-start | bytes 3145732
  97.4 20.1 %collective-permute-start.2 = (bf16[512,256]{1,0:T(8,128)(2,1)}, bf16[512,256]{1,0:T(8,128)(2,1)}, u32[]{:S(2)}, u32[]{:S(2)}) collective-permute-start(bf16[512,256]{1,0:T(8,128)(2,1)} %get-tuple-element.5), channel_id=1, source_target_pairs={{0,4},{1,5},{2,6},{3,7},{4,0},{5,1},{6,2},{7,3},{8,12},{9,13},{10,... | collective-permute-start | bytes 786440 | tf_op jit(solution)/shard_map/ppermute | solution.py:37
  99.9 17.7 %collective-permute-start.3 = (bf16[512,256]{1,0:T(8,128)(2,1)}, bf16[512,256]{1,0:T(8,128)(2,1)}, u32[]{:S(2)}, u32[]{:S(2)}) collective-permute-start(bf16[512,256]{1,0:T(8,128)(2,1)} %get-tuple-element.7), channel_id=1, source_target_pairs={{0,8},{1,9},{2,10},{3,11},{4,12},{5,13},{6,14},{7,15},{8,0},{9,1},... | collective-permute-start | bytes 786440 | tf_op jit(solution)/shard_map/ppermute | solution.py:37
  103.9 13.7 %collective-permute-start.4 = (bf16[512,256]{1,0:T(8,128)(2,1)S(1)}, bf16[512,256]{1,0:T(8,128)(2,1)}, u32[]{:S(2)}, u32[]{:S(2)}) collective-permute-start(bf16[512,256]{1,0:T(8,128)(2,1)S(1)} %get-tuple-element.6), channel_id=1, source_target_pairs={{0,12},{1,13},{2,14},{3,15},{4,8},{5,9},{6,10},{7,11},{8,4},{9,5},... | collective-permute-start | bytes 786440 | tf_op jit(solution)/shard_map/ppermute | solution.py:37
  109.5 3.4 %collective-permute-start.8 = (bf16[16,2,4352]{2,1,0:T(2,128)(2,1)S(1)}, bf16[16,2,4352]{2,1,0:T(2,128)(2,1)S(1)}, u32[]{:S(2)}, u32[]{:S(2)}) collective-permute-start(bf16[16,2,4352]{2,1,0:T(2,128)(2,1)S(1)} %all-to-all-done.3), channel_id=1, source_target_pairs={{0,16},{16,0},{32,48},{48,32},{64,80},{80,64},{96,112},{112,96},{1... | collective-permute-start | bytes 835592 | tf_op jit(solution)/shard_map/ppermute | solution.py:37
  114.3 8.5 %all-to-all-start.4 = ((f32[4,1,512]{2,1,0:T(1,128)}), f32[4,1,512]{2,1,0:T(1,128)S(1)}, u32[]{:S(2)}, u32[]{:S(2)}) async-start(f32[4,1,512]{2,1,0:T(1,128)} %broadcast_in_dim.81), calls=%async_computation.4 | async-start | bytes 16384 | tf_op jit(solution)/shard_map/all_to_all | solution.py:32
  119.0 20.6 %copy-start.3 = (bf16[32,1024]{1,0:T(8,128)(2,1)S(1)}, bf16[32,1024]{1,0:T(8,128)(2,1)}, u32[]{:S(2)}) copy-start(bf16[32,1024]{1,0:T(8,128)(2,1)} %param.13) | copy-start | bytes 196612
  125.4 13.1 %all-to-all-start.5 = ((bf16[4,67,512]{2,1,0:T(8,128)(2,1)}), bf16[4,67,512]{2,1,0:T(8,128)(2,1)S(1)}, u32[]{:S(2)}, u32[]{:S(2)}) async-start(bf16[4,67,512]{2,1,0:T(8,128)(2,1)} %pad_maximum_fusion.2), calls=%async_computation.5 | async-start | bytes 589824 | tf_op jit(solution)/shard_map/all_to_all | solution.py:222

commit v7 on v6

--- a/solution.py
+++ b/solution.py
@@ -98,7 +98,8 @@
     hot_mate, pick_mate = chosen_by(1 - core)
     hot_mine, pick_mine = chosen_by(core)
     from_mate = swapped(terms_of(pick_mate).astype(bf16), "dp", 1)
-    terms = (terms_of(pick_mine) + from_mate.astype(f32)).astype(bf16)
+    run_zero = zero_after(cot_run).astype(bf16)
+    terms = (terms_of(pick_mine + run_zero) + from_mate.astype(f32)).astype(bf16)
     term_width = down_width + up_width
     weight_own = value_weight.T.reshape(1, SEQS, -1)
     sent = jnp.concatenate(
@@ -142,6 +143,23 @@
     )
     summed = low_lines + up_lines
     low_came = lax.all_to_all(block, "tensor", 0, 0)
+
+    weight_mine = came[:, :, term_width:]
+    weight_mate = swapped(weight_mine, "dp", 1)
+    weight_mine = weight_mine.reshape(n_chips, KV // n_dp, width_own)
+    weight_mate = weight_mate.reshape(n_chips, KV // n_dp, width_own)
+    weight_t = jnp.stack(
+        (
+            jnp.where(core == 0, weight_mine, weight_mate),
+            jnp.where(core == 0, weight_mate, weight_mine),
+        ),
+        axis=1,
+    ).reshape(KV, width_own)
+    frozen_t = lax.dot_general(
+        weight_t, tokens, inner_dims, preferred_element_type=f32
+    ).astype(bf16)
+
+    low_came = low_came + zero_after(frozen_t).astype(bf16)
     whole = jnp.sum(low_came[:, :summed].astype(f32), axis=0)
     low_rows = whole[:low_lines].reshape(rows_own, ADA)
     up_grad = whole[low_lines:].reshape(outputs_own, ADA)
@@ -152,21 +170,6 @@
         .reshape(KV, ADA)
     )
 
-    weight_mine = came[:, :, term_width:]
-    weight_mate = swapped(weight_mine, "dp", 1)
-    weight_mine = weight_mine.reshape(n_chips, KV // n_dp, width_own)
-    weight_mate = weight_mate.reshape(n_chips, KV // n_dp, width_own)
-    weight_t = jnp.stack(
-        (
-            jnp.where(core == 0, weight_mine, weight_mate),
-            jnp.where(core == 0, weight_mate, weight_mine),
-        ),
-        axis=1,
-    ).reshape(KV, width_own)
-    frozen_t = lax.dot_general(
-        weight_t, tokens, inner_dims, preferred_element_type=f32
-    ).astype(bf16)
-
     down_scale = 1.0 / math.sqrt(D)
     up_scale = 1.0 / math.sqrt(R)
     back_low = (jnp.dot(cot_full, up_cat, preferred_element_type=f32) * col_mask).astype(bf16)
@@ -179,9 +182,6 @@
     own_grads = jnp.concatenate((down_seq, up_seq), axis=1).astype(bf16)
     grads_mine = spread(own_grads, "dp", n_chips, axis_index_groups=same_core)
 
-    adapter_back = lax.dot_general(back_low, down_cat, inner_dims, preferred_element_type=f32)
-    frozen_back = jnp.dot(cot_full, weight_t, preferred_element_type=f32)
-    grad_tokens = (frozen_back + adapter_back).astype(bf16)
     run_rows = Y_RUN * rows_own
 
     def run_of(x):
@@ -225,6 +225,10 @@
     grad_hidden = jnp.sum(last[rows_own:].reshape((3,) + by_task.shape), axis=0)
 
     last_zero = zero_after(hidden_x).astype(bf16)
+
+    adapter_back = lax.dot_general(back_low, down_cat, inner_dims, preferred_element_type=f32)
+    frozen_back = jnp.dot(cot_full, weight_t, preferred_element_type=f32)
+    grad_tokens = (frozen_back + last_zero.astype(f32) + adapter_back).astype(bf16)
 
     def head_grads(grads, pick):
         return lax.dot_general(

time: 142 us -> 146 us (1.028)
  waiting for transfers between devices: 26.6 us -> 16.3 us
  local copies, waits for them, and re-layouts: 15.5 us -> 22.9 us
  matrix products: 10.1 us -> 15.9 us
  between operations: 3.74 us -> 6.41 us
    all_to_all x3, waiting for transfers between devices: 8.12 us -> 3.87 us  [spread(): return lax.all_to_all(copies, axes, 0, 0, **kw)]
    reshape x2, local copies, waits for them, and re-layouts: 0.21 us -> 3.55 us  [hidden_terms(): grads.reshape(n_chips * SEQS, -1)]
    all_to_all x1, waiting for transfers between devices: 4.97 us -> 1.64 us  [shards(): lax.all_to_all(last, 'tensor', 0, 0, axis_index_groups=along_y).astype(f32)]
    all_to_all x1, waiting for transfers between devices: 2.98 us -> 0.41 us  [shards(): low_came = lax.all_to_all(block, 'tensor', 0, 0)]
    dot_general x2, matrix products: 0.35 us -> 2.26 us  [hidden_terms(): lax.dot_general(grads.reshape(n_chips * SEQS, -1), heads, inner_dims, pre...]
    dot_general x1, matrix products: 1.68 us -> 3.48 us  [shards(): frozen_back = jnp.dot(cot_full, weight_t, preferred_element_type=f32)]
    unnamed x12 -> x46, local copies, waits for them, and re-layouts: 0.95 us -> 2.57 us
  transfers between devices with their start and end apart: 15 -> 15, of which waited for: 7 -> 6; matrix products, arithmetic and copies ran while one was open for 16% -> 22% of each run, Pallas kernels for 0% -> 0%
where the time goes in v7:
time: 146 us; the launch traced here: 145 us
  starting transfers between devices  76 us (52%)
  local copies, waits for them, and re-layouts  22.9 us (16%)
  waiting for transfers between devices  16.3 us (11%)
  matrix products  15.9 us (11%)
  other arithmetic  7.35 us (5%)
  between operations  6.41 us (4%)
    ppermute x9, starting transfers between devices, swapped(): return lax.ppermute(block, axis, pairs)  25.5 us
    all_to_all x3, starting transfers between devices, spread(): return lax.all_to_all(copies, axes, 0, 0, **kw)  22.2 us
    all_to_all x1, starting transfers between devices, shards(): came = lax.all_to_all(sent, 'dp', 0, 0, axis_index_groups=same_core)  15.7 us
    ppermute x9, waiting for transfers between devices, swapped(): return lax.ppermute(block, axis, pairs)  10.4 us
    all_to_all x1, starting transfers between devices, shards(): low_came = lax.all_to_all(block, 'tensor', 0, 0)  6.64 us
    all_to_all x1, starting transfers between devices, shards(): lax.all_to_all(last, 'tensor', 0, 0, axis_index_groups=along_y).astype(f32)  5.92 us
    all_to_all x3, waiting for transfers between devices, spread(): return lax.all_to_all(copies, axes, 0, 0, **kw)  3.87 us
    reshape x2, local copies, waits for them, and re-layouts, hidden_terms(): grads.reshape(n_chips * SEQS, -1)  3.55 us
  transfers between devices with their start and end apart: 15, of which 6 were waited for; matrix products, arithmetic and copies ran while one was open for 22% of the time, Pallas kernels for 0%

profile of v7, /device:TPU:56, one launch (start us, length us, event | category | flops | bytes accessed | tf_op | source)
XLA Modules:
  0.0 144.8 jit_solution(8466917570506943207)
XLA Ops:
  0.6 1.6 %broadcast_in_dim.67 = bf16[4,64,512]{2,1,0:T(8,128)(2,1)} broadcast(bf16[64,512]{1,0:T(8,128)(2,1)} %param.17), dimensions={1,2} | broadcast | bytes 327680 | tf_op jit(solution)/shard_map/broadcast_in_dim | solution.py:31
  2.3 6.3 %all-to-all-start = ((bf16[4,64,512]{2,1,0:T(8,128)(2,1)}), bf16[4,64,512]{2,1,0:T(8,128)(2,1)S(1)}, u32[]{:S(2)}, u32[]{:S(2)}) async-start(bf16[4,64,512]{2,1,0:T(8,128)(2,1)} %broadcast_in_dim.67), calls=%async_computation | async-start | bytes 524288 | tf_op jit(solution)/shard_map/all_to_all | solution.py:32
  10.7 1.6 %multiply_convert_fusion = (bf16[32,16]{0,1:T(8,128)(2,1)S(1)}, f32[32,16]{0,1:T(8,128)}) fusion(bf16[32,1024]{1,0:T(8,128)(2,1)} %param.13, bf16[1024,16]{0,1:T(8,128)(2,1)} %param.14), kind=kOutput, calls=%fused_computation.54 | convolution fusion | flops 1051136 | bytes 101376 | tf_op jit(solution)/shard_map/dot_general | solution.py:83
  13.4 1.9 %collective-permute-start = (bf16[32,4352]{1,0:T(8,128)(2,1)S(1)}, bf16[32,4352]{1,0:T(8,128)(2,1)S(1)}, u32[]{:S(2)}, u32[]{:S(2)}) collective-permute-start(bf16[32,4352]{1,0:T(8,128)(2,1)S(1)} %convolution_convert_fusion), channel_id=1, source_target_pairs={{0,16},{16,0},{32,48},{48,32},{64,80},{80,64},{96,112},{112,96},{1... | collective-permute-start | bytes 835592 | tf_op jit(solution)/shard_map/ppermute | solution.py:37
  18.9 3.4 %collective-permute-start.5 = (bf16[256,512]{1,0:T(8,128)(2,1)S(1)}, bf16[256,512]{1,0:T(8,128)(2,1)S(1)}, u32[]{:S(2)}, u32[]{:S(2)}) collective-permute-start(bf16[256,512]{1,0:T(8,128)(2,1)S(1)} %bitcast.101), channel_id=1, source_target_pairs={{0,4},{1,5},{2,6},{3,7},{4,0},{5,1},{6,2},{7,3},{8,12},{9,13},{10,... | collective-permute-start | bytes 786440 | tf_op jit(solution)/shard_map/ppermute | solution.py:37
  24.2 15.7 %all-to-all-start.1 = ((bf16[16,2,8448]{2,1,0:T(2,128)(2,1)}), bf16[16,2,8448]{2,1,0:T(2,128)(2,1)S(1)}, u32[]{:S(2)}, u32[]{:S(2)}) async-start(bf16[16,2,8448]{2,1,0:T(2,128)(2,1)} %pad_maximum_fusion), calls=%async_computation.1 | async-start | bytes 1081344 | tf_op jit(solution)/shard_map/all_to_all | solution.py:112
  42.4 4.0 %collective-permute-start.7 = (bf16[256,512]{1,0:T(8,128)(2,1)S(1)}, bf16[256,512]{1,0:T(8,128)(2,1)S(1)}, u32[]{:S(2)}, u32[]{:S(2)}) collective-permute-start(bf16[256,512]{1,0:T(8,128)(2,1)S(1)} %bitcast.102), channel_id=1, source_target_pairs={{0,12},{1,13},{2,14},{3,15},{4,8},{5,9},{6,10},{7,11},{8,4},{9,5},... | collective-permute-start | bytes 786440 | tf_op jit(solution)/shard_map/ppermute | solution.py:37
  46.4 2.6 %collective-permute-start.6 = (bf16[256,512]{1,0:T(8,128)(2,1)S(1)}, bf16[256,512]{1,0:T(8,128)(2,1)S(1)}, u32[]{:S(2)}, u32[]{:S(2)}) collective-permute-start(bf16[256,512]{1,0:T(8,128)(2,1)S(1)} %bitcast.103), channel_id=1, source_target_pairs={{0,8},{1,9},{2,10},{3,11},{4,12},{5,13},{6,14},{7,15},{8,0},{9,1},... | collective-permute-start | bytes 786440 | tf_op jit(solution)/shard_map/ppermute | solution.py:37
  49.2 8.4 %collective-permute-done.6 = bf16[256,512]{1,0:T(8,128)(2,1)S(1)} collective-permute-done((bf16[256,512]{1,0:T(8,128)(2,1)S(1)}, bf16[256,512]{1,0:T(8,128)(2,1)S(1)}, u32[]{:S(2)}, u32[]{:S(2)}) %collective-permute-start.6) | collective-permute-done | bytes 262176 | tf_op jit(solution)/shard_map/ppermute | solution.py:37
  60.9 1.9 %collective-permute-start.1 = (bf16[16,2,4096]{2,1,0:T(2,128)(2,1)S(1)}, bf16[16,2,4096]{2,1,0:T(2,128)(2,1)}, u32[]{:S(2)}, u32[]{:S(2)}) collective-permute-start(bf16[16,2,4096]{2,1,0:T(2,128)(2,1)S(1)} %slice.70), channel_id=1, source_target_pairs={{0,16},{16,0},{32,48},{48,32},{64,80},{80,64},{96,112},{112,96},{1... | collective-permute-start | bytes 786440 | tf_op jit(solution)/shard_map/ppermute | solution.py:37
  64.2 6.6 %all-to-all-start.2 = ((bf16[16,4,512]{2,1,0:T(4,128)(2,1)}), bf16[16,4,512]{2,1,0:T(4,128)(2,1)S(1)}, u32[]{:S(2)}, u32[]{:S(2)}) async-start(bf16[16,4,512]{2,1,0:T(4,128)(2,1)} %pad_maximum_fusion.3), calls=%async_computation.2 | async-start | bytes 131072 | tf_op jit(solution)/shard_map/all_to_all | solution.py:145
  82.7 12.0 %all-to-all-start.3 = ((bf16[16,2,4352]{2,1,0:T(2,128)(2,1)}), bf16[16,2,4352]{2,1,0:T(2,128)(2,1)}, u32[]{:S(2)}, u32[]{:S(2)}) async-start(bf16[16,2,4352]{2,1,0:T(2,128)(2,1)} %broadcast_in_dim.79), calls=%async_computation.3 | async-start | bytes 557056 | tf_op jit(solution)/shard_map/all_to_all | solution.py:32
  95.7 3.0 %collective-permute-start.2 = (bf16[512,256]{1,0:T(8,128)(2,1)}, bf16[512,256]{1,0:T(8,128)(2,1)}, u32[]{:S(2)}, u32[]{:S(2)}) collective-permute-start(bf16[512,256]{1,0:T(8,128)(2,1)} %get-tuple-element.5), channel_id=1, source_target_pairs={{0,4},{1,5},{2,6},{3,7},{4,0},{5,1},{6,2},{7,3},{8,12},{9,13},{10,... | collective-permute-start | bytes 786440 | tf_op jit(solution)/shard_map/ppermute | solution.py:37
  98.6 4.0 %collective-permute-start.4 = (bf16[512,256]{1,0:T(8,128)(2,1)}, bf16[512,256]{1,0:T(8,128)(2,1)}, u32[]{:S(2)}, u32[]{:S(2)}) collective-permute-start(bf16[512,256]{1,0:T(8,128)(2,1)} %get-tuple-element.6), channel_id=1, source_target_pairs={{0,12},{1,13},{2,14},{3,15},{4,8},{5,9},{6,10},{7,11},{8,4},{9,5},... | collective-permute-start | bytes 786440 | tf_op jit(solution)/shard_map/ppermute | solution.py:37
  102.6 2.9 %collective-permute-start.3 = (bf16[512,256]{1,0:T(8,128)(2,1)}, bf16[512,256]{1,0:T(8,128)(2,1)}, u32[]{:S(2)}, u32[]{:S(2)}) collective-permute-start(bf16[512,256]{1,0:T(8,128)(2,1)} %get-tuple-element.7), channel_id=1, source_target_pairs={{0,8},{1,9},{2,10},{3,11},{4,12},{5,13},{6,14},{7,15},{8,0},{9,1},... | collective-permute-start | bytes 786440 | tf_op jit(solution)/shard_map/ppermute | solution.py:37
  106.2 1.8 %fusion.8 = f32[1024,512]{1,0:T(8,128)} fusion(bf16[1024,16]{0,1:T(8,128)(2,1)S(1)} %copy-done.4, bf16[512,2,8]{0,2,1:T(8,128)(2,1)S(1)} %copy-done.6), kind=kOutput, calls=%fused_computation.40 | convolution fusion | flops 16777216 | bytes 2146304 | tf_op jit(solution)/shard_map/dot_general | solution.py:229
  108.0 1.8 %reshape.232 = bf16[32,4352]{1,0:T(8,128)(2,1)} reshape(bf16[16,2,4352]{2,1,0:T(2,128)(2,1)} %all-to-all-done.3) | data formatting | bytes 557056 | tf_op jit(solution)/shard_map/reshape | solution.py:199
  109.8 1.9 %collective-permute-start.8 = (bf16[16,2,4352]{2,1,0:T(2,128)(2,1)}, bf16[16,2,4352]{2,1,0:T(2,128)(2,1)}, u32[]{:S(2)}, u32[]{:S(2)}) collective-permute-start(bf16[16,2,4352]{2,1,0:T(2,128)(2,1)} %all-to-all-done.3), channel_id=1, source_target_pairs={{0,16},{16,0},{32,48},{48,32},{64,80},{80,64},{96,112},{112,96},{1... | collective-permute-start | bytes 835592 | tf_op jit(solution)/shard_map/ppermute | solution.py:37
  113.5 1.8 %reshape.233 = bf16[32,4352]{1,0:T(8,128)(2,1)} reshape(bf16[16,2,4352]{2,1,0:T(2,128)(2,1)} %collective-permute-done.8) | data formatting | bytes 557056 | tf_op jit(solution)/shard_map/reshape | solution.py:199
  117.5 3.8 %all-to-all-start.4 = ((f32[4,1,512]{2,1,0:T(1,128)}), f32[4,1,512]{2,1,0:T(1,128)S(1)}, u32[]{:S(2)}, u32[]{:S(2)}) async-start(f32[4,1,512]{2,1,0:T(1,128)} %broadcast_in_dim.81), calls=%async_computation.4 | async-start | bytes 16384 | tf_op jit(solution)/shard_map/all_to_all | solution.py:32
  122.8 3.9 %all-to-all-done.4 = f32[4,1,512]{2,1,0:T(1,128)S(1)} async-done(((f32[4,1,512]{2,1,0:T(1,128)}), f32[4,1,512]{2,1,0:T(1,128)S(1)}, u32[]{:S(2)}, u32[]{:S(2)}) %all-to-all-start.4) | async-done | bytes 8224 | tf_op jit(solution)/shard_map/all_to_all | solution.py:32
  130.4 5.9 %all-to-all-start.5 = ((bf16[4,67,512]{2,1,0:T(8,128)(2,1)}), bf16[4,67,512]{2,1,0:T(8,128)(2,1)S(1)}, u32[]{:S(2)}, u32[]{:S(2)}) async-start(bf16[4,67,512]{2,1,0:T(8,128)(2,1)} %pad_maximum_fusion.2), calls=%async_computation.5 | async-start | bytes 589824 | tf_op jit(solution)/shard_map/all_to_all | solution.py:222
  137.8 3.5 %add_convert_fusion = bf16[1024,512]{1,0:T(8,128)(2,1)} fusion(f32[1024,512]{1,0:T(8,128)} %fusion.8, bf16[1024,512]{1,0:T(8,128)(2,1)S(1)} %bitcast.98, bf16[512,512]{1,0:T(8,128)(2,1)} %bitcast.111, f32[]{:T(128)S(6)} %convert_element_type.178), kind=kOutput, calls=%fused_computation.2 | convolution fusion | flops 538443776 | bytes 4718596 | tf_op jit(solution)/shard_map/dot_general | solution.py:230
  141.3 1.6 %all-to-all-done.5 = bf16[4,67,512]{2,1,0:T(8,128)(2,1)S(1)} async-done(((bf16[4,67,512]{2,1,0:T(8,128)(2,1)}), bf16[4,67,512]{2,1,0:T(8,128)(2,1)S(1)}, u32[]{:S(2)}, u32[]{:S(2)}) %all-to-all-start.5) | async-done | bytes 274464 | tf_op jit(solution)/shard_map/all_to_all | solution.py:222
  (147 shorter events, 36.5 us)
Async XLA Ops:
  0.6 59.2 %copy-start = (bf16[1024,512]{1,0:T(8,128)(2,1)S(1)}, bf16[1024,512]{1,0:T(8,128)(2,1)}, u32[]{:S(2)}) copy-start(bf16[1024,512]{1,0:T(8,128)(2,1)} %param.9) | copy-start | bytes 3145732
  2.3 14.3 %all-to-all-start = ((bf16[4,64,512]{2,1,0:T(8,128)(2,1)}), bf16[4,64,512]{2,1,0:T(8,128)(2,1)S(1)}, u32[]{:S(2)}, u32[]{:S(2)}) async-start(bf16[4,64,512]{2,1,0:T(8,128)(2,1)} %broadcast_in_dim.67), calls=%async_computation | async-start | bytes 524288 | tf_op jit(solution)/shard_map/all_to_all | solution.py:32
  13.4 8.9 %collective-permute-start = (bf16[32,4352]{1,0:T(8,128)(2,1)S(1)}, bf16[32,4352]{1,0:T(8,128)(2,1)S(1)}, u32[]{:S(2)}, u32[]{:S(2)}) collective-permute-start(bf16[32,4352]{1,0:T(8,128)(2,1)S(1)} %convolution_convert_fusion), channel_id=1, source_target_pairs={{0,16},{16,0},{32,48},{48,32},{64,80},{80,64},{96,112},{112,96},{1... | collective-permute-start | bytes 835592 | tf_op jit(solution)/shard_map/ppermute | solution.py:37
  17.0 22.9 %copy-start.16 = (s32[1,3]{1,0:T(1,128)S(1)}, s32[1,3]{1,0:T(1,128)}, u32[]{:S(2)}) copy-start(s32[1,3]{1,0:T(1,128)} %param.11) | copy-start | bytes 40
  18.9 30.2 %collective-permute-start.5 = (bf16[256,512]{1,0:T(8,128)(2,1)S(1)}, bf16[256,512]{1,0:T(8,128)(2,1)S(1)}, u32[]{:S(2)}, u32[]{:S(2)}) collective-permute-start(bf16[256,512]{1,0:T(8,128)(2,1)S(1)} %bitcast.101), channel_id=1, source_target_pairs={{0,4},{1,5},{2,6},{3,7},{4,0},{5,1},{6,2},{7,3},{8,12},{9,13},{10,... | collective-permute-start | bytes 786440 | tf_op jit(solution)/shard_map/ppermute | solution.py:37
  24.2 34.9 %all-to-all-start.1 = ((bf16[16,2,8448]{2,1,0:T(2,128)(2,1)}), bf16[16,2,8448]{2,1,0:T(2,128)(2,1)S(1)}, u32[]{:S(2)}, u32[]{:S(2)}) async-start(bf16[16,2,8448]{2,1,0:T(2,128)(2,1)} %pad_maximum_fusion), calls=%async_computation.1 | async-start | bytes 1081344 | tf_op jit(solution)/shard_map/all_to_all | solution.py:112
  42.4 16.6 %collective-permute-start.7 = (bf16[256,512]{1,0:T(8,128)(2,1)S(1)}, bf16[256,512]{1,0:T(8,128)(2,1)S(1)}, u32[]{:S(2)}, u32[]{:S(2)}) collective-permute-start(bf16[256,512]{1,0:T(8,128)(2,1)S(1)} %bitcast.102), channel_id=1, source_target_pairs={{0,12},{1,13},{2,14},{3,15},{4,8},{5,9},{6,10},{7,11},{8,4},{9,5},... | collective-permute-start | bytes 786440 | tf_op jit(solution)/shard_map/ppermute | solution.py:37
  46.4 11.1 %collective-permute-start.6 = (bf16[256,512]{1,0:T(8,128)(2,1)S(1)}, bf16[256,512]{1,0:T(8,128)(2,1)S(1)}, u32[]{:S(2)}, u32[]{:S(2)}) collective-permute-start(bf16[256,512]{1,0:T(8,128)(2,1)S(1)} %bitcast.103), channel_id=1, source_target_pairs={{0,8},{1,9},{2,10},{3,11},{4,12},{5,13},{6,14},{7,15},{8,0},{9,1},... | collective-permute-start | bytes 786440 | tf_op jit(solution)/shard_map/ppermute | solution.py:37
  60.9 9.9 %collective-permute-start.1 = (bf16[16,2,4096]{2,1,0:T(2,128)(2,1)S(1)}, bf16[16,2,4096]{2,1,0:T(2,128)(2,1)}, u32[]{:S(2)}, u32[]{:S(2)}) collective-permute-start(bf16[16,2,4096]{2,1,0:T(2,128)(2,1)S(1)} %slice.70), channel_id=1, source_target_pairs={{0,16},{16,0},{32,48},{48,32},{64,80},{80,64},{96,112},{112,96},{1... | collective-permute-start | bytes 786440 | tf_op jit(solution)/shard_map/ppermute | solution.py:37
  64.2 11.8 %all-to-all-start.2 = ((bf16[16,4,512]{2,1,0:T(4,128)(2,1)}), bf16[16,4,512]{2,1,0:T(4,128)(2,1)S(1)}, u32[]{:S(2)}, u32[]{:S(2)}) async-start(bf16[16,4,512]{2,1,0:T(4,128)(2,1)} %pad_maximum_fusion.3), calls=%async_computation.2 | async-start | bytes 131072 | tf_op jit(solution)/shard_map/all_to_all | solution.py:145
  81.1 25.1 %copy-start.4 = (bf16[1024,16]{0,1:T(8,128)(2,1)S(1)}, bf16[1024,16]{0,1:T(8,128)(2,1)}, u32[]{:S(2)}) copy-start(bf16[1024,16]{0,1:T(8,128)(2,1)} %copy-done.3) | copy-start | bytes 98308
  81.1 25.1 %copy-start.6 = (bf16[512,2,8]{0,2,1:T(8,128)(2,1)S(1)}, bf16[512,2,8]{0,2,1:T(8,128)(2,1)}, u32[]{:S(2)}) copy-start(bf16[512,2,8]{0,2,1:T(8,128)(2,1)} %copy-done.5) | copy-start | bytes 49156
  82.7 25.3 %all-to-all-start.3 = ((bf16[16,2,4352]{2,1,0:T(2,128)(2,1)}), bf16[16,2,4352]{2,1,0:T(2,128)(2,1)}, u32[]{:S(2)}, u32[]{:S(2)}) async-start(bf16[16,2,4352]{2,1,0:T(2,128)(2,1)} %broadcast_in_dim.79), calls=%async_computation.3 | async-start | bytes 557056 | tf_op jit(solution)/shard_map/all_to_all | solution.py:32
  94.7 18.1 %copy-start.20 = (s32[32]{0:T(128)S(1)}, s32[32]{0:T(128)}, u32[]{:S(2)}) copy-start(s32[32]{0:T(128)} %copy-done.19) | copy-start | bytes 388
  95.7 25.7 %collective-permute-start.2 = (bf16[512,256]{1,0:T(8,128)(2,1)}, bf16[512,256]{1,0:T(8,128)(2,1)}, u32[]{:S(2)}, u32[]{:S(2)}) collective-permute-start(bf16[512,256]{1,0:T(8,128)(2,1)} %get-tuple-element.5), channel_id=1, source_target_pairs={{0,4},{1,5},{2,6},{3,7},{4,0},{5,1},{6,2},{7,3},{8,12},{9,13},{10,... | collective-permute-start | bytes 786440 | tf_op jit(solution)/shard_map/ppermute | solution.py:37
  98.6 22.7 %collective-permute-start.4 = (bf16[512,256]{1,0:T(8,128)(2,1)}, bf16[512,256]{1,0:T(8,128)(2,1)}, u32[]{:S(2)}, u32[]{:S(2)}) collective-permute-start(bf16[512,256]{1,0:T(8,128)(2,1)} %get-tuple-element.6), channel_id=1, source_target_pairs={{0,12},{1,13},{2,14},{3,15},{4,8},{5,9},{6,10},{7,11},{8,4},{9,5},... | collective-permute-start | bytes 786440 | tf_op jit(solution)/shard_map/ppermute | solution.py:37
  102.6 13.8 %copy-start.18 = (s32[32]{0:T(128)S(1)}, s32[32]{0:T(128)}, u32[]{:S(2)}) copy-start(s32[32]{0:T(128)} %copy-done.17) | copy-start | bytes 388
  102.6 18.7 %collective-permute-start.3 = (bf16[512,256]{1,0:T(8,128)(2,1)}, bf16[512,256]{1,0:T(8,128)(2,1)}, u32[]{:S(2)}, u32[]{:S(2)}) collective-permute-start(bf16[512,256]{1,0:T(8,128)(2,1)} %get-tuple-element.7), channel_id=1, source_target_pairs={{0,8},{1,9},{2,10},{3,11},{4,12},{5,13},{6,14},{7,15},{8,0},{9,1},... | collective-permute-start | bytes 786440 | tf_op jit(solution)/shard_map/ppermute | solution.py:37
  108.0 20.5 %copy-start.14 = (bf16[32,16]{0,1:T(8,128)(2,1)S(1)}, bf16[32,16]{0,1:T(8,128)(2,1)}, u32[]{:S(2)}) copy-start(bf16[32,16]{0,1:T(8,128)(2,1)} %copy-done.13) | copy-start | bytes 3076
  109.8 3.8 %collective-permute-start.8 = (bf16[16,2,4352]{2,1,0:T(2,128)(2,1)}, bf16[16,2,4352]{2,1,0:T(2,128)(2,1)}, u32[]{:S(2)}, u32[]{:S(2)}) collective-permute-start(bf16[16,2,4352]{2,1,0:T(2,128)(2,1)} %all-to-all-done.3), channel_id=1, source_target_pairs={{0,16},{16,0},{32,48},{48,32},{64,80},{80,64},{96,112},{112,96},{1... | collective-permute-start | bytes 835592 | tf_op jit(solution)/shard_map/ppermute | solution.py:37
  115.3 21.0 %copy-start.12 = (bf16[32,16]{0,1:T(8,128)(2,1)S(1)}, bf16[32,16]{0,1:T(8,128)(2,1)}, u32[]{:S(2)}) copy-start(bf16[32,16]{0,1:T(8,128)(2,1)} %copy-done.11) | copy-start | bytes 3076
  117.5 9.2 %all-to-all-start.4 = ((f32[4,1,512]{2,1,0:T(1,128)}), f32[4,1,512]{2,1,0:T(1,128)S(1)}, u32[]{:S(2)}, u32[]{:S(2)}) async-start(f32[4,1,512]{2,1,0:T(1,128)} %broadcast_in_dim.81), calls=%async_computation.4 | async-start | bytes 16384 | tf_op jit(solution)/shard_map/all_to_all | solution.py:32
  122.6 13.7 %copy-start.1 = (bf16[32,4352]{1,0:T(8,128)(2,1)S(1)}, bf16[32,4352]{1,0:T(8,128)(2,1)}, u32[]{:S(2)}) copy-start(bf16[32,4352]{1,0:T(8,128)(2,1)} %reshape.233) | copy-start | bytes 835588
  130.4 12.6 %all-to-all-start.5 = ((bf16[4,67,512]{2,1,0:T(8,128)(2,1)}), bf16[4,67,512]{2,1,0:T(8,128)(2,1)S(1)}, u32[]{:S(2)}, u32[]{:S(2)}) async-start(bf16[4,67,512]{2,1,0:T(8,128)(2,1)} %pad_maximum_fusion.2), calls=%async_computation.5 | async-start | bytes 589824 | tf_op jit(solution)/shard_map/all_to_all | solution.py:222
  (12 other events, 43.8 us)

commit v8 on v6

--- a/solution.py
+++ b/solution.py
@@ -98,7 +98,8 @@
     hot_mate, pick_mate = chosen_by(1 - core)
     hot_mine, pick_mine = chosen_by(core)
     from_mate = swapped(terms_of(pick_mate).astype(bf16), "dp", 1)
-    terms = (terms_of(pick_mine) + from_mate.astype(f32)).astype(bf16)
+    run_zero = zero_after(cot_run).astype(bf16)
+    terms = (terms_of(pick_mine + run_zero) + from_mate.astype(f32)).astype(bf16)
     term_width = down_width + up_width
     weight_own = value_weight.T.reshape(1, SEQS, -1)
     sent = jnp.concatenate(
@@ -179,9 +180,6 @@
     own_grads = jnp.concatenate((down_seq, up_seq), axis=1).astype(bf16)
     grads_mine = spread(own_grads, "dp", n_chips, axis_index_groups=same_core)
 
-    adapter_back = lax.dot_general(back_low, down_cat, inner_dims, preferred_element_type=f32)
-    frozen_back = jnp.dot(cot_full, weight_t, preferred_element_type=f32)
-    grad_tokens = (frozen_back + adapter_back).astype(bf16)
     run_rows = Y_RUN * rows_own
 
     def run_of(x):
@@ -205,7 +203,8 @@
         spread(by_task.reshape(1, -1), "tensor", n_x, axis_index_groups=along_x), axis=0
     )
 
-    rows_x = frozen_kept.astype(f32)
+    task_zero = zero_after(by_task)
+    rows_x = frozen_kept.astype(f32) + task_zero.astype(f32)
     for other in frozen_came:
         rows_x = rows_x + other.astype(f32)
     last = jnp.concatenate(
@@ -225,6 +224,10 @@
     grad_hidden = jnp.sum(last[rows_own:].reshape((3,) + by_task.shape), axis=0)
 
     last_zero = zero_after(hidden_x).astype(bf16)
+
+    adapter_back = lax.dot_general(back_low + task_zero.astype(bf16), down_cat, inner_dims, preferred_element_type=f32)
+    frozen_back = jnp.dot(cot_full, weight_t, preferred_element_type=f32)
+    grad_tokens = (frozen_back + last_zero.astype(f32) + adapter_back).astype(bf16)
 
     def head_grads(grads, pick):
         return lax.dot_general(

time: 142 us -> 140 us (0.986)
  waiting for transfers between devices: 26.6 us -> 16.8 us
  local copies, waits for them, and re-layouts: 15.5 us -> 18.3 us
  between operations: 3.74 us -> 6.32 us
  matrix products: 10.1 us -> 11.9 us
    all_to_all x3, waiting for transfers between devices: 8.12 us -> 1.99 us  [spread(): return lax.all_to_all(copies, axes, 0, 0, **kw)]
    all_to_all x1, waiting for transfers between devices: 4.97 us -> 1.67 us  [shards(): lax.all_to_all(last, 'tensor', 0, 0, axis_index_groups=along_y).astype(f32)]
    dot_general x1, matrix products: 1.68 us -> 3.47 us  [shards(): frozen_back = jnp.dot(cot_full, weight_t, preferred_element_type=f32)]
    broadcast_in_dim x4 -> x3, local copies, waits for them, and re-layouts: 3.13 us -> 3.1 us  [spread(): copies = jnp.broadcast_to(block[None], (count,) + block.shape)]
  transfers between devices with their start and end apart: 15 -> 15, of which waited for: 7 -> 6; matrix products, arithmetic and copies ran while one was open for 16% -> 21% of each run, Pallas kernels for 0% -> 0%
where the time goes in v8:
time: 140 us; the launch traced here: 138 us
  starting transfers between devices  77.7 us (56%)
  local copies, waits for them, and re-layouts  18.3 us (13%)
  waiting for transfers between devices  16.8 us (12%)
  matrix products  11.9 us (8%)
  other arithmetic  7.39 us (5%)
  between operations  6.32 us (5%)
    ppermute x9, starting transfers between devices, swapped(): return lax.ppermute(block, axis, pairs)  26.6 us
    all_to_all x3, starting transfers between devices, spread(): return lax.all_to_all(copies, axes, 0, 0, **kw)  21.6 us
    all_to_all x1, starting transfers between devices, shards(): came = lax.all_to_all(sent, 'dp', 0, 0, axis_index_groups=same_core)  15.7 us
    ppermute x9, waiting for transfers between devices, swapped(): return lax.ppermute(block, axis, pairs)  10.8 us
    all_to_all x1, starting transfers between devices, shards(): low_came = lax.all_to_all(block, 'tensor', 0, 0)  7.28 us
    all_to_all x1, starting transfers between devices, shards(): lax.all_to_all(last, 'tensor', 0, 0, axis_index_groups=along_y).astype(f32)  6.51 us
    dot_general x1, matrix products, shards(): frozen_back = jnp.dot(cot_full, weight_t, preferred_element_type=f32)  3.47 us
    broadcast_in_dim x3, local copies, waits for them, and re-layouts, spread(): copies = jnp.broadcast_to(block[None], (count,) + block.shape)  3.1 us
  transfers between devices with their start and end apart: 15, of which 6 were waited for; matrix products, arithmetic and copies ran while one was open for 21% of the time, Pallas kernels for 0%

profile of v8, /device:TPU:56, one launch (start us, length us, event | category | flops | bytes accessed | tf_op | source)
XLA Modules:
  0.0 138.3 jit_solution(4917805810304701249)
XLA Ops:
  0.6 1.6 %broadcast_in_dim.65 = bf16[4,64,512]{2,1,0:T(8,128)(2,1)} broadcast(bf16[64,512]{1,0:T(8,128)(2,1)} %param.17), dimensions={1,2} | broadcast | bytes 327680 | tf_op jit(solution)/shard_map/broadcast_in_dim | solution.py:31
  2.3 6.3 %all-to-all-start = ((bf16[4,64,512]{2,1,0:T(8,128)(2,1)}), bf16[4,64,512]{2,1,0:T(8,128)(2,1)S(1)}, u32[]{:S(2)}, u32[]{:S(2)}) async-start(bf16[4,64,512]{2,1,0:T(8,128)(2,1)} %broadcast_in_dim.65), calls=%async_computation | async-start | bytes 524288 | tf_op jit(solution)/shard_map/all_to_all | solution.py:32
  12.8 1.9 %collective-permute-start = (bf16[32,4352]{1,0:T(8,128)(2,1)S(1)}, bf16[32,4352]{1,0:T(8,128)(2,1)S(1)}, u32[]{:S(2)}, u32[]{:S(2)}) collective-permute-start(bf16[32,4352]{1,0:T(8,128)(2,1)S(1)} %convolution_convert_fusion), channel_id=1, source_target_pairs={{0,16},{16,0},{32,48},{48,32},{64,80},{80,64},{96,112},{112,96},{1... | collective-permute-start | bytes 835592 | tf_op jit(solution)/shard_map/ppermute | solution.py:37
  16.0 3.4 %collective-permute-start.2 = (bf16[256,512]{1,0:T(8,128)(2,1)S(1)}, bf16[256,512]{1,0:T(8,128)(2,1)S(1)}, u32[]{:S(2)}, u32[]{:S(2)}) collective-permute-start(bf16[256,512]{1,0:T(8,128)(2,1)S(1)} %bitcast.93), channel_id=1, source_target_pairs={{0,4},{1,5},{2,6},{3,7},{4,0},{5,1},{6,2},{7,3},{8,12},{9,13},{10,... | collective-permute-start | bytes 786440 | tf_op jit(solution)/shard_map/ppermute | solution.py:37
  23.2 15.7 %all-to-all-start.1 = ((bf16[16,2,8448]{2,1,0:T(2,128)(2,1)}), bf16[16,2,8448]{2,1,0:T(2,128)(2,1)S(1)}, u32[]{:S(2)}, u32[]{:S(2)}) async-start(bf16[16,2,8448]{2,1,0:T(2,128)(2,1)} %pad_maximum_fusion), calls=%async_computation.1 | async-start | bytes 1081344 | tf_op jit(solution)/shard_map/all_to_all | solution.py:112
  41.4 4.6 %collective-permute-start.3 = (bf16[256,512]{1,0:T(8,128)(2,1)S(1)}, bf16[256,512]{1,0:T(8,128)(2,1)S(1)}, u32[]{:S(2)}, u32[]{:S(2)}) collective-permute-start(bf16[256,512]{1,0:T(8,128)(2,1)S(1)} %bitcast.95), channel_id=1, source_target_pairs={{0,8},{1,9},{2,10},{3,11},{4,12},{5,13},{6,14},{7,15},{8,0},{9,1},... | collective-permute-start | bytes 786440 | tf_op jit(solution)/shard_map/ppermute | solution.py:37
  46.1 2.4 %collective-permute-start.4 = (bf16[256,512]{1,0:T(8,128)(2,1)S(1)}, bf16[256,512]{1,0:T(8,128)(2,1)S(1)}, u32[]{:S(2)}, u32[]{:S(2)}) collective-permute-start(bf16[256,512]{1,0:T(8,128)(2,1)S(1)} %bitcast.96), channel_id=1, source_target_pairs={{0,12},{1,13},{2,14},{3,15},{4,8},{5,9},{6,10},{7,11},{8,4},{9,5},... | collective-permute-start | bytes 786440 | tf_op jit(solution)/shard_map/ppermute | solution.py:37
  48.6 4.2 %collective-permute-done.3 = bf16[256,512]{1,0:T(8,128)(2,1)S(1)} collective-permute-done((bf16[256,512]{1,0:T(8,128)(2,1)S(1)}, bf16[256,512]{1,0:T(8,128)(2,1)S(1)}, u32[]{:S(2)}, u32[]{:S(2)}) %collective-permute-start.3) | collective-permute-done | bytes 262176 | tf_op jit(solution)/shard_map/ppermute | solution.py:37
  52.8 5.5 %collective-permute-done.4 = bf16[256,512]{1,0:T(8,128)(2,1)S(1)} collective-permute-done((bf16[256,512]{1,0:T(8,128)(2,1)S(1)}, bf16[256,512]{1,0:T(8,128)(2,1)S(1)}, u32[]{:S(2)}, u32[]{:S(2)}) %collective-permute-start.4) | collective-permute-done | bytes 262176 | tf_op jit(solution)/shard_map/ppermute | solution.py:37
  61.3 7.3 %all-to-all-start.2 = ((bf16[16,4,512]{2,1,0:T(4,128)(2,1)}), bf16[16,4,512]{2,1,0:T(4,128)(2,1)S(1)}, u32[]{:S(2)}, u32[]{:S(2)}) async-start(bf16[16,4,512]{2,1,0:T(4,128)(2,1)} %pad_maximum_fusion.3), calls=%async_computation.2 | async-start | bytes 131072 | tf_op jit(solution)/shard_map/all_to_all | solution.py:145
  69.5 1.9 %collective-permute-start.1 = (bf16[16,2,4096]{2,1,0:T(2,128)(2,1)}, bf16[16,2,4096]{2,1,0:T(2,128)(2,1)}, u32[]{:S(2)}, u32[]{:S(2)}) collective-permute-start(bf16[16,2,4096]{2,1,0:T(2,128)(2,1)} %slice.70), channel_id=1, source_target_pairs={{0,16},{16,0},{32,48},{48,32},{64,80},{80,64},{96,112},{112,96},{1... | collective-permute-start | bytes 786440 | tf_op jit(solution)/shard_map/ppermute | solution.py:37
  71.4 2.3 %all-to-all-done.2 = bf16[16,4,512]{2,1,0:T(4,128)(2,1)S(1)} async-done(((bf16[16,4,512]{2,1,0:T(4,128)(2,1)}), bf16[16,4,512]{2,1,0:T(4,128)(2,1)S(1)}, u32[]{:S(2)}, u32[]{:S(2)}) %all-to-all-start.2) | async-done | bytes 65568 | tf_op jit(solution)/shard_map/all_to_all | solution.py:145
  76.4 12.0 %all-to-all-start.3 = ((bf16[16,2,4352]{2,1,0:T(2,128)(2,1)}), bf16[16,2,4352]{2,1,0:T(2,128)(2,1)S(1)}, u32[]{:S(2)}, u32[]{:S(2)}) async-start(bf16[16,2,4352]{2,1,0:T(2,128)(2,1)} %broadcast_in_dim.77), calls=%async_computation.3 | async-start | bytes 557056 | tf_op jit(solution)/shard_map/all_to_all | solution.py:32
  88.5 2.1 %broadcast_select_fusion.1 = (bf16[16,2,4096]{2,1,0:T(2,128)(2,1)}, bf16[16,2,4096]{2,1,0:T(2,128)(2,1)S(1)}) fusion(bf16[16,2,4096]{2,1,0:T(2,128)(2,1)} %collective-permute-done.1, pred[]{:T(512)S(6)} %eq.36, bf16[16,2,8448]{2,1,0:T(2,128)(2,1)S(1)} %all-to-all-done.1), kind=kLoop, calls=%fused_computation.26 | loop fusion | flops 262144 | bytes 1048577 | tf_op jit(solution)/shard_map/jit(_where)/select_n | solution.py:162
  93.8 2.5 %collective-permute-start.6 = (bf16[512,256]{1,0:T(8,128)(2,1)}, bf16[512,256]{1,0:T(8,128)(2,1)}, u32[]{:S(2)}, u32[]{:S(2)}) collective-permute-start(bf16[512,256]{1,0:T(8,128)(2,1)} %get-tuple-element.5), channel_id=1, source_target_pairs={{0,4},{1,5},{2,6},{3,7},{4,0},{5,1},{6,2},{7,3},{8,12},{9,13},{10,... | collective-permute-start | bytes 786440 | tf_op jit(solution)/shard_map/ppermute | solution.py:37
  96.3 4.0 %collective-permute-start.7 = (bf16[512,256]{1,0:T(8,128)(2,1)}, bf16[512,256]{1,0:T(8,128)(2,1)}, u32[]{:S(2)}, u32[]{:S(2)}) collective-permute-start(bf16[512,256]{1,0:T(8,128)(2,1)} %get-tuple-element.7), channel_id=1, source_target_pairs={{0,8},{1,9},{2,10},{3,11},{4,12},{5,13},{6,14},{7,15},{8,0},{9,1},... | collective-permute-start | bytes 786440 | tf_op jit(solution)/shard_map/ppermute | solution.py:37
  100.3 4.0 %collective-permute-start.8 = (bf16[512,256]{1,0:T(8,128)(2,1)S(1)}, bf16[512,256]{1,0:T(8,128)(2,1)}, u32[]{:S(2)}, u32[]{:S(2)}) collective-permute-start(bf16[512,256]{1,0:T(8,128)(2,1)S(1)} %get-tuple-element.6), channel_id=1, source_target_pairs={{0,12},{1,13},{2,14},{3,15},{4,8},{5,9},{6,10},{7,11},{8,4},{9,5},... | collective-permute-start | bytes 786440 | tf_op jit(solution)/shard_map/ppermute | solution.py:37
  104.3 1.9 %collective-permute-start.5 = (bf16[16,2,4352]{2,1,0:T(2,128)(2,1)S(1)}, bf16[16,2,4352]{2,1,0:T(2,128)(2,1)}, u32[]{:S(2)}, u32[]{:S(2)}) collective-permute-start(bf16[16,2,4352]{2,1,0:T(2,128)(2,1)S(1)} %all-to-all-done.3), channel_id=1, source_target_pairs={{0,16},{16,0},{32,48},{48,32},{64,80},{80,64},{96,112},{112,96},{1... | collective-permute-start | bytes 835592 | tf_op jit(solution)/shard_map/ppermute | solution.py:37
  111.9 3.2 %all-to-all-start.4 = ((f32[4,1,512]{2,1,0:T(1,128)}), f32[4,1,512]{2,1,0:T(1,128)S(1)}, u32[]{:S(2)}, u32[]{:S(2)}) async-start(f32[4,1,512]{2,1,0:T(1,128)} %broadcast_in_dim.78), calls=%async_computation.4 | async-start | bytes 16384 | tf_op jit(solution)/shard_map/all_to_all | solution.py:32
  115.2 1.8 %fusion.8 = f32[1024,512]{1,0:T(8,128)} fusion(bf16[1024,16]{0,1:T(8,128)(2,1)S(1)} %fusion.3, bf16[512,2,8]{0,2,1:T(8,128)(2,1)S(1)} %copy.44, bf16[]{:T(256)S(6)} %convert_element_type.174), kind=kOutput, calls=%fused_computation.38 | convolution fusion | flops 16793600 | bytes 2146306 | tf_op jit(solution)/shard_map/dot_general | solution.py:228
  118.5 2.0 %all-to-all-done.4 = f32[4,1,512]{2,1,0:T(1,128)S(1)} async-done(((f32[4,1,512]{2,1,0:T(1,128)}), f32[4,1,512]{2,1,0:T(1,128)S(1)}, u32[]{:S(2)}, u32[]{:S(2)}) %all-to-all-start.4) | async-done | bytes 8224 | tf_op jit(solution)/shard_map/all_to_all | solution.py:32
  123.3 6.5 %all-to-all-start.5 = ((bf16[4,67,512]{2,1,0:T(8,128)(2,1)}), bf16[4,67,512]{2,1,0:T(8,128)(2,1)S(1)}, u32[]{:S(2)}, u32[]{:S(2)}) async-start(bf16[4,67,512]{2,1,0:T(8,128)(2,1)} %pad_maximum_fusion.2), calls=%async_computation.5 | async-start | bytes 589824 | tf_op jit(solution)/shard_map/all_to_all | solution.py:221
  131.3 3.5 %add_convert_fusion = bf16[1024,512]{1,0:T(8,128)(2,1)} fusion(f32[1024,512]{1,0:T(8,128)} %fusion.8, bf16[1024,512]{1,0:T(8,128)(2,1)S(1)} %bitcast.92, bf16[512,512]{1,0:T(8,128)(2,1)} %bitcast.103, f32[]{:T(128)S(6)} %convert_element_type.173), kind=kOutput, calls=%fused_computation.2 | convolution fusion | flops 538443776 | bytes 4718596 | tf_op jit(solution)/shard_map/dot_general | solution.py:229
  134.8 1.7 %all-to-all-done.5 = bf16[4,67,512]{2,1,0:T(8,128)(2,1)S(1)} async-done(((bf16[4,67,512]{2,1,0:T(8,128)(2,1)}), bf16[4,67,512]{2,1,0:T(8,128)(2,1)S(1)}, u32[]{:S(2)}, u32[]{:S(2)}) %all-to-all-start.5) | async-done | bytes 274464 | tf_op jit(solution)/shard_map/all_to_all | solution.py:221
  (113 shorter events, 29.7 us)
Async XLA Ops:
  0.6 58.5 %copy-start = (bf16[1024,512]{1,0:T(8,128)(2,1)S(1)}, bf16[1024,512]{1,0:T(8,128)(2,1)}, u32[]{:S(2)}) copy-start(bf16[1024,512]{1,0:T(8,128)(2,1)} %param.9) | copy-start | bytes 3145732
  2.3 13.7 %all-to-all-start = ((bf16[4,64,512]{2,1,0:T(8,128)(2,1)}), bf16[4,64,512]{2,1,0:T(8,128)(2,1)S(1)}, u32[]{:S(2)}, u32[]{:S(2)}) async-start(bf16[4,64,512]{2,1,0:T(8,128)(2,1)} %broadcast_in_dim.65), calls=%async_computation | async-start | bytes 524288 | tf_op jit(solution)/shard_map/all_to_all | solution.py:32
  12.8 8.5 %collective-permute-start = (bf16[32,4352]{1,0:T(8,128)(2,1)S(1)}, bf16[32,4352]{1,0:T(8,128)(2,1)S(1)}, u32[]{:S(2)}, u32[]{:S(2)}) collective-permute-start(bf16[32,4352]{1,0:T(8,128)(2,1)S(1)} %convolution_convert_fusion), channel_id=1, source_target_pairs={{0,16},{16,0},{32,48},{48,32},{64,80},{80,64},{96,112},{112,96},{1... | collective-permute-start | bytes 835592 | tf_op jit(solution)/shard_map/ppermute | solution.py:37
  16.0 32.6 %collective-permute-start.2 = (bf16[256,512]{1,0:T(8,128)(2,1)S(1)}, bf16[256,512]{1,0:T(8,128)(2,1)S(1)}, u32[]{:S(2)}, u32[]{:S(2)}) collective-permute-start(bf16[256,512]{1,0:T(8,128)(2,1)S(1)} %bitcast.93), channel_id=1, source_target_pairs={{0,4},{1,5},{2,6},{3,7},{4,0},{5,1},{6,2},{7,3},{8,12},{9,13},{10,... | collective-permute-start | bytes 786440 | tf_op jit(solution)/shard_map/ppermute | solution.py:37
  19.4 19.5 %copy-start.4 = (s32[1,3]{1,0:T(1,128)S(1)}, s32[1,3]{1,0:T(1,128)}, u32[]{:S(2)}) copy-start(s32[1,3]{1,0:T(1,128)} %param.11) | copy-start | bytes 40
  23.2 35.2 %all-to-all-start.1 = ((bf16[16,2,8448]{2,1,0:T(2,128)(2,1)}), bf16[16,2,8448]{2,1,0:T(2,128)(2,1)S(1)}, u32[]{:S(2)}, u32[]{:S(2)}) async-start(bf16[16,2,8448]{2,1,0:T(2,128)(2,1)} %pad_maximum_fusion), calls=%async_computation.1 | async-start | bytes 1081344 | tf_op jit(solution)/shard_map/all_to_all | solution.py:112
  41.4 11.4 %collective-permute-start.3 = (bf16[256,512]{1,0:T(8,128)(2,1)S(1)}, bf16[256,512]{1,0:T(8,128)(2,1)S(1)}, u32[]{:S(2)}, u32[]{:S(2)}) collective-permute-start(bf16[256,512]{1,0:T(8,128)(2,1)S(1)} %bitcast.95), channel_id=1, source_target_pairs={{0,8},{1,9},{2,10},{3,11},{4,12},{5,13},{6,14},{7,15},{8,0},{9,1},... | collective-permute-start | bytes 786440 | tf_op jit(solution)/shard_map/ppermute | solution.py:37
  46.1 12.2 %collective-permute-start.4 = (bf16[256,512]{1,0:T(8,128)(2,1)S(1)}, bf16[256,512]{1,0:T(8,128)(2,1)S(1)}, u32[]{:S(2)}, u32[]{:S(2)}) collective-permute-start(bf16[256,512]{1,0:T(8,128)(2,1)S(1)} %bitcast.96), channel_id=1, source_target_pairs={{0,12},{1,13},{2,14},{3,15},{4,8},{5,9},{6,10},{7,11},{8,4},{9,5},... | collective-permute-start | bytes 786440 | tf_op jit(solution)/shard_map/ppermute | solution.py:37
  61.3 12.4 %all-to-all-start.2 = ((bf16[16,4,512]{2,1,0:T(4,128)(2,1)}), bf16[16,4,512]{2,1,0:T(4,128)(2,1)S(1)}, u32[]{:S(2)}, u32[]{:S(2)}) async-start(bf16[16,4,512]{2,1,0:T(4,128)(2,1)} %pad_maximum_fusion.3), calls=%async_computation.2 | async-start | bytes 131072 | tf_op jit(solution)/shard_map/all_to_all | solution.py:145
  69.5 19.0 %collective-permute-start.1 = (bf16[16,2,4096]{2,1,0:T(2,128)(2,1)}, bf16[16,2,4096]{2,1,0:T(2,128)(2,1)}, u32[]{:S(2)}, u32[]{:S(2)}) collective-permute-start(bf16[16,2,4096]{2,1,0:T(2,128)(2,1)} %slice.70), channel_id=1, source_target_pairs={{0,16},{16,0},{32,48},{48,32},{64,80},{80,64},{96,112},{112,96},{1... | collective-permute-start | bytes 786440 | tf_op jit(solution)/shard_map/ppermute | solution.py:37
  76.4 27.8 %all-to-all-start.3 = ((bf16[16,2,4352]{2,1,0:T(2,128)(2,1)}), bf16[16,2,4352]{2,1,0:T(2,128)(2,1)S(1)}, u32[]{:S(2)}, u32[]{:S(2)}) async-start(bf16[16,2,4352]{2,1,0:T(2,128)(2,1)} %broadcast_in_dim.77), calls=%async_computation.3 | async-start | bytes 557056 | tf_op jit(solution)/shard_map/all_to_all | solution.py:32
  92.0 1.8 %copy-start.2 = (bf16[16,2,16,512]{3,2,1,0:T(8,128)(2,1)}, bf16[16,2,16,512]{3,2,1,0:T(8,128)(2,1)S(1)}, u32[]{:S(2)}) copy-start(bf16[16,2,16,512]{3,2,1,0:T(8,128)(2,1)S(1)} %pad_maximum_fusion.1) | copy-start | bytes 1572868
  92.8 7.5 %copy-start.1 = (bf16[512,1024]{1,0:T(8,128)(2,1)}, bf16[512,1024]{1,0:T(8,128)(2,1)S(1)}, u32[]{:S(2)}) copy-start(bf16[512,1024]{1,0:T(8,128)(2,1)S(1)} %convolution_convert_fusion.1) | copy-start | bytes 3145732
  93.8 23.2 %collective-permute-start.6 = (bf16[512,256]{1,0:T(8,128)(2,1)}, bf16[512,256]{1,0:T(8,128)(2,1)}, u32[]{:S(2)}, u32[]{:S(2)}) collective-permute-start(bf16[512,256]{1,0:T(8,128)(2,1)} %get-tuple-element.5), channel_id=1, source_target_pairs={{0,4},{1,5},{2,6},{3,7},{4,0},{5,1},{6,2},{7,3},{8,12},{9,13},{10,... | collective-permute-start | bytes 786440 | tf_op jit(solution)/shard_map/ppermute | solution.py:37
  96.3 20.7 %collective-permute-start.7 = (bf16[512,256]{1,0:T(8,128)(2,1)}, bf16[512,256]{1,0:T(8,128)(2,1)}, u32[]{:S(2)}, u32[]{:S(2)}) collective-permute-start(bf16[512,256]{1,0:T(8,128)(2,1)} %get-tuple-element.7), channel_id=1, source_target_pairs={{0,8},{1,9},{2,10},{3,11},{4,12},{5,13},{6,14},{7,15},{8,0},{9,1},... | collective-permute-start | bytes 786440 | tf_op jit(solution)/shard_map/ppermute | solution.py:37
  100.3 16.7 %collective-permute-start.8 = (bf16[512,256]{1,0:T(8,128)(2,1)S(1)}, bf16[512,256]{1,0:T(8,128)(2,1)}, u32[]{:S(2)}, u32[]{:S(2)}) collective-permute-start(bf16[512,256]{1,0:T(8,128)(2,1)S(1)} %get-tuple-element.6), channel_id=1, source_target_pairs={{0,12},{1,13},{2,14},{3,15},{4,8},{5,9},{6,10},{7,11},{8,4},{9,5},... | collective-permute-start | bytes 786440 | tf_op jit(solution)/shard_map/ppermute | solution.py:37
  104.3 3.6 %collective-permute-start.5 = (bf16[16,2,4352]{2,1,0:T(2,128)(2,1)S(1)}, bf16[16,2,4352]{2,1,0:T(2,128)(2,1)}, u32[]{:S(2)}, u32[]{:S(2)}) collective-permute-start(bf16[16,2,4352]{2,1,0:T(2,128)(2,1)S(1)} %all-to-all-done.3), channel_id=1, source_target_pairs={{0,16},{16,0},{32,48},{48,32},{64,80},{80,64},{96,112},{112,96},{1... | collective-permute-start | bytes 835592 | tf_op jit(solution)/shard_map/ppermute | solution.py:37
  111.9 8.5 %all-to-all-start.4 = ((f32[4,1,512]{2,1,0:T(1,128)}), f32[4,1,512]{2,1,0:T(1,128)S(1)}, u32[]{:S(2)}, u32[]{:S(2)}) async-start(f32[4,1,512]{2,1,0:T(1,128)} %broadcast_in_dim.78), calls=%async_computation.4 | async-start | bytes 16384 | tf_op jit(solution)/shard_map/all_to_all | solution.py:32
  123.3 13.2 %all-to-all-start.5 = ((bf16[4,67,512]{2,1,0:T(8,128)(2,1)}), bf16[4,67,512]{2,1,0:T(8,128)(2,1)S(1)}, u32[]{:S(2)}, u32[]{:S(2)}) async-start(bf16[4,67,512]{2,1,0:T(8,128)(2,1)} %pad_maximum_fusion.2), calls=%async_computation.5 | async-start | bytes 589824 | tf_op jit(solution)/shard_map/all_to_all | solution.py:221
  131.3 6.2 %copy-start.3 = (bf16[32,1024]{1,0:T(8,128)(2,1)S(1)}, bf16[32,1024]{1,0:T(8,128)(2,1)}, u32[]{:S(2)}) copy-start(bf16[32,1024]{1,0:T(8,128)(2,1)} %param.13) | copy-start | bytes 196612

commit v9 on v8

--- a/solution.py
+++ b/solution.py
@@ -44,7 +44,7 @@
 
 def parts_of(value):
     parts = []
-    for _ in range(3):
+    for _ in range(2):
         part = lax.reduce_precision(value, 8, 7)
         parts.append(part.astype(bf16))
         value = value - part
@@ -203,7 +203,7 @@
         spread(by_task.reshape(1, -1), "tensor", n_x, axis_index_groups=along_x), axis=0
     )
 
-    task_zero = zero_after(by_task)
+    task_zero = zero_after(grads_mate)
     rows_x = frozen_kept.astype(f32) + task_zero.astype(f32)
     for other in frozen_came:
         rows_x = rows_x + other.astype(f32)
@@ -212,7 +212,7 @@
             rows_x.astype(bf16).T.reshape(Y_RUN, rows_own, KV),
             jnp.broadcast_to(
                 jnp.concatenate(parts_of(hidden_x), axis=0).reshape(1, -1, KV),
-                (Y_RUN, 3 * hidden_x.size // KV, KV),
+                (Y_RUN, 2 * hidden_x.size // KV, KV),
             ),
         ),
         axis=1,
@@ -221,7 +221,7 @@
         lax.all_to_all(last, "tensor", 0, 0, axis_index_groups=along_y).astype(f32), axis=0
     )
     frozen_rows = last[:rows_own]
-    grad_hidden = jnp.sum(last[rows_own:].reshape((3,) + by_task.shape), axis=0)
+    grad_hidden = jnp.sum(last[rows_own:].reshape((2,) + by_task.shape), axis=0)
 
     last_zero = zero_after(hidden_x).astype(bf16)
 
@@ -231,7 +231,7 @@
 
     def head_grads(grads, pick):
         return lax.dot_general(
-            pick + last_zero,
+            pick + task_zero.astype(bf16),
             grads.reshape(n_chips * SEQS, -1),
             outer_dims,
             preferred_element_type=f32,

time: 140 us -> 137 us (0.979)
  waiting for transfers between devices: 16.8 us -> 14.8 us
    all_to_all x1, waiting for transfers between devices: 1.67 us -> 0.01 us  [shards(): lax.all_to_all(last, 'tensor', 0, 0, axis_index_groups=along_y).astype(f32)]
    broadcast_in_dim x3 -> x4, local copies, waits for them, and re-layouts: 3.1 us -> 3.2 us  [spread(): copies = jnp.broadcast_to(block[None], (count,) + block.shape)]
  transfers between devices with their start and end apart: 15 -> 15, of which waited for: 6 -> 5; matrix products, arithmetic and copies ran while one was open for 21% -> 22% of each run, Pallas kernels for 0% -> 0%
where the time goes in v9:
time: 137 us; the launch traced here: 136 us
  starting transfers between devices  77.7 us (57%)
  local copies, waits for them, and re-layouts  17.5 us (13%)
  waiting for transfers between devices  14.8 us (11%)
  matrix products  11.9 us (9%)
  other arithmetic  7.39 us (5%)
  between operations  6.35 us (5%)
    ppermute x9, starting transfers between devices, swapped(): return lax.ppermute(block, axis, pairs)  26.6 us
    all_to_all x3, starting transfers between devices, spread(): return lax.all_to_all(copies, axes, 0, 0, **kw)  21.6 us
    all_to_all x1, starting transfers between devices, shards(): came = lax.all_to_all(sent, 'dp', 0, 0, axis_index_groups=same_core)  15.7 us
    ppermute x9, waiting for transfers between devices, swapped(): return lax.ppermute(block, axis, pairs)  10.7 us
    all_to_all x1, starting transfers between devices, shards(): low_came = lax.all_to_all(block, 'tensor', 0, 0)  7.28 us
    all_to_all x1, starting transfers between devices, shards(): lax.all_to_all(last, 'tensor', 0, 0, axis_index_groups=along_y).astype(f32)  6.51 us
    dot_general x1, matrix products, shards(): frozen_back = jnp.dot(cot_full, weight_t, preferred_element_type=f32)  3.47 us
    broadcast_in_dim x4, local copies, waits for them, and re-layouts, spread(): copies = jnp.broadcast_to(block[None], (count,) + block.shape)  3.2 us
  transfers between devices with their start and end apart: 15, of which 5 were waited for; matrix products, arithmetic and copies ran while one was open for 22% of the time, Pallas kernels for 0%

profile of v9, /device:TPU:56, one launch (start us, length us, event | category | flops | bytes accessed | tf_op | source)
XLA Modules:
  0.0 135.6 jit_solution(3907401033577824368)
XLA Ops:
  0.6 1.6 %broadcast_in_dim.67 = bf16[4,64,512]{2,1,0:T(8,128)(2,1)} broadcast(bf16[64,512]{1,0:T(8,128)(2,1)} %param.17), dimensions={1,2} | broadcast | bytes 327680 | tf_op jit(solution)/shard_map/broadcast_in_dim | solution.py:31
  2.3 6.3 %all-to-all-start = ((bf16[4,64,512]{2,1,0:T(8,128)(2,1)}), bf16[4,64,512]{2,1,0:T(8,128)(2,1)S(1)}, u32[]{:S(2)}, u32[]{:S(2)}) async-start(bf16[4,64,512]{2,1,0:T(8,128)(2,1)} %broadcast_in_dim.67), calls=%async_computation | async-start | bytes 524288 | tf_op jit(solution)/shard_map/all_to_all | solution.py:32
  12.8 1.9 %collective-permute-start = (bf16[32,4352]{1,0:T(8,128)(2,1)S(1)}, bf16[32,4352]{1,0:T(8,128)(2,1)S(1)}, u32[]{:S(2)}, u32[]{:S(2)}) collective-permute-start(bf16[32,4352]{1,0:T(8,128)(2,1)S(1)} %convolution_convert_fusion), channel_id=1, source_target_pairs={{0,16},{16,0},{32,48},{48,32},{64,80},{80,64},{96,112},{112,96},{1... | collective-permute-start | bytes 835592 | tf_op jit(solution)/shard_map/ppermute | solution.py:37
  16.0 3.4 %collective-permute-start.2 = (bf16[256,512]{1,0:T(8,128)(2,1)S(1)}, bf16[256,512]{1,0:T(8,128)(2,1)S(1)}, u32[]{:S(2)}, u32[]{:S(2)}) collective-permute-start(bf16[256,512]{1,0:T(8,128)(2,1)S(1)} %bitcast.94), channel_id=1, source_target_pairs={{0,4},{1,5},{2,6},{3,7},{4,0},{5,1},{6,2},{7,3},{8,12},{9,13},{10,... | collective-permute-start | bytes 786440 | tf_op jit(solution)/shard_map/ppermute | solution.py:37
  23.2 15.7 %all-to-all-start.1 = ((bf16[16,2,8448]{2,1,0:T(2,128)(2,1)}), bf16[16,2,8448]{2,1,0:T(2,128)(2,1)S(1)}, u32[]{:S(2)}, u32[]{:S(2)}) async-start(bf16[16,2,8448]{2,1,0:T(2,128)(2,1)} %pad_maximum_fusion), calls=%async_computation.1 | async-start | bytes 1081344 | tf_op jit(solution)/shard_map/all_to_all | solution.py:112
  41.4 4.6 %collective-permute-start.3 = (bf16[256,512]{1,0:T(8,128)(2,1)S(1)}, bf16[256,512]{1,0:T(8,128)(2,1)S(1)}, u32[]{:S(2)}, u32[]{:S(2)}) collective-permute-start(bf16[256,512]{1,0:T(8,128)(2,1)S(1)} %bitcast.96), channel_id=1, source_target_pairs={{0,8},{1,9},{2,10},{3,11},{4,12},{5,13},{6,14},{7,15},{8,0},{9,1},... | collective-permute-start | bytes 786440 | tf_op jit(solution)/shard_map/ppermute | solution.py:37
  46.1 2.4 %collective-permute-start.4 = (bf16[256,512]{1,0:T(8,128)(2,1)S(1)}, bf16[256,512]{1,0:T(8,128)(2,1)S(1)}, u32[]{:S(2)}, u32[]{:S(2)}) collective-permute-start(bf16[256,512]{1,0:T(8,128)(2,1)S(1)} %bitcast.97), channel_id=1, source_target_pairs={{0,12},{1,13},{2,14},{3,15},{4,8},{5,9},{6,10},{7,11},{8,4},{9,5},... | collective-permute-start | bytes 786440 | tf_op jit(solution)/shard_map/ppermute | solution.py:37
  48.6 4.2 %collective-permute-done.3 = bf16[256,512]{1,0:T(8,128)(2,1)S(1)} collective-permute-done((bf16[256,512]{1,0:T(8,128)(2,1)S(1)}, bf16[256,512]{1,0:T(8,128)(2,1)S(1)}, u32[]{:S(2)}, u32[]{:S(2)}) %collective-permute-start.3) | collective-permute-done | bytes 262176 | tf_op jit(solution)/shard_map/ppermute | solution.py:37
  52.8 5.5 %collective-permute-done.4 = bf16[256,512]{1,0:T(8,128)(2,1)S(1)} collective-permute-done((bf16[256,512]{1,0:T(8,128)(2,1)S(1)}, bf16[256,512]{1,0:T(8,128)(2,1)S(1)}, u32[]{:S(2)}, u32[]{:S(2)}) %collective-permute-start.4) | collective-permute-done | bytes 262176 | tf_op jit(solution)/shard_map/ppermute | solution.py:37
  61.3 7.3 %all-to-all-start.2 = ((bf16[16,4,512]{2,1,0:T(4,128)(2,1)}), bf16[16,4,512]{2,1,0:T(4,128)(2,1)S(1)}, u32[]{:S(2)}, u32[]{:S(2)}) async-start(bf16[16,4,512]{2,1,0:T(4,128)(2,1)} %pad_maximum_fusion.3), calls=%async_computation.2 | async-start | bytes 131072 | tf_op jit(solution)/shard_map/all_to_all | solution.py:145
  69.5 1.9 %collective-permute-start.1 = (bf16[16,2,4096]{2,1,0:T(2,128)(2,1)}, bf16[16,2,4096]{2,1,0:T(2,128)(2,1)}, u32[]{:S(2)}, u32[]{:S(2)}) collective-permute-start(bf16[16,2,4096]{2,1,0:T(2,128)(2,1)} %slice.70), channel_id=1, source_target_pairs={{0,16},{16,0},{32,48},{48,32},{64,80},{80,64},{96,112},{112,96},{1... | collective-permute-start | bytes 786440 | tf_op jit(solution)/shard_map/ppermute | solution.py:37
  71.4 2.3 %all-to-all-done.2 = bf16[16,4,512]{2,1,0:T(4,128)(2,1)S(1)} async-done(((bf16[16,4,512]{2,1,0:T(4,128)(2,1)}), bf16[16,4,512]{2,1,0:T(4,128)(2,1)S(1)}, u32[]{:S(2)}, u32[]{:S(2)}) %all-to-all-start.2) | async-done | bytes 65568 | tf_op jit(solution)/shard_map/all_to_all | solution.py:145
  76.4 12.0 %all-to-all-start.3 = ((bf16[16,2,4352]{2,1,0:T(2,128)(2,1)}), bf16[16,2,4352]{2,1,0:T(2,128)(2,1)S(1)}, u32[]{:S(2)}, u32[]{:S(2)}) async-start(bf16[16,2,4352]{2,1,0:T(2,128)(2,1)} %broadcast_in_dim.79), calls=%async_computation.3 | async-start | bytes 557056 | tf_op jit(solution)/shard_map/all_to_all | solution.py:32
  88.5 2.1 %broadcast_select_fusion.1 = (bf16[16,2,4096]{2,1,0:T(2,128)(2,1)}, bf16[16,2,4096]{2,1,0:T(2,128)(2,1)S(1)}) fusion(bf16[16,2,4096]{2,1,0:T(2,128)(2,1)} %collective-permute-done.1, pred[]{:T(512)S(6)} %eq.36, bf16[16,2,8448]{2,1,0:T(2,128)(2,1)S(1)} %all-to-all-done.1), kind=kLoop, calls=%fused_computation.26 | loop fusion | flops 262144 | bytes 1048577 | tf_op jit(solution)/shard_map/jit(_where)/select_n | solution.py:162
  93.8 2.5 %collective-permute-start.6 = (bf16[512,256]{1,0:T(8,128)(2,1)}, bf16[512,256]{1,0:T(8,128)(2,1)}, u32[]{:S(2)}, u32[]{:S(2)}) collective-permute-start(bf16[512,256]{1,0:T(8,128)(2,1)} %get-tuple-element.5), channel_id=1, source_target_pairs={{0,4},{1,5},{2,6},{3,7},{4,0},{5,1},{6,2},{7,3},{8,12},{9,13},{10,... | collective-permute-start | bytes 786440 | tf_op jit(solution)/shard_map/ppermute | solution.py:37
  96.3 4.0 %collective-permute-start.7 = (bf16[512,256]{1,0:T(8,128)(2,1)}, bf16[512,256]{1,0:T(8,128)(2,1)}, u32[]{:S(2)}, u32[]{:S(2)}) collective-permute-start(bf16[512,256]{1,0:T(8,128)(2,1)} %get-tuple-element.7), channel_id=1, source_target_pairs={{0,8},{1,9},{2,10},{3,11},{4,12},{5,13},{6,14},{7,15},{8,0},{9,1},... | collective-permute-start | bytes 786440 | tf_op jit(solution)/shard_map/ppermute | solution.py:37
  100.3 4.0 %collective-permute-start.8 = (bf16[512,256]{1,0:T(8,128)(2,1)}, bf16[512,256]{1,0:T(8,128)(2,1)}, u32[]{:S(2)}, u32[]{:S(2)}) collective-permute-start(bf16[512,256]{1,0:T(8,128)(2,1)} %get-tuple-element.6), channel_id=1, source_target_pairs={{0,12},{1,13},{2,14},{3,15},{4,8},{5,9},{6,10},{7,11},{8,4},{9,5},... | collective-permute-start | bytes 786440 | tf_op jit(solution)/shard_map/ppermute | solution.py:37
  104.3 1.9 %collective-permute-start.5 = (bf16[16,2,4352]{2,1,0:T(2,128)(2,1)S(1)}, bf16[16,2,4352]{2,1,0:T(2,128)(2,1)S(1)}, u32[]{:S(2)}, u32[]{:S(2)}) collective-permute-start(bf16[16,2,4352]{2,1,0:T(2,128)(2,1)S(1)} %all-to-all-done.3), channel_id=1, source_target_pairs={{0,16},{16,0},{32,48},{48,32},{64,80},{80,64},{96,112},{112,96},{1... | collective-permute-start | bytes 835592 | tf_op jit(solution)/shard_map/ppermute | solution.py:37
  111.0 3.2 %all-to-all-start.4 = ((f32[4,1,512]{2,1,0:T(1,128)}), f32[4,1,512]{2,1,0:T(1,128)S(1)}, u32[]{:S(2)}, u32[]{:S(2)}) async-start(f32[4,1,512]{2,1,0:T(1,128)} %broadcast_in_dim.81), calls=%async_computation.4 | async-start | bytes 16384 | tf_op jit(solution)/shard_map/all_to_all | solution.py:32
  114.3 1.8 %fusion.8 = f32[1024,512]{1,0:T(8,128)} fusion(bf16[1024,16]{0,1:T(8,128)(2,1)S(1)} %fusion.3, bf16[512,2,8]{0,2,1:T(8,128)(2,1)S(1)} %copy.44, bf16[]{:T(256)S(6)} %convert_element_type.172), kind=kOutput, calls=%fused_computation.38 | convolution fusion | flops 16793600 | bytes 2146306 | tf_op jit(solution)/shard_map/dot_general | solution.py:228
  116.1 1.3 fusion.6
  117.8 1.8 %all-to-all-done.4 = f32[4,1,512]{2,1,0:T(1,128)S(1)} async-done(((f32[4,1,512]{2,1,0:T(1,128)}), f32[4,1,512]{2,1,0:T(1,128)S(1)}, u32[]{:S(2)}, u32[]{:S(2)}) %all-to-all-start.4) | async-done | bytes 8224 | tf_op jit(solution)/shard_map/all_to_all | solution.py:32
  120.4 6.5 %all-to-all-start.5 = ((bf16[4,66,512]{2,1,0:T(8,128)(2,1)}), bf16[4,66,512]{2,1,0:T(8,128)(2,1)S(1)}, u32[]{:S(2)}, u32[]{:S(2)}) async-start(bf16[4,66,512]{2,1,0:T(8,128)(2,1)} %pad_maximum_fusion.2), calls=%async_computation.5 | async-start | bytes 589824 | tf_op jit(solution)/shard_map/all_to_all | solution.py:221
  130.2 3.5 %add_convert_fusion = bf16[1024,512]{1,0:T(8,128)(2,1)} fusion(f32[1024,512]{1,0:T(8,128)} %fusion.8, bf16[1024,512]{1,0:T(8,128)(2,1)S(1)} %bitcast.93, bf16[512,512]{1,0:T(8,128)(2,1)} %bitcast.104, f32[]{:T(128)S(6)} %convert_element_type.171), kind=kOutput, calls=%fused_computation.2 | convolution fusion | flops 538443776 | bytes 4718596 | tf_op jit(solution)/shard_map/dot_general | solution.py:229
  (114 shorter events, 27.5 us)
Async XLA Ops:
  0.6 58.5 %copy-start = (bf16[1024,512]{1,0:T(8,128)(2,1)S(1)}, bf16[1024,512]{1,0:T(8,128)(2,1)}, u32[]{:S(2)}) copy-start(bf16[1024,512]{1,0:T(8,128)(2,1)} %param.9) | copy-start | bytes 3145732
  2.3 13.7 %all-to-all-start = ((bf16[4,64,512]{2,1,0:T(8,128)(2,1)}), bf16[4,64,512]{2,1,0:T(8,128)(2,1)S(1)}, u32[]{:S(2)}, u32[]{:S(2)}) async-start(bf16[4,64,512]{2,1,0:T(8,128)(2,1)} %broadcast_in_dim.67), calls=%async_computation | async-start | bytes 524288 | tf_op jit(solution)/shard_map/all_to_all | solution.py:32
  12.8 8.5 %collective-permute-start = (bf16[32,4352]{1,0:T(8,128)(2,1)S(1)}, bf16[32,4352]{1,0:T(8,128)(2,1)S(1)}, u32[]{:S(2)}, u32[]{:S(2)}) collective-permute-start(bf16[32,4352]{1,0:T(8,128)(2,1)S(1)} %convolution_convert_fusion), channel_id=1, source_target_pairs={{0,16},{16,0},{32,48},{48,32},{64,80},{80,64},{96,112},{112,96},{1... | collective-permute-start | bytes 835592 | tf_op jit(solution)/shard_map/ppermute | solution.py:37
  16.0 32.6 %collective-permute-start.2 = (bf16[256,512]{1,0:T(8,128)(2,1)S(1)}, bf16[256,512]{1,0:T(8,128)(2,1)S(1)}, u32[]{:S(2)}, u32[]{:S(2)}) collective-permute-start(bf16[256,512]{1,0:T(8,128)(2,1)S(1)} %bitcast.94), channel_id=1, source_target_pairs={{0,4},{1,5},{2,6},{3,7},{4,0},{5,1},{6,2},{7,3},{8,12},{9,13},{10,... | collective-permute-start | bytes 786440 | tf_op jit(solution)/shard_map/ppermute | solution.py:37
  19.4 19.5 %copy-start.4 = (s32[1,3]{1,0:T(1,128)S(1)}, s32[1,3]{1,0:T(1,128)}, u32[]{:S(2)}) copy-start(s32[1,3]{1,0:T(1,128)} %param.11) | copy-start | bytes 40
  23.2 35.2 %all-to-all-start.1 = ((bf16[16,2,8448]{2,1,0:T(2,128)(2,1)}), bf16[16,2,8448]{2,1,0:T(2,128)(2,1)S(1)}, u32[]{:S(2)}, u32[]{:S(2)}) async-start(bf16[16,2,8448]{2,1,0:T(2,128)(2,1)} %pad_maximum_fusion), calls=%async_computation.1 | async-start | bytes 1081344 | tf_op jit(solution)/shard_map/all_to_all | solution.py:112
  41.4 11.4 %collective-permute-start.3 = (bf16[256,512]{1,0:T(8,128)(2,1)S(1)}, bf16[256,512]{1,0:T(8,128)(2,1)S(1)}, u32[]{:S(2)}, u32[]{:S(2)}) collective-permute-start(bf16[256,512]{1,0:T(8,128)(2,1)S(1)} %bitcast.96), channel_id=1, source_target_pairs={{0,8},{1,9},{2,10},{3,11},{4,12},{5,13},{6,14},{7,15},{8,0},{9,1},... | collective-permute-start | bytes 786440 | tf_op jit(solution)/shard_map/ppermute | solution.py:37
  46.1 12.2 %collective-permute-start.4 = (bf16[256,512]{1,0:T(8,128)(2,1)S(1)}, bf16[256,512]{1,0:T(8,128)(2,1)S(1)}, u32[]{:S(2)}, u32[]{:S(2)}) collective-permute-start(bf16[256,512]{1,0:T(8,128)(2,1)S(1)} %bitcast.97), channel_id=1, source_target_pairs={{0,12},{1,13},{2,14},{3,15},{4,8},{5,9},{6,10},{7,11},{8,4},{9,5},... | collective-permute-start | bytes 786440 | tf_op jit(solution)/shard_map/ppermute | solution.py:37
  61.3 12.4 %all-to-all-start.2 = ((bf16[16,4,512]{2,1,0:T(4,128)(2,1)}), bf16[16,4,512]{2,1,0:T(4,128)(2,1)S(1)}, u32[]{:S(2)}, u32[]{:S(2)}) async-start(bf16[16,4,512]{2,1,0:T(4,128)(2,1)} %pad_maximum_fusion.3), calls=%async_computation.2 | async-start | bytes 131072 | tf_op jit(solution)/shard_map/all_to_all | solution.py:145
  69.5 19.0 %collective-permute-start.1 = (bf16[16,2,4096]{2,1,0:T(2,128)(2,1)}, bf16[16,2,4096]{2,1,0:T(2,128)(2,1)}, u32[]{:S(2)}, u32[]{:S(2)}) collective-permute-start(bf16[16,2,4096]{2,1,0:T(2,128)(2,1)} %slice.70), channel_id=1, source_target_pairs={{0,16},{16,0},{32,48},{48,32},{64,80},{80,64},{96,112},{112,96},{1... | collective-permute-start | bytes 786440 | tf_op jit(solution)/shard_map/ppermute | solution.py:37
  76.4 27.8 %all-to-all-start.3 = ((bf16[16,2,4352]{2,1,0:T(2,128)(2,1)}), bf16[16,2,4352]{2,1,0:T(2,128)(2,1)S(1)}, u32[]{:S(2)}, u32[]{:S(2)}) async-start(bf16[16,2,4352]{2,1,0:T(2,128)(2,1)} %broadcast_in_dim.79), calls=%async_computation.3 | async-start | bytes 557056 | tf_op jit(solution)/shard_map/all_to_all | solution.py:32
  92.0 1.8 %copy-start.2 = (bf16[16,2,16,512]{3,2,1,0:T(8,128)(2,1)}, bf16[16,2,16,512]{3,2,1,0:T(8,128)(2,1)S(1)}, u32[]{:S(2)}) copy-start(bf16[16,2,16,512]{3,2,1,0:T(8,128)(2,1)S(1)} %pad_maximum_fusion.1) | copy-start | bytes 1572868
  92.8 7.5 %copy-start.1 = (bf16[512,1024]{1,0:T(8,128)(2,1)}, bf16[512,1024]{1,0:T(8,128)(2,1)S(1)}, u32[]{:S(2)}) copy-start(bf16[512,1024]{1,0:T(8,128)(2,1)S(1)} %convolution_convert_fusion.1) | copy-start | bytes 3145732
  93.8 22.3 %collective-permute-start.6 = (bf16[512,256]{1,0:T(8,128)(2,1)}, bf16[512,256]{1,0:T(8,128)(2,1)}, u32[]{:S(2)}, u32[]{:S(2)}) collective-permute-start(bf16[512,256]{1,0:T(8,128)(2,1)} %get-tuple-element.5), channel_id=1, source_target_pairs={{0,4},{1,5},{2,6},{3,7},{4,0},{5,1},{6,2},{7,3},{8,12},{9,13},{10,... | collective-permute-start | bytes 786440 | tf_op jit(solution)/shard_map/ppermute | solution.py:37
  96.3 19.8 %collective-permute-start.7 = (bf16[512,256]{1,0:T(8,128)(2,1)}, bf16[512,256]{1,0:T(8,128)(2,1)}, u32[]{:S(2)}, u32[]{:S(2)}) collective-permute-start(bf16[512,256]{1,0:T(8,128)(2,1)} %get-tuple-element.7), channel_id=1, source_target_pairs={{0,8},{1,9},{2,10},{3,11},{4,12},{5,13},{6,14},{7,15},{8,0},{9,1},... | collective-permute-start | bytes 786440 | tf_op jit(solution)/shard_map/ppermute | solution.py:37
  100.3 15.8 %collective-permute-start.8 = (bf16[512,256]{1,0:T(8,128)(2,1)}, bf16[512,256]{1,0:T(8,128)(2,1)}, u32[]{:S(2)}, u32[]{:S(2)}) collective-permute-start(bf16[512,256]{1,0:T(8,128)(2,1)} %get-tuple-element.6), channel_id=1, source_target_pairs={{0,12},{1,13},{2,14},{3,15},{4,8},{5,9},{6,10},{7,11},{8,4},{9,5},... | collective-permute-start | bytes 786440 | tf_op jit(solution)/shard_map/ppermute | solution.py:37
  104.3 3.5 %collective-permute-start.5 = (bf16[16,2,4352]{2,1,0:T(2,128)(2,1)S(1)}, bf16[16,2,4352]{2,1,0:T(2,128)(2,1)S(1)}, u32[]{:S(2)}, u32[]{:S(2)}) collective-permute-start(bf16[16,2,4352]{2,1,0:T(2,128)(2,1)S(1)} %all-to-all-done.3), channel_id=1, source_target_pairs={{0,16},{16,0},{32,48},{48,32},{64,80},{80,64},{96,112},{112,96},{1... | collective-permute-start | bytes 835592 | tf_op jit(solution)/shard_map/ppermute | solution.py:37
  111.0 8.5 %all-to-all-start.4 = ((f32[4,1,512]{2,1,0:T(1,128)}), f32[4,1,512]{2,1,0:T(1,128)S(1)}, u32[]{:S(2)}, u32[]{:S(2)}) async-start(f32[4,1,512]{2,1,0:T(1,128)} %broadcast_in_dim.81), calls=%async_computation.4 | async-start | bytes 16384 | tf_op jit(solution)/shard_map/all_to_all | solution.py:32
  120.4 13.3 %all-to-all-start.5 = ((bf16[4,66,512]{2,1,0:T(8,128)(2,1)}), bf16[4,66,512]{2,1,0:T(8,128)(2,1)S(1)}, u32[]{:S(2)}, u32[]{:S(2)}) async-start(bf16[4,66,512]{2,1,0:T(8,128)(2,1)} %pad_maximum_fusion.2), calls=%async_computation.5 | async-start | bytes 589824 | tf_op jit(solution)/shard_map/all_to_all | solution.py:221
  130.2 4.5 %copy-start.3 = (bf16[32,1024]{1,0:T(8,128)(2,1)S(1)}, bf16[32,1024]{1,0:T(8,128)(2,1)}, u32[]{:S(2)}) copy-start(bf16[32,1024]{1,0:T(8,128)(2,1)} %param.13) | copy-start | bytes 196612

commit v10 on v9

--- a/solution.py
+++ b/solution.py
@@ -54,10 +54,10 @@
 def gathered(block, part, count, stride):
     every = jnp.zeros((count,) + block.shape, block.dtype)
     every = lax.dynamic_update_index_in_dim(every, block, part, 0)
-    for step in range(1, count):
-        other = swapped(block, "tensor", step * stride)
+    others = [swapped(block, "tensor", step * stride) for step in range(1, count)]
+    for step, other in enumerate(others, 1):
         every = lax.dynamic_update_index_in_dim(every, other, part ^ step, 0)
-    return every.reshape((count * block.shape[0],) + block.shape[1:])
+    return every.reshape((count * block.shape[0],) + block.shape[1:]), others[0]
 
 
 def shards(
@@ -116,9 +116,10 @@
     down_cat = down_pick.reshape(SEQS, width_own, R).transpose(1, 0, 2).reshape(width_own, ADA)
 
     place_x = place // Y_RUN
-    cot_full = gathered(cot_run, place_x, n_x, Y_RUN)
-
-    first, second = seq_lengths[0, 0], seq_lengths[0, 1]
+    cot_full, cot_came = gathered(cot_run, place_x, n_x, Y_RUN)
+
+    lengths = seq_lengths[0] + zero_after(cot_came)
+    first, second = lengths[0], lengths[1]
     places = jnp.arange(rows_total, dtype=jnp.int32)[:, None]
     in_second = (places >= first) & (places < first + second)
     in_first = jnp.broadcast_to(places < first, (rows_total, R))
@@ -153,10 +154,8 @@
         .reshape(KV, ADA)
     )
 
-    weight_mine = came[:, :, term_width:]
+    weight_mine = came[:, :, term_width:].reshape(n_chips, KV // n_dp, width_own)
     weight_mate = swapped(weight_mine, "dp", 1)
-    weight_mine = weight_mine.reshape(n_chips, KV // n_dp, width_own)
-    weight_mate = weight_mate.reshape(n_chips, KV // n_dp, width_own)
     weight_t = jnp.stack(
         (
             jnp.where(core == 0, weight_mine, weight_mate),

time: 137 us -> 135 us (0.985)
  starting transfers between devices: 77.7 us -> 75.3 us
  between operations: 6.35 us -> 7.74 us
    ppermute x9, waiting for transfers between devices: 10.7 us -> 1.04 us  [swapped(): return lax.ppermute(block, axis, pairs)]
    all_to_all x1, waiting for transfers between devices: 0.01 us -> 8.61 us  [shards(): came = lax.all_to_all(sent, 'dp', 0, 0, axis_index_groups=same_core)]
    all_to_all x3, starting transfers between devices: 21.6 us -> 19.2 us  [spread(): return lax.all_to_all(copies, axes, 0, 0, **kw)]
    select_n x1 -> x0, other arithmetic: 2.11 us -> none  [shards(): jnp.where(core == 0, weight_mine, weight_mate)]
    dynamic_update_slice x3, local copies, waits for them, and re-layouts: 0.07 us -> 1.97 us  [gathered(): every = lax.dynamic_update_index_in_dim(every, other, part ^ step, 0)]
  transfers between devices with their start and end apart: 15 -> 15, of which waited for: 5 -> 4; matrix products, arithmetic and copies ran while one was open for 22% -> 22% of each run, Pallas kernels for 0% -> 0%
where the time goes in v10:
time: 135 us; the launch traced here: 134 us
  starting transfers between devices  75.3 us (56%)
  local copies, waits for them, and re-layouts  18.2 us (13%)
  waiting for transfers between devices  14.3 us (11%)
  matrix products  11.9 us (9%)
  between operations  7.74 us (6%)
  other arithmetic  6.29 us (5%)
    ppermute x9, starting transfers between devices, swapped(): return lax.ppermute(block, axis, pairs)  26.6 us
    all_to_all x3, starting transfers between devices, spread(): return lax.all_to_all(copies, axes, 0, 0, **kw)  19.2 us
    all_to_all x1, starting transfers between devices, shards(): came = lax.all_to_all(sent, 'dp', 0, 0, axis_index_groups=same_core)  15.7 us
    all_to_all x1, waiting for transfers between devices, shards(): came = lax.all_to_all(sent, 'dp', 0, 0, axis_index_groups=same_core)  8.61 us
    all_to_all x1, starting transfers between devices, shards(): low_came = lax.all_to_all(block, 'tensor', 0, 0)  7.3 us
    all_to_all x1, starting transfers between devices, shards(): lax.all_to_all(last, 'tensor', 0, 0, axis_index_groups=along_y).astype(f32)  6.5 us
    dot_general x1, matrix products, shards(): frozen_back = jnp.dot(cot_full, weight_t, preferred_element_type=f32)  3.47 us
    broadcast_in_dim x4, local copies, waits for them, and re-layouts, spread(): copies = jnp.broadcast_to(block[None], (count,) + block.shape)  3.2 us
  transfers between devices with their start and end apart: 15, of which 4 were waited for; matrix products, arithmetic and copies ran while one was open for 22% of the time, Pallas kernels for 0%

profile of v10, /device:TPU:56, one launch (start us, length us, event | category | flops | bytes accessed | tf_op | source)
XLA Modules:
  0.0 133.7 jit_solution(1378322621654840935)
XLA Ops:
  0.6 1.6 %broadcast_in_dim.67 = bf16[4,64,512]{2,1,0:T(8,128)(2,1)} broadcast(bf16[64,512]{1,0:T(8,128)(2,1)} %param.17), dimensions={1,2} | broadcast | bytes 327680 | tf_op jit(solution)/shard_map/broadcast_in_dim | solution.py:31
  2.3 6.3 %all-to-all-start = ((bf16[4,64,512]{2,1,0:T(8,128)(2,1)}), bf16[4,64,512]{2,1,0:T(8,128)(2,1)S(1)}, u32[]{:S(2)}, u32[]{:S(2)}) async-start(bf16[4,64,512]{2,1,0:T(8,128)(2,1)} %broadcast_in_dim.67), calls=%async_computation | async-start | bytes 524288 | tf_op jit(solution)/shard_map/all_to_all | solution.py:32
  12.8 1.9 %collective-permute-start = (bf16[32,4352]{1,0:T(8,128)(2,1)S(1)}, bf16[32,4352]{1,0:T(8,128)(2,1)S(1)}, u32[]{:S(2)}, u32[]{:S(2)}) collective-permute-start(bf16[32,4352]{1,0:T(8,128)(2,1)S(1)} %convolution_convert_fusion), channel_id=1, source_target_pairs={{0,16},{16,0},{32,48},{48,32},{64,80},{80,64},{96,112},{112,96},{1... | collective-permute-start | bytes 835592 | tf_op jit(solution)/shard_map/ppermute | solution.py:37
  16.0 3.4 %collective-permute-start.2 = (bf16[256,512]{1,0:T(8,128)(2,1)S(1)}, bf16[256,512]{1,0:T(8,128)(2,1)S(1)}, u32[]{:S(2)}, u32[]{:S(2)}) collective-permute-start(bf16[256,512]{1,0:T(8,128)(2,1)S(1)} %bitcast.104), channel_id=1, source_target_pairs={{0,4},{1,5},{2,6},{3,7},{4,0},{5,1},{6,2},{7,3},{8,12},{9,13},{10,... | collective-permute-start | bytes 786440 | tf_op jit(solution)/shard_map/ppermute | solution.py:37
  19.4 4.6 %collective-permute-start.3 = (bf16[256,512]{1,0:T(8,128)(2,1)S(1)}, bf16[256,512]{1,0:T(8,128)(2,1)}, u32[]{:S(2)}, u32[]{:S(2)}) collective-permute-start(bf16[256,512]{1,0:T(8,128)(2,1)S(1)} %bitcast.105), channel_id=1, source_target_pairs={{0,8},{1,9},{2,10},{3,11},{4,12},{5,13},{6,14},{7,15},{8,0},{9,1},... | collective-permute-start | bytes 786440 | tf_op jit(solution)/shard_map/ppermute | solution.py:37
  24.1 2.4 %collective-permute-start.4 = (bf16[256,512]{1,0:T(8,128)(2,1)S(1)}, bf16[256,512]{1,0:T(8,128)(2,1)}, u32[]{:S(2)}, u32[]{:S(2)}) collective-permute-start(bf16[256,512]{1,0:T(8,128)(2,1)S(1)} %bitcast.106), channel_id=1, source_target_pairs={{0,12},{1,13},{2,14},{3,15},{4,8},{5,9},{6,10},{7,11},{8,4},{9,5},... | collective-permute-start | bytes 786440 | tf_op jit(solution)/shard_map/ppermute | solution.py:37
  29.0 1.3 pad_maximum_fusion
  30.3 15.7 %all-to-all-start.1 = ((bf16[16,2,8448]{2,1,0:T(2,128)(2,1)}), bf16[16,2,8448]{2,1,0:T(2,128)(2,1)S(1)}, u32[]{:S(2)}, u32[]{:S(2)}) async-start(bf16[16,2,8448]{2,1,0:T(2,128)(2,1)} %pad_maximum_fusion), calls=%async_computation.1 | async-start | bytes 1081344 | tf_op jit(solution)/shard_map/all_to_all | solution.py:112
  52.6 8.6 %all-to-all-done.1 = bf16[16,2,8448]{2,1,0:T(2,128)(2,1)S(1)} async-done(((bf16[16,2,8448]{2,1,0:T(2,128)(2,1)}), bf16[16,2,8448]{2,1,0:T(2,128)(2,1)S(1)}, u32[]{:S(2)}, u32[]{:S(2)}) %all-to-all-start.1) | async-done | bytes 540704 | tf_op jit(solution)/shard_map/all_to_all | solution.py:112
  64.2 7.3 %all-to-all-start.2 = ((bf16[16,4,512]{2,1,0:T(4,128)(2,1)}), bf16[16,4,512]{2,1,0:T(4,128)(2,1)S(1)}, u32[]{:S(2)}, u32[]{:S(2)}) async-start(bf16[16,4,512]{2,1,0:T(4,128)(2,1)} %pad_maximum_fusion.3), calls=%async_computation.2 | async-start | bytes 131072 | tf_op jit(solution)/shard_map/all_to_all | solution.py:146
  71.9 1.9 %collective-permute-start.1 = (bf16[16,16,512]{2,1,0:T(8,128)(2,1)S(1)}, bf16[16,16,512]{2,1,0:T(8,128)(2,1)}, u32[]{:S(2)}, u32[]{:S(2)}) collective-permute-start(bf16[16,16,512]{2,1,0:T(8,128)(2,1)S(1)} %reshape.179), channel_id=1, source_target_pairs={{0,16},{16,0},{32,48},{48,32},{64,80},{80,64},{96,112},{112,96},{1... | collective-permute-start | bytes 786440 | tf_op jit(solution)/shard_map/ppermute | solution.py:37
  73.8 2.8 %all-to-all-done.2 = bf16[16,4,512]{2,1,0:T(4,128)(2,1)S(1)} async-done(((bf16[16,4,512]{2,1,0:T(4,128)(2,1)}), bf16[16,4,512]{2,1,0:T(4,128)(2,1)S(1)}, u32[]{:S(2)}, u32[]{:S(2)}) %all-to-all-start.2) | async-done | bytes 65568 | tf_op jit(solution)/shard_map/all_to_all | solution.py:146
  79.3 9.7 %all-to-all-start.3 = ((bf16[16,2,4352]{2,1,0:T(2,128)(2,1)}), bf16[16,2,4352]{2,1,0:T(2,128)(2,1)S(1)}, u32[]{:S(2)}, u32[]{:S(2)}) async-start(bf16[16,2,4352]{2,1,0:T(2,128)(2,1)} %broadcast_in_dim.79), calls=%async_computation.3 | async-start | bytes 557056 | tf_op jit(solution)/shard_map/all_to_all | solution.py:32
  90.9 1.0 constant_dynamic-slice_fusion.2
  91.9 2.5 %collective-permute-start.6 = (bf16[512,256]{1,0:T(8,128)(2,1)}, bf16[512,256]{1,0:T(8,128)(2,1)}, u32[]{:S(2)}, u32[]{:S(2)}) collective-permute-start(bf16[512,256]{1,0:T(8,128)(2,1)} %get-tuple-element.5), channel_id=1, source_target_pairs={{0,4},{1,5},{2,6},{3,7},{4,0},{5,1},{6,2},{7,3},{8,12},{9,13},{10,... | collective-permute-start | bytes 786440 | tf_op jit(solution)/shard_map/ppermute | solution.py:37
  94.4 4.0 %collective-permute-start.7 = (bf16[512,256]{1,0:T(8,128)(2,1)}, bf16[512,256]{1,0:T(8,128)(2,1)}, u32[]{:S(2)}, u32[]{:S(2)}) collective-permute-start(bf16[512,256]{1,0:T(8,128)(2,1)} %get-tuple-element.7), channel_id=1, source_target_pairs={{0,8},{1,9},{2,10},{3,11},{4,12},{5,13},{6,14},{7,15},{8,0},{9,1},... | collective-permute-start | bytes 786440 | tf_op jit(solution)/shard_map/ppermute | solution.py:37
  98.4 4.0 %collective-permute-start.8 = (bf16[512,256]{1,0:T(8,128)(2,1)}, bf16[512,256]{1,0:T(8,128)(2,1)}, u32[]{:S(2)}, u32[]{:S(2)}) collective-permute-start(bf16[512,256]{1,0:T(8,128)(2,1)} %get-tuple-element.6), channel_id=1, source_target_pairs={{0,12},{1,13},{2,14},{3,15},{4,8},{5,9},{6,10},{7,11},{8,4},{9,5},... | collective-permute-start | bytes 786440 | tf_op jit(solution)/shard_map/ppermute | solution.py:37
  102.4 1.9 %collective-permute-start.5 = (bf16[16,2,4352]{2,1,0:T(2,128)(2,1)S(1)}, bf16[16,2,4352]{2,1,0:T(2,128)(2,1)S(1)}, u32[]{:S(2)}, u32[]{:S(2)}) collective-permute-start(bf16[16,2,4352]{2,1,0:T(2,128)(2,1)S(1)} %all-to-all-done.3), channel_id=1, source_target_pairs={{0,16},{16,0},{32,48},{48,32},{64,80},{80,64},{96,112},{112,96},{1... | collective-permute-start | bytes 835592 | tf_op jit(solution)/shard_map/ppermute | solution.py:37
  109.1 3.2 %all-to-all-start.4 = ((f32[4,1,512]{2,1,0:T(1,128)}), f32[4,1,512]{2,1,0:T(1,128)S(1)}, u32[]{:S(2)}, u32[]{:S(2)}) async-start(f32[4,1,512]{2,1,0:T(1,128)} %broadcast_in_dim.81), calls=%async_computation.4 | async-start | bytes 16384 | tf_op jit(solution)/shard_map/all_to_all | solution.py:32
  112.4 1.8 %fusion.8 = f32[1024,512]{1,0:T(8,128)} fusion(bf16[1024,16]{0,1:T(8,128)(2,1)S(1)} %fusion.3, bf16[512,2,8]{0,2,1:T(8,128)(2,1)S(1)} %copy.47, bf16[]{:T(256)S(6)} %convert_element_type.184), kind=kOutput, calls=%fused_computation.38 | convolution fusion | flops 16793600 | bytes 2146306 | tf_op jit(solution)/shard_map/dot_general | solution.py:227
  114.2 1.3 %fusion.6 = bf16[256,512]{0,1:T(8,128)(2,1)S(1)} fusion(bf16[512,256]{1,0:T(8,128)(2,1)} %collective-permute-done.8, bf16[512,256]{1,0:T(8,128)(2,1)} %collective-permute-done.7, bf16[512,256]{1,0:T(8,128)(2,1)} %collective-permute-done.6, f32[]{:T(128)S(6)} %convert_element_type.172, bf16[512,1024]{1,0:T(8,128)(2,1)} %copy-done.1, s32[]{:T(128)S(6)} %select_n.62), kind=kLoop, calls=%fused_computation.26 | loop fusion | flops 1179648 | bytes 1310728 | tf_op jit(solution)/shard_map/transpose | solution.py:211
  115.9 1.8 %all-to-all-done.4 = f32[4,1,512]{2,1,0:T(1,128)S(1)} async-done(((f32[4,1,512]{2,1,0:T(1,128)}), f32[4,1,512]{2,1,0:T(1,128)S(1)}, u32[]{:S(2)}, u32[]{:S(2)}) %all-to-all-start.4) | async-done | bytes 8224 | tf_op jit(solution)/shard_map/all_to_all | solution.py:32
  118.5 6.5 %all-to-all-start.5 = ((bf16[4,66,512]{2,1,0:T(8,128)(2,1)}), bf16[4,66,512]{2,1,0:T(8,128)(2,1)S(1)}, u32[]{:S(2)}, u32[]{:S(2)}) async-start(bf16[4,66,512]{2,1,0:T(8,128)(2,1)} %pad_maximum_fusion.2), calls=%async_computation.5 | async-start | bytes 589824 | tf_op jit(solution)/shard_map/all_to_all | solution.py:220
  128.4 3.5 %add_convert_fusion = bf16[1024,512]{1,0:T(8,128)(2,1)} fusion(f32[1024,512]{1,0:T(8,128)} %fusion.8, bf16[1024,512]{1,0:T(8,128)(2,1)S(1)} %bitcast.103, bf16[512,512]{1,0:T(8,128)(2,1)} %bitcast.115, f32[]{:T(128)S(6)} %convert_element_type.183), kind=kOutput, calls=%fused_computation.2 | convolution fusion | flops 538443776 | bytes 4718596 | tf_op jit(solution)/shard_map/dot_general | solution.py:228
  (116 shorter events, 26.9 us)
Async XLA Ops:
  0.6 61.4 %copy-start = (bf16[1024,512]{1,0:T(8,128)(2,1)S(1)}, bf16[1024,512]{1,0:T(8,128)(2,1)}, u32[]{:S(2)}) copy-start(bf16[1024,512]{1,0:T(8,128)(2,1)} %param.9) | copy-start | bytes 3145732
  2.3 13.7 %all-to-all-start = ((bf16[4,64,512]{2,1,0:T(8,128)(2,1)}), bf16[4,64,512]{2,1,0:T(8,128)(2,1)S(1)}, u32[]{:S(2)}, u32[]{:S(2)}) async-start(bf16[4,64,512]{2,1,0:T(8,128)(2,1)} %broadcast_in_dim.67), calls=%async_computation | async-start | bytes 524288 | tf_op jit(solution)/shard_map/all_to_all | solution.py:32
  12.8 15.6 %collective-permute-start = (bf16[32,4352]{1,0:T(8,128)(2,1)S(1)}, bf16[32,4352]{1,0:T(8,128)(2,1)S(1)}, u32[]{:S(2)}, u32[]{:S(2)}) collective-permute-start(bf16[32,4352]{1,0:T(8,128)(2,1)S(1)} %convolution_convert_fusion), channel_id=1, source_target_pairs={{0,16},{16,0},{32,48},{48,32},{64,80},{80,64},{96,112},{112,96},{1... | collective-permute-start | bytes 835592 | tf_op jit(solution)/shard_map/ppermute | solution.py:37
  16.0 30.1 %collective-permute-start.2 = (bf16[256,512]{1,0:T(8,128)(2,1)S(1)}, bf16[256,512]{1,0:T(8,128)(2,1)S(1)}, u32[]{:S(2)}, u32[]{:S(2)}) collective-permute-start(bf16[256,512]{1,0:T(8,128)(2,1)S(1)} %bitcast.104), channel_id=1, source_target_pairs={{0,4},{1,5},{2,6},{3,7},{4,0},{5,1},{6,2},{7,3},{8,12},{9,13},{10,... | collective-permute-start | bytes 786440 | tf_op jit(solution)/shard_map/ppermute | solution.py:37
  19.4 31.2 %collective-permute-start.3 = (bf16[256,512]{1,0:T(8,128)(2,1)S(1)}, bf16[256,512]{1,0:T(8,128)(2,1)}, u32[]{:S(2)}, u32[]{:S(2)}) collective-permute-start(bf16[256,512]{1,0:T(8,128)(2,1)S(1)} %bitcast.105), channel_id=1, source_target_pairs={{0,8},{1,9},{2,10},{3,11},{4,12},{5,13},{6,14},{7,15},{8,0},{9,1},... | collective-permute-start | bytes 786440 | tf_op jit(solution)/shard_map/ppermute | solution.py:37
  24.1 27.6 %collective-permute-start.4 = (bf16[256,512]{1,0:T(8,128)(2,1)S(1)}, bf16[256,512]{1,0:T(8,128)(2,1)}, u32[]{:S(2)}, u32[]{:S(2)}) collective-permute-start(bf16[256,512]{1,0:T(8,128)(2,1)S(1)} %bitcast.106), channel_id=1, source_target_pairs={{0,12},{1,13},{2,14},{3,15},{4,8},{5,9},{6,10},{7,11},{8,4},{9,5},... | collective-permute-start | bytes 786440 | tf_op jit(solution)/shard_map/ppermute | solution.py:37
  29.0 19.1 %copy-start.4 = (s32[1,3]{1,0:T(1,128)S(1)}, s32[1,3]{1,0:T(1,128)}, u32[]{:S(2)}) copy-start(s32[1,3]{1,0:T(1,128)} %param.11) | copy-start | bytes 40
  30.3 30.9 %all-to-all-start.1 = ((bf16[16,2,8448]{2,1,0:T(2,128)(2,1)}), bf16[16,2,8448]{2,1,0:T(2,128)(2,1)S(1)}, u32[]{:S(2)}, u32[]{:S(2)}) async-start(bf16[16,2,8448]{2,1,0:T(2,128)(2,1)} %pad_maximum_fusion), calls=%async_computation.1 | async-start | bytes 1081344 | tf_op jit(solution)/shard_map/all_to_all | solution.py:112
  64.2 12.5 %all-to-all-start.2 = ((bf16[16,4,512]{2,1,0:T(4,128)(2,1)}), bf16[16,4,512]{2,1,0:T(4,128)(2,1)S(1)}, u32[]{:S(2)}, u32[]{:S(2)}) async-start(bf16[16,4,512]{2,1,0:T(4,128)(2,1)} %pad_maximum_fusion.3), calls=%async_computation.2 | async-start | bytes 131072 | tf_op jit(solution)/shard_map/all_to_all | solution.py:146
  71.9 17.2 %collective-permute-start.1 = (bf16[16,16,512]{2,1,0:T(8,128)(2,1)S(1)}, bf16[16,16,512]{2,1,0:T(8,128)(2,1)}, u32[]{:S(2)}, u32[]{:S(2)}) collective-permute-start(bf16[16,16,512]{2,1,0:T(8,128)(2,1)S(1)} %reshape.179), channel_id=1, source_target_pairs={{0,16},{16,0},{32,48},{48,32},{64,80},{80,64},{96,112},{112,96},{1... | collective-permute-start | bytes 786440 | tf_op jit(solution)/shard_map/ppermute | solution.py:37
  79.3 23.1 %all-to-all-start.3 = ((bf16[16,2,4352]{2,1,0:T(2,128)(2,1)}), bf16[16,2,4352]{2,1,0:T(2,128)(2,1)S(1)}, u32[]{:S(2)}, u32[]{:S(2)}) async-start(bf16[16,2,4352]{2,1,0:T(2,128)(2,1)} %broadcast_in_dim.79), calls=%async_computation.3 | async-start | bytes 557056 | tf_op jit(solution)/shard_map/all_to_all | solution.py:32
  90.1 1.8 %copy-start.2 = (bf16[16,2,16,512]{3,2,1,0:T(8,128)(2,1)}, bf16[16,2,16,512]{3,2,1,0:T(8,128)(2,1)S(1)}, u32[]{:S(2)}) copy-start(bf16[16,2,16,512]{3,2,1,0:T(8,128)(2,1)S(1)} %pad_maximum_fusion.1) | copy-start | bytes 1572868
  90.9 7.5 %copy-start.1 = (bf16[512,1024]{1,0:T(8,128)(2,1)}, bf16[512,1024]{1,0:T(8,128)(2,1)S(1)}, u32[]{:S(2)}) copy-start(bf16[512,1024]{1,0:T(8,128)(2,1)S(1)} %convolution_convert_fusion.1) | copy-start | bytes 3145732
  91.9 22.3 %collective-permute-start.6 = (bf16[512,256]{1,0:T(8,128)(2,1)}, bf16[512,256]{1,0:T(8,128)(2,1)}, u32[]{:S(2)}, u32[]{:S(2)}) collective-permute-start(bf16[512,256]{1,0:T(8,128)(2,1)} %get-tuple-element.5), channel_id=1, source_target_pairs={{0,4},{1,5},{2,6},{3,7},{4,0},{5,1},{6,2},{7,3},{8,12},{9,13},{10,... | collective-permute-start | bytes 786440 | tf_op jit(solution)/shard_map/ppermute | solution.py:37
  94.4 19.8 %collective-permute-start.7 = (bf16[512,256]{1,0:T(8,128)(2,1)}, bf16[512,256]{1,0:T(8,128)(2,1)}, u32[]{:S(2)}, u32[]{:S(2)}) collective-permute-start(bf16[512,256]{1,0:T(8,128)(2,1)} %get-tuple-element.7), channel_id=1, source_target_pairs={{0,8},{1,9},{2,10},{3,11},{4,12},{5,13},{6,14},{7,15},{8,0},{9,1},... | collective-permute-start | bytes 786440 | tf_op jit(solution)/shard_map/ppermute | solution.py:37
  98.4 15.8 %collective-permute-start.8 = (bf16[512,256]{1,0:T(8,128)(2,1)}, bf16[512,256]{1,0:T(8,128)(2,1)}, u32[]{:S(2)}, u32[]{:S(2)}) collective-permute-start(bf16[512,256]{1,0:T(8,128)(2,1)} %get-tuple-element.6), channel_id=1, source_target_pairs={{0,12},{1,13},{2,14},{3,15},{4,8},{5,9},{6,10},{7,11},{8,4},{9,5},... | collective-permute-start | bytes 786440 | tf_op jit(solution)/shard_map/ppermute | solution.py:37
  102.4 3.5 %collective-permute-start.5 = (bf16[16,2,4352]{2,1,0:T(2,128)(2,1)S(1)}, bf16[16,2,4352]{2,1,0:T(2,128)(2,1)S(1)}, u32[]{:S(2)}, u32[]{:S(2)}) collective-permute-start(bf16[16,2,4352]{2,1,0:T(2,128)(2,1)S(1)} %all-to-all-done.3), channel_id=1, source_target_pairs={{0,16},{16,0},{32,48},{48,32},{64,80},{80,64},{96,112},{112,96},{1... | collective-permute-start | bytes 835592 | tf_op jit(solution)/shard_map/ppermute | solution.py:37
  109.1 8.5 %all-to-all-start.4 = ((f32[4,1,512]{2,1,0:T(1,128)}), f32[4,1,512]{2,1,0:T(1,128)S(1)}, u32[]{:S(2)}, u32[]{:S(2)}) async-start(f32[4,1,512]{2,1,0:T(1,128)} %broadcast_in_dim.81), calls=%async_computation.4 | async-start | bytes 16384 | tf_op jit(solution)/shard_map/all_to_all | solution.py:32
  118.5 13.3 %all-to-all-start.5 = ((bf16[4,66,512]{2,1,0:T(8,128)(2,1)}), bf16[4,66,512]{2,1,0:T(8,128)(2,1)S(1)}, u32[]{:S(2)}, u32[]{:S(2)}) async-start(bf16[4,66,512]{2,1,0:T(8,128)(2,1)} %pad_maximum_fusion.2), calls=%async_computation.5 | async-start | bytes 589824 | tf_op jit(solution)/shard_map/all_to_all | solution.py:220
  128.3 4.5 %copy-start.3 = (bf16[32,1024]{1,0:T(8,128)(2,1)S(1)}, bf16[32,1024]{1,0:T(8,128)(2,1)}, u32[]{:S(2)}) copy-start(bf16[32,1024]{1,0:T(8,128)(2,1)} %param.13) | copy-start | bytes 196612

commit v11 on v9

--- a/solution.py
+++ b/solution.py
@@ -153,10 +153,8 @@
         .reshape(KV, ADA)
     )
 
-    weight_mine = came[:, :, term_width:]
+    weight_mine = came[:, :, term_width:].reshape(n_chips, KV // n_dp, width_own)
     weight_mate = swapped(weight_mine, "dp", 1)
-    weight_mine = weight_mine.reshape(n_chips, KV // n_dp, width_own)
-    weight_mate = weight_mate.reshape(n_chips, KV // n_dp, width_own)
     weight_t = jnp.stack(
         (
             jnp.where(core == 0, weight_mine, weight_mate),

time: 137 us -> 134 us (0.978)
  local copies, waits for them, and re-layouts: 17.5 us -> 15.7 us
    select_n x1 -> x0, other arithmetic: 2.11 us -> none  [shards(): jnp.where(core == 0, weight_mine, weight_mate)]
  transfers between devices with their start and end apart: 15 -> 15, of which waited for: 5 -> 5; matrix products, arithmetic and copies ran while one was open for 22% -> 20% of each run, Pallas kernels for 0% -> 0%
where the time goes in v11:
time: 134 us; the launch traced here: 133 us
  starting transfers between devices  77.7 us (58%)
  local copies, waits for them, and re-layouts  15.7 us (12%)
  waiting for transfers between devices  15.3 us (11%)
  matrix products  11.9 us (9%)
  between operations  6.34 us (5%)
  other arithmetic  6.29 us (5%)
    ppermute x9, starting transfers between devices, swapped(): return lax.ppermute(block, axis, pairs)  26.6 us
    all_to_all x3, starting transfers between devices, spread(): return lax.all_to_all(copies, axes, 0, 0, **kw)  21.6 us
    all_to_all x1, starting transfers between devices, shards(): came = lax.all_to_all(sent, 'dp', 0, 0, axis_index_groups=same_core)  15.7 us
    ppermute x9, waiting for transfers between devices, swapped(): return lax.ppermute(block, axis, pairs)  10.7 us
    all_to_all x1, starting transfers between devices, shards(): low_came = lax.all_to_all(block, 'tensor', 0, 0)  7.28 us
    all_to_all x1, starting transfers between devices, shards(): lax.all_to_all(last, 'tensor', 0, 0, axis_index_groups=along_y).astype(f32)  6.51 us
    dot_general x1, matrix products, shards(): frozen_back = jnp.dot(cot_full, weight_t, preferred_element_type=f32)  3.47 us
    broadcast_in_dim x4, local copies, waits for them, and re-layouts, spread(): copies = jnp.broadcast_to(block[None], (count,) + block.shape)  3.2 us
  transfers between devices with their start and end apart: 15, of which 5 were waited for; matrix products, arithmetic and copies ran while one was open for 20% of the time, Pallas kernels for 0%

profile of v11, /device:TPU:56, one launch (start us, length us, event | category | flops | bytes accessed | tf_op | source)
XLA Modules:
  0.0 133.2 jit_solution(2623436995644593895)
XLA Ops:
  0.6 1.6 %broadcast_in_dim.67 = bf16[4,64,512]{2,1,0:T(8,128)(2,1)} broadcast(bf16[64,512]{1,0:T(8,128)(2,1)} %param.17), dimensions={1,2} | broadcast | bytes 327680 | tf_op jit(solution)/shard_map/broadcast_in_dim | solution.py:31
  2.3 6.3 %all-to-all-start = ((bf16[4,64,512]{2,1,0:T(8,128)(2,1)}), bf16[4,64,512]{2,1,0:T(8,128)(2,1)S(1)}, u32[]{:S(2)}, u32[]{:S(2)}) async-start(bf16[4,64,512]{2,1,0:T(8,128)(2,1)} %broadcast_in_dim.67), calls=%async_computation | async-start | bytes 524288 | tf_op jit(solution)/shard_map/all_to_all | solution.py:32
  12.8 1.9 %collective-permute-start = (bf16[32,4352]{1,0:T(8,128)(2,1)S(1)}, bf16[32,4352]{1,0:T(8,128)(2,1)S(1)}, u32[]{:S(2)}, u32[]{:S(2)}) collective-permute-start(bf16[32,4352]{1,0:T(8,128)(2,1)S(1)} %convolution_convert_fusion), channel_id=1, source_target_pairs={{0,16},{16,0},{32,48},{48,32},{64,80},{80,64},{96,112},{112,96},{1... | collective-permute-start | bytes 835592 | tf_op jit(solution)/shard_map/ppermute | solution.py:37
  16.0 3.4 %collective-permute-start.2 = (bf16[256,512]{1,0:T(8,128)(2,1)S(1)}, bf16[256,512]{1,0:T(8,128)(2,1)S(1)}, u32[]{:S(2)}, u32[]{:S(2)}) collective-permute-start(bf16[256,512]{1,0:T(8,128)(2,1)S(1)} %bitcast.100), channel_id=1, source_target_pairs={{0,4},{1,5},{2,6},{3,7},{4,0},{5,1},{6,2},{7,3},{8,12},{9,13},{10,... | collective-permute-start | bytes 786440 | tf_op jit(solution)/shard_map/ppermute | solution.py:37
  21.9 1.3 pad_maximum_fusion
  23.2 15.7 %all-to-all-start.1 = ((bf16[16,2,8448]{2,1,0:T(2,128)(2,1)}), bf16[16,2,8448]{2,1,0:T(2,128)(2,1)S(1)}, u32[]{:S(2)}, u32[]{:S(2)}) async-start(bf16[16,2,8448]{2,1,0:T(2,128)(2,1)} %pad_maximum_fusion), calls=%async_computation.1 | async-start | bytes 1081344 | tf_op jit(solution)/shard_map/all_to_all | solution.py:112
  41.4 4.6 %collective-permute-start.3 = (bf16[256,512]{1,0:T(8,128)(2,1)S(1)}, bf16[256,512]{1,0:T(8,128)(2,1)S(1)}, u32[]{:S(2)}, u32[]{:S(2)}) collective-permute-start(bf16[256,512]{1,0:T(8,128)(2,1)S(1)} %bitcast.102), channel_id=1, source_target_pairs={{0,8},{1,9},{2,10},{3,11},{4,12},{5,13},{6,14},{7,15},{8,0},{9,1},... | collective-permute-start | bytes 786440 | tf_op jit(solution)/shard_map/ppermute | solution.py:37
  46.1 2.4 %collective-permute-start.4 = (bf16[256,512]{1,0:T(8,128)(2,1)S(1)}, bf16[256,512]{1,0:T(8,128)(2,1)S(1)}, u32[]{:S(2)}, u32[]{:S(2)}) collective-permute-start(bf16[256,512]{1,0:T(8,128)(2,1)S(1)} %bitcast.103), channel_id=1, source_target_pairs={{0,12},{1,13},{2,14},{3,15},{4,8},{5,9},{6,10},{7,11},{8,4},{9,5},... | collective-permute-start | bytes 786440 | tf_op jit(solution)/shard_map/ppermute | solution.py:37
  48.6 4.2 %collective-permute-done.3 = bf16[256,512]{1,0:T(8,128)(2,1)S(1)} collective-permute-done((bf16[256,512]{1,0:T(8,128)(2,1)S(1)}, bf16[256,512]{1,0:T(8,128)(2,1)S(1)}, u32[]{:S(2)}, u32[]{:S(2)}) %collective-permute-start.3) | collective-permute-done | bytes 262176 | tf_op jit(solution)/shard_map/ppermute | solution.py:37
  52.8 5.5 %collective-permute-done.4 = bf16[256,512]{1,0:T(8,128)(2,1)S(1)} collective-permute-done((bf16[256,512]{1,0:T(8,128)(2,1)S(1)}, bf16[256,512]{1,0:T(8,128)(2,1)S(1)}, u32[]{:S(2)}, u32[]{:S(2)}) %collective-permute-start.4) | collective-permute-done | bytes 262176 | tf_op jit(solution)/shard_map/ppermute | solution.py:37
  61.3 7.3 %all-to-all-start.2 = ((bf16[16,4,512]{2,1,0:T(4,128)(2,1)}), bf16[16,4,512]{2,1,0:T(4,128)(2,1)S(1)}, u32[]{:S(2)}, u32[]{:S(2)}) async-start(bf16[16,4,512]{2,1,0:T(4,128)(2,1)} %pad_maximum_fusion.3), calls=%async_computation.2 | async-start | bytes 131072 | tf_op jit(solution)/shard_map/all_to_all | solution.py:145
  69.0 1.9 %collective-permute-start.1 = (bf16[16,16,512]{2,1,0:T(8,128)(2,1)S(1)}, bf16[16,16,512]{2,1,0:T(8,128)(2,1)}, u32[]{:S(2)}, u32[]{:S(2)}) collective-permute-start(bf16[16,16,512]{2,1,0:T(8,128)(2,1)S(1)} %reshape.168), channel_id=1, source_target_pairs={{0,16},{16,0},{32,48},{48,32},{64,80},{80,64},{96,112},{112,96},{1... | collective-permute-start | bytes 786440 | tf_op jit(solution)/shard_map/ppermute | solution.py:37
  70.9 2.8 %all-to-all-done.2 = bf16[16,4,512]{2,1,0:T(4,128)(2,1)S(1)} async-done(((bf16[16,4,512]{2,1,0:T(4,128)(2,1)}), bf16[16,4,512]{2,1,0:T(4,128)(2,1)S(1)}, u32[]{:S(2)}, u32[]{:S(2)}) %all-to-all-start.2) | async-done | bytes 65568 | tf_op jit(solution)/shard_map/all_to_all | solution.py:145
  76.4 12.0 %all-to-all-start.3 = ((bf16[16,2,4352]{2,1,0:T(2,128)(2,1)}), bf16[16,2,4352]{2,1,0:T(2,128)(2,1)S(1)}, u32[]{:S(2)}, u32[]{:S(2)}) async-start(bf16[16,2,4352]{2,1,0:T(2,128)(2,1)} %broadcast_in_dim.79), calls=%async_computation.3 | async-start | bytes 557056 | tf_op jit(solution)/shard_map/all_to_all | solution.py:32
  91.4 2.5 %collective-permute-start.6 = (bf16[512,256]{1,0:T(8,128)(2,1)}, bf16[512,256]{1,0:T(8,128)(2,1)}, u32[]{:S(2)}, u32[]{:S(2)}) collective-permute-start(bf16[512,256]{1,0:T(8,128)(2,1)} %get-tuple-element.5), channel_id=1, source_target_pairs={{0,4},{1,5},{2,6},{3,7},{4,0},{5,1},{6,2},{7,3},{8,12},{9,13},{10,... | collective-permute-start | bytes 786440 | tf_op jit(solution)/shard_map/ppermute | solution.py:37
  93.9 4.0 %collective-permute-start.7 = (bf16[512,256]{1,0:T(8,128)(2,1)}, bf16[512,256]{1,0:T(8,128)(2,1)}, u32[]{:S(2)}, u32[]{:S(2)}) collective-permute-start(bf16[512,256]{1,0:T(8,128)(2,1)} %get-tuple-element.7), channel_id=1, source_target_pairs={{0,8},{1,9},{2,10},{3,11},{4,12},{5,13},{6,14},{7,15},{8,0},{9,1},... | collective-permute-start | bytes 786440 | tf_op jit(solution)/shard_map/ppermute | solution.py:37
  97.9 4.0 %collective-permute-start.8 = (bf16[512,256]{1,0:T(8,128)(2,1)}, bf16[512,256]{1,0:T(8,128)(2,1)}, u32[]{:S(2)}, u32[]{:S(2)}) collective-permute-start(bf16[512,256]{1,0:T(8,128)(2,1)} %get-tuple-element.6), channel_id=1, source_target_pairs={{0,12},{1,13},{2,14},{3,15},{4,8},{5,9},{6,10},{7,11},{8,4},{9,5},... | collective-permute-start | bytes 786440 | tf_op jit(solution)/shard_map/ppermute | solution.py:37
  101.9 1.9 %collective-permute-start.5 = (bf16[16,2,4352]{2,1,0:T(2,128)(2,1)S(1)}, bf16[16,2,4352]{2,1,0:T(2,128)(2,1)S(1)}, u32[]{:S(2)}, u32[]{:S(2)}) collective-permute-start(bf16[16,2,4352]{2,1,0:T(2,128)(2,1)S(1)} %all-to-all-done.3), channel_id=1, source_target_pairs={{0,16},{16,0},{32,48},{48,32},{64,80},{80,64},{96,112},{112,96},{1... | collective-permute-start | bytes 835592 | tf_op jit(solution)/shard_map/ppermute | solution.py:37
  108.6 3.2 %all-to-all-start.4 = ((f32[4,1,512]{2,1,0:T(1,128)}), f32[4,1,512]{2,1,0:T(1,128)S(1)}, u32[]{:S(2)}, u32[]{:S(2)}) async-start(f32[4,1,512]{2,1,0:T(1,128)} %broadcast_in_dim.81), calls=%async_computation.4 | async-start | bytes 16384 | tf_op jit(solution)/shard_map/all_to_all | solution.py:32
  111.9 1.8 %fusion.8 = f32[1024,512]{1,0:T(8,128)} fusion(bf16[1024,16]{0,1:T(8,128)(2,1)S(1)} %fusion.3, bf16[512,2,8]{0,2,1:T(8,128)(2,1)S(1)} %copy.47, bf16[]{:T(256)S(6)} %convert_element_type.172), kind=kOutput, calls=%fused_computation.38 | convolution fusion | flops 16793600 | bytes 2146306 | tf_op jit(solution)/shard_map/dot_general | solution.py:226
  113.7 1.3 %fusion.6 = bf16[256,512]{0,1:T(8,128)(2,1)S(1)} fusion(bf16[512,256]{1,0:T(8,128)(2,1)} %collective-permute-done.8, bf16[512,256]{1,0:T(8,128)(2,1)} %collective-permute-done.7, bf16[512,256]{1,0:T(8,128)(2,1)} %collective-permute-done.6, f32[]{:T(128)S(6)} %convert_element_type.160, bf16[512,1024]{1,0:T(8,128)(2,1)} %copy-done.1, s32[]{:T(128)S(6)} %select_n.62), kind=kLoop, calls=%fused_computation.26 | loop fusion | flops 1179648 | bytes 1310728 | tf_op jit(solution)/shard_map/transpose | solution.py:210
  115.4 1.8 %all-to-all-done.4 = f32[4,1,512]{2,1,0:T(1,128)S(1)} async-done(((f32[4,1,512]{2,1,0:T(1,128)}), f32[4,1,512]{2,1,0:T(1,128)S(1)}, u32[]{:S(2)}, u32[]{:S(2)}) %all-to-all-start.4) | async-done | bytes 8224 | tf_op jit(solution)/shard_map/all_to_all | solution.py:32
  118.0 6.5 %all-to-all-start.5 = ((bf16[4,66,512]{2,1,0:T(8,128)(2,1)}), bf16[4,66,512]{2,1,0:T(8,128)(2,1)S(1)}, u32[]{:S(2)}, u32[]{:S(2)}) async-start(bf16[4,66,512]{2,1,0:T(8,128)(2,1)} %pad_maximum_fusion.2), calls=%async_computation.5 | async-start | bytes 589824 | tf_op jit(solution)/shard_map/all_to_all | solution.py:219
  127.8 3.5 %add_convert_fusion = bf16[1024,512]{1,0:T(8,128)(2,1)} fusion(f32[1024,512]{1,0:T(8,128)} %fusion.8, bf16[1024,512]{1,0:T(8,128)(2,1)S(1)} %bitcast.99, bf16[512,512]{1,0:T(8,128)(2,1)} %bitcast.110, f32[]{:T(128)S(6)} %convert_element_type.171), kind=kOutput, calls=%fused_computation.2 | convolution fusion | flops 538443776 | bytes 4718596 | tf_op jit(solution)/shard_map/dot_general | solution.py:227
  (113 shorter events, 25.4 us)
Async XLA Ops:
  0.6 58.5 %copy-start = (bf16[1024,512]{1,0:T(8,128)(2,1)S(1)}, bf16[1024,512]{1,0:T(8,128)(2,1)}, u32[]{:S(2)}) copy-start(bf16[1024,512]{1,0:T(8,128)(2,1)} %param.9) | copy-start | bytes 3145732
  2.3 13.7 %all-to-all-start = ((bf16[4,64,512]{2,1,0:T(8,128)(2,1)}), bf16[4,64,512]{2,1,0:T(8,128)(2,1)S(1)}, u32[]{:S(2)}, u32[]{:S(2)}) async-start(bf16[4,64,512]{2,1,0:T(8,128)(2,1)} %broadcast_in_dim.67), calls=%async_computation | async-start | bytes 524288 | tf_op jit(solution)/shard_map/all_to_all | solution.py:32
  12.8 8.5 %collective-permute-start = (bf16[32,4352]{1,0:T(8,128)(2,1)S(1)}, bf16[32,4352]{1,0:T(8,128)(2,1)S(1)}, u32[]{:S(2)}, u32[]{:S(2)}) collective-permute-start(bf16[32,4352]{1,0:T(8,128)(2,1)S(1)} %convolution_convert_fusion), channel_id=1, source_target_pairs={{0,16},{16,0},{32,48},{48,32},{64,80},{80,64},{96,112},{112,96},{1... | collective-permute-start | bytes 835592 | tf_op jit(solution)/shard_map/ppermute | solution.py:37
  16.0 32.6 %collective-permute-start.2 = (bf16[256,512]{1,0:T(8,128)(2,1)S(1)}, bf16[256,512]{1,0:T(8,128)(2,1)S(1)}, u32[]{:S(2)}, u32[]{:S(2)}) collective-permute-start(bf16[256,512]{1,0:T(8,128)(2,1)S(1)} %bitcast.100), channel_id=1, source_target_pairs={{0,4},{1,5},{2,6},{3,7},{4,0},{5,1},{6,2},{7,3},{8,12},{9,13},{10,... | collective-permute-start | bytes 786440 | tf_op jit(solution)/shard_map/ppermute | solution.py:37
  19.4 19.5 %copy-start.4 = (s32[1,3]{1,0:T(1,128)S(1)}, s32[1,3]{1,0:T(1,128)}, u32[]{:S(2)}) copy-start(s32[1,3]{1,0:T(1,128)} %param.11) | copy-start | bytes 40
  23.2 35.2 %all-to-all-start.1 = ((bf16[16,2,8448]{2,1,0:T(2,128)(2,1)}), bf16[16,2,8448]{2,1,0:T(2,128)(2,1)S(1)}, u32[]{:S(2)}, u32[]{:S(2)}) async-start(bf16[16,2,8448]{2,1,0:T(2,128)(2,1)} %pad_maximum_fusion), calls=%async_computation.1 | async-start | bytes 1081344 | tf_op jit(solution)/shard_map/all_to_all | solution.py:112
  41.4 11.4 %collective-permute-start.3 = (bf16[256,512]{1,0:T(8,128)(2,1)S(1)}, bf16[256,512]{1,0:T(8,128)(2,1)S(1)}, u32[]{:S(2)}, u32[]{:S(2)}) collective-permute-start(bf16[256,512]{1,0:T(8,128)(2,1)S(1)} %bitcast.102), channel_id=1, source_target_pairs={{0,8},{1,9},{2,10},{3,11},{4,12},{5,13},{6,14},{7,15},{8,0},{9,1},... | collective-permute-start | bytes 786440 | tf_op jit(solution)/shard_map/ppermute | solution.py:37
  46.1 12.2 %collective-permute-start.4 = (bf16[256,512]{1,0:T(8,128)(2,1)S(1)}, bf16[256,512]{1,0:T(8,128)(2,1)S(1)}, u32[]{:S(2)}, u32[]{:S(2)}) collective-permute-start(bf16[256,512]{1,0:T(8,128)(2,1)S(1)} %bitcast.103), channel_id=1, source_target_pairs={{0,12},{1,13},{2,14},{3,15},{4,8},{5,9},{6,10},{7,11},{8,4},{9,5},... | collective-permute-start | bytes 786440 | tf_op jit(solution)/shard_map/ppermute | solution.py:37
  61.3 12.4 %all-to-all-start.2 = ((bf16[16,4,512]{2,1,0:T(4,128)(2,1)}), bf16[16,4,512]{2,1,0:T(4,128)(2,1)S(1)}, u32[]{:S(2)}, u32[]{:S(2)}) async-start(bf16[16,4,512]{2,1,0:T(4,128)(2,1)} %pad_maximum_fusion.3), calls=%async_computation.2 | async-start | bytes 131072 | tf_op jit(solution)/shard_map/all_to_all | solution.py:145
  69.0 19.6 %collective-permute-start.1 = (bf16[16,16,512]{2,1,0:T(8,128)(2,1)S(1)}, bf16[16,16,512]{2,1,0:T(8,128)(2,1)}, u32[]{:S(2)}, u32[]{:S(2)}) collective-permute-start(bf16[16,16,512]{2,1,0:T(8,128)(2,1)S(1)} %reshape.168), channel_id=1, source_target_pairs={{0,16},{16,0},{32,48},{48,32},{64,80},{80,64},{96,112},{112,96},{1... | collective-permute-start | bytes 786440 | tf_op jit(solution)/shard_map/ppermute | solution.py:37
  76.4 25.4 %all-to-all-start.3 = ((bf16[16,2,4352]{2,1,0:T(2,128)(2,1)}), bf16[16,2,4352]{2,1,0:T(2,128)(2,1)S(1)}, u32[]{:S(2)}, u32[]{:S(2)}) async-start(bf16[16,2,4352]{2,1,0:T(2,128)(2,1)} %broadcast_in_dim.79), calls=%async_computation.3 | async-start | bytes 557056 | tf_op jit(solution)/shard_map/all_to_all | solution.py:32
  89.6 1.8 %copy-start.2 = (bf16[16,2,16,512]{3,2,1,0:T(8,128)(2,1)}, bf16[16,2,16,512]{3,2,1,0:T(8,128)(2,1)S(1)}, u32[]{:S(2)}) copy-start(bf16[16,2,16,512]{3,2,1,0:T(8,128)(2,1)S(1)} %pad_maximum_fusion.1) | copy-start | bytes 1572868
  90.4 7.5 %copy-start.1 = (bf16[512,1024]{1,0:T(8,128)(2,1)}, bf16[512,1024]{1,0:T(8,128)(2,1)S(1)}, u32[]{:S(2)}) copy-start(bf16[512,1024]{1,0:T(8,128)(2,1)S(1)} %convolution_convert_fusion.1) | copy-start | bytes 3145732
  91.4 22.3 %collective-permute-start.6 = (bf16[512,256]{1,0:T(8,128)(2,1)}, bf16[512,256]{1,0:T(8,128)(2,1)}, u32[]{:S(2)}, u32[]{:S(2)}) collective-permute-start(bf16[512,256]{1,0:T(8,128)(2,1)} %get-tuple-element.5), channel_id=1, source_target_pairs={{0,4},{1,5},{2,6},{3,7},{4,0},{5,1},{6,2},{7,3},{8,12},{9,13},{10,... | collective-permute-start | bytes 786440 | tf_op jit(solution)/shard_map/ppermute | solution.py:37
  93.9 19.8 %collective-permute-start.7 = (bf16[512,256]{1,0:T(8,128)(2,1)}, bf16[512,256]{1,0:T(8,128)(2,1)}, u32[]{:S(2)}, u32[]{:S(2)}) collective-permute-start(bf16[512,256]{1,0:T(8,128)(2,1)} %get-tuple-element.7), channel_id=1, source_target_pairs={{0,8},{1,9},{2,10},{3,11},{4,12},{5,13},{6,14},{7,15},{8,0},{9,1},... | collective-permute-start | bytes 786440 | tf_op jit(solution)/shard_map/ppermute | solution.py:37
  97.9 15.8 %collective-permute-start.8 = (bf16[512,256]{1,0:T(8,128)(2,1)}, bf16[512,256]{1,0:T(8,128)(2,1)}, u32[]{:S(2)}, u32[]{:S(2)}) collective-permute-start(bf16[512,256]{1,0:T(8,128)(2,1)} %get-tuple-element.6), channel_id=1, source_target_pairs={{0,12},{1,13},{2,14},{3,15},{4,8},{5,9},{6,10},{7,11},{8,4},{9,5},... | collective-permute-start | bytes 786440 | tf_op jit(solution)/shard_map/ppermute | solution.py:37
  101.9 3.5 %collective-permute-start.5 = (bf16[16,2,4352]{2,1,0:T(2,128)(2,1)S(1)}, bf16[16,2,4352]{2,1,0:T(2,128)(2,1)S(1)}, u32[]{:S(2)}, u32[]{:S(2)}) collective-permute-start(bf16[16,2,4352]{2,1,0:T(2,128)(2,1)S(1)} %all-to-all-done.3), channel_id=1, source_target_pairs={{0,16},{16,0},{32,48},{48,32},{64,80},{80,64},{96,112},{112,96},{1... | collective-permute-start | bytes 835592 | tf_op jit(solution)/shard_map/ppermute | solution.py:37
  108.6 8.5 %all-to-all-start.4 = ((f32[4,1,512]{2,1,0:T(1,128)}), f32[4,1,512]{2,1,0:T(1,128)S(1)}, u32[]{:S(2)}, u32[]{:S(2)}) async-start(f32[4,1,512]{2,1,0:T(1,128)} %broadcast_in_dim.81), calls=%async_computation.4 | async-start | bytes 16384 | tf_op jit(solution)/shard_map/all_to_all | solution.py:32
  118.0 13.3 %all-to-all-start.5 = ((bf16[4,66,512]{2,1,0:T(8,128)(2,1)}), bf16[4,66,512]{2,1,0:T(8,128)(2,1)S(1)}, u32[]{:S(2)}, u32[]{:S(2)}) async-start(bf16[4,66,512]{2,1,0:T(8,128)(2,1)} %pad_maximum_fusion.2), calls=%async_computation.5 | async-start | bytes 589824 | tf_op jit(solution)/shard_map/all_to_all | solution.py:219
  127.8 4.5 %copy-start.3 = (bf16[32,1024]{1,0:T(8,128)(2,1)S(1)}, bf16[32,1024]{1,0:T(8,128)(2,1)}, u32[]{:S(2)}) copy-start(bf16[32,1024]{1,0:T(8,128)(2,1)} %param.13) | copy-start | bytes 196612

commit v12 on v11

--- a/solution.py
+++ b/solution.py
@@ -118,13 +118,13 @@
     place_x = place // Y_RUN
     cot_full = gathered(cot_run, place_x, n_x, Y_RUN)
 
-    first, second = seq_lengths[0, 0], seq_lengths[0, 1]
+    first = seq_lengths[:, :1]
+    both = first + seq_lengths[:, 1:2]
     places = jnp.arange(rows_total, dtype=jnp.int32)[:, None]
-    in_second = (places >= first) & (places < first + second)
-    in_first = jnp.broadcast_to(places < first, (rows_total, R))
-    col_mask = jnp.concatenate(
-        (in_first, jnp.broadcast_to(in_second, (rows_total, R))), axis=1
-    ).astype(f32)
+    column = jnp.arange(ADA, dtype=jnp.int32)[None, :]
+    in_first = places < first
+    inside = jnp.where(column < R, in_first, (places < both) & ~in_first)
+    col_mask = inside.astype(f32)
 
     low_part = (jnp.dot(tokens, down_cat, preferred_element_type=f32) * col_mask).astype(bf16)
     up_part = lax.dot_general(cot_full, low_part, outer_dims, preferred_element_type=f32).astype(

time: 134 us -> 135 us (level)
  no operation moved by 1% of the time
where the time goes in v12:
time: 135 us; the launch traced here: 134 us
  starting transfers between devices  77.7 us (58%)
  local copies, waits for them, and re-layouts  16.4 us (12%)
  waiting for transfers between devices  15.3 us (11%)
  matrix products  11.9 us (9%)
  between operations  6.35 us (5%)
  other arithmetic  6.3 us (5%)
    ppermute x9, starting transfers between devices, swapped(): return lax.ppermute(block, axis, pairs)  26.6 us
    all_to_all x3, starting transfers between devices, spread(): return lax.all_to_all(copies, axes, 0, 0, **kw)  21.6 us
    all_to_all x1, starting transfers between devices, shards(): came = lax.all_to_all(sent, 'dp', 0, 0, axis_index_groups=same_core)  15.7 us
    ppermute x9, waiting for transfers between devices, swapped(): return lax.ppermute(block, axis, pairs)  10.7 us
    all_to_all x1, starting transfers between devices, shards(): low_came = lax.all_to_all(block, 'tensor', 0, 0)  7.28 us
    all_to_all x1, starting transfers between devices, shards(): lax.all_to_all(last, 'tensor', 0, 0, axis_index_groups=along_y).astype(f32)  6.5 us
    dot_general x1, matrix products, shards(): frozen_back = jnp.dot(cot_full, weight_t, preferred_element_type=f32)  3.47 us
    broadcast_in_dim x4, local copies, waits for them, and re-layouts, spread(): copies = jnp.broadcast_to(block[None], (count,) + block.shape)  3.21 us
  transfers between devices with their start and end apart: 15, of which 5 were waited for; matrix products, arithmetic and copies ran while one was open for 20% of the time, Pallas kernels for 0%

profile of v12, /device:TPU:56, one launch (start us, length us, event | category | flops | bytes accessed | tf_op | source)
XLA Modules:
  0.0 133.9 jit_solution(14711599454705648163)
XLA Ops:
  0.6 1.6 %broadcast_in_dim.82 = bf16[4,64,512]{2,1,0:T(8,128)(2,1)} broadcast(bf16[64,512]{1,0:T(8,128)(2,1)} %param.17), dimensions={1,2} | broadcast | bytes 327680 | tf_op jit(solution)/shard_map/broadcast_in_dim | solution.py:31
  2.3 6.3 %all-to-all-start = ((bf16[4,64,512]{2,1,0:T(8,128)(2,1)}), bf16[4,64,512]{2,1,0:T(8,128)(2,1)S(1)}, u32[]{:S(2)}, u32[]{:S(2)}) async-start(bf16[4,64,512]{2,1,0:T(8,128)(2,1)} %broadcast_in_dim.82), calls=%async_computation | async-start | bytes 524288 | tf_op jit(solution)/shard_map/all_to_all | solution.py:32
  12.8 1.9 %collective-permute-start = (bf16[32,4352]{1,0:T(8,128)(2,1)S(1)}, bf16[32,4352]{1,0:T(8,128)(2,1)S(1)}, u32[]{:S(2)}, u32[]{:S(2)}) collective-permute-start(bf16[32,4352]{1,0:T(8,128)(2,1)S(1)} %convolution_convert_fusion), channel_id=1, source_target_pairs={{0,16},{16,0},{32,48},{48,32},{64,80},{80,64},{96,112},{112,96},{1... | collective-permute-start | bytes 835592 | tf_op jit(solution)/shard_map/ppermute | solution.py:37
  14.7 1.3 fusion.42
  17.3 3.4 %collective-permute-start.2 = (bf16[256,512]{1,0:T(8,128)(2,1)S(1)}, bf16[256,512]{1,0:T(8,128)(2,1)S(1)}, u32[]{:S(2)}, u32[]{:S(2)}) collective-permute-start(bf16[256,512]{1,0:T(8,128)(2,1)S(1)} %bitcast.100), channel_id=1, source_target_pairs={{0,4},{1,5},{2,6},{3,7},{4,0},{5,1},{6,2},{7,3},{8,12},{9,13},{10,... | collective-permute-start | bytes 786440 | tf_op jit(solution)/shard_map/ppermute | solution.py:37
  24.5 15.7 %all-to-all-start.1 = ((bf16[16,2,8448]{2,1,0:T(2,128)(2,1)}), bf16[16,2,8448]{2,1,0:T(2,128)(2,1)S(1)}, u32[]{:S(2)}, u32[]{:S(2)}) async-start(bf16[16,2,8448]{2,1,0:T(2,128)(2,1)} %pad_maximum_fusion), calls=%async_computation.1 | async-start | bytes 1081344 | tf_op jit(solution)/shard_map/all_to_all | solution.py:112
  42.2 4.6 %collective-permute-start.3 = (bf16[256,512]{1,0:T(8,128)(2,1)S(1)}, bf16[256,512]{1,0:T(8,128)(2,1)S(1)}, u32[]{:S(2)}, u32[]{:S(2)}) collective-permute-start(bf16[256,512]{1,0:T(8,128)(2,1)S(1)} %bitcast.102), channel_id=1, source_target_pairs={{0,8},{1,9},{2,10},{3,11},{4,12},{5,13},{6,14},{7,15},{8,0},{9,1},... | collective-permute-start | bytes 786440 | tf_op jit(solution)/shard_map/ppermute | solution.py:37
  46.8 2.4 %collective-permute-start.4 = (bf16[256,512]{1,0:T(8,128)(2,1)S(1)}, bf16[256,512]{1,0:T(8,128)(2,1)S(1)}, u32[]{:S(2)}, u32[]{:S(2)}) collective-permute-start(bf16[256,512]{1,0:T(8,128)(2,1)S(1)} %bitcast.103), channel_id=1, source_target_pairs={{0,12},{1,13},{2,14},{3,15},{4,8},{5,9},{6,10},{7,11},{8,4},{9,5},... | collective-permute-start | bytes 786440 | tf_op jit(solution)/shard_map/ppermute | solution.py:37
  49.4 4.2 %collective-permute-done.3 = bf16[256,512]{1,0:T(8,128)(2,1)S(1)} collective-permute-done((bf16[256,512]{1,0:T(8,128)(2,1)S(1)}, bf16[256,512]{1,0:T(8,128)(2,1)S(1)}, u32[]{:S(2)}, u32[]{:S(2)}) %collective-permute-start.3) | collective-permute-done | bytes 262176 | tf_op jit(solution)/shard_map/ppermute | solution.py:37
  53.6 5.5 %collective-permute-done.4 = bf16[256,512]{1,0:T(8,128)(2,1)S(1)} collective-permute-done((bf16[256,512]{1,0:T(8,128)(2,1)S(1)}, bf16[256,512]{1,0:T(8,128)(2,1)S(1)}, u32[]{:S(2)}, u32[]{:S(2)}) %collective-permute-start.4) | collective-permute-done | bytes 262176 | tf_op jit(solution)/shard_map/ppermute | solution.py:37
  62.0 7.3 %all-to-all-start.2 = ((bf16[16,4,512]{2,1,0:T(4,128)(2,1)}), bf16[16,4,512]{2,1,0:T(4,128)(2,1)S(1)}, u32[]{:S(2)}, u32[]{:S(2)}) async-start(bf16[16,4,512]{2,1,0:T(4,128)(2,1)} %pad_maximum_fusion.3), calls=%async_computation.2 | async-start | bytes 131072 | tf_op jit(solution)/shard_map/all_to_all | solution.py:145
  69.7 1.9 %collective-permute-start.1 = (bf16[16,16,512]{2,1,0:T(8,128)(2,1)S(1)}, bf16[16,16,512]{2,1,0:T(8,128)(2,1)}, u32[]{:S(2)}, u32[]{:S(2)}) collective-permute-start(bf16[16,16,512]{2,1,0:T(8,128)(2,1)S(1)} %reshape.175), channel_id=1, source_target_pairs={{0,16},{16,0},{32,48},{48,32},{64,80},{80,64},{96,112},{112,96},{1... | collective-permute-start | bytes 786440 | tf_op jit(solution)/shard_map/ppermute | solution.py:37
  71.6 2.8 %all-to-all-done.2 = bf16[16,4,512]{2,1,0:T(4,128)(2,1)S(1)} async-done(((bf16[16,4,512]{2,1,0:T(4,128)(2,1)}), bf16[16,4,512]{2,1,0:T(4,128)(2,1)S(1)}, u32[]{:S(2)}, u32[]{:S(2)}) %all-to-all-start.2) | async-done | bytes 65568 | tf_op jit(solution)/shard_map/all_to_all | solution.py:145
  77.2 12.0 %all-to-all-start.3 = ((bf16[16,2,4352]{2,1,0:T(2,128)(2,1)}), bf16[16,2,4352]{2,1,0:T(2,128)(2,1)S(1)}, u32[]{:S(2)}, u32[]{:S(2)}) async-start(bf16[16,2,4352]{2,1,0:T(2,128)(2,1)} %broadcast_in_dim.95), calls=%async_computation.3 | async-start | bytes 557056 | tf_op jit(solution)/shard_map/all_to_all | solution.py:32
  92.1 2.5 %collective-permute-start.6 = (bf16[512,256]{1,0:T(8,128)(2,1)}, bf16[512,256]{1,0:T(8,128)(2,1)}, u32[]{:S(2)}, u32[]{:S(2)}) collective-permute-start(bf16[512,256]{1,0:T(8,128)(2,1)} %get-tuple-element.5), channel_id=1, source_target_pairs={{0,4},{1,5},{2,6},{3,7},{4,0},{5,1},{6,2},{7,3},{8,12},{9,13},{10,... | collective-permute-start | bytes 786440 | tf_op jit(solution)/shard_map/ppermute | solution.py:37
  94.6 4.0 %collective-permute-start.7 = (bf16[512,256]{1,0:T(8,128)(2,1)}, bf16[512,256]{1,0:T(8,128)(2,1)}, u32[]{:S(2)}, u32[]{:S(2)}) collective-permute-start(bf16[512,256]{1,0:T(8,128)(2,1)} %get-tuple-element.7), channel_id=1, source_target_pairs={{0,8},{1,9},{2,10},{3,11},{4,12},{5,13},{6,14},{7,15},{8,0},{9,1},... | collective-permute-start | bytes 786440 | tf_op jit(solution)/shard_map/ppermute | solution.py:37
  98.6 4.0 %collective-permute-start.8 = (bf16[512,256]{1,0:T(8,128)(2,1)}, bf16[512,256]{1,0:T(8,128)(2,1)}, u32[]{:S(2)}, u32[]{:S(2)}) collective-permute-start(bf16[512,256]{1,0:T(8,128)(2,1)} %get-tuple-element.6), channel_id=1, source_target_pairs={{0,12},{1,13},{2,14},{3,15},{4,8},{5,9},{6,10},{7,11},{8,4},{9,5},... | collective-permute-start | bytes 786440 | tf_op jit(solution)/shard_map/ppermute | solution.py:37
  102.6 1.9 %collective-permute-start.5 = (bf16[16,2,4352]{2,1,0:T(2,128)(2,1)S(1)}, bf16[16,2,4352]{2,1,0:T(2,128)(2,1)S(1)}, u32[]{:S(2)}, u32[]{:S(2)}) collective-permute-start(bf16[16,2,4352]{2,1,0:T(2,128)(2,1)S(1)} %all-to-all-done.3), channel_id=1, source_target_pairs={{0,16},{16,0},{32,48},{48,32},{64,80},{80,64},{96,112},{112,96},{1... | collective-permute-start | bytes 835592 | tf_op jit(solution)/shard_map/ppermute | solution.py:37
  109.4 3.2 %all-to-all-start.4 = ((f32[4,1,512]{2,1,0:T(1,128)}), f32[4,1,512]{2,1,0:T(1,128)S(1)}, u32[]{:S(2)}, u32[]{:S(2)}) async-start(f32[4,1,512]{2,1,0:T(1,128)} %broadcast_in_dim.97), calls=%async_computation.4 | async-start | bytes 16384 | tf_op jit(solution)/shard_map/all_to_all | solution.py:32
  112.6 1.8 %fusion.8 = f32[1024,512]{1,0:T(8,128)} fusion(bf16[1024,16]{0,1:T(8,128)(2,1)S(1)} %fusion.3, bf16[512,2,8]{0,2,1:T(8,128)(2,1)S(1)} %copy.47, bf16[]{:T(256)S(6)} %convert_element_type.172), kind=kOutput, calls=%fused_computation.37 | convolution fusion | flops 16793600 | bytes 2146306 | tf_op jit(solution)/shard_map/dot_general | solution.py:226
  114.4 1.3 %fusion.6 = bf16[256,512]{0,1:T(8,128)(2,1)S(1)} fusion(bf16[512,256]{1,0:T(8,128)(2,1)} %collective-permute-done.8, bf16[512,256]{1,0:T(8,128)(2,1)} %collective-permute-done.7, bf16[512,256]{1,0:T(8,128)(2,1)} %collective-permute-done.6, f32[]{:T(128)S(6)} %convert_element_type.160, bf16[512,1024]{1,0:T(8,128)(2,1)} %copy-done.1, s32[]{:T(128)S(6)} %select_n.66), kind=kLoop, calls=%fused_computation.26 | loop fusion | flops 1179648 | bytes 1310728 | tf_op jit(solution)/shard_map/transpose | solution.py:210
  116.1 1.8 %all-to-all-done.4 = f32[4,1,512]{2,1,0:T(1,128)S(1)} async-done(((f32[4,1,512]{2,1,0:T(1,128)}), f32[4,1,512]{2,1,0:T(1,128)S(1)}, u32[]{:S(2)}, u32[]{:S(2)}) %all-to-all-start.4) | async-done | bytes 8224 | tf_op jit(solution)/shard_map/all_to_all | solution.py:32
  118.7 6.5 %all-to-all-start.5 = ((bf16[4,66,512]{2,1,0:T(8,128)(2,1)}), bf16[4,66,512]{2,1,0:T(8,128)(2,1)S(1)}, u32[]{:S(2)}, u32[]{:S(2)}) async-start(bf16[4,66,512]{2,1,0:T(8,128)(2,1)} %pad_maximum_fusion.2), calls=%async_computation.5 | async-start | bytes 589824 | tf_op jit(solution)/shard_map/all_to_all | solution.py:219
  128.6 3.5 %add_convert_fusion = bf16[1024,512]{1,0:T(8,128)(2,1)} fusion(f32[1024,512]{1,0:T(8,128)} %fusion.8, bf16[1024,512]{1,0:T(8,128)(2,1)S(1)} %bitcast.99, bf16[512,512]{1,0:T(8,128)(2,1)} %bitcast.110, f32[]{:T(128)S(6)} %convert_element_type.171), kind=kOutput, calls=%fused_computation.2 | convolution fusion | flops 538443776 | bytes 4718596 | tf_op jit(solution)/shard_map/dot_general | solution.py:227
  (110 shorter events, 26.1 us)
Async XLA Ops:
  0.6 59.2 %copy-start = (bf16[1024,512]{1,0:T(8,128)(2,1)S(1)}, bf16[1024,512]{1,0:T(8,128)(2,1)}, u32[]{:S(2)}) copy-start(bf16[1024,512]{1,0:T(8,128)(2,1)} %param.9) | copy-start | bytes 3145732
  2.3 15.0 %all-to-all-start = ((bf16[4,64,512]{2,1,0:T(8,128)(2,1)}), bf16[4,64,512]{2,1,0:T(8,128)(2,1)S(1)}, u32[]{:S(2)}, u32[]{:S(2)}) async-start(bf16[4,64,512]{2,1,0:T(8,128)(2,1)} %broadcast_in_dim.82), calls=%async_computation | async-start | bytes 524288 | tf_op jit(solution)/shard_map/all_to_all | solution.py:32
  12.8 9.8 %collective-permute-start = (bf16[32,4352]{1,0:T(8,128)(2,1)S(1)}, bf16[32,4352]{1,0:T(8,128)(2,1)S(1)}, u32[]{:S(2)}, u32[]{:S(2)}) collective-permute-start(bf16[32,4352]{1,0:T(8,128)(2,1)S(1)} %convolution_convert_fusion), channel_id=1, source_target_pairs={{0,16},{16,0},{32,48},{48,32},{64,80},{80,64},{96,112},{112,96},{1... | collective-permute-start | bytes 835592 | tf_op jit(solution)/shard_map/ppermute | solution.py:37
  17.3 32.1 %collective-permute-start.2 = (bf16[256,512]{1,0:T(8,128)(2,1)S(1)}, bf16[256,512]{1,0:T(8,128)(2,1)S(1)}, u32[]{:S(2)}, u32[]{:S(2)}) collective-permute-start(bf16[256,512]{1,0:T(8,128)(2,1)S(1)} %bitcast.100), channel_id=1, source_target_pairs={{0,4},{1,5},{2,6},{3,7},{4,0},{5,1},{6,2},{7,3},{8,12},{9,13},{10,... | collective-permute-start | bytes 786440 | tf_op jit(solution)/shard_map/ppermute | solution.py:37
  24.5 34.6 %all-to-all-start.1 = ((bf16[16,2,8448]{2,1,0:T(2,128)(2,1)}), bf16[16,2,8448]{2,1,0:T(2,128)(2,1)S(1)}, u32[]{:S(2)}, u32[]{:S(2)}) async-start(bf16[16,2,8448]{2,1,0:T(2,128)(2,1)} %pad_maximum_fusion), calls=%async_computation.1 | async-start | bytes 1081344 | tf_op jit(solution)/shard_map/all_to_all | solution.py:112
  42.2 11.4 %collective-permute-start.3 = (bf16[256,512]{1,0:T(8,128)(2,1)S(1)}, bf16[256,512]{1,0:T(8,128)(2,1)S(1)}, u32[]{:S(2)}, u32[]{:S(2)}) collective-permute-start(bf16[256,512]{1,0:T(8,128)(2,1)S(1)} %bitcast.102), channel_id=1, source_target_pairs={{0,8},{1,9},{2,10},{3,11},{4,12},{5,13},{6,14},{7,15},{8,0},{9,1},... | collective-permute-start | bytes 786440 | tf_op jit(solution)/shard_map/ppermute | solution.py:37
  46.8 12.2 %collective-permute-start.4 = (bf16[256,512]{1,0:T(8,128)(2,1)S(1)}, bf16[256,512]{1,0:T(8,128)(2,1)S(1)}, u32[]{:S(2)}, u32[]{:S(2)}) collective-permute-start(bf16[256,512]{1,0:T(8,128)(2,1)S(1)} %bitcast.103), channel_id=1, source_target_pairs={{0,12},{1,13},{2,14},{3,15},{4,8},{5,9},{6,10},{7,11},{8,4},{9,5},... | collective-permute-start | bytes 786440 | tf_op jit(solution)/shard_map/ppermute | solution.py:37
  62.0 12.4 %all-to-all-start.2 = ((bf16[16,4,512]{2,1,0:T(4,128)(2,1)}), bf16[16,4,512]{2,1,0:T(4,128)(2,1)S(1)}, u32[]{:S(2)}, u32[]{:S(2)}) async-start(bf16[16,4,512]{2,1,0:T(4,128)(2,1)} %pad_maximum_fusion.3), calls=%async_computation.2 | async-start | bytes 131072 | tf_op jit(solution)/shard_map/all_to_all | solution.py:145
  69.7 19.6 %collective-permute-start.1 = (bf16[16,16,512]{2,1,0:T(8,128)(2,1)S(1)}, bf16[16,16,512]{2,1,0:T(8,128)(2,1)}, u32[]{:S(2)}, u32[]{:S(2)}) collective-permute-start(bf16[16,16,512]{2,1,0:T(8,128)(2,1)S(1)} %reshape.175), channel_id=1, source_target_pairs={{0,16},{16,0},{32,48},{48,32},{64,80},{80,64},{96,112},{112,96},{1... | collective-permute-start | bytes 786440 | tf_op jit(solution)/shard_map/ppermute | solution.py:37
  77.2 25.4 %all-to-all-start.3 = ((bf16[16,2,4352]{2,1,0:T(2,128)(2,1)}), bf16[16,2,4352]{2,1,0:T(2,128)(2,1)S(1)}, u32[]{:S(2)}, u32[]{:S(2)}) async-start(bf16[16,2,4352]{2,1,0:T(2,128)(2,1)} %broadcast_in_dim.95), calls=%async_computation.3 | async-start | bytes 557056 | tf_op jit(solution)/shard_map/all_to_all | solution.py:32
  90.3 1.8 %copy-start.2 = (bf16[16,2,16,512]{3,2,1,0:T(8,128)(2,1)}, bf16[16,2,16,512]{3,2,1,0:T(8,128)(2,1)S(1)}, u32[]{:S(2)}) copy-start(bf16[16,2,16,512]{3,2,1,0:T(8,128)(2,1)S(1)} %pad_maximum_fusion.1) | copy-start | bytes 1572868
  91.1 7.5 %copy-start.1 = (bf16[512,1024]{1,0:T(8,128)(2,1)}, bf16[512,1024]{1,0:T(8,128)(2,1)S(1)}, u32[]{:S(2)}) copy-start(bf16[512,1024]{1,0:T(8,128)(2,1)S(1)} %convolution_convert_fusion.1) | copy-start | bytes 3145732
  92.1 22.3 %collective-permute-start.6 = (bf16[512,256]{1,0:T(8,128)(2,1)}, bf16[512,256]{1,0:T(8,128)(2,1)}, u32[]{:S(2)}, u32[]{:S(2)}) collective-permute-start(bf16[512,256]{1,0:T(8,128)(2,1)} %get-tuple-element.5), channel_id=1, source_target_pairs={{0,4},{1,5},{2,6},{3,7},{4,0},{5,1},{6,2},{7,3},{8,12},{9,13},{10,... | collective-permute-start | bytes 786440 | tf_op jit(solution)/shard_map/ppermute | solution.py:37
  94.6 19.8 %collective-permute-start.7 = (bf16[512,256]{1,0:T(8,128)(2,1)}, bf16[512,256]{1,0:T(8,128)(2,1)}, u32[]{:S(2)}, u32[]{:S(2)}) collective-permute-start(bf16[512,256]{1,0:T(8,128)(2,1)} %get-tuple-element.7), channel_id=1, source_target_pairs={{0,8},{1,9},{2,10},{3,11},{4,12},{5,13},{6,14},{7,15},{8,0},{9,1},... | collective-permute-start | bytes 786440 | tf_op jit(solution)/shard_map/ppermute | solution.py:37
  98.6 15.8 %collective-permute-start.8 = (bf16[512,256]{1,0:T(8,128)(2,1)}, bf16[512,256]{1,0:T(8,128)(2,1)}, u32[]{:S(2)}, u32[]{:S(2)}) collective-permute-start(bf16[512,256]{1,0:T(8,128)(2,1)} %get-tuple-element.6), channel_id=1, source_target_pairs={{0,12},{1,13},{2,14},{3,15},{4,8},{5,9},{6,10},{7,11},{8,4},{9,5},... | collective-permute-start | bytes 786440 | tf_op jit(solution)/shard_map/ppermute | solution.py:37
  102.6 3.5 %collective-permute-start.5 = (bf16[16,2,4352]{2,1,0:T(2,128)(2,1)S(1)}, bf16[16,2,4352]{2,1,0:T(2,128)(2,1)S(1)}, u32[]{:S(2)}, u32[]{:S(2)}) collective-permute-start(bf16[16,2,4352]{2,1,0:T(2,128)(2,1)S(1)} %all-to-all-done.3), channel_id=1, source_target_pairs={{0,16},{16,0},{32,48},{48,32},{64,80},{80,64},{96,112},{112,96},{1... | collective-permute-start | bytes 835592 | tf_op jit(solution)/shard_map/ppermute | solution.py:37
  109.4 8.5 %all-to-all-start.4 = ((f32[4,1,512]{2,1,0:T(1,128)}), f32[4,1,512]{2,1,0:T(1,128)S(1)}, u32[]{:S(2)}, u32[]{:S(2)}) async-start(f32[4,1,512]{2,1,0:T(1,128)} %broadcast_in_dim.97), calls=%async_computation.4 | async-start | bytes 16384 | tf_op jit(solution)/shard_map/all_to_all | solution.py:32
  118.7 13.3 %all-to-all-start.5 = ((bf16[4,66,512]{2,1,0:T(8,128)(2,1)}), bf16[4,66,512]{2,1,0:T(8,128)(2,1)S(1)}, u32[]{:S(2)}, u32[]{:S(2)}) async-start(bf16[4,66,512]{2,1,0:T(8,128)(2,1)} %pad_maximum_fusion.2), calls=%async_computation.5 | async-start | bytes 589824 | tf_op jit(solution)/shard_map/all_to_all | solution.py:219
  128.6 4.5 %copy-start.3 = (bf16[32,1024]{1,0:T(8,128)(2,1)S(1)}, bf16[32,1024]{1,0:T(8,128)(2,1)}, u32[]{:S(2)}) copy-start(bf16[32,1024]{1,0:T(8,128)(2,1)} %param.13) | copy-start | bytes 196612

commit v13 on v11

--- a/solution.py
+++ b/solution.py
@@ -186,7 +186,7 @@
     frozen_kept = run_of(place_x)
     frozen_came = [
         swapped(run_of(place_x ^ step), "tensor", step * Y_RUN)
-        for step in range(1, n_x)
+        for step in (2, 3, 1)
     ]
     grads_mate = swapped(grads_mine, "dp", 1)
 

time: 134 us -> 134 us (level)
  no operation moved by 1% of the time
where the time goes in v13:
time: 134 us; the launch traced here: 132 us
  starting transfers between devices  76.9 us (57%)
  local copies, waits for them, and re-layouts  15.7 us (12%)
  waiting for transfers between devices  15.3 us (11%)
  matrix products  11.9 us (9%)
  between operations  6.35 us (5%)
  other arithmetic  6.29 us (5%)
    ppermute x9, starting transfers between devices, swapped(): return lax.ppermute(block, axis, pairs)  25.4 us
    all_to_all x3, starting transfers between devices, spread(): return lax.all_to_all(copies, axes, 0, 0, **kw)  22 us
    all_to_all x1, starting transfers between devices, shards(): came = lax.all_to_all(sent, 'dp', 0, 0, axis_index_groups=same_core)  15.7 us
    ppermute x9, waiting for transfers between devices, swapped(): return lax.ppermute(block, axis, pairs)  10.7 us
    all_to_all x1, starting transfers between devices, shards(): low_came = lax.all_to_all(block, 'tensor', 0, 0)  7.28 us
    all_to_all x1, starting transfers between devices, shards(): lax.all_to_all(last, 'tensor', 0, 0, axis_index_groups=along_y).astype(f32)  6.55 us
    dot_general x1, matrix products, shards(): frozen_back = jnp.dot(cot_full, weight_t, preferred_element_type=f32)  3.47 us
    broadcast_in_dim x4, local copies, waits for them, and re-layouts, spread(): copies = jnp.broadcast_to(block[None], (count,) + block.shape)  3.2 us
  transfers between devices with their start and end apart: 15, of which 5 were waited for; matrix products, arithmetic and copies ran while one was open for 20% of the time, Pallas kernels for 0%

profile of v13, /device:TPU:56, one launch (start us, length us, event | category | flops | bytes accessed | tf_op | source)
XLA Modules:
  0.0 132.5 jit_solution(7173828063203386765)
XLA Ops:
  0.6 1.6 %broadcast_in_dim.67 = bf16[4,64,512]{2,1,0:T(8,128)(2,1)} broadcast(bf16[64,512]{1,0:T(8,128)(2,1)} %param.17), dimensions={1,2} | broadcast | bytes 327680 | tf_op jit(solution)/shard_map/broadcast_in_dim | solution.py:31
  2.3 6.3 %all-to-all-start = ((bf16[4,64,512]{2,1,0:T(8,128)(2,1)}), bf16[4,64,512]{2,1,0:T(8,128)(2,1)S(1)}, u32[]{:S(2)}, u32[]{:S(2)}) async-start(bf16[4,64,512]{2,1,0:T(8,128)(2,1)} %broadcast_in_dim.67), calls=%async_computation | async-start | bytes 524288 | tf_op jit(solution)/shard_map/all_to_all | solution.py:32
  12.8 1.9 %collective-permute-start = (bf16[32,4352]{1,0:T(8,128)(2,1)S(1)}, bf16[32,4352]{1,0:T(8,128)(2,1)S(1)}, u32[]{:S(2)}, u32[]{:S(2)}) collective-permute-start(bf16[32,4352]{1,0:T(8,128)(2,1)S(1)} %convolution_convert_fusion), channel_id=1, source_target_pairs={{0,16},{16,0},{32,48},{48,32},{64,80},{80,64},{96,112},{112,96},{1... | collective-permute-start | bytes 835592 | tf_op jit(solution)/shard_map/ppermute | solution.py:37
  16.0 3.4 %collective-permute-start.2 = (bf16[256,512]{1,0:T(8,128)(2,1)S(1)}, bf16[256,512]{1,0:T(8,128)(2,1)S(1)}, u32[]{:S(2)}, u32[]{:S(2)}) collective-permute-start(bf16[256,512]{1,0:T(8,128)(2,1)S(1)} %bitcast.100), channel_id=1, source_target_pairs={{0,4},{1,5},{2,6},{3,7},{4,0},{5,1},{6,2},{7,3},{8,12},{9,13},{10,... | collective-permute-start | bytes 786440 | tf_op jit(solution)/shard_map/ppermute | solution.py:37
  21.9 1.3 pad_maximum_fusion
  23.2 15.7 %all-to-all-start.1 = ((bf16[16,2,8448]{2,1,0:T(2,128)(2,1)}), bf16[16,2,8448]{2,1,0:T(2,128)(2,1)S(1)}, u32[]{:S(2)}, u32[]{:S(2)}) async-start(bf16[16,2,8448]{2,1,0:T(2,128)(2,1)} %pad_maximum_fusion), calls=%async_computation.1 | async-start | bytes 1081344 | tf_op jit(solution)/shard_map/all_to_all | solution.py:112
  41.4 4.6 %collective-permute-start.3 = (bf16[256,512]{1,0:T(8,128)(2,1)S(1)}, bf16[256,512]{1,0:T(8,128)(2,1)S(1)}, u32[]{:S(2)}, u32[]{:S(2)}) collective-permute-start(bf16[256,512]{1,0:T(8,128)(2,1)S(1)} %bitcast.102), channel_id=1, source_target_pairs={{0,8},{1,9},{2,10},{3,11},{4,12},{5,13},{6,14},{7,15},{8,0},{9,1},... | collective-permute-start | bytes 786440 | tf_op jit(solution)/shard_map/ppermute | solution.py:37
  46.1 2.4 %collective-permute-start.4 = (bf16[256,512]{1,0:T(8,128)(2,1)S(1)}, bf16[256,512]{1,0:T(8,128)(2,1)S(1)}, u32[]{:S(2)}, u32[]{:S(2)}) collective-permute-start(bf16[256,512]{1,0:T(8,128)(2,1)S(1)} %bitcast.103), channel_id=1, source_target_pairs={{0,12},{1,13},{2,14},{3,15},{4,8},{5,9},{6,10},{7,11},{8,4},{9,5},... | collective-permute-start | bytes 786440 | tf_op jit(solution)/shard_map/ppermute | solution.py:37
  48.6 4.2 %collective-permute-done.3 = bf16[256,512]{1,0:T(8,128)(2,1)S(1)} collective-permute-done((bf16[256,512]{1,0:T(8,128)(2,1)S(1)}, bf16[256,512]{1,0:T(8,128)(2,1)S(1)}, u32[]{:S(2)}, u32[]{:S(2)}) %collective-permute-start.3) | collective-permute-done | bytes 262176 | tf_op jit(solution)/shard_map/ppermute | solution.py:37
  52.8 5.5 %collective-permute-done.4 = bf16[256,512]{1,0:T(8,128)(2,1)S(1)} collective-permute-done((bf16[256,512]{1,0:T(8,128)(2,1)S(1)}, bf16[256,512]{1,0:T(8,128)(2,1)S(1)}, u32[]{:S(2)}, u32[]{:S(2)}) %collective-permute-start.4) | collective-permute-done | bytes 262176 | tf_op jit(solution)/shard_map/ppermute | solution.py:37
  61.3 7.3 %all-to-all-start.2 = ((bf16[16,4,512]{2,1,0:T(4,128)(2,1)}), bf16[16,4,512]{2,1,0:T(4,128)(2,1)S(1)}, u32[]{:S(2)}, u32[]{:S(2)}) async-start(bf16[16,4,512]{2,1,0:T(4,128)(2,1)} %pad_maximum_fusion.3), calls=%async_computation.2 | async-start | bytes 131072 | tf_op jit(solution)/shard_map/all_to_all | solution.py:145
  69.0 1.9 %collective-permute-start.1 = (bf16[16,16,512]{2,1,0:T(8,128)(2,1)S(1)}, bf16[16,16,512]{2,1,0:T(8,128)(2,1)}, u32[]{:S(2)}, u32[]{:S(2)}) collective-permute-start(bf16[16,16,512]{2,1,0:T(8,128)(2,1)S(1)} %reshape.168), channel_id=1, source_target_pairs={{0,16},{16,0},{32,48},{48,32},{64,80},{80,64},{96,112},{112,96},{1... | collective-permute-start | bytes 786440 | tf_op jit(solution)/shard_map/ppermute | solution.py:37
  70.9 2.8 %all-to-all-done.2 = bf16[16,4,512]{2,1,0:T(4,128)(2,1)S(1)} async-done(((bf16[16,4,512]{2,1,0:T(4,128)(2,1)}), bf16[16,4,512]{2,1,0:T(4,128)(2,1)S(1)}, u32[]{:S(2)}, u32[]{:S(2)}) %all-to-all-start.2) | async-done | bytes 65568 | tf_op jit(solution)/shard_map/all_to_all | solution.py:145
  76.4 12.0 %all-to-all-start.3 = ((bf16[16,2,4352]{2,1,0:T(2,128)(2,1)}), bf16[16,2,4352]{2,1,0:T(2,128)(2,1)S(1)}, u32[]{:S(2)}, u32[]{:S(2)}) async-start(bf16[16,2,4352]{2,1,0:T(2,128)(2,1)} %broadcast_in_dim.79), calls=%async_computation.3 | async-start | bytes 557056 | tf_op jit(solution)/shard_map/all_to_all | solution.py:32
  91.4 3.1 %collective-permute-start.6 = (bf16[512,256]{1,0:T(8,128)(2,1)}, bf16[512,256]{1,0:T(8,128)(2,1)}, u32[]{:S(2)}, u32[]{:S(2)}) collective-permute-start(bf16[512,256]{1,0:T(8,128)(2,1)} %get-tuple-element.5), channel_id=1, source_target_pairs={{0,8},{1,9},{2,10},{3,11},{4,12},{5,13},{6,14},{7,15},{8,0},{9,1},... | collective-permute-start | bytes 786440 | tf_op jit(solution)/shard_map/ppermute | solution.py:37
  94.5 3.9 %collective-permute-start.7 = (bf16[512,256]{1,0:T(8,128)(2,1)}, bf16[512,256]{1,0:T(8,128)(2,1)}, u32[]{:S(2)}, u32[]{:S(2)}) collective-permute-start(bf16[512,256]{1,0:T(8,128)(2,1)} %get-tuple-element.7), channel_id=1, source_target_pairs={{0,12},{1,13},{2,14},{3,15},{4,8},{5,9},{6,10},{7,11},{8,4},{9,5},... | collective-permute-start | bytes 786440 | tf_op jit(solution)/shard_map/ppermute | solution.py:37
  98.5 2.2 %collective-permute-start.8 = (bf16[512,256]{1,0:T(8,128)(2,1)}, bf16[512,256]{1,0:T(8,128)(2,1)}, u32[]{:S(2)}, u32[]{:S(2)}) collective-permute-start(bf16[512,256]{1,0:T(8,128)(2,1)} %get-tuple-element.6), channel_id=1, source_target_pairs={{0,4},{1,5},{2,6},{3,7},{4,0},{5,1},{6,2},{7,3},{8,12},{9,13},{10,... | collective-permute-start | bytes 786440 | tf_op jit(solution)/shard_map/ppermute | solution.py:37
  100.7 1.9 %collective-permute-start.5 = (bf16[16,2,4352]{2,1,0:T(2,128)(2,1)S(1)}, bf16[16,2,4352]{2,1,0:T(2,128)(2,1)S(1)}, u32[]{:S(2)}, u32[]{:S(2)}) collective-permute-start(bf16[16,2,4352]{2,1,0:T(2,128)(2,1)S(1)} %all-to-all-done.3), channel_id=1, source_target_pairs={{0,16},{16,0},{32,48},{48,32},{64,80},{80,64},{96,112},{112,96},{1... | collective-permute-start | bytes 835592 | tf_op jit(solution)/shard_map/ppermute | solution.py:37
  107.4 3.7 %all-to-all-start.4 = ((f32[4,1,512]{2,1,0:T(1,128)}), f32[4,1,512]{2,1,0:T(1,128)S(1)}, u32[]{:S(2)}, u32[]{:S(2)}) async-start(f32[4,1,512]{2,1,0:T(1,128)} %broadcast_in_dim.81), calls=%async_computation.4 | async-start | bytes 16384 | tf_op jit(solution)/shard_map/all_to_all | solution.py:32
  111.1 1.8 %fusion.8 = f32[1024,512]{1,0:T(8,128)} fusion(bf16[1024,16]{0,1:T(8,128)(2,1)S(1)} %fusion.3, bf16[512,2,8]{0,2,1:T(8,128)(2,1)S(1)} %copy.47, bf16[]{:T(256)S(6)} %convert_element_type.172), kind=kOutput, calls=%fused_computation.38 | convolution fusion | flops 16793600 | bytes 2146306 | tf_op jit(solution)/shard_map/dot_general | solution.py:226
  112.9 1.3 %fusion.6 = bf16[256,512]{0,1:T(8,128)(2,1)S(1)} fusion(bf16[512,256]{1,0:T(8,128)(2,1)} %collective-permute-done.8, bf16[512,256]{1,0:T(8,128)(2,1)} %collective-permute-done.7, bf16[512,256]{1,0:T(8,128)(2,1)} %collective-permute-done.6, f32[]{:T(128)S(6)} %convert_element_type.160, bf16[512,1024]{1,0:T(8,128)(2,1)} %copy-done.1, s32[]{:T(128)S(6)} %select_n.62), kind=kLoop, calls=%fused_computation.26 | loop fusion | flops 1179648 | bytes 1310728 | tf_op jit(solution)/shard_map/transpose | solution.py:210
  114.6 1.8 %all-to-all-done.4 = f32[4,1,512]{2,1,0:T(1,128)S(1)} async-done(((f32[4,1,512]{2,1,0:T(1,128)}), f32[4,1,512]{2,1,0:T(1,128)S(1)}, u32[]{:S(2)}, u32[]{:S(2)}) %all-to-all-start.4) | async-done | bytes 8224 | tf_op jit(solution)/shard_map/all_to_all | solution.py:32
  117.3 6.5 %all-to-all-start.5 = ((bf16[4,66,512]{2,1,0:T(8,128)(2,1)}), bf16[4,66,512]{2,1,0:T(8,128)(2,1)S(1)}, u32[]{:S(2)}, u32[]{:S(2)}) async-start(bf16[4,66,512]{2,1,0:T(8,128)(2,1)} %pad_maximum_fusion.2), calls=%async_computation.5 | async-start | bytes 589824 | tf_op jit(solution)/shard_map/all_to_all | solution.py:219
  127.1 3.5 %add_convert_fusion = bf16[1024,512]{1,0:T(8,128)(2,1)} fusion(f32[1024,512]{1,0:T(8,128)} %fusion.8, bf16[1024,512]{1,0:T(8,128)(2,1)S(1)} %bitcast.99, bf16[512,512]{1,0:T(8,128)(2,1)} %bitcast.110, f32[]{:T(128)S(6)} %convert_element_type.171), kind=kOutput, calls=%fused_computation.2 | convolution fusion | flops 538443776 | bytes 4718596 | tf_op jit(solution)/shard_map/dot_general | solution.py:227
  (113 shorter events, 25.3 us)
Async XLA Ops:
  0.6 58.5 %copy-start = (bf16[1024,512]{1,0:T(8,128)(2,1)S(1)}, bf16[1024,512]{1,0:T(8,128)(2,1)}, u32[]{:S(2)}) copy-start(bf16[1024,512]{1,0:T(8,128)(2,1)} %param.9) | copy-start | bytes 3145732
  2.3 13.7 %all-to-all-start = ((bf16[4,64,512]{2,1,0:T(8,128)(2,1)}), bf16[4,64,512]{2,1,0:T(8,128)(2,1)S(1)}, u32[]{:S(2)}, u32[]{:S(2)}) async-start(bf16[4,64,512]{2,1,0:T(8,128)(2,1)} %broadcast_in_dim.67), calls=%async_computation | async-start | bytes 524288 | tf_op jit(solution)/shard_map/all_to_all | solution.py:32
  12.8 8.5 %collective-permute-start = (bf16[32,4352]{1,0:T(8,128)(2,1)S(1)}, bf16[32,4352]{1,0:T(8,128)(2,1)S(1)}, u32[]{:S(2)}, u32[]{:S(2)}) collective-permute-start(bf16[32,4352]{1,0:T(8,128)(2,1)S(1)} %convolution_convert_fusion), channel_id=1, source_target_pairs={{0,16},{16,0},{32,48},{48,32},{64,80},{80,64},{96,112},{112,96},{1... | collective-permute-start | bytes 835592 | tf_op jit(solution)/shard_map/ppermute | solution.py:37
  16.0 32.6 %collective-permute-start.2 = (bf16[256,512]{1,0:T(8,128)(2,1)S(1)}, bf16[256,512]{1,0:T(8,128)(2,1)S(1)}, u32[]{:S(2)}, u32[]{:S(2)}) collective-permute-start(bf16[256,512]{1,0:T(8,128)(2,1)S(1)} %bitcast.100), channel_id=1, source_target_pairs={{0,4},{1,5},{2,6},{3,7},{4,0},{5,1},{6,2},{7,3},{8,12},{9,13},{10,... | collective-permute-start | bytes 786440 | tf_op jit(solution)/shard_map/ppermute | solution.py:37
  19.4 19.5 %copy-start.4 = (s32[1,3]{1,0:T(1,128)S(1)}, s32[1,3]{1,0:T(1,128)}, u32[]{:S(2)}) copy-start(s32[1,3]{1,0:T(1,128)} %param.11) | copy-start | bytes 40
  23.2 35.2 %all-to-all-start.1 = ((bf16[16,2,8448]{2,1,0:T(2,128)(2,1)}), bf16[16,2,8448]{2,1,0:T(2,128)(2,1)S(1)}, u32[]{:S(2)}, u32[]{:S(2)}) async-start(bf16[16,2,8448]{2,1,0:T(2,128)(2,1)} %pad_maximum_fusion), calls=%async_computation.1 | async-start | bytes 1081344 | tf_op jit(solution)/shard_map/all_to_all | solution.py:112
  41.4 11.4 %collective-permute-start.3 = (bf16[256,512]{1,0:T(8,128)(2,1)S(1)}, bf16[256,512]{1,0:T(8,128)(2,1)S(1)}, u32[]{:S(2)}, u32[]{:S(2)}) collective-permute-start(bf16[256,512]{1,0:T(8,128)(2,1)S(1)} %bitcast.102), channel_id=1, source_target_pairs={{0,8},{1,9},{2,10},{3,11},{4,12},{5,13},{6,14},{7,15},{8,0},{9,1},... | collective-permute-start | bytes 786440 | tf_op jit(solution)/shard_map/ppermute | solution.py:37
  46.1 12.2 %collective-permute-start.4 = (bf16[256,512]{1,0:T(8,128)(2,1)S(1)}, bf16[256,512]{1,0:T(8,128)(2,1)S(1)}, u32[]{:S(2)}, u32[]{:S(2)}) collective-permute-start(bf16[256,512]{1,0:T(8,128)(2,1)S(1)} %bitcast.103), channel_id=1, source_target_pairs={{0,12},{1,13},{2,14},{3,15},{4,8},{5,9},{6,10},{7,11},{8,4},{9,5},... | collective-permute-start | bytes 786440 | tf_op jit(solution)/shard_map/ppermute | solution.py:37
  61.3 12.4 %all-to-all-start.2 = ((bf16[16,4,512]{2,1,0:T(4,128)(2,1)}), bf16[16,4,512]{2,1,0:T(4,128)(2,1)S(1)}, u32[]{:S(2)}, u32[]{:S(2)}) async-start(bf16[16,4,512]{2,1,0:T(4,128)(2,1)} %pad_maximum_fusion.3), calls=%async_computation.2 | async-start | bytes 131072 | tf_op jit(solution)/shard_map/all_to_all | solution.py:145
  69.0 19.6 %collective-permute-start.1 = (bf16[16,16,512]{2,1,0:T(8,128)(2,1)S(1)}, bf16[16,16,512]{2,1,0:T(8,128)(2,1)}, u32[]{:S(2)}, u32[]{:S(2)}) collective-permute-start(bf16[16,16,512]{2,1,0:T(8,128)(2,1)S(1)} %reshape.168), channel_id=1, source_target_pairs={{0,16},{16,0},{32,48},{48,32},{64,80},{80,64},{96,112},{112,96},{1... | collective-permute-start | bytes 786440 | tf_op jit(solution)/shard_map/ppermute | solution.py:37
  76.4 24.2 %all-to-all-start.3 = ((bf16[16,2,4352]{2,1,0:T(2,128)(2,1)}), bf16[16,2,4352]{2,1,0:T(2,128)(2,1)S(1)}, u32[]{:S(2)}, u32[]{:S(2)}) async-start(bf16[16,2,4352]{2,1,0:T(2,128)(2,1)} %broadcast_in_dim.79), calls=%async_computation.3 | async-start | bytes 557056 | tf_op jit(solution)/shard_map/all_to_all | solution.py:32
  89.6 1.8 %copy-start.2 = (bf16[16,2,16,512]{3,2,1,0:T(8,128)(2,1)}, bf16[16,2,16,512]{3,2,1,0:T(8,128)(2,1)S(1)}, u32[]{:S(2)}) copy-start(bf16[16,2,16,512]{3,2,1,0:T(8,128)(2,1)S(1)} %pad_maximum_fusion.1) | copy-start | bytes 1572868
  90.4 8.1 %copy-start.1 = (bf16[512,1024]{1,0:T(8,128)(2,1)}, bf16[512,1024]{1,0:T(8,128)(2,1)S(1)}, u32[]{:S(2)}) copy-start(bf16[512,1024]{1,0:T(8,128)(2,1)S(1)} %convolution_convert_fusion.1) | copy-start | bytes 3145732
  91.4 21.5 %collective-permute-start.6 = (bf16[512,256]{1,0:T(8,128)(2,1)}, bf16[512,256]{1,0:T(8,128)(2,1)}, u32[]{:S(2)}, u32[]{:S(2)}) collective-permute-start(bf16[512,256]{1,0:T(8,128)(2,1)} %get-tuple-element.5), channel_id=1, source_target_pairs={{0,8},{1,9},{2,10},{3,11},{4,12},{5,13},{6,14},{7,15},{8,0},{9,1},... | collective-permute-start | bytes 786440 | tf_op jit(solution)/shard_map/ppermute | solution.py:37
  94.5 18.4 %collective-permute-start.7 = (bf16[512,256]{1,0:T(8,128)(2,1)}, bf16[512,256]{1,0:T(8,128)(2,1)}, u32[]{:S(2)}, u32[]{:S(2)}) collective-permute-start(bf16[512,256]{1,0:T(8,128)(2,1)} %get-tuple-element.7), channel_id=1, source_target_pairs={{0,12},{1,13},{2,14},{3,15},{4,8},{5,9},{6,10},{7,11},{8,4},{9,5},... | collective-permute-start | bytes 786440 | tf_op jit(solution)/shard_map/ppermute | solution.py:37
  98.5 14.4 %collective-permute-start.8 = (bf16[512,256]{1,0:T(8,128)(2,1)}, bf16[512,256]{1,0:T(8,128)(2,1)}, u32[]{:S(2)}, u32[]{:S(2)}) collective-permute-start(bf16[512,256]{1,0:T(8,128)(2,1)} %get-tuple-element.6), channel_id=1, source_target_pairs={{0,4},{1,5},{2,6},{3,7},{4,0},{5,1},{6,2},{7,3},{8,12},{9,13},{10,... | collective-permute-start | bytes 786440 | tf_op jit(solution)/shard_map/ppermute | solution.py:37
  100.7 3.5 %collective-permute-start.5 = (bf16[16,2,4352]{2,1,0:T(2,128)(2,1)S(1)}, bf16[16,2,4352]{2,1,0:T(2,128)(2,1)S(1)}, u32[]{:S(2)}, u32[]{:S(2)}) collective-permute-start(bf16[16,2,4352]{2,1,0:T(2,128)(2,1)S(1)} %all-to-all-done.3), channel_id=1, source_target_pairs={{0,16},{16,0},{32,48},{48,32},{64,80},{80,64},{96,112},{112,96},{1... | collective-permute-start | bytes 835592 | tf_op jit(solution)/shard_map/ppermute | solution.py:37
  107.4 9.0 %all-to-all-start.4 = ((f32[4,1,512]{2,1,0:T(1,128)}), f32[4,1,512]{2,1,0:T(1,128)S(1)}, u32[]{:S(2)}, u32[]{:S(2)}) async-start(f32[4,1,512]{2,1,0:T(1,128)} %broadcast_in_dim.81), calls=%async_computation.4 | async-start | bytes 16384 | tf_op jit(solution)/shard_map/all_to_all | solution.py:32
  117.3 13.3 %all-to-all-start.5 = ((bf16[4,66,512]{2,1,0:T(8,128)(2,1)}), bf16[4,66,512]{2,1,0:T(8,128)(2,1)S(1)}, u32[]{:S(2)}, u32[]{:S(2)}) async-start(bf16[4,66,512]{2,1,0:T(8,128)(2,1)} %pad_maximum_fusion.2), calls=%async_computation.5 | async-start | bytes 589824 | tf_op jit(solution)/shard_map/all_to_all | solution.py:219
  127.1 4.5 %copy-start.3 = (bf16[32,1024]{1,0:T(8,128)(2,1)S(1)}, bf16[32,1024]{1,0:T(8,128)(2,1)}, u32[]{:S(2)}) copy-start(bf16[32,1024]{1,0:T(8,128)(2,1)} %param.13) | copy-start | bytes 196612
